TPU v7x, 32 devices: a whole 2x2x4 slice. The times are simulated.
32 devices in a mesh: parts: 2 (over x), seq: 16 (over z, y, core).
Axes of the slice: x: 2, y: 2, z: 4, core: 2. Of those that a mesh axis runs over, the one named last changes fastest.
Arguments:
- tokens: bfloat16 [131072, 512], P(('parts', 'seq')), parts along dimension 0, may hold values from -6 to 6
- w_value: bfloat16 [512, 512], replicated, may hold values from -0.25 to 0.25
- w_gate: bfloat16 [512, 512], replicated, may hold values from -0.25 to 0.25
- first_block: bfloat16 [256, 256], replicated, may hold values from -0.375 to 0.375
- second_block: bfloat16 [256, 256], replicated, may hold values from -0.375 to 0.375
- third_block: bfloat16 [256, 256], replicated, may hold values from -0.375 to 0.375
- fourth_block: bfloat16 [256, 256], replicated, may hold values from -0.375 to 0.375
- kernel: bfloat16 [512, 256, 256], P('seq'), may hold values from -6 to 6
- skip_gain: float32 [512], replicated, may hold values from 0.25 to 2
- cotangent: bfloat16 [131072, 512], P(('parts', 'seq')), parts along dimension 0, may hold values from -6 to 6
Outputs:
- grad_tokens: bfloat16 [131072, 512], P(('parts', 'seq')), parts along dimension 0
- grad_kernel: bfloat16 [1024, 256, 256], P(('parts', 'seq')), parts along dimension 0
- grad_weights: float32 [4, 512, 512], P('parts'), parts along dimension 0
- grad_skip: float32 [1024], P('parts'), parts along dimension 0
There are 2 independent parts, one for each index of `parts`. A program takes and returns all parts, laid end to end along the dimension named above; an argument that names none is the same for every part. Nothing has to cross between parts.
All inputs are finite; a program needn't handle non-finite values.
Results may differ from a plain program's by a relative error of at most 0.025.
Values may be sent and summed in bfloat16 or wider, within the bound.
No kernel may reach another device: no remote copies, remote signals or barrier semaphores. Data moves between devices by JAX's collectives and lax.ppermute only.
A program may use at most 128 MiB of HBM per device.

v0:
```python
import jax
import jax.numpy as jnp
from jax import lax
from jax.sharding import PartitionSpec as P

D = 512
N1 = 256
N2 = 256


def on_device(
    tokens,
    w_value,
    w_gate,
    first_block,
    second_block,
    third_block,
    fourth_block,
    kernel,
    skip_gain,
    cotangent,
):
    f32 = jnp.float32
    bf16 = jnp.bfloat16
    n_devices = lax.axis_size("seq")
    rows_here = N1 // n_devices
    local_rows = tokens.shape[0]
    value = jnp.dot(tokens, w_value, preferred_element_type=f32).astype(bf16)
    gate = jnp.dot(tokens, w_gate, preferred_element_type=f32).astype(bf16)
    cube = value.reshape(rows_here, N2, D)
    section_one = jnp.einsum("abc,pb->cap", cube, first_block, preferred_element_type=f32).astype(
        bf16
    )
    spectrum = jnp.einsum(
        "cap,qa->cqp",
        lax.all_to_all(section_one, "seq", split_axis=0, concat_axis=1, tiled=True),
        second_block,
        preferred_element_type=f32,
    )
    filtered = (spectrum * kernel.astype(f32)).astype(bf16)
    section_three = jnp.einsum(
        "cqp,rq->crp", filtered, third_block, preferred_element_type=f32
    ).astype(bf16)
    split_three = section_three.reshape(section_three.shape[0], n_devices, rows_here, N2)
    conv = jnp.einsum(
        "crp,sp->rsc",
        lax.all_to_all(split_three, "seq", split_axis=1, concat_axis=0, tiled=True)[:, 0],
        fourth_block,
        preferred_element_type=f32,
    )
    mixed = conv.reshape(local_rows, D) + skip_gain * value.astype(f32)
    upstream = cotangent.astype(f32)
    d_mix = (upstream * gate.astype(f32)).astype(bf16)
    d_gate = (upstream * mixed).astype(bf16)
    d_mix_cube = d_mix.reshape(rows_here, N2, D)
    d_three = jnp.einsum(
        "rsc,sp->crp", d_mix_cube, fourth_block, preferred_element_type=f32
    ).astype(bf16)
    d_freq = jnp.einsum(
        "crp,rq->cqp",
        lax.all_to_all(d_three, "seq", split_axis=0, concat_axis=1, tiled=True),
        third_block,
        preferred_element_type=f32,
    )
    grad_kernel = (d_freq * spectrum).astype(bf16)
    d_spec = (d_freq * kernel.astype(f32)).astype(bf16)
    d_one = jnp.einsum("cqp,qa->cap", d_spec, second_block, preferred_element_type=f32).astype(bf16)
    split_one = d_one.reshape(d_one.shape[0], n_devices, rows_here, N2)
    d_cube = jnp.einsum(
        "cap,pb->abc",
        lax.all_to_all(split_one, "seq", split_axis=1, concat_axis=0, tiled=True)[:, 0],
        first_block,
        preferred_element_type=f32,
    )
    d_value = (d_cube.reshape(local_rows, D) + skip_gain * d_mix.astype(f32)).astype(bf16)
    grad_tokens = (
        jnp.dot(d_value, w_value.T, preferred_element_type=f32)
        + jnp.dot(d_gate, w_gate.T, preferred_element_type=f32)
    ).astype(bf16)
    factor = 1.0 / jnp.sqrt(jnp.asarray(N1 * N2, f32))
    value_term = jnp.dot(tokens.T, d_value, preferred_element_type=f32) * factor
    gate_term = jnp.dot(tokens.T, d_gate, preferred_element_type=f32) * factor
    skip_term = jnp.sum(d_mix.astype(f32) * value.astype(f32), axis=0) * factor
    value_total, gate_total, skip_total = (
        lax.psum(value_term.astype(jnp.bfloat16), "seq").astype(jnp.float32),
        lax.psum(gate_term.astype(jnp.bfloat16), "seq").astype(jnp.float32),
        lax.psum(skip_term.astype(jnp.bfloat16), "seq").astype(jnp.float32),
    )
    return (grad_tokens, grad_kernel, jnp.stack([value_total, gate_total]), skip_total)


def solution(mesh):
    in_specs = (
        P(("parts", "seq"), None),
        P(),
        P(),
        P(),
        P(),
        P(),
        P(),
        P("seq", None, None),
        P(),
        P(("parts", "seq"), None),
    )
    out_specs = (
        P(("parts", "seq"), None),
        P(("parts", "seq"), None, None),
        P("parts", None, None),
        P("parts"),
    )
    return jax.shard_map(
        on_device, mesh=mesh, in_specs=in_specs, out_specs=out_specs, check_vma=False
    )
```

profile of v0, /device:TPU:0, one launch (start us, length us, event | category | flops | bytes accessed | tf_op | source)
XLA Modules:
  0.0 597.7 jit_solution(15915618487453710336)
XLA Ops:
  7.2 6.0 %fusion = bf16[4096,512]{1,0:T(8,128)(2,1)S(1)} fusion(bf16[4096,512]{1,0:T(8,128)(2,1)} %param.19, bf16[4096,512]{1,0:T(8,128)(2,1)} %param.10, bf16[512,512]{1,0:T(8,128)(2,1)} %param.12), kind=kOutput, calls=%fused_computation.7 | convolution fusion | flops 2157969408 | bytes 13107200 | tf_op jit(solution)/shard_map/dot_general | solution.py:29
  16.5 4.4 copy.60
  20.9 7.4 %all-to-all-start = ((bf16[512,16,256]{2,1,0:T(8,128)(2,1)}), bf16[512,16,256]{2,1,0:T(8,128)(2,1)}, u32[]{:S(2)}, u32[]{:S(2)}) async-start(bf16[512,16,256]{2,1,0:T(8,128)(2,1)} %copy.60), calls=%async_computation | async-start | bytes 8388608 | tf_op jit(solution)/shard_map/all_to_all | solution.py:61
  28.4 4.6 convolution_convert_fusion
  36.3 4.4 copy.70
  40.7 65.4 %all-to-all-done = bf16[512,16,256]{2,1,0:T(8,128)(2,1)} async-done(((bf16[512,16,256]{2,1,0:T(8,128)(2,1)}), bf16[512,16,256]{2,1,0:T(8,128)(2,1)}, u32[]{:S(2)}, u32[]{:S(2)}) %all-to-all-start) | async-done | bytes 4194336 | tf_op jit(solution)/shard_map/all_to_all | solution.py:61
  106.0 19.7 %all-to-all-start.2 = ((bf16[512,16,256]{2,1,0:T(8,128)(2,1)}), bf16[512,16,256]{2,1,0:T(8,128)(2,1)}, u32[]{:S(2)}, u32[]{:S(2)}) async-start(bf16[512,16,256]{2,1,0:T(8,128)(2,1)} %copy.70), calls=%async_computation.2 | async-start | bytes 8388608 | tf_op jit(solution)/shard_map/all_to_all | solution.py:36
  125.7 6.4 %copy.63 = bf16[32,256,256]{1,2,0:T(8,128)(2,1)} copy(bf16[32,256,256]{2,1,0:T(8,128)(2,1)} %param.17) | data formatting | bytes 8388608 | tf_op args[7]
  132.2 4.7 copy.61
  136.8 66.6 %all-to-all-done.2 = bf16[512,16,256]{2,1,0:T(8,128)(2,1)} async-done(((bf16[512,16,256]{2,1,0:T(8,128)(2,1)}), bf16[512,16,256]{2,1,0:T(8,128)(2,1)}, u32[]{:S(2)}, u32[]{:S(2)}) %all-to-all-start.2) | async-done | bytes 4194336 | tf_op jit(solution)/shard_map/all_to_all | solution.py:36
  217.6 19.7 %all-to-all-start.3 = ((bf16[32,16,16,256]{3,2,0,1:T(8,128)(2,1)}), bf16[32,16,16,256]{3,2,0,1:T(8,128)(2,1)}, u32[]{:S(2)}, u32[]{:S(2)}) async-start(bf16[32,16,16,256]{3,2,0,1:T(8,128)(2,1)} %copy.74), calls=%async_computation.3 | async-start | bytes 8388608 | tf_op jit(solution)/shard_map/all_to_all | solution.py:47
  237.3 6.0 fusion.13
  245.6 69.4 %all-to-all-done.3 = bf16[32,16,16,256]{3,2,0,1:T(8,128)(2,1)} async-done(((bf16[32,16,16,256]{3,2,0,1:T(8,128)(2,1)}), bf16[32,16,16,256]{3,2,0,1:T(8,128)(2,1)}, u32[]{:S(2)}, u32[]{:S(2)}) %all-to-all-start.3) | async-done | bytes 4194336 | tf_op jit(solution)/shard_map/all_to_all | solution.py:47
  314.9 19.7 %all-to-all-start.1 = ((bf16[32,16,16,256]{3,2,0,1:T(8,128)(2,1)}), bf16[32,16,16,256]{3,2,0,1:T(8,128)(2,1)}, u32[]{:S(2)}, u32[]{:S(2)}) async-start(bf16[32,16,16,256]{3,2,0,1:T(8,128)(2,1)} %copy.66), calls=%async_computation.1 | async-start | bytes 8388608 | tf_op jit(solution)/shard_map/all_to_all | solution.py:71
  334.7 6.4 %copy.76 = bf16[32,256,256]{2,1,0:T(8,128)(2,1)} copy(bf16[32,256,256]{1,2,0:T(8,128)(2,1)} %get-tuple-element.25) | data formatting | bytes 8388608
  344.7 4.5 fusion.32
  349.3 63.0 %all-to-all-done.1 = bf16[32,16,16,256]{3,2,0,1:T(8,128)(2,1)} async-done(((bf16[32,16,16,256]{3,2,0,1:T(8,128)(2,1)}), bf16[32,16,16,256]{3,2,0,1:T(8,128)(2,1)}, u32[]{:S(2)}, u32[]{:S(2)}) %all-to-all-start.1) | async-done | bytes 4194336 | tf_op jit(solution)/shard_map/all_to_all | solution.py:71
  416.1 4.5 fusion.24
  420.6 10.9 %fusion.7 = (f32[512]{0:T(512)S(1)}, bf16[4096,512]{1,0:T(8,128)(2,1)}, bf16[4096,512]{1,0:T(8,128)(2,1)S(1)}) fusion(bf16[4096,512]{1,0:T(8,128)(2,1)} %copy-done.6, bf16[4096,512]{1,0:T(8,128)(2,1)} %copy-done.5, f32[512]{0:T(512)S(1)} %copy-done.13, f32[512,16,256]{0,2,1:T(8,128)} %fusion.24, f32[512,16,256]{0,2,1:T(8,128)S(1)} %bitcast.101, ...), kind=kLoop, calls=%fused_computation.14 | loop fusion | flops 25165312 | bytes 37752832 | tf_op jit(solution)/shard_map/reduce_sum | solution.py:83
  431.5 8.2 %fusion.22 = bf16[1,512,512]{1,2,0:T(8,128)(2,1)} fusion(bf16[4096,512]{1,0:T(8,128)(2,1)} %get-tuple-element.23, bf16[4096,512]{1,0:T(8,128)(2,1)} %param.10), kind=kOutput, calls=%fused_computation.31 | convolution fusion | flops 2148007936 | bytes 8912896 | tf_op jit(solution)/shard_map/dot_general | solution.py:81
  439.7 5.9 fusion.35
  448.7 47.7 %psum.23 = bf16[512]{0:T(512)(128)(2,1)S(1)} all-reduce(bf16[512]{0:T(512)(128)(2,1)S(1)} %multiply_convert_fusion), channel_id=1, replica_groups=mesh['parts'=2,'seq'=16] {'seq'}, use_global_device_ids=true, to_apply=%region_3.0 | all-reduce | flops 512 | bytes 2048 | tf_op jit(solution)/shard_map/psum | solution.py:87
  497.0 9.2 %add_convert_fusion = bf16[4096,512]{1,0:T(8,128)(2,1)} fusion(f32[4096,512]{1,0:T(8,128)} %fusion.35, bf16[4096,512]{1,0:T(8,128)(2,1)} %copy-done.3, bf16[512,512]{1,0:T(8,128)(2,1)S(1)} %copy-done.12), kind=kOutput, calls=%fused_computation.17 | convolution fusion | flops 2151677952 | bytes 17301504 | tf_op jit(solution)/shard_map/dot_general | solution.py:78
  506.2 81.5 %all-reduce.3.cloned.1.call-done = (bf16[1,512,512]{1,2,0:T(8,128)(2,1)}, bf16[1,512,512]{1,2,0:T(8,128)(2,1)}) async-done(((bf16[1,512,512]{1,2,0:T(8,128)(2,1)}, bf16[1,512,512]{1,2,0:T(8,128)(2,1)}), (bf16[1,512,512]{1,2,0:T(8,128)(2,1)}, bf16[1,512,512]{1,2,0:T(8,128)(2,1)})) %all-reduce.3.cloned.1.call-update) | async-done | bytes 1048592 | tf_op jit(solution)/shard_map/psum | solution.py:86
  (52 shorter events, 37.5 us)
Async XLA Ops:
  7.2 21.2 %copy-start = (bf16[512,512]{1,0:T(8,128)(2,1)S(1)}, bf16[512,512]{1,0:T(8,128)(2,1)}, u32[]{:S(2)}) copy-start(bf16[512,512]{1,0:T(8,128)(2,1)} %param.11) | copy-start | bytes 1572868
  7.2 8.0 %copy-start.10 = (bf16[256,256]{1,0:T(8,128)(2,1)S(1)}, bf16[256,256]{1,0:T(8,128)(2,1)}, u32[]{:S(2)}) copy-start(bf16[256,256]{1,0:T(8,128)(2,1)} %param.16) | copy-start | bytes 393220
  13.2 1.9 copy-start.5
  20.9 85.1 %all-to-all-start = ((bf16[512,16,256]{2,1,0:T(8,128)(2,1)}), bf16[512,16,256]{2,1,0:T(8,128)(2,1)}, u32[]{:S(2)}, u32[]{:S(2)}) async-start(bf16[512,16,256]{2,1,0:T(8,128)(2,1)} %copy.60), calls=%async_computation | async-start | bytes 8388608 | tf_op jit(solution)/shard_map/all_to_all | solution.py:61
  28.4 6.6 %copy-start.11 = (bf16[256,256]{1,0:T(8,128)(2,1)S(1)}, bf16[256,256]{1,0:T(8,128)(2,1)}, u32[]{:S(2)}) copy-start(bf16[256,256]{1,0:T(8,128)(2,1)} %param.13) | copy-start | bytes 393220
  33.0 2.0 copy-start.6
  106.0 97.4 %all-to-all-start.2 = ((bf16[512,16,256]{2,1,0:T(8,128)(2,1)}), bf16[512,16,256]{2,1,0:T(8,128)(2,1)}, u32[]{:S(2)}, u32[]{:S(2)}) async-start(bf16[512,16,256]{2,1,0:T(8,128)(2,1)} %copy.70), calls=%async_computation.2 | async-start | bytes 8388608 | tf_op jit(solution)/shard_map/all_to_all | solution.py:36
  203.4 3.4 copy-start.7
  203.4 3.5 copy-start.8
  206.9 1.3 copy-start.9
  208.2 5.6 copy-start.1
  208.2 5.6 copy-start.2
  217.6 97.4 %all-to-all-start.3 = ((bf16[32,16,16,256]{3,2,0,1:T(8,128)(2,1)}), bf16[32,16,16,256]{3,2,0,1:T(8,128)(2,1)}, u32[]{:S(2)}, u32[]{:S(2)}) async-start(bf16[32,16,16,256]{3,2,0,1:T(8,128)(2,1)} %copy.74), calls=%async_computation.3 | async-start | bytes 8388608 | tf_op jit(solution)/shard_map/all_to_all | solution.py:47
  314.9 97.4 %all-to-all-start.1 = ((bf16[32,16,16,256]{3,2,0,1:T(8,128)(2,1)}), bf16[32,16,16,256]{3,2,0,1:T(8,128)(2,1)}, u32[]{:S(2)}, u32[]{:S(2)}) async-start(bf16[32,16,16,256]{3,2,0,1:T(8,128)(2,1)} %copy.66), calls=%async_computation.1 | async-start | bytes 8388608 | tf_op jit(solution)/shard_map/all_to_all | solution.py:71
  334.6 253.1 %all-reduce.3.cloned.1.call-start = ((), (), s32[]{:S(2)}) async-start(), calls=%async_computation.4 | async-start | bytes 2097152 | tf_op jit(solution)/shard_map/psum | solution.py:86
  412.3 8.3 %slice-start = ((s8[8388608]{0:T(1024)(128)(4,1)}), s8[4194304]{0:T(1024)(128)(4,1)S(1)}, s32[]{:S(2)}) async-start(s8[8388608]{0:T(1024)(128)(4,1)} %bitcast.100), calls=%async_computation.5 | async-start | bytes 8388608
  416.1 4.5 slice-start.1
  416.1 4.5 copy-start.13
  431.5 14.1 %copy-start.3 = (bf16[4096,512]{1,0:T(8,128)(2,1)}, bf16[4096,512]{1,0:T(8,128)(2,1)S(1)}, u32[]{:S(2)}) copy-start(bf16[4096,512]{1,0:T(8,128)(2,1)S(1)} %get-tuple-element.24) | copy-start | bytes 12582916
  431.5 8.2 %copy-start.4 = (bf16[4096,512]{1,0:T(8,128)(2,1)S(1)}, bf16[4096,512]{1,0:T(8,128)(2,1)}, u32[]{:S(2)}) copy-start(bf16[4096,512]{1,0:T(8,128)(2,1)} %get-tuple-element.23) | copy-start | bytes 12582916
  439.7 5.9 copy-start.14
  445.6 51.5 %copy-start.12 = (bf16[512,512]{1,0:T(8,128)(2,1)S(1)}, bf16[512,512]{1,0:T(8,128)(2,1)}, u32[]{:S(2)}) copy-start(bf16[512,512]{1,0:T(8,128)(2,1)} %param.12) | copy-start | bytes 1572868
Sparse Core Ops, SparseCore 0:
  497.1 90.5 all-reduce.2
where the time goes:
time: 598 us
  waiting for transfers between devices  346 us (58%)
  starting transfers between devices  66.6 us (11%)
  matrix products  60.5 us (10%)
  local copies, waits for them, and re-layouts  50.1 us (8%)
  blocking collectives  47.7 us (8%)
  between operations  14.3 us (2%)
  other arithmetic  12.8 us (2%)
    psum x1, waiting for transfers between devices, on_device(): lax.psum(gate_term.astype(jnp.bfloat16), 'seq').astype(jnp.float32)  81.5 us
    all_to_all x1, waiting for transfers between devices, on_device(): lax.all_to_all(split_three, 'seq', split_axis=1, concat_axis=0, tiled=True)  69.4 us
    all_to_all x1, waiting for transfers between devices, on_device(): lax.all_to_all(section_one, 'seq', split_axis=0, concat_axis=1, tiled=True)  66.6 us
    all_to_all x1, waiting for transfers between devices, on_device(): lax.all_to_all(d_three, 'seq', split_axis=0, concat_axis=1, tiled=True)  65.4 us
    all_to_all x1, waiting for transfers between devices, on_device(): lax.all_to_all(split_one, 'seq', split_axis=1, concat_axis=0, tiled=True)  63 us
    psum x1, blocking collectives, on_device(): lax.psum(skip_term.astype(jnp.bfloat16), 'seq').astype(jnp.float32)  47.7 us
    unnamed x37, local copies, waits for them, and re-layouts  21.5 us
    all_to_all x1, starting transfers between devices, on_device(): lax.all_to_all(section_one, 'seq', split_axis=0, concat_axis=1, tiled=True)  19.7 us
  transfers between devices with their start and end apart: 5, of which 5 were waited for; matrix products, arithmetic and copies ran while one was open for 9% of the time, Pallas kernels for 0%

commit v1 on v0

v1 whole, which is shorter than its diff:
```python
import jax
import jax.numpy as jnp
from jax import lax
from jax.sharding import PartitionSpec as P

D = 512
N1 = 256
N2 = 256


def partners(n):
    return [0] + list(range(n - 1, 0, -1))


def exchange(pieces, steps):
    n = lax.axis_size("seq")
    out = []
    for piece, k in zip(pieces, steps):
        if k == 0:
            out.append(piece)
        else:
            out.append(lax.ppermute(piece, "seq", [(i, i ^ k) for i in range(n)]))
    return out


def swap(array, steps):
    me = lax.axis_index("seq")
    pieces = [lax.dynamic_index_in_dim(array, me ^ k, 0, keepdims=False) for k in steps]
    return jnp.stack(exchange(pieces, steps))


def on_device(
    tokens,
    w_value,
    w_gate,
    first_block,
    second_block,
    third_block,
    fourth_block,
    kernel,
    skip_gain,
    cotangent,
):
    f32 = jnp.float32
    bf16 = jnp.bfloat16
    n = lax.axis_size("seq")
    me = lax.axis_index("seq")
    rows = N1 // n
    chans = D // n
    local_rows = tokens.shape[0]
    steps = partners(n)
    order = me ^ jnp.array(steps)
    inverse = jnp.array([steps.index(k) for k in range(n)])[me ^ jnp.arange(n)]
    value = jnp.dot(tokens, w_value, preferred_element_type=f32).astype(bf16)
    gate = jnp.dot(tokens, w_gate, preferred_element_type=f32).astype(bf16)
    upstream = cotangent.astype(f32)
    d_mix = (upstream * gate.astype(f32)).astype(bf16)
    cube = value.reshape(rows, N2, D)
    section_one = jnp.einsum("abc,pb->cap", cube, first_block, preferred_element_type=f32).astype(
        bf16
    )
    one_in = swap(section_one.reshape(n, chans, rows, N2), steps)
    d_mix_cube = d_mix.reshape(rows, N2, D)
    d_three = jnp.einsum(
        "rsc,sp->crp", d_mix_cube, fourth_block, preferred_element_type=f32
    ).astype(bf16)
    three_in = swap(d_three.reshape(n, chans, rows, N2), steps)
    second_order = second_block.reshape(N1, n, rows)[:, order]
    third_order = third_block.reshape(n, rows, N1)[order]
    spectrum = jnp.einsum("kcap,qka->cqp", one_in, second_order, preferred_element_type=f32)
    filtered = (spectrum * kernel.astype(f32)).astype(bf16)
    section_three = jnp.einsum(
        "cqp,drq->dcrp", filtered, third_block.reshape(n, rows, N1), preferred_element_type=f32
    ).astype(bf16)
    three_out = swap(section_three, steps)[inverse]
    d_freq = jnp.einsum("kcrp,krq->cqp", three_in, third_order, preferred_element_type=f32)
    grad_kernel = (d_freq * spectrum).astype(bf16)
    d_spec = (d_freq * kernel.astype(f32)).astype(bf16)
    d_one = jnp.einsum(
        "cqp,qda->dcap", d_spec, second_block.reshape(N1, n, rows), preferred_element_type=f32
    ).astype(bf16)
    one_out = swap(d_one, steps)[inverse]
    conv = jnp.einsum(
        "kcrp,sp->rskc", three_out, fourth_block, preferred_element_type=f32
    )
    mixed = conv.reshape(local_rows, D) + skip_gain * value.astype(f32)
    d_gate = (upstream * mixed).astype(bf16)
    factor = 1.0 / jnp.sqrt(jnp.asarray(N1 * N2, f32))

    def total(term):
        parts = swap(term.astype(bf16).reshape(n, -1, D), steps)
        mine = jnp.sum(parts.astype(f32), axis=0).astype(bf16)
        got = jnp.stack(exchange([mine] * n, steps))[inverse]
        return got.reshape(term.shape).astype(f32)

    gate_total = total(jnp.dot(tokens.T, d_gate, preferred_element_type=f32) * factor)
    skip_term = jnp.sum(d_mix.astype(f32) * value.astype(f32), axis=0) * factor
    skip_total = lax.psum(skip_term.astype(bf16), "seq").astype(f32)
    d_cube = jnp.einsum("kcap,pb->abkc", one_out, first_block, preferred_element_type=f32)
    d_value = (d_cube.reshape(local_rows, D) + skip_gain * d_mix.astype(f32)).astype(bf16)
    grad_tokens = (
        jnp.dot(d_value, w_value.T, preferred_element_type=f32)
        + jnp.dot(d_gate, w_gate.T, preferred_element_type=f32)
    ).astype(bf16)
    value_total = total(jnp.dot(tokens.T, d_value, preferred_element_type=f32) * factor)
    return (grad_tokens, grad_kernel, jnp.stack([value_total, gate_total]), skip_total)


def solution(mesh):
    in_specs = (
        P(("parts", "seq"), None),
        P(),
        P(),
        P(),
        P(),
        P(),
        P(),
        P("seq", None, None),
        P(),
        P(("parts", "seq"), None),
    )
    out_specs = (
        P(("parts", "seq"), None),
        P(("parts", "seq"), None, None),
        P("parts", None, None),
        P("parts"),
    )
    return jax.shard_map(
        on_device, mesh=mesh, in_specs=in_specs, out_specs=out_specs, check_vma=False
    )
```

time: 598 us -> 819 us (1.37)
  starting transfers between devices: 66.6 us -> 233 us
  local copies, waits for them, and re-layouts: 50.1 us -> 144 us
  waiting for transfers between devices: 346 us -> 327 us
  blocking collectives: 47.7 us -> 31.8 us
  between operations: 14.3 us -> 2.17 us
    ppermute x0 -> x120, waiting for transfers between devices: none -> 327 us  [exchange(): out.append(lax.ppermute(piece, 'seq', [(i, i ^ k) for i in range(n)]))]
    all_to_all x4 -> x0, waiting for transfers between devices: 264 us -> none  [the longest x1 69.4 us: on_device(): lax.all_to_all(split_three, 'seq', split_axis=1, concat_axis=0, tiled=True)]
    ppermute x0 -> x120, starting transfers between devices: none -> 233 us  [exchange(): out.append(lax.ppermute(piece, 'seq', [(i, i ^ k) for i in range(n)]))]
    psum x1 -> x0, waiting for transfers between devices: 81.5 us -> none  [on_device(): lax.psum(gate_term.astype(jnp.bfloat16), 'seq').astype(jnp.float32)]
    all_to_all x4 -> x0, starting transfers between devices: 66.5 us -> none  [the longest x1 19.7 us: on_device(): lax.all_to_all(section_one, 'seq', split_axis=0, concat_axis=1, tiled=True)]
    another operation x0 -> x21, local copies, waits for them, and re-layouts: none -> 42.3 us  [the longest x19 42.3 us: swap(): return jnp.stack(exchange(pieces, steps))]
    unnamed x37 -> x142, local copies, waits for them, and re-layouts: 21.5 us -> 55.6 us
    psum x1, blocking collectives: 47.7 us -> 31.8 us  [on_device(): skip_total = lax.psum(skip_term.astype(bf16), 'seq').astype(f32)]
  transfers between devices with their start and end apart: 5 -> 120, of which waited for: 5 -> 62; matrix products, arithmetic and copies ran while one was open for 9% -> 10% of each run, Pallas kernels for 0% -> 0%
where the time goes in v1:
time: 819 us; the launch traced here: 812 us
  waiting for transfers between devices  327 us (40%)
  starting transfers between devices  233 us (28%)
  local copies, waits for them, and re-layouts  144 us (18%)
  matrix products  59.8 us (7%)
  blocking collectives  31.8 us (4%)
  other arithmetic  13.4 us (2%)
    ppermute x120, waiting for transfers between devices, exchange(): out.append(lax.ppermute(piece, 'seq', [(i, i ^ k) for i in range(n)]))  327 us
    ppermute x120, starting transfers between devices, exchange(): out.append(lax.ppermute(piece, 'seq', [(i, i ^ k) for i in range(n)]))  233 us
    unnamed x142, local copies, waits for them, and re-layouts  55.6 us
    another operation x19, local copies, waits for them, and re-layouts, swap(): return jnp.stack(exchange(pieces, steps))  42.3 us
    psum x1, blocking collectives, on_device(): skip_total = lax.psum(skip_term.astype(bf16), 'seq').astype(f32)  31.8 us
  transfers between devices with their start and end apart: 120, of which 62 were waited for; matrix products, arithmetic and copies ran while one was open for 10% of the time, Pallas kernels for 0%

profile of v1, /device:TPU:0, one launch (start us, length us, event | category | flops | bytes accessed | tf_op | source)
XLA Modules:
  0.0 812.2 jit_solution(6221799356309913970)
XLA Ops:
  42.6 11.3 %collective-permute-start.5 = (bf16[32,16,256]{2,1,0:T(8,128)(2,1)S(1)}, bf16[32,16,256]{2,1,0:T(8,128)(2,1)S(1)}, u32[]{:S(2)}, u32[]{:S(2)}) collective-permute-start(bf16[32,16,256]{2,1,0:T(8,128)(2,1)S(1)} %bitcast.741), channel_id=1, source_target_pairs={{0,10},{1,11},{2,8},{3,9},{4,14},{5,15},{6,12},{7,13},{8,2},{9,3},... | collective-permute-start | bytes 786440 | tf_op jit(solution)/shard_map/ppermute | solution.py:22
  54.9 9.0 %collective-permute-start.6 = (bf16[32,16,256]{2,1,0:T(8,128)(2,1)S(1)}, bf16[32,16,256]{2,1,0:T(8,128)(2,1)S(1)}, u32[]{:S(2)}, u32[]{:S(2)}) collective-permute-start(bf16[32,16,256]{2,1,0:T(8,128)(2,1)S(1)} %bitcast.740), channel_id=1, source_target_pairs={{0,9},{1,8},{2,11},{3,10},{4,13},{5,12},{6,15},{7,14},{8,1},{9,0},... | collective-permute-start | bytes 786440 | tf_op jit(solution)/shard_map/ppermute | solution.py:22
  64.9 10.6 %collective-permute-start.7 = (bf16[32,16,256]{2,1,0:T(8,128)(2,1)S(1)}, bf16[32,16,256]{2,1,0:T(8,128)(2,1)S(1)}, u32[]{:S(2)}, u32[]{:S(2)}) collective-permute-start(bf16[32,16,256]{2,1,0:T(8,128)(2,1)S(1)} %bitcast.739), channel_id=1, source_target_pairs={{0,8},{1,9},{2,10},{3,11},{4,12},{5,13},{6,14},{7,15},{8,0},{9,1},... | collective-permute-start | bytes 786440 | tf_op jit(solution)/shard_map/ppermute | solution.py:22
  122.3 13.3 %collective-permute-done.10 = bf16[32,16,256]{2,1,0:T(8,128)(2,1)S(1)} collective-permute-done((bf16[32,16,256]{2,1,0:T(8,128)(2,1)S(1)}, bf16[32,16,256]{2,1,0:T(8,128)(2,1)S(1)}, u32[]{:S(2)}, u32[]{:S(2)}) %collective-permute-start.10) | collective-permute-done | bytes 262176 | tf_op jit(solution)/shard_map/ppermute | solution.py:22
  137.8 9.1 %collective-permute-done.11 = bf16[32,16,256]{2,1,0:T(8,128)(2,1)S(1)} collective-permute-done((bf16[32,16,256]{2,1,0:T(8,128)(2,1)S(1)}, bf16[32,16,256]{2,1,0:T(8,128)(2,1)S(1)}, u32[]{:S(2)}, u32[]{:S(2)}) %collective-permute-start.11) | collective-permute-done | bytes 262176 | tf_op jit(solution)/shard_map/ppermute | solution.py:22
  157.9 25.7 %collective-permute-start.38 = (bf16[32,16,256]{2,1,0:T(8,128)(2,1)S(1)}, bf16[32,16,256]{2,1,0:T(8,128)(2,1)S(1)}, u32[]{:S(2)}, u32[]{:S(2)}) collective-permute-start(bf16[32,16,256]{2,1,0:T(8,128)(2,1)S(1)} %bitcast.725), channel_id=1, source_target_pairs={{0,7},{1,6},{2,5},{3,4},{4,3},{5,2},{6,1},{7,0},{8,15},{9,14},{10,... | collective-permute-start | bytes 786440 | tf_op jit(solution)/shard_map/ppermute | solution.py:22
  249.5 13.6 %fusion.17 = bf16[32,256,16,16]{1,3,2,0:T(8,128)(2,1)} fusion(bf16[256,16,16,1]{0,2,1,3:T(8,128)(2,1)S(1)} %bitcast.693, bf16[32,256,256]{2,1,0:T(8,128)(2,1)S(1)} %copy-done.5, f32[256,32,256,1]{2,0,3,1:T(8,128)S(1)} %fusion.32), kind=kOutput, calls=%fused_computation.33 | convolution fusion | flops 1082130432 | bytes 16908288 | tf_op jit(solution)/shard_map/cqp,qda->dcap/dot_general | solution.py:79
  263.1 22.8 %stack.387 = bf16[16,32,16,256]{3,0,2,1:T(8,128)(2,1)} concatenate(bf16[1,32,16,256]{3,0,2,1:T(2,128)(2,1)S(1)} %copy.193, bf16[1,32,16,256]{3,0,2,1:T(2,128)(2,1)S(1)} %copy.134, bf16[1,32,16,256]{3,0,2,1:T(2,128)(2,1)S(1)} %copy.135, bf16[1,32,16,256]{3,0,2,1:T(2,128)(2,1)S(1)} %copy.136, bf16[1,32,16,256]{3,0,2,1:T(2,128)(2,1)S(1)} %copy.137, bf16[1,32,16,256]{3,0,2,1:T(2,128)(2,1)} %copy.138, ...), dimensions={0} | concatenate | bytes 8388608 | tf_op jit(solution)/shard_map/stack | solution.py:29
  285.9 9.2 %fusion.8 = (bf16[32,256,256]{2,1,0:T(8,128)(2,1)}, f32[256,32,256,1]{2,0,3,1:T(8,128)S(1)}) fusion(f32[256,32,256,1]{2,0,3,1:T(8,128)} %copy-done.7, bf16[16,32,16,256]{3,0,2,1:T(8,128)(2,1)} %stack.387, bf16[16,256,16]{1,2,0:T(8,128)(2,1)S(1)} %gather_fusion.3), kind=kOutput, calls=%fused_computation.23 | convolution fusion | flops 1077936128 | bytes 25296896 | tf_op jit(solution)/shard_map/kcap,qka->cqp/dot_general | solution.py:70
  304.6 9.4 %collective-permute-done.45 = bf16[32,16,256]{2,1,0:T(8,128)(2,1)S(1)} collective-permute-done((bf16[32,16,256]{2,1,0:T(8,128)(2,1)S(1)}, bf16[32,16,256]{2,1,0:T(8,128)(2,1)S(1)}, u32[]{:S(2)}, u32[]{:S(2)}) %collective-permute-start.45) | collective-permute-done | bytes 262176 | tf_op jit(solution)/shard_map/ppermute | solution.py:22
  325.2 19.1 %collective-permute-start.49 = (bf16[32,16,256]{2,1,0:T(8,128)(2,1)S(1)}, bf16[32,16,256]{2,1,0:T(8,128)(2,1)S(1)}, u32[]{:S(2)}, u32[]{:S(2)}) collective-permute-start(bf16[32,16,256]{2,1,0:T(8,128)(2,1)S(1)} %get-tuple-element.20), channel_id=1, source_target_pairs={{0,11},{1,10},{2,9},{3,8},{4,15},{5,14},{6,13},{7,12},{8,3},{9,2},... | collective-permute-start | bytes 786440 | tf_op jit(solution)/shard_map/ppermute | solution.py:22
  345.0 11.1 %collective-permute-start.50 = (bf16[32,16,256]{2,1,0:T(8,128)(2,1)S(1)}, bf16[32,16,256]{2,1,0:T(8,128)(2,1)S(1)}, u32[]{:S(2)}, u32[]{:S(2)}) collective-permute-start(bf16[32,16,256]{2,1,0:T(8,128)(2,1)S(1)} %get-tuple-element.19), channel_id=1, source_target_pairs={{0,10},{1,11},{2,8},{3,9},{4,14},{5,15},{6,12},{7,13},{8,2},{9,3},... | collective-permute-start | bytes 786440 | tf_op jit(solution)/shard_map/ppermute | solution.py:22
  365.8 11.2 %collective-permute-done.50 = bf16[32,16,256]{2,1,0:T(8,128)(2,1)S(1)} collective-permute-done((bf16[32,16,256]{2,1,0:T(8,128)(2,1)S(1)}, bf16[32,16,256]{2,1,0:T(8,128)(2,1)S(1)}, u32[]{:S(2)}, u32[]{:S(2)}) %collective-permute-start.50) | collective-permute-done | bytes 262176 | tf_op jit(solution)/shard_map/ppermute | solution.py:22
  446.2 20.4 %collective-permute-start.19 = (bf16[32,16,256]{2,1,0:T(8,128)(2,1)S(1)}, bf16[32,16,256]{2,1,0:T(8,128)(2,1)S(1)}, u32[]{:S(2)}, u32[]{:S(2)}) collective-permute-start(bf16[32,16,256]{2,1,0:T(8,128)(2,1)S(1)} %get-tuple-element.51), channel_id=1, source_target_pairs={{0,11},{1,10},{2,9},{3,8},{4,15},{5,14},{6,13},{7,12},{8,3},{9,2},... | collective-permute-start | bytes 786440 | tf_op jit(solution)/shard_map/ppermute | solution.py:22
  467.3 10.8 %collective-permute-start.20 = (bf16[32,16,256]{2,1,0:T(8,128)(2,1)S(1)}, bf16[32,16,256]{2,1,0:T(8,128)(2,1)S(1)}, u32[]{:S(2)}, u32[]{:S(2)}) collective-permute-start(bf16[32,16,256]{2,1,0:T(8,128)(2,1)S(1)} %get-tuple-element.50), channel_id=1, source_target_pairs={{0,10},{1,11},{2,8},{3,9},{4,14},{5,15},{6,12},{7,13},{8,2},{9,3},... | collective-permute-start | bytes 786440 | tf_op jit(solution)/shard_map/ppermute | solution.py:22
  478.9 9.4 %collective-permute-done.19 = bf16[32,16,256]{2,1,0:T(8,128)(2,1)S(1)} collective-permute-done((bf16[32,16,256]{2,1,0:T(8,128)(2,1)S(1)}, bf16[32,16,256]{2,1,0:T(8,128)(2,1)S(1)}, u32[]{:S(2)}, u32[]{:S(2)}) %collective-permute-start.19) | collective-permute-done | bytes 262176 | tf_op jit(solution)/shard_map/ppermute | solution.py:22
  489.0 10.7 %collective-permute-done.20 = bf16[32,16,256]{2,1,0:T(8,128)(2,1)S(1)} collective-permute-done((bf16[32,16,256]{2,1,0:T(8,128)(2,1)S(1)}, bf16[32,16,256]{2,1,0:T(8,128)(2,1)S(1)}, u32[]{:S(2)}, u32[]{:S(2)}) %collective-permute-start.20) | collective-permute-done | bytes 262176 | tf_op jit(solution)/shard_map/ppermute | solution.py:22
  500.5 10.4 %collective-permute-done.21 = bf16[32,16,256]{2,1,0:T(8,128)(2,1)S(1)} collective-permute-done((bf16[32,16,256]{2,1,0:T(8,128)(2,1)S(1)}, bf16[32,16,256]{2,1,0:T(8,128)(2,1)S(1)}, u32[]{:S(2)}, u32[]{:S(2)}) %collective-permute-start.21) | collective-permute-done | bytes 262176 | tf_op jit(solution)/shard_map/ppermute | solution.py:22
  551.1 11.8 %copy.209 = f32[64,8,16,256]{3,1,2,0:T(8,128)} copy(f32[64,8,16,256]{3,2,1,0:T(8,128)S(1)} %bitcast.684) | data formatting | bytes 16777216
  562.9 9.1 %copy.116 = f32[4096,512]{1,0:T(8,128)} copy(f32[4096,512]{0,1:T(8,128)} %bitcast.686) | data formatting | bytes 16777216 | tf_op jit(solution)/shard_map/reshape | solution.py:100
  575.5 11.5 %copy.210 = f32[64,8,16,256]{3,1,2,0:T(8,128)} copy(f32[64,8,16,256]{3,2,1,0:T(8,128)S(1)} %bitcast.685) | data formatting | bytes 16777216
  586.9 9.1 %copy.165 = f32[4096,512]{1,0:T(8,128)} copy(f32[4096,512]{0,1:T(8,128)} %bitcast.687) | data formatting | bytes 16777216 | tf_op jit(solution)/shard_map/reshape | solution.py:86
  596.0 11.1 %fusion.7 = (f32[512]{0:T(512)S(1)}, bf16[4096,512]{1,0:T(8,128)(2,1)S(1)}, bf16[4096,512]{1,0:T(8,128)(2,1)S(1)}) fusion(bf16[4096,512]{1,0:T(8,128)(2,1)} %copy-done.3, bf16[4096,512]{1,0:T(8,128)(2,1)} %copy-done.2, f32[4096,512]{1,0:T(8,128)} %copy.116, f32[512]{0:T(512)S(1)} %copy-done.31, f32[4096,512]{1,0:T(8,128)} %copy.165, bf16[4096,512]{1,0:T(8,128)(2,1)} %param.21), kind=kLoop, calls=%fused_computation.21 | loop fusion | flops 25165312 | bytes 37752832 | tf_op jit(solution)/shard_map/reduce_sum | solution.py:97
  654.0 31.8 %psum.7 = bf16[512]{0:T(512)(128)(2,1)S(1)} all-reduce(bf16[512]{0:T(512)(128)(2,1)S(1)} %multiply_convert_fusion), channel_id=1, replica_groups=mesh['parts'=2,'seq'=16] {'seq'}, use_global_device_ids=true, to_apply=%region_1.2 | all-reduce | flops 512 | bytes 2048 | tf_op jit(solution)/shard_map/psum | solution.py:98
  (451 shorter events, 488.7 us)
Async XLA Ops:
  18.8 46.1 %collective-permute-start.2 = (bf16[32,16,256]{2,1,0:T(8,128)(2,1)}, bf16[32,16,256]{2,1,0:T(8,128)(2,1)}, u32[]{:S(2)}, u32[]{:S(2)}) collective-permute-start(bf16[32,16,256]{2,1,0:T(8,128)(2,1)} %bitcast.681), channel_id=1, source_target_pairs={{0,13},{1,12},{2,15},{3,14},{4,9},{5,8},{6,11},{7,10},{8,5},{9,4},... | collective-permute-start | bytes 786440 | tf_op jit(solution)/shard_map/ppermute | solution.py:22
  22.8 53.6 %collective-permute-start.3 = (bf16[32,16,256]{2,1,0:T(8,128)(2,1)}, bf16[32,16,256]{2,1,0:T(8,128)(2,1)}, u32[]{:S(2)}, u32[]{:S(2)}) collective-permute-start(bf16[32,16,256]{2,1,0:T(8,128)(2,1)} %bitcast.680), channel_id=1, source_target_pairs={{0,12},{1,13},{2,14},{3,15},{4,8},{5,9},{6,10},{7,11},{8,4},{9,5},... | collective-permute-start | bytes 786440 | tf_op jit(solution)/shard_map/ppermute | solution.py:22
  24.0 66.6 %collective-permute-start.4 = (bf16[32,16,256]{2,1,0:T(8,128)(2,1)}, bf16[32,16,256]{2,1,0:T(8,128)(2,1)}, u32[]{:S(2)}, u32[]{:S(2)}) collective-permute-start(bf16[32,16,256]{2,1,0:T(8,128)(2,1)} %bitcast.679), channel_id=1, source_target_pairs={{0,11},{1,10},{2,9},{3,8},{4,15},{5,14},{6,13},{7,12},{8,3},{9,2},... | collective-permute-start | bytes 786440 | tf_op jit(solution)/shard_map/ppermute | solution.py:22
  42.6 53.9 %collective-permute-start.5 = (bf16[32,16,256]{2,1,0:T(8,128)(2,1)S(1)}, bf16[32,16,256]{2,1,0:T(8,128)(2,1)S(1)}, u32[]{:S(2)}, u32[]{:S(2)}) collective-permute-start(bf16[32,16,256]{2,1,0:T(8,128)(2,1)S(1)} %bitcast.741), channel_id=1, source_target_pairs={{0,10},{1,11},{2,8},{3,9},{4,14},{5,15},{6,12},{7,13},{8,2},{9,3},... | collective-permute-start | bytes 786440 | tf_op jit(solution)/shard_map/ppermute | solution.py:22
  54.9 47.1 %collective-permute-start.6 = (bf16[32,16,256]{2,1,0:T(8,128)(2,1)S(1)}, bf16[32,16,256]{2,1,0:T(8,128)(2,1)S(1)}, u32[]{:S(2)}, u32[]{:S(2)}) collective-permute-start(bf16[32,16,256]{2,1,0:T(8,128)(2,1)S(1)} %bitcast.740), channel_id=1, source_target_pairs={{0,9},{1,8},{2,11},{3,10},{4,13},{5,12},{6,15},{7,14},{8,1},{9,0},... | collective-permute-start | bytes 786440 | tf_op jit(solution)/shard_map/ppermute | solution.py:22
  64.9 42.7 %collective-permute-start.7 = (bf16[32,16,256]{2,1,0:T(8,128)(2,1)S(1)}, bf16[32,16,256]{2,1,0:T(8,128)(2,1)S(1)}, u32[]{:S(2)}, u32[]{:S(2)}) collective-permute-start(bf16[32,16,256]{2,1,0:T(8,128)(2,1)S(1)} %bitcast.739), channel_id=1, source_target_pairs={{0,8},{1,9},{2,10},{3,11},{4,12},{5,13},{6,14},{7,15},{8,0},{9,1},... | collective-permute-start | bytes 786440 | tf_op jit(solution)/shard_map/ppermute | solution.py:22
  102.0 44.9 %collective-permute-start.11 = (bf16[32,16,256]{2,1,0:T(8,128)(2,1)S(1)}, bf16[32,16,256]{2,1,0:T(8,128)(2,1)S(1)}, u32[]{:S(2)}, u32[]{:S(2)}) collective-permute-start(bf16[32,16,256]{2,1,0:T(8,128)(2,1)S(1)} %bitcast.732), channel_id=1, source_target_pairs={{0,4},{1,5},{2,6},{3,7},{4,0},{5,1},{6,2},{7,3},{8,12},{9,13},{10,... | collective-permute-start | bytes 786440 | tf_op jit(solution)/shard_map/ppermute | solution.py:22
  149.4 45.6 %collective-permute-start.35 = (bf16[32,16,256]{2,1,0:T(8,128)(2,1)S(1)}, bf16[32,16,256]{2,1,0:T(8,128)(2,1)S(1)}, u32[]{:S(2)}, u32[]{:S(2)}) collective-permute-start(bf16[32,16,256]{2,1,0:T(8,128)(2,1)S(1)} %bitcast.728), channel_id=1, source_target_pairs={{0,10},{1,11},{2,8},{3,9},{4,14},{5,15},{6,12},{7,13},{8,2},{9,3},... | collective-permute-start | bytes 786440 | tf_op jit(solution)/shard_map/ppermute | solution.py:22
  152.6 46.3 %collective-permute-start.36 = (bf16[32,16,256]{2,1,0:T(8,128)(2,1)S(1)}, bf16[32,16,256]{2,1,0:T(8,128)(2,1)S(1)}, u32[]{:S(2)}, u32[]{:S(2)}) collective-permute-start(bf16[32,16,256]{2,1,0:T(8,128)(2,1)S(1)} %bitcast.727), channel_id=1, source_target_pairs={{0,9},{1,8},{2,11},{3,10},{4,13},{5,12},{6,15},{7,14},{8,1},{9,0},... | collective-permute-start | bytes 786440 | tf_op jit(solution)/shard_map/ppermute | solution.py:22
  152.7 52.5 %collective-permute-start.37 = (bf16[32,16,256]{2,1,0:T(8,128)(2,1)S(1)}, bf16[32,16,256]{2,1,0:T(8,128)(2,1)S(1)}, u32[]{:S(2)}, u32[]{:S(2)}) collective-permute-start(bf16[32,16,256]{2,1,0:T(8,128)(2,1)S(1)} %bitcast.726), channel_id=1, source_target_pairs={{0,8},{1,9},{2,10},{3,11},{4,12},{5,13},{6,14},{7,15},{8,0},{9,1},... | collective-permute-start | bytes 786440 | tf_op jit(solution)/shard_map/ppermute | solution.py:22
  157.9 53.7 %collective-permute-start.38 = (bf16[32,16,256]{2,1,0:T(8,128)(2,1)S(1)}, bf16[32,16,256]{2,1,0:T(8,128)(2,1)S(1)}, u32[]{:S(2)}, u32[]{:S(2)}) collective-permute-start(bf16[32,16,256]{2,1,0:T(8,128)(2,1)S(1)} %bitcast.725), channel_id=1, source_target_pairs={{0,7},{1,6},{2,5},{3,4},{4,3},{5,2},{6,1},{7,0},{8,15},{9,14},{10,... | collective-permute-start | bytes 786440 | tf_op jit(solution)/shard_map/ppermute | solution.py:22
  303.0 237.9 %collective-permute-start.29 = (bf16[32,16,256]{2,1,0:T(8,128)(2,1)S(1)}, bf16[32,16,256]{2,1,0:T(8,128)(2,1)}, u32[]{:S(2)}, u32[]{:S(2)}) collective-permute-start(bf16[32,16,256]{2,1,0:T(8,128)(2,1)S(1)} %get-tuple-element.42), channel_id=1, source_target_pairs={{0,1},{1,0},{2,3},{3,2},{4,5},{5,4},{6,7},{7,6},{8,9},{9,8},{10,11... | collective-permute-start | bytes 786440 | tf_op jit(solution)/shard_map/ppermute | solution.py:22
  303.3 231.1 %collective-permute-start.27 = (bf16[32,16,256]{2,1,0:T(8,128)(2,1)S(1)}, bf16[32,16,256]{2,1,0:T(8,128)(2,1)S(1)}, u32[]{:S(2)}, u32[]{:S(2)}) collective-permute-start(bf16[32,16,256]{2,1,0:T(8,128)(2,1)S(1)} %get-tuple-element.43), channel_id=1, source_target_pairs={{0,3},{1,2},{2,1},{3,0},{4,7},{5,6},{6,5},{7,4},{8,11},{9,10},{10,... | collective-permute-start | bytes 786440 | tf_op jit(solution)/shard_map/ppermute | solution.py:22
  304.6 229.1 %collective-permute-start.26 = (bf16[32,16,256]{2,1,0:T(8,128)(2,1)S(1)}, bf16[32,16,256]{2,1,0:T(8,128)(2,1)S(1)}, u32[]{:S(2)}, u32[]{:S(2)}) collective-permute-start(bf16[32,16,256]{2,1,0:T(8,128)(2,1)S(1)} %get-tuple-element.44), channel_id=1, source_target_pairs={{0,4},{1,5},{2,6},{3,7},{4,0},{5,1},{6,2},{7,3},{8,12},{9,13},{10,... | collective-permute-start | bytes 786440 | tf_op jit(solution)/shard_map/ppermute | solution.py:22
  446.2 42.0 %collective-permute-start.19 = (bf16[32,16,256]{2,1,0:T(8,128)(2,1)S(1)}, bf16[32,16,256]{2,1,0:T(8,128)(2,1)S(1)}, u32[]{:S(2)}, u32[]{:S(2)}) collective-permute-start(bf16[32,16,256]{2,1,0:T(8,128)(2,1)S(1)} %get-tuple-element.51), channel_id=1, source_target_pairs={{0,11},{1,10},{2,9},{3,8},{4,15},{5,14},{6,13},{7,12},{8,3},{9,2},... | collective-permute-start | bytes 786440 | tf_op jit(solution)/shard_map/ppermute | solution.py:22
  651.6 41.9 %collective-permute-start.96 = (bf16[32,512]{1,0:T(8,128)(2,1)S(1)}, bf16[32,512]{1,0:T(8,128)(2,1)S(1)}, u32[]{:S(2)}, u32[]{:S(2)}) collective-permute-start(bf16[32,512]{1,0:T(8,128)(2,1)S(1)} %get-tuple-element.97), channel_id=1, source_target_pairs={{0,9},{1,8},{2,11},{3,10},{4,13},{5,12},{6,15},{7,14},{8,1},{9,0},... | collective-permute-start | bytes 98312 | tf_op jit(solution)/shard_map/ppermute | solution.py:22
  693.6 61.0 %collective-permute-start.88 = (bf16[32,512]{1,0:T(8,128)(2,1)S(1)}, bf16[32,512]{1,0:T(8,128)(2,1)S(1)}, u32[]{:S(2)}, u32[]{:S(2)}) collective-permute-start(bf16[32,512]{1,0:T(8,128)(2,1)S(1)} %get-tuple-element.5), channel_id=1, source_target_pairs={{0,2},{1,3},{2,0},{3,1},{4,6},{5,7},{6,4},{7,5},{8,10},{9,11},{10,... | collective-permute-start | bytes 98312 | tf_op jit(solution)/shard_map/ppermute | solution.py:22
  695.4 59.1 %collective-permute-start.87 = (bf16[32,512]{1,0:T(8,128)(2,1)S(1)}, bf16[32,512]{1,0:T(8,128)(2,1)S(1)}, u32[]{:S(2)}, u32[]{:S(2)}) collective-permute-start(bf16[32,512]{1,0:T(8,128)(2,1)S(1)} %get-tuple-element.5), channel_id=1, source_target_pairs={{0,3},{1,2},{2,1},{3,0},{4,7},{5,6},{6,5},{7,4},{8,11},{9,10},{10,... | collective-permute-start | bytes 98312 | tf_op jit(solution)/shard_map/ppermute | solution.py:22
  695.4 57.3 %collective-permute-start.86 = (bf16[32,512]{1,0:T(8,128)(2,1)S(1)}, bf16[32,512]{1,0:T(8,128)(2,1)S(1)}, u32[]{:S(2)}, u32[]{:S(2)}) collective-permute-start(bf16[32,512]{1,0:T(8,128)(2,1)S(1)} %get-tuple-element.5), channel_id=1, source_target_pairs={{0,4},{1,5},{2,6},{3,7},{4,0},{5,1},{6,2},{7,3},{8,12},{9,13},{10,... | collective-permute-start | bytes 98312 | tf_op jit(solution)/shard_map/ppermute | solution.py:22
  695.5 57.1 %collective-permute-start.85 = (bf16[32,512]{1,0:T(8,128)(2,1)S(1)}, bf16[32,512]{1,0:T(8,128)(2,1)S(1)}, u32[]{:S(2)}, u32[]{:S(2)}) collective-permute-start(bf16[32,512]{1,0:T(8,128)(2,1)S(1)} %get-tuple-element.5), channel_id=1, source_target_pairs={{0,5},{1,4},{2,7},{3,6},{4,1},{5,0},{6,3},{7,2},{8,13},{9,12},{10,... | collective-permute-start | bytes 98312 | tf_op jit(solution)/shard_map/ppermute | solution.py:22
  752.7 56.2 %collective-permute-start.118 = (bf16[32,512]{1,0:T(8,128)(2,1)S(1)}, bf16[32,512]{1,0:T(8,128)(2,1)S(1)}, u32[]{:S(2)}, u32[]{:S(2)}) collective-permute-start(bf16[32,512]{1,0:T(8,128)(2,1)S(1)} %get-tuple-element.7), channel_id=1, source_target_pairs={{0,2},{1,3},{2,0},{3,1},{4,6},{5,7},{6,4},{7,5},{8,10},{9,11},{10,... | collective-permute-start | bytes 98312 | tf_op jit(solution)/shard_map/ppermute | solution.py:22
  752.8 56.0 %collective-permute-start.117 = (bf16[32,512]{1,0:T(8,128)(2,1)S(1)}, bf16[32,512]{1,0:T(8,128)(2,1)S(1)}, u32[]{:S(2)}, u32[]{:S(2)}) collective-permute-start(bf16[32,512]{1,0:T(8,128)(2,1)S(1)} %get-tuple-element.7), channel_id=1, source_target_pairs={{0,3},{1,2},{2,1},{3,0},{4,7},{5,6},{6,5},{7,4},{8,11},{9,10},{10,... | collective-permute-start | bytes 98312 | tf_op jit(solution)/shard_map/ppermute | solution.py:22
  754.5 54.2 %collective-permute-start.116 = (bf16[32,512]{1,0:T(8,128)(2,1)S(1)}, bf16[32,512]{1,0:T(8,128)(2,1)S(1)}, u32[]{:S(2)}, u32[]{:S(2)}) collective-permute-start(bf16[32,512]{1,0:T(8,128)(2,1)S(1)} %get-tuple-element.7), channel_id=1, source_target_pairs={{0,4},{1,5},{2,6},{3,7},{4,0},{5,1},{6,2},{7,3},{8,12},{9,13},{10,... | collective-permute-start | bytes 98312 | tf_op jit(solution)/shard_map/ppermute | solution.py:22
  754.6 54.2 %collective-permute-start.115 = (bf16[32,512]{1,0:T(8,128)(2,1)S(1)}, bf16[32,512]{1,0:T(8,128)(2,1)S(1)}, u32[]{:S(2)}, u32[]{:S(2)}) collective-permute-start(bf16[32,512]{1,0:T(8,128)(2,1)S(1)} %get-tuple-element.7), channel_id=1, source_target_pairs={{0,5},{1,4},{2,7},{3,6},{4,1},{5,0},{6,3},{7,2},{8,13},{9,12},{10,... | collective-permute-start | bytes 98312 | tf_op jit(solution)/shard_map/ppermute | solution.py:22
  (129 other events, 1684.8 us)

commit v2 on v0

v2 whole, which is shorter than its diff:
```python
import functools

import jax
import jax.numpy as jnp
from jax import lax
from jax.experimental import pallas as pl
from jax.experimental.pallas import tpu as pltpu
from jax.sharding import PartitionSpec as P

D = 512
N1 = 256
N2 = 256
GROUP = 16
VMEM_LIMIT = 56 * 1024 * 1024

f32 = jnp.float32
bf16 = jnp.bfloat16


def dot_nn(a, b):
    return jnp.dot(a, b, preferred_element_type=f32)


def dot_nt(a, b):
    return lax.dot_general(a, b, (((1,), (1,)), ((), ())), preferred_element_type=f32)


def dot_tn(a, b):
    return lax.dot_general(a, b, (((0,), (0,)), ((), ())), preferred_element_type=f32)


def params():
    return pltpu.CompilerParams(vmem_limit_bytes=VMEM_LIMIT)


def whole(shape):
    return pl.BlockSpec(shape, lambda i: (0,) * len(shape))


def rows_of(step):
    return pl.BlockSpec((N2, D), lambda i: (i, 0))


def by_device(n, chans):
    return pl.BlockSpec((n, 1, chans, N2), lambda i: (0, i, 0, 0))


def section_one_kernel(tokens, w_value, first, out, w_turned):
    @pl.when(pl.program_id(0) == 0)
    def _():
        w_turned[...] = w_value[...].T

    value_t = dot_nt(w_turned[...], tokens[...]).astype(bf16)
    section = dot_nt(value_t, first[...]).astype(bf16)
    out[...] = section.reshape(out.shape)


def d_three_kernel(
    tokens, cotangent, w_value, w_gate, fourth, out, value_out, d_mix_out, skip_out
):
    value = dot_nn(tokens[...], w_value[...]).astype(bf16)
    gate = dot_nn(tokens[...], w_gate[...]).astype(bf16)
    d_mix = (cotangent[...].astype(f32) * gate.astype(f32)).astype(bf16)
    value_out[...] = value
    d_mix_out[...] = d_mix
    term = jnp.sum(d_mix.astype(f32) * value.astype(f32), axis=0, keepdims=True)

    @pl.when(pl.program_id(0) == 0)
    def _():
        skip_out[...] = jnp.zeros_like(skip_out)

    skip_out[...] += term
    section = dot_tn(d_mix, fourth[...]).astype(bf16)
    out[...] = section.reshape(out.shape)


def turn_in(swap, arrived, by_channel):
    def body(i, _):
        rows = pl.ds(pl.multiple_of(i * GROUP, GROUP), GROUP)
        block = arrived[rows].reshape(GROUP * GROUP, N2)
        turned = dot_nn(swap[...], block).astype(bf16)
        by_channel[:, rows, :] = turned.reshape(GROUP, GROUP, N2)
        return 0

    lax.fori_loop(0, N1 // GROUP, body, 0, unroll=2)


def turn_out(swap, by_channel, out):
    def body(i, _):
        rows = pl.ds(pl.multiple_of(i * GROUP, GROUP), GROUP)
        block = by_channel[:, rows, :].reshape(GROUP * GROUP, N2)
        turned = dot_nn(swap[...], block).astype(bf16)
        out[rows] = turned.reshape(GROUP, GROUP, N2)
        return 0

    lax.fori_loop(0, N1 // GROUP, body, 0, unroll=2)


def home_forward_kernel(arrived, kernel, second, third, swap, out, spectrum_out, by_channel):
    turn_in(swap, arrived, by_channel)

    def body(c, _):
        spectrum = dot_nn(second[...], by_channel[c])
        spectrum_out[c] = spectrum
        filtered = (spectrum * kernel[c].astype(f32)).astype(bf16)
        by_channel[c] = dot_nn(third[...], filtered).astype(bf16)
        return 0

    lax.fori_loop(0, GROUP, body, 0, unroll=2)
    turn_out(swap, by_channel, out)


def home_backward_kernel(
    arrived, kernel, spectrum, second_t, third_t, swap, out, grad_kernel, by_channel
):
    turn_in(swap, arrived, by_channel)

    def body(c, _):
        d_freq = dot_nn(third_t[...], by_channel[c])
        grad_kernel[c] = (d_freq * spectrum[c]).astype(bf16)
        d_spec = (d_freq * kernel[c].astype(f32)).astype(bf16)
        by_channel[c] = dot_nn(second_t[...], d_spec).astype(bf16)
        return 0

    lax.fori_loop(0, GROUP, body, 0, unroll=2)
    turn_out(swap, by_channel, out)


def accumulate(total, term):
    @pl.when(pl.program_id(0) == 0)
    def _():
        total[...] = term

    @pl.when(pl.program_id(0) > 0)
    def _():
        total[...] += term


def gate_kernel(
    arrived, tokens, value, cotangent, fourth, w_gate, skip, factor, partial, grad_w, total
):
    conv = dot_nt(fourth[...], arrived[...].reshape(D, N2))
    mixed = conv + skip[...] * value[...].astype(f32)
    d_gate = (cotangent[...].astype(f32) * mixed).astype(bf16)
    partial[...] = dot_nt(d_gate, w_gate[...])
    accumulate(total, dot_tn(tokens[...], d_gate))

    @pl.when(pl.program_id(0) == pl.num_programs(0) - 1)
    def _():
        grad_w[...] = (total[...] * factor[0, 0]).astype(bf16)


def value_kernel(
    arrived, tokens, d_mix, partial, first_t, w_value, skip, factor, grad_tokens, grad_w, total
):
    d_cube = dot_nt(first_t[...], arrived[...].reshape(D, N2))
    d_value = (d_cube + skip[...] * d_mix[...].astype(f32)).astype(bf16)
    grad_tokens[...] = (partial[...] + dot_nt(d_value, w_value[...])).astype(bf16)
    accumulate(total, dot_tn(tokens[...], d_value))

    @pl.when(pl.program_id(0) == pl.num_programs(0) - 1)
    def _():
        grad_w[...] = (total[...] * factor[0, 0]).astype(bf16)


def on_device(
    tokens,
    w_value,
    w_gate,
    first_block,
    second_block,
    third_block,
    fourth_block,
    kernel,
    skip_gain,
    cotangent,
):
    n = lax.axis_size("seq")
    rows = N1 // n
    chans = D // n
    local_rows = tokens.shape[0]
    sections = (n, rows, chans, N2)
    factor = (1.0 / jnp.sqrt(jnp.asarray(N1 * N2, f32))).reshape(1, 1)
    skip = skip_gain.reshape(1, D)
    square = whole((D, D))
    block = whole((N1, N2))
    line = whole((1, D))
    row = rows_of(0)
    sent = by_device(n, chans)
    one = pl.BlockSpec(memory_space=pltpu.SMEM)
    place = jnp.arange(GROUP * GROUP)
    swap = (
        place[None, :] == ((place % GROUP) * GROUP + place // GROUP)[:, None]
    ).astype(bf16)

    def cost(gflop, mib):
        scale = rows / 16
        return pl.CostEstimate(
            flops=int(gflop * 1e9 * scale), bytes_accessed=int(mib * 2**20 * scale), transcendentals=0
        )

    def shape(dims, dtype=bf16):
        return jax.ShapeDtypeStruct(dims, dtype)

    def transfer(array):
        return lax.all_to_all(array, "seq", split_axis=0, concat_axis=0, tiled=True)

    one_sent = pl.pallas_call(
        section_one_kernel,
        grid=(rows,),
        in_specs=[row, square, block],
        out_specs=sent,
        out_shape=shape(sections),
        scratch_shapes=[pltpu.VMEM((D, D), bf16)],
        compiler_params=params(),
        cost_estimate=cost(3.2, 9),
    )(tokens, w_value, first_block)
    one_home = transfer(one_sent)

    three_sent, value, d_mix, skip_term = pl.pallas_call(
        d_three_kernel,
        grid=(rows,),
        in_specs=[row, row, square, square, block],
        out_specs=[sent, row, row, line],
        out_shape=[
            shape(sections),
            shape((local_rows, D)),
            shape((local_rows, D)),
            shape((1, D), f32),
        ],
        compiler_params=params(),
        cost_estimate=cost(5.4, 21),
    )(tokens, cotangent, w_value, w_gate, fourth_block)
    three_home = transfer(three_sent)

    at_home = pl.BlockSpec((N1, GROUP, N2), lambda i: (0, i, 0))
    filters = pl.BlockSpec((GROUP, N1, N2), lambda i: (i, 0, 0))
    three_back, spectrum = pl.pallas_call(
        home_forward_kernel,
        grid=(chans // GROUP,),
        in_specs=[at_home, filters, block, block, block],
        out_specs=[at_home, filters],
        out_shape=[shape((N1, chans, N2)), shape((chans, N1, N2), f32)],
        scratch_shapes=[pltpu.VMEM((GROUP, N1, N2), bf16)],
        compiler_params=params(),
        cost_estimate=cost(4.3, 20),
    )(one_home.reshape(N1, chans, N2), kernel, second_block, third_block, swap)
    three_here = transfer(three_back.reshape(sections))

    one_back, grad_kernel = pl.pallas_call(
        home_backward_kernel,
        grid=(chans // GROUP,),
        in_specs=[at_home, filters, filters, block, block, block],
        out_specs=[at_home, filters],
        out_shape=[shape((N1, chans, N2)), shape((chans, N1, N2))],
        scratch_shapes=[pltpu.VMEM((GROUP, N1, N2), bf16)],
        compiler_params=params(),
        cost_estimate=cost(4.3, 24),
    )(
        three_home.reshape(N1, chans, N2),
        kernel,
        spectrum,
        second_block.T,
        third_block.T,
        swap,
    )
    one_here = transfer(one_back.reshape(sections))

    partial, gate_term = pl.pallas_call(
        gate_kernel,
        grid=(rows,),
        in_specs=[sent, row, row, row, block, square, line, one],
        out_specs=[row, square],
        out_shape=[shape((local_rows, D), f32), shape((D, D))],
        scratch_shapes=[pltpu.VMEM((D, D), f32)],
        compiler_params=params(),
        cost_estimate=cost(5.4, 25),
    )(three_here, tokens, value, cotangent, fourth_block, w_gate, skip, factor)

    grad_tokens, value_term = pl.pallas_call(
        value_kernel,
        grid=(rows,),
        in_specs=[sent, row, row, row, block, square, line, one],
        out_specs=[row, square],
        out_shape=[shape((local_rows, D)), shape((D, D))],
        scratch_shapes=[pltpu.VMEM((D, D), f32)],
        compiler_params=params(),
        cost_estimate=cost(5.4, 25),
    )(one_here, tokens, d_mix, partial, first_block.T, w_value, skip, factor)

    gate_total, skip_total = lax.psum(
        (gate_term, (skip_term.reshape(D) * factor[0, 0]).astype(bf16)), "seq"
    )
    parts = transfer(value_term.reshape(n, D // n, D))
    mine = jnp.sum(parts.astype(f32), axis=0).astype(bf16)
    value_total = transfer(jnp.broadcast_to(mine, (n, D // n, D))).reshape(D, D)
    return (
        grad_tokens,
        grad_kernel,
        jnp.stack([value_total, gate_total]).astype(f32),
        skip_total.astype(f32),
    )


def solution(mesh):
    in_specs = (
        P(("parts", "seq"), None),
        P(),
        P(),
        P(),
        P(),
        P(),
        P(),
        P("seq", None, None),
        P(),
        P(("parts", "seq"), None),
    )
    out_specs = (
        P(("parts", "seq"), None),
        P(("parts", "seq"), None, None),
        P("parts", None, None),
        P("parts"),
    )
    return jax.shard_map(
        on_device, mesh=mesh, in_specs=in_specs, out_specs=out_specs, check_vma=False
    )
```

time: 598 us -> 565 us (0.945)
  Pallas kernels: 0 us -> 113 us
  matrix products: 60.5 us -> 0 us
  waiting for transfers between devices: 346 us -> 288 us
  local copies, waits for them, and re-layouts: 50.1 us -> 3.12 us
  blocking collectives: 47.7 us -> 70.3 us
  other arithmetic: 12.8 us -> 3.94 us
    pallas_call x0 -> x6, Pallas kernels: none -> 113 us  [the longest x1 20.6 us: on_device(): pl.pallas_call(home_backward_kernel, grid=(chans // GROUP,), in_specs=[at...]
    dot_general x14 -> x0, matrix products: 60.5 us -> none  [the longest x1 9.2 us: on_device(): jnp.dot(d_gate, w_gate.T, preferred_element_type=f32)]
    all_to_all x4 -> x5, waiting for transfers between devices: 264 us -> 228 us  [transfer(): return lax.all_to_all(array, 'seq', split_axis=0, concat_axis=0, tiled=True)]
    all_to_all x0 -> x1, blocking collectives: none -> 34.1 us  [transfer(): return lax.all_to_all(array, 'seq', split_axis=0, concat_axis=0, tiled=True)]
    psum x1, waiting for transfers between devices: 81.5 us -> 58.9 us  [on_device(): lax.psum((gate_term, (skip_term.reshape(D) * factor[0, 0]).astype(bf16)),...]
    unnamed x37 -> x11, local copies, waits for them, and re-layouts: 21.5 us -> 2.29 us
    all_to_all x4 -> x0, local copies, waits for them, and re-layouts: 15 us -> none  [the longest x1 4.69 us: on_device(): lax.all_to_all(d_three, 'seq', split_axis=0, concat_axis=1, tiled=True)]
    psum x1, blocking collectives: 47.7 us -> 36.1 us  [on_device(): lax.psum((gate_term, (skip_term.reshape(D) * factor[0, 0]).astype(bf16)),...]
  transfers between devices with their start and end apart: 5 -> 6, of which waited for: 5 -> 5; matrix products, arithmetic and copies ran while one was open for 9% -> 1% of each run, Pallas kernels for 0% -> 14%
where the time goes in v2:
time: 565 us; the launch traced here: 563 us
  waiting for transfers between devices  288 us (51%)
  Pallas kernels  113 us (20%)
  starting transfers between devices  70.9 us (13%)
  blocking collectives  70.3 us (12%)
  between operations  14.1 us (2%)
    all_to_all x5, waiting for transfers between devices, transfer(): return lax.all_to_all(array, 'seq', split_axis=0, concat_axis=0, tiled=True)  228 us
    all_to_all x5, starting transfers between devices, transfer(): return lax.all_to_all(array, 'seq', split_axis=0, concat_axis=0, tiled=True)  70.9 us
    psum x1, waiting for transfers between devices, on_device(): lax.psum((gate_term, (skip_term.reshape(D) * factor[0, 0]).astype(bf16)),...  58.9 us
    psum x1, blocking collectives, on_device(): lax.psum((gate_term, (skip_term.reshape(D) * factor[0, 0]).astype(bf16)),...  36.1 us
    all_to_all x1, blocking collectives, transfer(): return lax.all_to_all(array, 'seq', split_axis=0, concat_axis=0, tiled=True)  34.1 us
    pallas_call x1, Pallas kernels, on_device(): pl.pallas_call(home_backward_kernel, grid=(chans // GROUP,), in_specs=[at...  20.6 us
    pallas_call x1, Pallas kernels, on_device(): pl.pallas_call(home_forward_kernel, grid=(chans // GROUP,), in_specs=[at_...  20.2 us
    pallas_call x1, Pallas kernels, on_device(): pl.pallas_call(d_three_kernel, grid=(rows,), in_specs=[row, row, square,...  19.4 us
  transfers between devices with their start and end apart: 6, of which 5 were waited for; matrix products, arithmetic and copies ran while one was open for 1% of the time, Pallas kernels for 14%

profile of v2, /device:TPU:0, one launch (start us, length us, event | category | flops | bytes accessed | tf_op | source)
XLA Modules:
  0.0 563.1 jit_solution(7363384588806623628)
XLA Ops:
  7.2 14.3 %shard_map.130 = bf16[16,16,32,256]{3,2,1,0:T(8,128)(2,1)} custom-call(bf16[4096,512]{1,0:T(8,128)(2,1)} %tokens.7, bf16[512,512]{1,0:T(8,128)(2,1)} %w_value.5, bf16[256,256]{1,0:T(8,128)(2,1)} %first.1), custom_call_target="tpu_custom_call" | custom-call | flops 3200000000 | bytes 9437184 | tf_op jit(solution)/shard_map/pallas_call | solution.py:208
  21.5 7.4 %all-to-all-start.1 = ((bf16[16,16,32,256]{3,2,1,0:T(8,128)(2,1)}), bf16[16,16,32,256]{3,2,1,0:T(8,128)(2,1)}, u32[]{:S(2)}, u32[]{:S(2)}) async-start(bf16[16,16,32,256]{3,2,1,0:T(8,128)(2,1)} %shard_map.130), calls=%async_computation.1 | async-start | bytes 8388608 | tf_op jit(solution)/shard_map/all_to_all | solution.py:206
  29.0 19.4 %shard_map.129 = (bf16[16,16,32,256]{3,2,1,0:T(8,128)(2,1)}, bf16[4096,512]{1,0:T(8,128)(2,1)}, bf16[4096,512]{1,0:T(8,128)(2,1)}, f32[1,512]{1,0:T(1,128)}) custom-call(bf16[4096,512]{1,0:T(8,128)(2,1)} %tokens.7, bf16[4096,512]{1,0:T(8,128)(2,1)} %cotangent.3, bf16[512,512]{1,0:T(8,128)(2,1)} %w_value.5, bf16[512,512]{1,0:T(8,128)(2,1)} %w_gate.3, ...), custom_call_target="tpu_custom_call" | custom-call | flops 5400000000 | bytes 22020096 | tf_op jit(solution)/shard_map/pallas_call | solution.py:220
  48.4 58.3 %all-to-all-done.1 = bf16[16,16,32,256]{3,2,1,0:T(8,128)(2,1)} async-done(((bf16[16,16,32,256]{3,2,1,0:T(8,128)(2,1)}), bf16[16,16,32,256]{3,2,1,0:T(8,128)(2,1)}, u32[]{:S(2)}, u32[]{:S(2)}) %all-to-all-start.1) | async-done | bytes 4194336 | tf_op jit(solution)/shard_map/all_to_all | solution.py:206
  106.6 19.7 %all-to-all-start = ((bf16[16,16,32,256]{3,2,1,0:T(8,128)(2,1)}), bf16[16,16,32,256]{3,2,1,0:T(8,128)(2,1)}, u32[]{:S(2)}, u32[]{:S(2)}) async-start(bf16[16,16,32,256]{3,2,1,0:T(8,128)(2,1)} %get-tuple-element.16), calls=%async_computation | async-start | bytes 8388608 | tf_op jit(solution)/shard_map/all_to_all | solution.py:206
  126.3 0.8 fusion.swap
  127.1 20.2 %shard_map.131 = (bf16[256,32,256]{2,1,0:T(8,128)(2,1)}, f32[32,256,256]{2,1,0:T(8,128)}) custom-call(bf16[256,32,256]{2,1,0:T(8,128)(2,1)} %bitcast.1.arrived, bf16[32,256,256]{2,1,0:T(8,128)(2,1)} %kernel.3, bf16[256,256]{1,0:T(8,128)(2,1)} %second.1, bf16[256,256]{1,0:T(8,128)(2,1)} %third.1, bf16[256,256]{1,0:T(8,128)(2,1)} %fusion.swap), custom_call_target="tpu_custom_call" | custom-call | flops 4300000256 | bytes 20971520 | tf_op jit(solution)/shard_map/pallas_call | solution.py:238
  147.3 56.8 %all-to-all-done = bf16[16,16,32,256]{3,2,1,0:T(8,128)(2,1)} async-done(((bf16[16,16,32,256]{3,2,1,0:T(8,128)(2,1)}), bf16[16,16,32,256]{3,2,1,0:T(8,128)(2,1)}, u32[]{:S(2)}, u32[]{:S(2)}) %all-to-all-start) | async-done | bytes 4194336 | tf_op jit(solution)/shard_map/all_to_all | solution.py:206
  204.0 19.8 %all-to-all-start.3 = ((bf16[16,16,32,256]{3,2,1,0:T(8,128)(2,1)}), bf16[16,16,32,256]{3,2,1,0:T(8,128)(2,1)}, u32[]{:S(2)}, u32[]{:S(2)}) async-start(bf16[16,16,32,256]{3,2,1,0:T(8,128)(2,1)} %bitcast.12), calls=%async_computation.3 | async-start | bytes 8388608 | tf_op jit(solution)/shard_map/all_to_all | solution.py:206
  223.8 0.8 copy.14
  224.6 0.8 copy.15
  225.4 20.6 %shard_map.132 = (bf16[256,32,256]{2,1,0:T(8,128)(2,1)}, bf16[32,256,256]{2,1,0:T(8,128)(2,1)}) custom-call(bf16[256,32,256]{2,1,0:T(8,128)(2,1)} %bitcast.arrived, bf16[32,256,256]{2,1,0:T(8,128)(2,1)} %kernel.3, f32[32,256,256]{2,1,0:T(8,128)} %get-tuple-element.17.spectrum, bf16[256,256]{1,0:T(8,128)(2,1)} %bitcast.15, bf16[256,256]{1,0:T(8,128)(2,1)} %bitcast.16, ...), custom_call_target="tpu_custom_call" | custom-call | flops 4300000256 | bytes 25165824 | tf_op jit(solution)/shard_map/pallas_call | solution.py:250
  246.0 55.5 %all-to-all-done.3.arrived = bf16[16,16,32,256]{3,2,1,0:T(8,128)(2,1)} async-done(((bf16[16,16,32,256]{3,2,1,0:T(8,128)(2,1)}), bf16[16,16,32,256]{3,2,1,0:T(8,128)(2,1)}, u32[]{:S(2)}, u32[]{:S(2)}) %all-to-all-start.3) | async-done | bytes 4194336 | tf_op jit(solution)/shard_map/all_to_all | solution.py:206
  301.5 19.8 %all-to-all-start.2 = ((bf16[16,16,32,256]{3,2,1,0:T(8,128)(2,1)}), bf16[16,16,32,256]{3,2,1,0:T(8,128)(2,1)}, u32[]{:S(2)}, u32[]{:S(2)}) async-start(bf16[16,16,32,256]{3,2,1,0:T(8,128)(2,1)} %bitcast.11), calls=%async_computation.2 | async-start | bytes 8388608 | tf_op jit(solution)/shard_map/all_to_all | solution.py:206
  321.4 0.8 copy.16
  322.1 19.2 %shard_map.133 = (f32[4096,512]{1,0:T(8,128)}, bf16[512,512]{1,0:T(8,128)(2,1)}) custom-call(bf16[16,16,32,256]{3,2,1,0:T(8,128)(2,1)} %all-to-all-done.3.arrived, bf16[4096,512]{1,0:T(8,128)(2,1)} %tokens.7, bf16[4096,512]{1,0:T(8,128)(2,1)} %get-tuple-element.21.value, bf16[4096,512]{1,0:T(8,128)(2,1)} %cotangent.3, bf16[256,256]{1,0:T(8,128)(2,1)} %fourth.3, ...), custom_call_target="tpu_custom_call" | custom-call | flops 5400000000 | bytes 26214400 | tf_op jit(solution)/shard_map/pallas_call | solution.py:269
  341.3 57.7 %all-to-all-done.2.arrived = bf16[16,16,32,256]{3,2,1,0:T(8,128)(2,1)} async-done(((bf16[16,16,32,256]{3,2,1,0:T(8,128)(2,1)}), bf16[16,16,32,256]{3,2,1,0:T(8,128)(2,1)}, u32[]{:S(2)}, u32[]{:S(2)}) %all-to-all-start.2) | async-done | bytes 4194336 | tf_op jit(solution)/shard_map/all_to_all | solution.py:206
  399.0 19.2 %shard_map.134 = (bf16[4096,512]{1,0:T(8,128)(2,1)}, bf16[512,512]{1,0:T(8,128)(2,1)}) custom-call(bf16[16,16,32,256]{3,2,1,0:T(8,128)(2,1)} %all-to-all-done.2.arrived, bf16[4096,512]{1,0:T(8,128)(2,1)} %tokens.7, bf16[4096,512]{1,0:T(8,128)(2,1)} %get-tuple-element.19.d_mix, f32[4096,512]{1,0:T(8,128)} %get-tuple-element.22.partial, ...), custom_call_target="tpu_custom_call" | custom-call | flops 5400000000 | bytes 26214400 | tf_op jit(solution)/shard_map/pallas_call | solution.py:280
  418.2 34.1 %all_to_all.30 = bf16[16,32,512]{2,1,0:T(8,128)(2,1)S(1)} all-to-all(bf16[16,32,512]{2,1,0:T(8,128)(2,1)} %bitcast.18), channel_id=1, replica_groups=mesh['parts'=2,'seq'=16] {'seq'}, dimensions={0} | all-to-all | bytes 1048576 | tf_op jit(solution)/shard_map/all_to_all | solution.py:206
  452.4 0.8 broadcast_in_dim.2
  453.3 4.1 all-to-all-start.5
  458.2 36.1 %psum.15 = bf16[512]{0:T(512)(128)(2,1)S(1)} all-reduce(bf16[512]{0:T(512)(128)(2,1)S(1)} %convert_reduce_fusion), channel_id=1, replica_groups=mesh['parts'=2,'seq'=16] {'seq'}, use_global_device_ids=true, to_apply=%region_2.3 | all-reduce | flops 512 | bytes 2048 | tf_op jit(solution)/shard_map/psum | solution.py:291
  494.9 58.9 %all-reduce.2.cloned.1.call-done = bf16[1,512,512]{2,1,0:T(8,128)(2,1)} async-done(((bf16[1,512,512]{2,1,0:T(8,128)(2,1)}), bf16[1,512,512]{2,1,0:T(8,128)(2,1)}) %all-reduce.2.cloned.1.call-update) | async-done | bytes 524304 | tf_op jit(solution)/shard_map/psum | solution.py:291
  553.8 2.5 maximum_convert_fusion
  (15 shorter events, 1.4 us)
Async XLA Ops:
  21.5 85.1 %all-to-all-start.1 = ((bf16[16,16,32,256]{3,2,1,0:T(8,128)(2,1)}), bf16[16,16,32,256]{3,2,1,0:T(8,128)(2,1)}, u32[]{:S(2)}, u32[]{:S(2)}) async-start(bf16[16,16,32,256]{3,2,1,0:T(8,128)(2,1)} %shard_map.130), calls=%async_computation.1 | async-start | bytes 8388608 | tf_op jit(solution)/shard_map/all_to_all | solution.py:206
  106.6 97.4 %all-to-all-start = ((bf16[16,16,32,256]{3,2,1,0:T(8,128)(2,1)}), bf16[16,16,32,256]{3,2,1,0:T(8,128)(2,1)}, u32[]{:S(2)}, u32[]{:S(2)}) async-start(bf16[16,16,32,256]{3,2,1,0:T(8,128)(2,1)} %get-tuple-element.16), calls=%async_computation | async-start | bytes 8388608 | tf_op jit(solution)/shard_map/all_to_all | solution.py:206
  204.0 19.8 %copy-start = (bf16[256,256]{1,0:T(8,128)(2,1)S(1)}, bf16[256,256]{1,0:T(8,128)(2,1)}, u32[]{:S(2)}) copy-start(bf16[256,256]{1,0:T(8,128)(2,1)} %second.1) | copy-start | bytes 393220
  204.0 20.6 %copy-start.1 = (bf16[256,256]{1,0:T(8,128)(2,1)S(1)}, bf16[256,256]{1,0:T(8,128)(2,1)}, u32[]{:S(2)}) copy-start(bf16[256,256]{1,0:T(8,128)(2,1)} %third.1) | copy-start | bytes 393220
  204.0 97.5 %all-to-all-start.3 = ((bf16[16,16,32,256]{3,2,1,0:T(8,128)(2,1)}), bf16[16,16,32,256]{3,2,1,0:T(8,128)(2,1)}, u32[]{:S(2)}, u32[]{:S(2)}) async-start(bf16[16,16,32,256]{3,2,1,0:T(8,128)(2,1)} %bitcast.12), calls=%async_computation.3 | async-start | bytes 8388608 | tf_op jit(solution)/shard_map/all_to_all | solution.py:206
  301.5 19.8 %copy-start.2 = (bf16[256,256]{1,0:T(8,128)(2,1)S(1)}, bf16[256,256]{1,0:T(8,128)(2,1)}, u32[]{:S(2)}) copy-start(bf16[256,256]{1,0:T(8,128)(2,1)} %first.1) | copy-start | bytes 393220
  301.5 97.5 %all-to-all-start.2 = ((bf16[16,16,32,256]{3,2,1,0:T(8,128)(2,1)}), bf16[16,16,32,256]{3,2,1,0:T(8,128)(2,1)}, u32[]{:S(2)}, u32[]{:S(2)}) async-start(bf16[16,16,32,256]{3,2,1,0:T(8,128)(2,1)} %bitcast.11), calls=%async_computation.2 | async-start | bytes 8388608 | tf_op jit(solution)/shard_map/all_to_all | solution.py:206
  399.0 59.1 %copy-start.3 = (f32[1,512]{1,0:T(1,128)S(1)}, f32[1,512]{1,0:T(1,128)}, u32[]{:S(2)}) copy-start(f32[1,512]{1,0:T(1,128)} %get-tuple-element.27) | copy-start | bytes 6148
  453.3 100.5 %all-to-all-start.5 = ((bf16[16,32,512]{2,1,0:T(8,128)(2,1)}), bf16[16,32,512]{2,1,0:T(8,128)(2,1)S(1)}, u32[]{:S(2)}, u32[]{:S(2)}) async-start(bf16[16,32,512]{2,1,0:T(8,128)(2,1)} %broadcast_in_dim.2), calls=%async_computation.5 | async-start | bytes 1048576 | tf_op jit(solution)/shard_map/all_to_all | solution.py:206
  457.4 96.4 %all-reduce.2.cloned.1.call-start = ((), (), s32[]{:S(2)}) async-start(), calls=%async_computation.6 | async-start | bytes 1048576 | tf_op jit(solution)/shard_map/psum | solution.py:291
Sparse Core Ops, SparseCore 0:
  462.2 91.5 all-reduce.1

commit v3 on v2

--- a/solution.py
+++ b/solution.py
@@ -37,41 +37,62 @@
     return pl.BlockSpec(shape, lambda i: (0,) * len(shape))
 
 
-def rows_of(step):
-    return pl.BlockSpec((N2, D), lambda i: (i, 0))
-
-
-def by_device(n, chans):
-    return pl.BlockSpec((n, 1, chans, N2), lambda i: (0, i, 0, 0))
-
-
-def section_one_kernel(tokens, w_value, first, out, w_turned):
+def rows_of(per):
+    return pl.BlockSpec((per * N2, D), lambda i: (i, 0))
+
+
+def by_device(n, per, chans):
+    return pl.BlockSpec((n, per, chans, N2), lambda i: (0, i, 0, 0))
+
+
+def row_slice(r):
+    return slice(r * N2, (r + 1) * N2)
+
+
+def section_one_kernel(tokens, w_value, first, out, w_turned, first_turned):
     @pl.when(pl.program_id(0) == 0)
     def _():
         w_turned[...] = w_value[...].T
-
-    value_t = dot_nt(w_turned[...], tokens[...]).astype(bf16)
-    section = dot_nt(value_t, first[...]).astype(bf16)
-    out[...] = section.reshape(out.shape)
+        first_turned[...] = first[...].T
+
+    n, per, chans, _ = out.shape
+    for r in range(per):
+        value_t = dot_nt(w_turned[...], tokens[row_slice(r)]).astype(bf16)
+        section = dot_nn(value_t, first_turned[...]).astype(bf16)
+        out[:, r] = section.reshape(n, chans, N2)
 
 
 def d_three_kernel(
-    tokens, cotangent, w_value, w_gate, fourth, out, value_out, d_mix_out, skip_out
+    tokens,
+    cotangent,
+    w_value,
+    w_gate,
+    fourth,
+    out,
+    value_out,
+    d_mix_out,
+    tokens_t_out,
+    skip_out,
 ):
-    value = dot_nn(tokens[...], w_value[...]).astype(bf16)
-    gate = dot_nn(tokens[...], w_gate[...]).astype(bf16)
-    d_mix = (cotangent[...].astype(f32) * gate.astype(f32)).astype(bf16)
-    value_out[...] = value
-    d_mix_out[...] = d_mix
-    term = jnp.sum(d_mix.astype(f32) * value.astype(f32), axis=0, keepdims=True)
+    n, per, chans, _ = out.shape
 
     @pl.when(pl.program_id(0) == 0)
     def _():
         skip_out[...] = jnp.zeros_like(skip_out)
 
-    skip_out[...] += term
-    section = dot_tn(d_mix, fourth[...]).astype(bf16)
-    out[...] = section.reshape(out.shape)
+    for r in range(per):
+        here = row_slice(r)
+        value = dot_nn(tokens[here], w_value[...]).astype(bf16)
+        gate = dot_nn(tokens[here], w_gate[...]).astype(bf16)
+        d_mix = (cotangent[here].astype(f32) * gate.astype(f32)).astype(bf16)
+        value_out[here] = value
+        d_mix_out[here] = d_mix
+        tokens_t_out[:, here] = tokens[here].T
+        skip_out[...] += jnp.sum(
+            d_mix.astype(f32) * value.astype(f32), axis=0, keepdims=True
+        )
+        section = dot_tn(d_mix, fourth[...]).astype(bf16)
+        out[:, r] = section.reshape(n, chans, N2)
 
 
 def turn_in(swap, arrived, by_channel):
@@ -136,31 +157,51 @@
         total[...] += term
 
 
+def finish(total, factor, grad_w):
+    @pl.when(pl.program_id(0) == pl.num_programs(0) - 1)
+    def _():
+        grad_w[...] = (total[...] * factor[0, 0]).astype(bf16)
+
+
 def gate_kernel(
-    arrived, tokens, value, cotangent, fourth, w_gate, skip, factor, partial, grad_w, total
+    arrived,
+    tokens_t,
+    value,
+    cotangent,
+    fourth,
+    w_gate_t,
+    skip,
+    factor,
+    partial,
+    grad_w,
+    total,
+    d_gate,
 ):
-    conv = dot_nt(fourth[...], arrived[...].reshape(D, N2))
-    mixed = conv + skip[...] * value[...].astype(f32)
-    d_gate = (cotangent[...].astype(f32) * mixed).astype(bf16)
-    partial[...] = dot_nt(d_gate, w_gate[...])
-    accumulate(total, dot_tn(tokens[...], d_gate))
-
-    @pl.when(pl.program_id(0) == pl.num_programs(0) - 1)
-    def _():
-        grad_w[...] = (total[...] * factor[0, 0]).astype(bf16)
-
-
-def value_kernel(
-    arrived, tokens, d_mix, partial, first_t, w_value, skip, factor, grad_tokens, grad_w, total
-):
-    d_cube = dot_nt(first_t[...], arrived[...].reshape(D, N2))
-    d_value = (d_cube + skip[...] * d_mix[...].astype(f32)).astype(bf16)
-    grad_tokens[...] = (partial[...] + dot_nt(d_value, w_value[...])).astype(bf16)
-    accumulate(total, dot_tn(tokens[...], d_value))
-
-    @pl.when(pl.program_id(0) == pl.num_programs(0) - 1)
-    def _():
-        grad_w[...] = (total[...] * factor[0, 0]).astype(bf16)
+    for r in range(arrived.shape[1]):
+        here = row_slice(r)
+        conv = dot_nt(fourth[...], arrived[:, r].reshape(D, N2))
+        mixed = conv + skip[...] * value[here].astype(f32)
+        d_gate[here] = (cotangent[here].astype(f32) * mixed).astype(bf16)
+        partial[here] = dot_nn(d_gate[here], w_gate_t[...])
+    accumulate(total, dot_nn(tokens_t[...], d_gate[...]))
+    finish(total, factor, grad_w)
+
+
+def value_kernel(arrived, tokens_t, d_mix, first_t, skip, factor, _, d_value, grad_w, total):
+    for r in range(arrived.shape[1]):
+        here = row_slice(r)
+        d_cube = dot_nt(first_t[...], arrived[:, r].reshape(D, N2))
+        d_value[here] = (d_cube + skip[...] * d_mix[here].astype(f32)).astype(bf16)
+    accumulate(total, dot_nn(tokens_t[...], d_value[...]))
+    finish(total, factor, grad_w)
+
+
+def tokens_kernel(d_value, partial, w_value_t, grad_tokens):
+    for r in range(d_value.shape[0] // N2):
+        here = row_slice(r)
+        grad_tokens[here] = (
+            partial[here] + dot_nn(d_value[here], w_value_t[...])
+        ).astype(bf16)
 
 
 def on_device(
@@ -185,8 +226,10 @@
     square = whole((D, D))
     block = whole((N1, N2))
     line = whole((1, D))
-    row = rows_of(0)
-    sent = by_device(n, chans)
+    per = min(4, rows)
+    row = rows_of(per)
+    column = pl.BlockSpec((D, per * N2), lambda i: (0, i))
+    sent = by_device(n, per, chans)
     one = pl.BlockSpec(memory_space=pltpu.SMEM)
     place = jnp.arange(GROUP * GROUP)
     swap = (
@@ -207,29 +250,30 @@
 
     one_sent = pl.pallas_call(
         section_one_kernel,
-        grid=(rows,),
+        grid=(rows // per,),
         in_specs=[row, square, block],
         out_specs=sent,
         out_shape=shape(sections),
-        scratch_shapes=[pltpu.VMEM((D, D), bf16)],
+        scratch_shapes=[pltpu.VMEM((D, D), bf16), pltpu.VMEM((N2, N2), bf16)],
         compiler_params=params(),
         cost_estimate=cost(3.2, 9),
     )(tokens, w_value, first_block)
     one_home = transfer(one_sent)
 
-    three_sent, value, d_mix, skip_term = pl.pallas_call(
+    three_sent, value, d_mix, tokens_t, skip_term = pl.pallas_call(
         d_three_kernel,
-        grid=(rows,),
+        grid=(rows // per,),
         in_specs=[row, row, square, square, block],
-        out_specs=[sent, row, row, line],
+        out_specs=[sent, row, row, column, line],
         out_shape=[
             shape(sections),
             shape((local_rows, D)),
             shape((local_rows, D)),
+            shape((D, local_rows)),
             shape((1, D), f32),
         ],
         compiler_params=params(),
-        cost_estimate=cost(5.4, 21),
+        cost_estimate=cost(5.4, 25),
     )(tokens, cotangent, w_value, w_gate, fourth_block)
     three_home = transfer(three_sent)
 
@@ -268,32 +312,42 @@
 
     partial, gate_term = pl.pallas_call(
         gate_kernel,
-        grid=(rows,),
-        in_specs=[sent, row, row, row, block, square, line, one],
+        grid=(rows // per,),
+        in_specs=[sent, column, row, row, block, square, line, one],
         out_specs=[row, square],
         out_shape=[shape((local_rows, D), f32), shape((D, D))],
-        scratch_shapes=[pltpu.VMEM((D, D), f32)],
+        scratch_shapes=[pltpu.VMEM((D, D), f32), pltpu.VMEM((per * N2, D), bf16)],
         compiler_params=params(),
         cost_estimate=cost(5.4, 25),
-    )(three_here, tokens, value, cotangent, fourth_block, w_gate, skip, factor)
-
-    grad_tokens, value_term = pl.pallas_call(
+    )(three_here, tokens_t, value, cotangent, fourth_block, w_gate.T, skip, factor)
+
+    skip_rows = jnp.pad((skip_term * factor[0, 0]).astype(bf16), ((0, GROUP - 1), (0, 0)))
+    early = lax.psum(jnp.concatenate([gate_term, skip_rows]), "seq")
+
+    d_value, value_term = pl.pallas_call(
         value_kernel,
-        grid=(rows,),
-        in_specs=[sent, row, row, row, block, square, line, one],
+        grid=(rows // per,),
+        in_specs=[sent, column, row, block, line, one, pl.BlockSpec(memory_space=pl.ANY)],
         out_specs=[row, square],
         out_shape=[shape((local_rows, D)), shape((D, D))],
         scratch_shapes=[pltpu.VMEM((D, D), f32)],
         compiler_params=params(),
-        cost_estimate=cost(5.4, 25),
-    )(one_here, tokens, d_mix, partial, first_block.T, w_value, skip, factor)
-
-    gate_total, skip_total = lax.psum(
-        (gate_term, (skip_term.reshape(D) * factor[0, 0]).astype(bf16)), "seq"
-    )
+        cost_estimate=cost(3.3, 17),
+    )(one_here, tokens_t, d_mix, first_block.T, skip, factor, early)
+
     parts = transfer(value_term.reshape(n, D // n, D))
+    grad_tokens = pl.pallas_call(
+        tokens_kernel,
+        grid=(rows // per,),
+        in_specs=[row, row, square],
+        out_specs=row,
+        out_shape=shape((local_rows, D)),
+        compiler_params=params(),
+        cost_estimate=cost(2.1, 16),
+    )(d_value, partial, w_value.T)
     mine = jnp.sum(parts.astype(f32), axis=0).astype(bf16)
     value_total = transfer(jnp.broadcast_to(mine, (n, D // n, D))).reshape(D, D)
+    gate_total, skip_total = early[:D], early[D]
     return (
         grad_tokens,
         grad_kernel,

time: 565 us -> 528 us (0.935)
  blocking collectives: 70.3 us -> 19.6 us
  waiting for transfers between devices: 288 us -> 318 us
  Pallas kernels: 113 us -> 94.6 us
    psum x1 -> x0, blocking collectives: 36.1 us -> none  [on_device(): lax.psum((gate_term, (skip_term.reshape(D) * factor[0, 0]).astype(bf16)),...]
    pallas_call x4 -> x5, Pallas kernels: 72.1 us -> 53.9 us  [the longest x1 14 us: on_device(): pl.pallas_call(d_three_kernel, grid=(rows // per,), in_specs=[row, row, s...]
    all_to_all x5, waiting for transfers between devices: 228 us -> 245 us  [transfer(): return lax.all_to_all(array, 'seq', split_axis=0, concat_axis=0, tiled=True)]
    psum x1, waiting for transfers between devices: 58.9 us -> 73.6 us  [on_device(): early = lax.psum(jnp.concatenate([gate_term, skip_rows]), 'seq')]
    all_to_all x1, blocking collectives: 34.1 us -> 19.6 us  [transfer(): return lax.all_to_all(array, 'seq', split_axis=0, concat_axis=0, tiled=True)]
  transfers between devices with their start and end apart: 6 -> 6, of which waited for: 5 -> 6; matrix products, arithmetic and copies ran while one was open for 1% -> 1% of each run, Pallas kernels for 14% -> 14%
where the time goes in v3:
time: 528 us
  waiting for transfers between devices  318 us (60%)
  Pallas kernels  94.6 us (18%)
  starting transfers between devices  70.9 us (13%)
  blocking collectives  19.6 us (4%)
  between operations  14.1 us (3%)
    all_to_all x5, waiting for transfers between devices, transfer(): return lax.all_to_all(array, 'seq', split_axis=0, concat_axis=0, tiled=True)  245 us
    psum x1, waiting for transfers between devices, on_device(): early = lax.psum(jnp.concatenate([gate_term, skip_rows]), 'seq')  73.6 us
    all_to_all x5, starting transfers between devices, transfer(): return lax.all_to_all(array, 'seq', split_axis=0, concat_axis=0, tiled=True)  70.9 us
    pallas_call x1, Pallas kernels, on_device(): pl.pallas_call(home_backward_kernel, grid=(chans // GROUP,), in_specs=[at...  20.6 us
    pallas_call x1, Pallas kernels, on_device(): pl.pallas_call(home_forward_kernel, grid=(chans // GROUP,), in_specs=[at_...  20.1 us
    all_to_all x1, blocking collectives, transfer(): return lax.all_to_all(array, 'seq', split_axis=0, concat_axis=0, tiled=True)  19.6 us
    pallas_call x1, Pallas kernels, on_device(): pl.pallas_call(d_three_kernel, grid=(rows // per,), in_specs=[row, row, s...  14 us
    pallas_call x1, Pallas kernels, on_device(): pl.pallas_call(gate_kernel, grid=(rows // per,), in_specs=[sent, column,...  13.1 us
  transfers between devices with their start and end apart: 6, of which 6 were waited for; matrix products, arithmetic and copies ran while one was open for 1% of the time, Pallas kernels for 14%

profile of v3, /device:TPU:0, one launch (start us, length us, event | category | flops | bytes accessed | tf_op | source)
XLA Modules:
  0.0 527.6 jit_solution(5813696277899425167)
XLA Ops:
  7.2 9.2 %shard_map.130 = bf16[16,16,32,256]{3,2,1,0:T(8,128)(2,1)} custom-call(bf16[4096,512]{1,0:T(8,128)(2,1)} %tokens.3, bf16[512,512]{1,0:T(8,128)(2,1)} %w_value.3, bf16[256,256]{1,0:T(8,128)(2,1)} %first.1), custom_call_target="tpu_custom_call" | custom-call | flops 3200000000 | bytes 9437184 | tf_op jit(solution)/shard_map/pallas_call | solution.py:251
  16.4 7.4 %all-to-all-start.1 = ((bf16[16,16,32,256]{3,2,1,0:T(8,128)(2,1)}), bf16[16,16,32,256]{3,2,1,0:T(8,128)(2,1)}, u32[]{:S(2)}, u32[]{:S(2)}) async-start(bf16[16,16,32,256]{3,2,1,0:T(8,128)(2,1)} %shard_map.130), calls=%async_computation.1 | async-start | bytes 8388608 | tf_op jit(solution)/shard_map/all_to_all | solution.py:249
  23.8 14.0 %shard_map.129 = (bf16[16,16,32,256]{3,2,1,0:T(8,128)(2,1)}, bf16[4096,512]{1,0:T(8,128)(2,1)}, bf16[4096,512]{1,0:T(8,128)(2,1)}, bf16[512,4096]{1,0:T(8,128)(2,1)}, f32[1,512]{1,0:T(1,128)}) custom-call(bf16[4096,512]{1,0:T(8,128)(2,1)} %tokens.3, bf16[4096,512]{1,0:T(8,128)(2,1)} %cotangent.3, bf16[512,512]{1,0:T(8,128)(2,1)} %w_value.3, ...), custom_call_target="tpu_custom_call" | custom-call | flops 5400000000 | bytes 26214400 | tf_op jit(solution)/shard_map/pallas_call | solution.py:263
  37.9 63.6 %all-to-all-done.1 = bf16[16,16,32,256]{3,2,1,0:T(8,128)(2,1)} async-done(((bf16[16,16,32,256]{3,2,1,0:T(8,128)(2,1)}), bf16[16,16,32,256]{3,2,1,0:T(8,128)(2,1)}, u32[]{:S(2)}, u32[]{:S(2)}) %all-to-all-start.1) | async-done | bytes 4194336 | tf_op jit(solution)/shard_map/all_to_all | solution.py:249
  101.5 19.7 %all-to-all-start = ((bf16[16,16,32,256]{3,2,1,0:T(8,128)(2,1)}), bf16[16,16,32,256]{3,2,1,0:T(8,128)(2,1)}, u32[]{:S(2)}, u32[]{:S(2)}) async-start(bf16[16,16,32,256]{3,2,1,0:T(8,128)(2,1)} %get-tuple-element.17), calls=%async_computation | async-start | bytes 8388608 | tf_op jit(solution)/shard_map/all_to_all | solution.py:249
  122.0 20.1 %shard_map.131 = (bf16[256,32,256]{2,1,0:T(8,128)(2,1)}, f32[32,256,256]{2,1,0:T(8,128)}) custom-call(bf16[256,32,256]{2,1,0:T(8,128)(2,1)} %bitcast.1.arrived, bf16[32,256,256]{2,1,0:T(8,128)(2,1)} %kernel.3, bf16[256,256]{1,0:T(8,128)(2,1)} %second.1, bf16[256,256]{1,0:T(8,128)(2,1)} %third.1, bf16[256,256]{1,0:T(8,128)(2,1)} %fusion.2.swap), custom_call_target="tpu_custom_call" | custom-call | flops 4300000256 | bytes 20971520 | tf_op jit(solution)/shard_map/pallas_call | solution.py:282
  142.1 56.8 %all-to-all-done = bf16[16,16,32,256]{3,2,1,0:T(8,128)(2,1)} async-done(((bf16[16,16,32,256]{3,2,1,0:T(8,128)(2,1)}), bf16[16,16,32,256]{3,2,1,0:T(8,128)(2,1)}, u32[]{:S(2)}, u32[]{:S(2)}) %all-to-all-start) | async-done | bytes 4194336 | tf_op jit(solution)/shard_map/all_to_all | solution.py:249
  198.9 19.8 %all-to-all-start.3 = ((bf16[16,16,32,256]{3,2,1,0:T(8,128)(2,1)}), bf16[16,16,32,256]{3,2,1,0:T(8,128)(2,1)}, u32[]{:S(2)}, u32[]{:S(2)}) async-start(bf16[16,16,32,256]{3,2,1,0:T(8,128)(2,1)} %bitcast.16), calls=%async_computation.3 | async-start | bytes 8388608 | tf_op jit(solution)/shard_map/all_to_all | solution.py:249
  220.2 20.6 %shard_map.132 = (bf16[256,32,256]{2,1,0:T(8,128)(2,1)}, bf16[32,256,256]{2,1,0:T(8,128)(2,1)}) custom-call(bf16[256,32,256]{2,1,0:T(8,128)(2,1)} %bitcast.arrived, bf16[32,256,256]{2,1,0:T(8,128)(2,1)} %kernel.3, f32[32,256,256]{2,1,0:T(8,128)} %get-tuple-element.18.spectrum, bf16[256,256]{1,0:T(8,128)(2,1)} %bitcast.20, bf16[256,256]{1,0:T(8,128)(2,1)} %bitcast.21, ...), custom_call_target="tpu_custom_call" | custom-call | flops 4300000256 | bytes 25165824 | tf_op jit(solution)/shard_map/pallas_call | solution.py:294
  240.9 55.5 %all-to-all-done.3.arrived = bf16[16,16,32,256]{3,2,1,0:T(8,128)(2,1)} async-done(((bf16[16,16,32,256]{3,2,1,0:T(8,128)(2,1)}), bf16[16,16,32,256]{3,2,1,0:T(8,128)(2,1)}, u32[]{:S(2)}, u32[]{:S(2)}) %all-to-all-start.3) | async-done | bytes 4194336 | tf_op jit(solution)/shard_map/all_to_all | solution.py:249
  296.4 19.8 %all-to-all-start.2 = ((bf16[16,16,32,256]{3,2,1,0:T(8,128)(2,1)}), bf16[16,16,32,256]{3,2,1,0:T(8,128)(2,1)}, u32[]{:S(2)}, u32[]{:S(2)}) async-start(bf16[16,16,32,256]{3,2,1,0:T(8,128)(2,1)} %bitcast.15), calls=%async_computation.2 | async-start | bytes 8388608 | tf_op jit(solution)/shard_map/all_to_all | solution.py:249
  316.3 1.0 copy.17
  317.3 13.1 %shard_map.133 = (f32[4096,512]{1,0:T(8,128)}, bf16[512,512]{1,0:T(8,128)(2,1)}) custom-call(bf16[16,16,32,256]{3,2,1,0:T(8,128)(2,1)} %all-to-all-done.3.arrived, bf16[512,4096]{1,0:T(8,128)(2,1)} %get-tuple-element.20.tokens_t, bf16[4096,512]{1,0:T(8,128)(2,1)} %get-tuple-element.23.value, bf16[4096,512]{1,0:T(8,128)(2,1)} %cotangent.3, ...), custom_call_target="tpu_custom_call" | custom-call | flops 5400000000 | bytes 26214400 | tf_op jit(solution)/shard_map/pallas_call | solution.py:313
  330.4 1.9 fusion.1
  333.1 64.4 %all-to-all-done.2.arrived = bf16[16,16,32,256]{3,2,1,0:T(8,128)(2,1)} async-done(((bf16[16,16,32,256]{3,2,1,0:T(8,128)(2,1)}), bf16[16,16,32,256]{3,2,1,0:T(8,128)(2,1)}, u32[]{:S(2)}, u32[]{:S(2)}) %all-to-all-start.2) | async-done | bytes 4194336 | tf_op jit(solution)/shard_map/all_to_all | solution.py:249
  397.5 73.6 %all-reduce.3.cloned.1.call-done._ = bf16[528,512]{1,0:T(8,128)(2,1)} async-done(((bf16[528,512]{1,0:T(8,128)(2,1)}), bf16[528,512]{1,0:T(8,128)(2,1)}) %all-reduce.3.cloned.1.call-update) | async-done | bytes 540688 | tf_op jit(solution)/shard_map/psum | solution.py:325
  471.1 9.1 %shard_map.134 = (bf16[4096,512]{1,0:T(8,128)(2,1)}, bf16[512,512]{1,0:T(8,128)(2,1)}) custom-call(bf16[16,16,32,256]{3,2,1,0:T(8,128)(2,1)} %all-to-all-done.2.arrived, bf16[512,4096]{1,0:T(8,128)(2,1)} %get-tuple-element.20.tokens_t, bf16[4096,512]{1,0:T(8,128)(2,1)} %get-tuple-element.21.d_mix, bf16[256,256]{1,0:T(8,128)(2,1)} %bitcast.19, ...), custom_call_target="tpu_custom_call" | custom-call | flops 3300000000 | bytes 17825792 | tf_op jit(solution)/shard_map/pallas_call | solution.py:327
  480.1 19.6 %all_to_all.30 = bf16[16,32,512]{2,1,0:T(8,128)(2,1)S(1)} all-to-all(bf16[16,32,512]{2,1,0:T(8,128)(2,1)} %bitcast.22), channel_id=1, replica_groups=mesh['parts'=2,'seq'=16] {'seq'}, dimensions={0} | all-to-all | bytes 1048576 | tf_op jit(solution)/shard_map/all_to_all | solution.py:249
  499.8 0.9 broadcast_in_dim.2
  500.7 4.1 all-to-all-start.5
  504.8 1.0 copy.18
  505.8 8.5 %shard_map.135 = bf16[4096,512]{1,0:T(8,128)(2,1)} custom-call(bf16[4096,512]{1,0:T(8,128)(2,1)} %get-tuple-element.26.d_value, f32[4096,512]{1,0:T(8,128)} %get-tuple-element.27.partial, bf16[512,512]{1,0:T(8,128)(2,1)} %bitcast.17), custom_call_target="tpu_custom_call" | custom-call | flops 2100000000 | bytes 16777216 | tf_op jit(solution)/shard_map/pallas_call | solution.py:339
  514.9 4.4 all-to-all-done.5
  519.3 1.5 maximum_convert_fusion
  (25 shorter events, 3.8 us)
Async XLA Ops:
  16.4 85.1 %all-to-all-start.1 = ((bf16[16,16,32,256]{3,2,1,0:T(8,128)(2,1)}), bf16[16,16,32,256]{3,2,1,0:T(8,128)(2,1)}, u32[]{:S(2)}, u32[]{:S(2)}) async-start(bf16[16,16,32,256]{3,2,1,0:T(8,128)(2,1)} %shard_map.130), calls=%async_computation.1 | async-start | bytes 8388608 | tf_op jit(solution)/shard_map/all_to_all | solution.py:249
  101.5 97.4 %all-to-all-start = ((bf16[16,16,32,256]{3,2,1,0:T(8,128)(2,1)}), bf16[16,16,32,256]{3,2,1,0:T(8,128)(2,1)}, u32[]{:S(2)}, u32[]{:S(2)}) async-start(bf16[16,16,32,256]{3,2,1,0:T(8,128)(2,1)} %get-tuple-element.17), calls=%async_computation | async-start | bytes 8388608 | tf_op jit(solution)/shard_map/all_to_all | solution.py:249
  198.9 19.8 %copy-start.3 = (bf16[256,256]{1,0:T(8,128)(2,1)S(1)}, bf16[256,256]{1,0:T(8,128)(2,1)}, u32[]{:S(2)}) copy-start(bf16[256,256]{1,0:T(8,128)(2,1)} %second.1) | copy-start | bytes 393220
  198.9 20.6 %copy-start.4 = (bf16[256,256]{1,0:T(8,128)(2,1)S(1)}, bf16[256,256]{1,0:T(8,128)(2,1)}, u32[]{:S(2)}) copy-start(bf16[256,256]{1,0:T(8,128)(2,1)} %third.1) | copy-start | bytes 393220
  198.9 97.5 %all-to-all-start.3 = ((bf16[16,16,32,256]{3,2,1,0:T(8,128)(2,1)}), bf16[16,16,32,256]{3,2,1,0:T(8,128)(2,1)}, u32[]{:S(2)}, u32[]{:S(2)}) async-start(bf16[16,16,32,256]{3,2,1,0:T(8,128)(2,1)} %bitcast.16), calls=%async_computation.3 | async-start | bytes 8388608 | tf_op jit(solution)/shard_map/all_to_all | solution.py:249
  296.4 19.9 %copy-start.1 = (bf16[512,512]{1,0:T(8,128)(2,1)S(1)}, bf16[512,512]{1,0:T(8,128)(2,1)}, u32[]{:S(2)}) copy-start(bf16[512,512]{1,0:T(8,128)(2,1)} %w_gate.1) | copy-start | bytes 1572868
  296.4 20.9 %copy-start.6 = (f32[1,512]{1,0:T(1,128)S(1)}, f32[1,512]{1,0:T(1,128)}, u32[]{:S(2)}) copy-start(f32[1,512]{1,0:T(1,128)} %get-tuple-element.25) | copy-start | bytes 6148
  296.4 101.1 %all-to-all-start.2 = ((bf16[16,16,32,256]{3,2,1,0:T(8,128)(2,1)}), bf16[16,16,32,256]{3,2,1,0:T(8,128)(2,1)}, u32[]{:S(2)}, u32[]{:S(2)}) async-start(bf16[16,16,32,256]{3,2,1,0:T(8,128)(2,1)} %bitcast.15), calls=%async_computation.2 | async-start | bytes 8388608 | tf_op jit(solution)/shard_map/all_to_all | solution.py:249
  316.2 154.8 %all-reduce.3.cloned.1.call-start = ((), (), s32[]{:S(2)}) async-start(), calls=%async_computation.6 | async-start | bytes 1081344 | tf_op jit(solution)/shard_map/psum | solution.py:325
  317.3 15.0 %copy-start.5 = (bf16[256,256]{1,0:T(8,128)(2,1)S(1)}, bf16[256,256]{1,0:T(8,128)(2,1)}, u32[]{:S(2)}) copy-start(bf16[256,256]{1,0:T(8,128)(2,1)} %first.1) | copy-start | bytes 393220
  471.1 33.7 %copy-start.2 = (bf16[512,512]{1,0:T(8,128)(2,1)S(1)}, bf16[512,512]{1,0:T(8,128)(2,1)}, u32[]{:S(2)}) copy-start(bf16[512,512]{1,0:T(8,128)(2,1)} %w_value.3) | copy-start | bytes 1572868
  500.7 18.6 %all-to-all-start.5 = ((bf16[16,32,512]{2,1,0:T(8,128)(2,1)}), bf16[16,32,512]{2,1,0:T(8,128)(2,1)S(1)}, u32[]{:S(2)}, u32[]{:S(2)}) async-start(bf16[16,32,512]{2,1,0:T(8,128)(2,1)} %broadcast_in_dim.2), calls=%async_computation.5 | async-start | bytes 1048576 | tf_op jit(solution)/shard_map/all_to_all | solution.py:249
  505.8 8.5 %copy-start = (bf16[528,512]{1,0:T(8,128)(2,1)S(1)}, bf16[528,512]{1,0:T(8,128)(2,1)}, u32[]{:S(2)}) copy-start(bf16[528,512]{1,0:T(8,128)(2,1)} %all-reduce.3.cloned.1.call-done._) | copy-start | bytes 1622020
Sparse Core Ops, SparseCore 0:
  332.4 138.5 all-reduce.2

commit v4 on v3

--- a/solution.py
+++ b/solution.py
@@ -11,6 +11,7 @@
 N1 = 256
 N2 = 256
 GROUP = 16
+LANES = 128
 VMEM_LIMIT = 56 * 1024 * 1024
 
 f32 = jnp.float32
@@ -187,21 +188,48 @@
     finish(total, factor, grad_w)
 
 
-def value_kernel(arrived, tokens_t, d_mix, first_t, skip, factor, _, d_value, grad_w, total):
+def value_row(arrived, d_mix, first_t, skip, r):
+    d_cube = dot_nt(first_t[...], arrived[:, r].reshape(D, N2))
+    return (d_cube + skip[...] * d_mix[row_slice(r)].astype(f32)).astype(bf16)
+
+
+def value_kernel(arrived, tokens_t, d_mix, first_t, skip, factor, _, grad_w, total, d_value):
     for r in range(arrived.shape[1]):
-        here = row_slice(r)
-        d_cube = dot_nt(first_t[...], arrived[:, r].reshape(D, N2))
-        d_value[here] = (d_cube + skip[...] * d_mix[here].astype(f32)).astype(bf16)
+        d_value[row_slice(r)] = value_row(arrived, d_mix, first_t, skip, r)
     accumulate(total, dot_nn(tokens_t[...], d_value[...]))
     finish(total, factor, grad_w)
 
 
-def tokens_kernel(d_value, partial, w_value_t, grad_tokens):
-    for r in range(d_value.shape[0] // N2):
-        here = row_slice(r)
-        grad_tokens[here] = (
-            partial[here] + dot_nn(d_value[here], w_value_t[...])
+def tokens_kernel(arrived, d_mix, partial, first_t, skip, w_value_t, grad_tokens):
+    for r in range(arrived.shape[1]):
+        d_value = value_row(arrived, d_mix, first_t, skip, r)
+        grad_tokens[row_slice(r)] = (
+            partial[row_slice(r)] + dot_nn(d_value, w_value_t[...])
         ).astype(bf16)
+
+
+def sum_over_seq(term, n):
+    me = lax.axis_index("seq")
+    bits = n.bit_length() - 1
+
+    def from_partner(array, b):
+        return lax.ppermute(array, "seq", [(i, i ^ (1 << b)) for i in range(n)])
+
+    part = term.reshape((2,) * bits + (term.shape[0] // n, term.shape[1]))
+    for b in range(bits):
+        axis = bits - 1 - b
+        bit = (me >> b) & 1
+        kept = lax.dynamic_index_in_dim(part, bit, axis, keepdims=False)
+        sent = lax.dynamic_index_in_dim(part, 1 - bit, axis, keepdims=False)
+        part = (kept.astype(f32) + from_partner(sent, b).astype(f32)).astype(bf16)
+    for b in reversed(range(bits)):
+        axis = bits - 1 - b
+        bit = (me >> b) & 1
+        other = from_partner(part, b)
+        part = jnp.where(
+            bit == 0, jnp.stack([part, other], axis), jnp.stack([other, part], axis)
+        )
+    return part.reshape(term.shape)
 
 
 def on_device(
@@ -321,33 +349,34 @@
         cost_estimate=cost(5.4, 25),
     )(three_here, tokens_t, value, cotangent, fourth_block, w_gate.T, skip, factor)
 
-    skip_rows = jnp.pad((skip_term * factor[0, 0]).astype(bf16), ((0, GROUP - 1), (0, 0)))
-    early = lax.psum(jnp.concatenate([gate_term, skip_rows]), "seq")
-
-    d_value, value_term = pl.pallas_call(
+    skip_lanes = jnp.broadcast_to((skip_term * factor[0, 0]).astype(bf16).T, (D, LANES))
+    early = sum_over_seq(jnp.concatenate([gate_term, skip_lanes], axis=1), n)
+
+    first_t = first_block.T
+    value_term = pl.pallas_call(
         value_kernel,
         grid=(rows // per,),
         in_specs=[sent, column, row, block, line, one, pl.BlockSpec(memory_space=pl.ANY)],
-        out_specs=[row, square],
-        out_shape=[shape((local_rows, D)), shape((D, D))],
-        scratch_shapes=[pltpu.VMEM((D, D), f32)],
-        compiler_params=params(),
-        cost_estimate=cost(3.3, 17),
-    )(one_here, tokens_t, d_mix, first_block.T, skip, factor, early)
+        out_specs=square,
+        out_shape=shape((D, D)),
+        scratch_shapes=[pltpu.VMEM((D, D), f32), pltpu.VMEM((per * N2, D), bf16)],
+        compiler_params=params(),
+        cost_estimate=cost(3.3, 13),
+    )(one_here, tokens_t, d_mix, first_t, skip, factor, early)
 
     parts = transfer(value_term.reshape(n, D // n, D))
     grad_tokens = pl.pallas_call(
         tokens_kernel,
         grid=(rows // per,),
-        in_specs=[row, row, square],
+        in_specs=[sent, row, row, block, line, square],
         out_specs=row,
         out_shape=shape((local_rows, D)),
         compiler_params=params(),
-        cost_estimate=cost(2.1, 16),
-    )(d_value, partial, w_value.T)
+        cost_estimate=cost(3.3, 20),
+    )(one_here, d_mix, partial, first_t, skip, w_value.T)
     mine = jnp.sum(parts.astype(f32), axis=0).astype(bf16)
     value_total = transfer(jnp.broadcast_to(mine, (n, D // n, D))).reshape(D, D)
-    gate_total, skip_total = early[:D], early[D]
+    gate_total, skip_total = early[:, :D], early[:, D]
     return (
         grad_tokens,
         grad_kernel,

time: 528 us -> 471 us (0.89)
  waiting for transfers between devices: 318 us -> 265 us
  between operations: 14.1 us -> 0.88 us
  starting transfers between devices: 70.9 us -> 79.7 us
    ppermute x0 -> x8, waiting for transfers between devices: none -> 86.7 us  [from_partner(): return lax.ppermute(array, 'seq', [(i, i ^ 1 << b) for i in range(n)])]
    psum x1 -> x0, waiting for transfers between devices: 73.6 us -> none  [on_device(): early = lax.psum(jnp.concatenate([gate_term, skip_rows]), 'seq')]
    all_to_all x5, waiting for transfers between devices: 245 us -> 178 us  [transfer(): return lax.all_to_all(array, 'seq', split_axis=0, concat_axis=0, tiled=True)]
    ppermute x0 -> x8, starting transfers between devices: none -> 8.82 us  [from_partner(): return lax.ppermute(array, 'seq', [(i, i ^ 1 << b) for i in range(n)])]
  transfers between devices with their start and end apart: 6 -> 13, of which waited for: 6 -> 12; matrix products, arithmetic and copies ran while one was open for 1% -> 2% of each run, Pallas kernels for 14% -> 17%
where the time goes in v4:
time: 471 us; the launch traced here: 470 us
  waiting for transfers between devices  265 us (56%)
  Pallas kernels  95.7 us (20%)
  starting transfers between devices  79.7 us (17%)
  blocking collectives  18.1 us (4%)
  local copies, waits for them, and re-layouts  5.52 us (1%)
  other arithmetic  5.48 us (1%)
    all_to_all x5, waiting for transfers between devices, transfer(): return lax.all_to_all(array, 'seq', split_axis=0, concat_axis=0, tiled=True)  178 us
    ppermute x8, waiting for transfers between devices, from_partner(): return lax.ppermute(array, 'seq', [(i, i ^ 1 << b) for i in range(n)])  86.7 us
    all_to_all x5, starting transfers between devices, transfer(): return lax.all_to_all(array, 'seq', split_axis=0, concat_axis=0, tiled=True)  70.9 us
    pallas_call x1, Pallas kernels, on_device(): pl.pallas_call(home_backward_kernel, grid=(chans // GROUP,), in_specs=[at...  20.6 us
    pallas_call x1, Pallas kernels, on_device(): pl.pallas_call(home_forward_kernel, grid=(chans // GROUP,), in_specs=[at_...  20.1 us
    all_to_all x1, blocking collectives, transfer(): return lax.all_to_all(array, 'seq', split_axis=0, concat_axis=0, tiled=True)  18.1 us
    pallas_call x1, Pallas kernels, on_device(): pl.pallas_call(d_three_kernel, grid=(rows // per,), in_specs=[row, row, s...  14 us
    pallas_call x1, Pallas kernels, on_device(): pl.pallas_call(gate_kernel, grid=(rows // per,), in_specs=[sent, column,...  13.1 us
  transfers between devices with their start and end apart: 13, of which 12 were waited for; matrix products, arithmetic and copies ran while one was open for 2% of the time, Pallas kernels for 17%

profile of v4, /device:TPU:0, one launch (start us, length us, event | category | flops | bytes accessed | tf_op | source)
XLA Modules:
  0.0 470.4 jit_solution(12278048505445452439)
XLA Ops:
  0.6 9.2 %shard_map.130 = bf16[16,16,32,256]{3,2,1,0:T(8,128)(2,1)} custom-call(bf16[4096,512]{1,0:T(8,128)(2,1)} %tokens.3, bf16[512,512]{1,0:T(8,128)(2,1)} %w_value.3, bf16[256,256]{1,0:T(8,128)(2,1)} %first.1), custom_call_target="tpu_custom_call" | custom-call | flops 3200000000 | bytes 9437184 | tf_op jit(solution)/shard_map/pallas_call | solution.py:279
  9.8 7.4 %all-to-all-start.1 = ((bf16[16,16,32,256]{3,2,1,0:T(8,128)(2,1)}), bf16[16,16,32,256]{3,2,1,0:T(8,128)(2,1)}, u32[]{:S(2)}, u32[]{:S(2)}) async-start(bf16[16,16,32,256]{3,2,1,0:T(8,128)(2,1)} %shard_map.130), calls=%async_computation.1 | async-start | bytes 8388608 | tf_op jit(solution)/shard_map/all_to_all | solution.py:277
  17.3 14.0 %shard_map.129 = (bf16[16,16,32,256]{3,2,1,0:T(8,128)(2,1)}, bf16[4096,512]{1,0:T(8,128)(2,1)}, bf16[4096,512]{1,0:T(8,128)(2,1)}, bf16[512,4096]{1,0:T(8,128)(2,1)}, f32[1,512]{1,0:T(1,128)}) custom-call(bf16[4096,512]{1,0:T(8,128)(2,1)} %tokens.3, bf16[4096,512]{1,0:T(8,128)(2,1)} %cotangent.3, bf16[512,512]{1,0:T(8,128)(2,1)} %w_value.3, ...), custom_call_target="tpu_custom_call" | custom-call | flops 5400000000 | bytes 26214400 | tf_op jit(solution)/shard_map/pallas_call | solution.py:291
  31.3 63.6 %all-to-all-done.1 = bf16[16,16,32,256]{3,2,1,0:T(8,128)(2,1)} async-done(((bf16[16,16,32,256]{3,2,1,0:T(8,128)(2,1)}), bf16[16,16,32,256]{3,2,1,0:T(8,128)(2,1)}, u32[]{:S(2)}, u32[]{:S(2)}) %all-to-all-start.1) | async-done | bytes 4194336 | tf_op jit(solution)/shard_map/all_to_all | solution.py:277
  95.0 19.7 %all-to-all-start = ((bf16[16,16,32,256]{3,2,1,0:T(8,128)(2,1)}), bf16[16,16,32,256]{3,2,1,0:T(8,128)(2,1)}, u32[]{:S(2)}, u32[]{:S(2)}) async-start(bf16[16,16,32,256]{3,2,1,0:T(8,128)(2,1)} %get-tuple-element.15), calls=%async_computation | async-start | bytes 8388608 | tf_op jit(solution)/shard_map/all_to_all | solution.py:277
  115.4 20.1 %shard_map.131 = (bf16[256,32,256]{2,1,0:T(8,128)(2,1)}, f32[32,256,256]{2,1,0:T(8,128)}) custom-call(bf16[256,32,256]{2,1,0:T(8,128)(2,1)} %bitcast.1.arrived, bf16[32,256,256]{2,1,0:T(8,128)(2,1)} %kernel.3, bf16[256,256]{1,0:T(8,128)(2,1)} %second.1, bf16[256,256]{1,0:T(8,128)(2,1)} %third.1, bf16[256,256]{1,0:T(8,128)(2,1)} %fusion.2.swap), custom_call_target="tpu_custom_call" | custom-call | flops 4300000256 | bytes 20971520 | tf_op jit(solution)/shard_map/pallas_call | solution.py:310
  135.5 56.8 %all-to-all-done = bf16[16,16,32,256]{3,2,1,0:T(8,128)(2,1)} async-done(((bf16[16,16,32,256]{3,2,1,0:T(8,128)(2,1)}), bf16[16,16,32,256]{3,2,1,0:T(8,128)(2,1)}, u32[]{:S(2)}, u32[]{:S(2)}) %all-to-all-start) | async-done | bytes 4194336 | tf_op jit(solution)/shard_map/all_to_all | solution.py:277
  192.3 19.8 %all-to-all-start.3 = ((bf16[16,16,32,256]{3,2,1,0:T(8,128)(2,1)}), bf16[16,16,32,256]{3,2,1,0:T(8,128)(2,1)}, u32[]{:S(2)}, u32[]{:S(2)}) async-start(bf16[16,16,32,256]{3,2,1,0:T(8,128)(2,1)} %bitcast.55), calls=%async_computation.3 | async-start | bytes 8388608 | tf_op jit(solution)/shard_map/all_to_all | solution.py:277
  213.7 20.6 %shard_map.132 = (bf16[256,32,256]{2,1,0:T(8,128)(2,1)}, bf16[32,256,256]{2,1,0:T(8,128)(2,1)}) custom-call(bf16[256,32,256]{2,1,0:T(8,128)(2,1)} %bitcast.arrived, bf16[32,256,256]{2,1,0:T(8,128)(2,1)} %kernel.3, f32[32,256,256]{2,1,0:T(8,128)} %get-tuple-element.16.spectrum, bf16[256,256]{1,0:T(8,128)(2,1)} %bitcast.68, bf16[256,256]{1,0:T(8,128)(2,1)} %bitcast.69, ...), custom_call_target="tpu_custom_call" | custom-call | flops 4300000256 | bytes 25165824 | tf_op jit(solution)/shard_map/pallas_call | solution.py:322
  234.3 55.5 %all-to-all-done.3.arrived = bf16[16,16,32,256]{3,2,1,0:T(8,128)(2,1)} async-done(((bf16[16,16,32,256]{3,2,1,0:T(8,128)(2,1)}), bf16[16,16,32,256]{3,2,1,0:T(8,128)(2,1)}, u32[]{:S(2)}, u32[]{:S(2)}) %all-to-all-start.3) | async-done | bytes 4194336 | tf_op jit(solution)/shard_map/all_to_all | solution.py:277
  289.8 19.8 %all-to-all-start.2 = ((bf16[16,16,32,256]{3,2,1,0:T(8,128)(2,1)}), bf16[16,16,32,256]{3,2,1,0:T(8,128)(2,1)}, u32[]{:S(2)}, u32[]{:S(2)}) async-start(bf16[16,16,32,256]{3,2,1,0:T(8,128)(2,1)} %bitcast.54), calls=%async_computation.2 | async-start | bytes 8388608 | tf_op jit(solution)/shard_map/all_to_all | solution.py:277
  310.7 13.1 %shard_map.133 = (f32[4096,512]{1,0:T(8,128)}, bf16[512,512]{1,0:T(8,128)(2,1)}) custom-call(bf16[16,16,32,256]{3,2,1,0:T(8,128)(2,1)} %all-to-all-done.3.arrived, bf16[512,4096]{1,0:T(8,128)(2,1)} %get-tuple-element.20.tokens_t, bf16[4096,512]{1,0:T(8,128)(2,1)} %get-tuple-element.21.value, bf16[4096,512]{1,0:T(8,128)(2,1)} %cotangent.3, ...), custom_call_target="tpu_custom_call" | custom-call | flops 5400000000 | bytes 26214400 | tf_op jit(solution)/shard_map/pallas_call | solution.py:341
  328.9 10.8 %collective-permute-done.1 = bf16[2,2,32,640]{3,2,0,1:T(8,128)(2,1)S(1)} collective-permute-done((bf16[2,2,32,640]{3,2,0,1:T(8,128)(2,1)S(1)}, bf16[2,2,32,640]{3,2,0,1:T(8,128)(2,1)S(1)}, u32[]{:S(2)}, u32[]{:S(2)}) %collective-permute-start.1) | collective-permute-done | bytes 163872 | tf_op jit(solution)/shard_map/ppermute | solution.py:216
  339.9 40.1 %collective-permute-done.2 = bf16[2,32,640]{2,1,0:T(8,128)(2,1)S(1)} collective-permute-done((bf16[2,32,640]{2,1,0:T(8,128)(2,1)S(1)}, bf16[2,32,640]{2,1,0:T(8,128)(2,1)S(1)}, u32[]{:S(2)}, u32[]{:S(2)}) %collective-permute-start.2) | collective-permute-done | bytes 81952 | tf_op jit(solution)/shard_map/ppermute | solution.py:216
  380.1 4.6 collective-permute-start.3
  384.6 20.8 %collective-permute-done.3 = bf16[32,640]{1,0:T(8,128)(2,1)S(1)} collective-permute-done((bf16[32,640]{1,0:T(8,128)(2,1)S(1)}, bf16[32,640]{1,0:T(8,128)(2,1)S(1)}, u32[]{:S(2)}, u32[]{:S(2)}) %collective-permute-start.3) | collective-permute-done | bytes 40992 | tf_op jit(solution)/shard_map/ppermute | solution.py:216
  406.3 4.1 collective-permute-done.4
  410.6 4.4 collective-permute-done.5
  416.6 3.7 collective-permute-done.6
  423.0 8.2 %shard_map.135 = bf16[512,512]{1,0:T(8,128)(2,1)} custom-call(bf16[16,16,32,256]{3,2,1,0:T(8,128)(2,1)} %all-to-all-done.2.arrived, bf16[512,4096]{1,0:T(8,128)(2,1)} %get-tuple-element.20.tokens_t, bf16[4096,512]{1,0:T(8,128)(2,1)} %get-tuple-element.18.d_mix, bf16[256,256]{1,0:T(8,128)(2,1)} %bitcast.61, f32[1,512]{1,0:T(1,128)} %bitcast.79, ...), custom_call_target="tpu_custom_call" | custom-call | flops 3300000000 | bytes 13631488 | tf_op jit(solution)/shard_map/pallas_call | solution.py:356
  431.2 18.1 %all_to_all.30 = bf16[16,32,512]{2,1,0:T(8,128)(2,1)S(1)} all-to-all(bf16[16,32,512]{2,1,0:T(8,128)(2,1)} %bitcast.58), channel_id=1, replica_groups=mesh['parts'=2,'seq'=16] {'seq'}, dimensions={0} | all-to-all | bytes 1048576 | tf_op jit(solution)/shard_map/all_to_all | solution.py:277
  450.3 4.1 all-to-all-start.5
  455.5 10.4 %shard_map.134 = bf16[4096,512]{1,0:T(8,128)(2,1)} custom-call(bf16[16,16,32,256]{3,2,1,0:T(8,128)(2,1)} %all-to-all-done.2.arrived, bf16[4096,512]{1,0:T(8,128)(2,1)} %get-tuple-element.18.d_mix, f32[4096,512]{1,0:T(8,128)} %get-tuple-element.22.partial, bf16[256,256]{1,0:T(8,128)(2,1)} %bitcast.62, f32[1,512]{1,0:T(1,128)} %bitcast.80, ...), custom_call_target="tpu_custom_call" | custom-call | flops 3300000000 | bytes 20971520 | tf_op jit(solution)/shard_map/pallas_call | solution.py:368
  466.6 2.3 all-to-all-done.5
  (58 shorter events, 18.0 us)
Async XLA Ops:
  9.8 85.1 %all-to-all-start.1 = ((bf16[16,16,32,256]{3,2,1,0:T(8,128)(2,1)}), bf16[16,16,32,256]{3,2,1,0:T(8,128)(2,1)}, u32[]{:S(2)}, u32[]{:S(2)}) async-start(bf16[16,16,32,256]{3,2,1,0:T(8,128)(2,1)} %shard_map.130), calls=%async_computation.1 | async-start | bytes 8388608 | tf_op jit(solution)/shard_map/all_to_all | solution.py:277
  95.0 97.4 %all-to-all-start = ((bf16[16,16,32,256]{3,2,1,0:T(8,128)(2,1)}), bf16[16,16,32,256]{3,2,1,0:T(8,128)(2,1)}, u32[]{:S(2)}, u32[]{:S(2)}) async-start(bf16[16,16,32,256]{3,2,1,0:T(8,128)(2,1)} %get-tuple-element.15), calls=%async_computation | async-start | bytes 8388608 | tf_op jit(solution)/shard_map/all_to_all | solution.py:277
  192.3 19.8 %copy-start.3 = (bf16[256,256]{1,0:T(8,128)(2,1)S(1)}, bf16[256,256]{1,0:T(8,128)(2,1)}, u32[]{:S(2)}) copy-start(bf16[256,256]{1,0:T(8,128)(2,1)} %second.1) | copy-start | bytes 393220
  192.3 20.6 %copy-start.4 = (bf16[256,256]{1,0:T(8,128)(2,1)S(1)}, bf16[256,256]{1,0:T(8,128)(2,1)}, u32[]{:S(2)}) copy-start(bf16[256,256]{1,0:T(8,128)(2,1)} %third.1) | copy-start | bytes 393220
  192.3 97.5 %all-to-all-start.3 = ((bf16[16,16,32,256]{3,2,1,0:T(8,128)(2,1)}), bf16[16,16,32,256]{3,2,1,0:T(8,128)(2,1)}, u32[]{:S(2)}, u32[]{:S(2)}) async-start(bf16[16,16,32,256]{3,2,1,0:T(8,128)(2,1)} %bitcast.55), calls=%async_computation.3 | async-start | bytes 8388608 | tf_op jit(solution)/shard_map/all_to_all | solution.py:277
  289.8 19.8 %copy-start.1 = (bf16[512,512]{1,0:T(8,128)(2,1)S(1)}, bf16[512,512]{1,0:T(8,128)(2,1)}, u32[]{:S(2)}) copy-start(bf16[512,512]{1,0:T(8,128)(2,1)} %w_gate.1) | copy-start | bytes 1572868
  289.8 20.9 %copy-start.6 = (f32[1,512]{1,0:T(1,128)S(1)}, f32[1,512]{1,0:T(1,128)}, u32[]{:S(2)}) copy-start(f32[1,512]{1,0:T(1,128)} %get-tuple-element.25) | copy-start | bytes 6148
  289.8 133.2 %all-to-all-start.2 = ((bf16[16,16,32,256]{3,2,1,0:T(8,128)(2,1)}), bf16[16,16,32,256]{3,2,1,0:T(8,128)(2,1)}, u32[]{:S(2)}, u32[]{:S(2)}) async-start(bf16[16,16,32,256]{3,2,1,0:T(8,128)(2,1)} %bitcast.54), calls=%async_computation.2 | async-start | bytes 8388608 | tf_op jit(solution)/shard_map/all_to_all | solution.py:277
  323.8 81.7 %copy-start.5 = (bf16[256,256]{1,0:T(8,128)(2,1)S(1)}, bf16[256,256]{1,0:T(8,128)(2,1)}, u32[]{:S(2)}) copy-start(bf16[256,256]{1,0:T(8,128)(2,1)} %first.1) | copy-start | bytes 393220
  325.2 1.7 collective-permute-start
  327.0 12.7 %collective-permute-start.1 = (bf16[2,2,32,640]{3,2,0,1:T(8,128)(2,1)S(1)}, bf16[2,2,32,640]{3,2,0,1:T(8,128)(2,1)S(1)}, u32[]{:S(2)}, u32[]{:S(2)}) collective-permute-start(bf16[2,2,32,640]{3,2,0,1:T(8,128)(2,1)S(1)} %dynamic-slice_bitcast_fusion), channel_id=1, source_target_pairs={{0,2},{1,3},{2,0},{3,1},{4,6},{5,7},{6,4},{7,5},{8,10},{9,11},{10,... | collective-permute-start | bytes 491528 | tf_op jit(solution)/shard_map/ppermute | solution.py:216
  339.8 40.2 %collective-permute-start.2 = (bf16[2,32,640]{2,1,0:T(8,128)(2,1)S(1)}, bf16[2,32,640]{2,1,0:T(8,128)(2,1)S(1)}, u32[]{:S(2)}, u32[]{:S(2)}) collective-permute-start(bf16[2,32,640]{2,1,0:T(8,128)(2,1)S(1)} %dynamic-slice_bitcast_fusion.1), channel_id=1, source_target_pairs={{0,4},{1,5},{2,6},{3,7},{4,0},{5,1},{6,2},{7,3},{8,12},{9,13},{10,... | collective-permute-start | bytes 245768 | tf_op jit(solution)/shard_map/ppermute | solution.py:216
  380.1 25.4 %collective-permute-start.3 = (bf16[32,640]{1,0:T(8,128)(2,1)S(1)}, bf16[32,640]{1,0:T(8,128)(2,1)S(1)}, u32[]{:S(2)}, u32[]{:S(2)}) collective-permute-start(bf16[32,640]{1,0:T(8,128)(2,1)S(1)} %dynamic-slice_bitcast_fusion.2), channel_id=1, source_target_pairs={{0,8},{1,9},{2,10},{3,11},{4,12},{5,13},{6,14},{7,15},{8,0},{9,1},... | collective-permute-start | bytes 122888 | tf_op jit(solution)/shard_map/ppermute | solution.py:216
  405.5 5.0 %collective-permute-start.4 = (bf16[32,640]{1,0:T(8,128)(2,1)S(1)}, bf16[32,640]{1,0:T(8,128)(2,1)S(1)}, u32[]{:S(2)}, u32[]{:S(2)}) collective-permute-start(bf16[32,640]{1,0:T(8,128)(2,1)S(1)} %fusion.4), channel_id=1, source_target_pairs={{0,8},{1,9},{2,10},{3,11},{4,12},{5,13},{6,14},{7,15},{8,0},{9,1},... | collective-permute-start | bytes 122888 | tf_op jit(solution)/shard_map/ppermute | solution.py:216
  410.4 4.5 collective-permute-start.5
  415.0 5.4 %collective-permute-start.6 = (bf16[2,2,32,640]{3,2,1,0:T(8,128)(2,1)S(1)}, bf16[2,2,32,640]{3,2,1,0:T(8,128)(2,1)S(1)}, u32[]{:S(2)}, u32[]{:S(2)}) collective-permute-start(bf16[2,2,32,640]{3,2,1,0:T(8,128)(2,1)S(1)} %maximum_select_fusion.2), channel_id=1, source_target_pairs={{0,2},{1,3},{2,0},{3,1},{4,6},{5,7},{6,4},{7,5},{8,10},{9,11},{10,... | collective-permute-start | bytes 491528 | tf_op jit(solution)/shard_map/ppermute | solution.py:216
  420.4 1.7 collective-permute-start.7
  423.0 31.4 %copy-start.2 = (bf16[512,512]{1,0:T(8,128)(2,1)S(1)}, bf16[512,512]{1,0:T(8,128)(2,1)}, u32[]{:S(2)}) copy-start(bf16[512,512]{1,0:T(8,128)(2,1)} %w_value.3) | copy-start | bytes 1572868
  450.3 18.6 %all-to-all-start.5 = ((bf16[16,32,512]{2,1,0:T(8,128)(2,1)}), bf16[16,32,512]{2,1,0:T(8,128)(2,1)S(1)}, u32[]{:S(2)}, u32[]{:S(2)}) async-start(bf16[16,32,512]{2,1,0:T(8,128)(2,1)} %broadcast_in_dim.14), calls=%async_computation.5 | async-start | bytes 1048576 | tf_op jit(solution)/shard_map/all_to_all | solution.py:277
  455.5 10.4 %copy-start = (bf16[2,2,2,2,32,640]{5,4,3,2,1,0:T(8,128)(2,1)S(1)}, bf16[2,2,2,2,32,640]{5,4,3,2,1,0:T(8,128)(2,1)}, u32[]{:S(2)}) copy-start(bf16[2,2,2,2,32,640]{5,4,3,2,1,0:T(8,128)(2,1)} %maximum_select_fusion) | copy-start | bytes 1966084

commit v5 on v4

--- a/solution.py
+++ b/solution.py
@@ -26,10 +26,6 @@
     return lax.dot_general(a, b, (((1,), (1,)), ((), ())), preferred_element_type=f32)
 
 
-def dot_tn(a, b):
-    return lax.dot_general(a, b, (((0,), (0,)), ((), ())), preferred_element_type=f32)
-
-
 def params():
     return pltpu.CompilerParams(vmem_limit_bytes=VMEM_LIMIT)
 
@@ -50,16 +46,15 @@
     return slice(r * N2, (r + 1) * N2)
 
 
-def section_one_kernel(tokens, w_value, first, out, w_turned, first_turned):
+def section_one_kernel(tokens, w_value, first, out, first_turned):
     @pl.when(pl.program_id(0) == 0)
     def _():
-        w_turned[...] = w_value[...].T
         first_turned[...] = first[...].T
 
     n, per, chans, _ = out.shape
+    value = dot_nn(tokens[...], w_value[...]).astype(bf16)
     for r in range(per):
-        value_t = dot_nt(w_turned[...], tokens[row_slice(r)]).astype(bf16)
-        section = dot_nn(value_t, first_turned[...]).astype(bf16)
+        section = dot_nn(value[row_slice(r)].T, first_turned[...]).astype(bf16)
         out[:, r] = section.reshape(n, chans, N2)
 
 
@@ -72,6 +67,7 @@
     out,
     value_out,
     d_mix_out,
+    d_mix_t_out,
     tokens_t_out,
     skip_out,
 ):
@@ -92,7 +88,9 @@
         skip_out[...] += jnp.sum(
             d_mix.astype(f32) * value.astype(f32), axis=0, keepdims=True
         )
-        section = dot_tn(d_mix, fourth[...]).astype(bf16)
+        d_mix_t = d_mix.T
+        d_mix_t_out[:, here] = d_mix_t
+        section = dot_nn(d_mix_t, fourth[...]).astype(bf16)
         out[:, r] = section.reshape(n, chans, N2)
 
 
@@ -188,48 +186,64 @@
     finish(total, factor, grad_w)
 
 
-def value_row(arrived, d_mix, first_t, skip, r):
-    d_cube = dot_nt(first_t[...], arrived[:, r].reshape(D, N2))
-    return (d_cube + skip[...] * d_mix[row_slice(r)].astype(f32)).astype(bf16)
-
-
-def value_kernel(arrived, tokens_t, d_mix, first_t, skip, factor, _, grad_w, total, d_value):
+def value_kernel(
+    arrived, tokens, d_mix_t, first, skip_column, factor, _, grad_w, total, d_value_t
+):
     for r in range(arrived.shape[1]):
-        d_value[row_slice(r)] = value_row(arrived, d_mix, first_t, skip, r)
-    accumulate(total, dot_nn(tokens_t[...], d_value[...]))
-    finish(total, factor, grad_w)
+        here = row_slice(r)
+        d_cube_t = dot_nn(arrived[:, r].reshape(D, N2), first[...])
+        d_value_t[:, here] = (
+            d_cube_t + skip_column[...] * d_mix_t[:, here].astype(f32)
+        ).astype(bf16)
+    accumulate(total, dot_nn(d_value_t[...], tokens[...]))
+
+    @pl.when(pl.program_id(0) == pl.num_programs(0) - 1)
+    def _():
+        grad_w[...] = (total[...] * factor[0, 0]).astype(bf16).T
 
 
 def tokens_kernel(arrived, d_mix, partial, first_t, skip, w_value_t, grad_tokens):
     for r in range(arrived.shape[1]):
-        d_value = value_row(arrived, d_mix, first_t, skip, r)
-        grad_tokens[row_slice(r)] = (
-            partial[row_slice(r)] + dot_nn(d_value, w_value_t[...])
-        ).astype(bf16)
-
-
-def sum_over_seq(term, n):
+        here = row_slice(r)
+        d_cube = dot_nt(first_t[...], arrived[:, r].reshape(D, N2))
+        d_value = (d_cube + skip[...] * d_mix[here].astype(f32)).astype(bf16)
+        grad_tokens[here] = (partial[here] + dot_nn(d_value, w_value_t[...])).astype(bf16)
+
+
+def sum_kernel(parts, _, out):
+    total = jnp.sum(parts[...].astype(f32), axis=0, keepdims=True).astype(bf16)
+    out[...] = jnp.broadcast_to(total, out.shape)
+
+
+def from_partner(array, b, n):
+    return lax.ppermute(array, "seq", [(i, i ^ (1 << b)) for i in range(n)])
+
+
+def halve_over_seq(term, n):
     me = lax.axis_index("seq")
     bits = n.bit_length() - 1
-
-    def from_partner(array, b):
-        return lax.ppermute(array, "seq", [(i, i ^ (1 << b)) for i in range(n)])
-
     part = term.reshape((2,) * bits + (term.shape[0] // n, term.shape[1]))
     for b in range(bits):
         axis = bits - 1 - b
         bit = (me >> b) & 1
         kept = lax.dynamic_index_in_dim(part, bit, axis, keepdims=False)
         sent = lax.dynamic_index_in_dim(part, 1 - bit, axis, keepdims=False)
-        part = (kept.astype(f32) + from_partner(sent, b).astype(f32)).astype(bf16)
+        part = (kept.astype(f32) + from_partner(sent, b, n).astype(f32)).astype(bf16)
+    return part
+
+
+def double_over_seq(part, n):
+    me = lax.axis_index("seq")
+    bits = n.bit_length() - 1
+    lanes = part.shape[-1]
     for b in reversed(range(bits)):
         axis = bits - 1 - b
         bit = (me >> b) & 1
-        other = from_partner(part, b)
+        other = from_partner(part, b, n)
         part = jnp.where(
             bit == 0, jnp.stack([part, other], axis), jnp.stack([other, part], axis)
         )
-    return part.reshape(term.shape)
+    return part.reshape(-1, lanes)
 
 
 def on_device(
@@ -282,21 +296,22 @@
         in_specs=[row, square, block],
         out_specs=sent,
         out_shape=shape(sections),
-        scratch_shapes=[pltpu.VMEM((D, D), bf16), pltpu.VMEM((N2, N2), bf16)],
+        scratch_shapes=[pltpu.VMEM((N2, N2), bf16)],
         compiler_params=params(),
         cost_estimate=cost(3.2, 9),
     )(tokens, w_value, first_block)
     one_home = transfer(one_sent)
 
-    three_sent, value, d_mix, tokens_t, skip_term = pl.pallas_call(
+    three_sent, value, d_mix, d_mix_t, tokens_t, skip_term = pl.pallas_call(
         d_three_kernel,
         grid=(rows // per,),
         in_specs=[row, row, square, square, block],
-        out_specs=[sent, row, row, column, line],
+        out_specs=[sent, row, row, column, column, line],
         out_shape=[
             shape(sections),
             shape((local_rows, D)),
             shape((local_rows, D)),
+            shape((D, local_rows)),
             shape((D, local_rows)),
             shape((1, D), f32),
         ],
@@ -350,19 +365,19 @@
     )(three_here, tokens_t, value, cotangent, fourth_block, w_gate.T, skip, factor)
 
     skip_lanes = jnp.broadcast_to((skip_term * factor[0, 0]).astype(bf16).T, (D, LANES))
-    early = sum_over_seq(jnp.concatenate([gate_term, skip_lanes], axis=1), n)
-
-    first_t = first_block.T
+    early = halve_over_seq(jnp.concatenate([gate_term, skip_lanes], axis=1), n)
+
+    unread = pl.BlockSpec(memory_space=pl.ANY)
     value_term = pl.pallas_call(
         value_kernel,
         grid=(rows // per,),
-        in_specs=[sent, column, row, block, line, one, pl.BlockSpec(memory_space=pl.ANY)],
+        in_specs=[sent, row, column, block, whole((D, 1)), one, unread],
         out_specs=square,
         out_shape=shape((D, D)),
-        scratch_shapes=[pltpu.VMEM((D, D), f32), pltpu.VMEM((per * N2, D), bf16)],
+        scratch_shapes=[pltpu.VMEM((D, D), f32), pltpu.VMEM((D, per * N2), bf16)],
         compiler_params=params(),
         cost_estimate=cost(3.3, 13),
-    )(one_here, tokens_t, d_mix, first_t, skip, factor, early)
+    )(one_here, tokens, d_mix_t, first_block, skip_gain.reshape(D, 1), factor, early)
 
     parts = transfer(value_term.reshape(n, D // n, D))
     grad_tokens = pl.pallas_call(
@@ -373,9 +388,18 @@
         out_shape=shape((local_rows, D)),
         compiler_params=params(),
         cost_estimate=cost(3.3, 20),
-    )(one_here, d_mix, partial, first_t, skip, w_value.T)
-    mine = jnp.sum(parts.astype(f32), axis=0).astype(bf16)
-    value_total = transfer(jnp.broadcast_to(mine, (n, D // n, D))).reshape(D, D)
+    )(one_here, d_mix, partial, first_block.T, skip, w_value.T)
+    own = pl.pallas_call(
+        sum_kernel,
+        grid=(1,),
+        in_specs=[whole(parts.shape), unread],
+        out_specs=whole(parts.shape),
+        out_shape=shape(parts.shape),
+        compiler_params=params(),
+        cost_estimate=cost(0.001, 1),
+    )(parts, grad_tokens)
+    value_total = transfer(own).reshape(D, D)
+    early = double_over_seq(early, n)
     gate_total, skip_total = early[:, :D], early[:, D]
     return (
         grad_tokens,

time: 471 us -> 463 us (0.983)
  blocking collectives: 18.1 us -> 0 us
  starting transfers between devices: 79.7 us -> 85.9 us
    all_to_all x1 -> x0, blocking collectives: 18.1 us -> none  [transfer(): return lax.all_to_all(array, 'seq', split_axis=0, concat_axis=0, tiled=True)]
    all_to_all x5 -> x6, waiting for transfers between devices: 178 us -> 187 us  [transfer(): return lax.all_to_all(array, 'seq', split_axis=0, concat_axis=0, tiled=True)]
    ppermute x8, waiting for transfers between devices: 86.7 us -> 79.5 us  [from_partner(): return lax.ppermute(array, 'seq', [(i, i ^ 1 << b) for i in range(n)])]
    all_to_all x5 -> x6, starting transfers between devices: 70.9 us -> 74 us  [transfer(): return lax.all_to_all(array, 'seq', split_axis=0, concat_axis=0, tiled=True)]
    pallas_call x1 -> x2, Pallas kernels: 8.19 us -> 11 us  [the longest x1 9.08 us: on_device(): pl.pallas_call(value_kernel, grid=(rows // per,), in_specs=[sent, row, co...]
  transfers between devices with their start and end apart: 13 -> 14, of which waited for: 12 -> 11; matrix products, arithmetic and copies ran while one was open for 2% -> 2% of each run, Pallas kernels for 17% -> 17%
where the time goes in v5:
time: 463 us; the launch traced here: 462 us
  waiting for transfers between devices  267 us (58%)
  Pallas kernels  97.1 us (21%)
  starting transfers between devices  85.9 us (19%)
  local copies, waits for them, and re-layouts  6.38 us (1%)
  other arithmetic  5.2 us (1%)
    all_to_all x6, waiting for transfers between devices, transfer(): return lax.all_to_all(array, 'seq', split_axis=0, concat_axis=0, tiled=True)  187 us
    ppermute x8, waiting for transfers between devices, from_partner(): return lax.ppermute(array, 'seq', [(i, i ^ 1 << b) for i in range(n)])  79.5 us
    all_to_all x6, starting transfers between devices, transfer(): return lax.all_to_all(array, 'seq', split_axis=0, concat_axis=0, tiled=True)  74 us
    pallas_call x1, Pallas kernels, on_device(): pl.pallas_call(home_backward_kernel, grid=(chans // GROUP,), in_specs=[at...  20.6 us
    pallas_call x1, Pallas kernels, on_device(): pl.pallas_call(home_forward_kernel, grid=(chans // GROUP,), in_specs=[at_...  20.1 us
    pallas_call x1, Pallas kernels, on_device(): pl.pallas_call(d_three_kernel, grid=(rows // per,), in_specs=[row, row, s...  14.5 us
    pallas_call x1, Pallas kernels, on_device(): pl.pallas_call(gate_kernel, grid=(rows // per,), in_specs=[sent, column,...  13.3 us
    ppermute x8, starting transfers between devices, from_partner(): return lax.ppermute(array, 'seq', [(i, i ^ 1 << b) for i in range(n)])  11.9 us
  transfers between devices with their start and end apart: 14, of which 11 were waited for; matrix products, arithmetic and copies ran while one was open for 2% of the time, Pallas kernels for 17%

profile of v5, /device:TPU:0, one launch (start us, length us, event | category | flops | bytes accessed | tf_op | source)
XLA Modules:
  0.0 462.2 jit_solution(2175695911137731906)
XLA Ops:
  0.6 7.2 %shard_map.130 = bf16[16,16,32,256]{3,2,1,0:T(8,128)(2,1)} custom-call(bf16[4096,512]{1,0:T(8,128)(2,1)} %tokens.5, bf16[512,512]{1,0:T(8,128)(2,1)} %w_value.3, bf16[256,256]{1,0:T(8,128)(2,1)} %first.3), custom_call_target="tpu_custom_call" | custom-call | flops 3200000000 | bytes 9437184 | tf_op jit(solution)/shard_map/pallas_call | solution.py:293
  7.9 7.4 %all-to-all-start.1 = ((bf16[16,16,32,256]{3,2,1,0:T(8,128)(2,1)}), bf16[16,16,32,256]{3,2,1,0:T(8,128)(2,1)}, u32[]{:S(2)}, u32[]{:S(2)}) async-start(bf16[16,16,32,256]{3,2,1,0:T(8,128)(2,1)} %shard_map.130), calls=%async_computation.1 | async-start | bytes 8388608 | tf_op jit(solution)/shard_map/all_to_all | solution.py:291
  15.3 14.5 %shard_map.129 = (bf16[16,16,32,256]{3,2,1,0:T(8,128)(2,1)}, bf16[4096,512]{1,0:T(8,128)(2,1)}, bf16[4096,512]{1,0:T(8,128)(2,1)}, bf16[512,4096]{1,0:T(8,128)(2...) custom-call(bf16[4096,512]{1,0:T(8,128)(2,1)} %tokens.5, bf16[4096,512]{1,0:T(8,128)(2,1)} %cotangent.3, ...), custom_call_target="tpu_custom_call" | custom-call | flops 5400000000 | bytes 26214400 | tf_op jit(solution)/shard_map/pallas_call | solution.py:305
  29.8 63.2 %all-to-all-done.1 = bf16[16,16,32,256]{3,2,1,0:T(8,128)(2,1)} async-done(((bf16[16,16,32,256]{3,2,1,0:T(8,128)(2,1)}), bf16[16,16,32,256]{3,2,1,0:T(8,128)(2,1)}, u32[]{:S(2)}, u32[]{:S(2)}) %all-to-all-start.1) | async-done | bytes 4194336 | tf_op jit(solution)/shard_map/all_to_all | solution.py:291
  93.0 19.7 %all-to-all-start = ((bf16[16,16,32,256]{3,2,1,0:T(8,128)(2,1)}), bf16[16,16,32,256]{3,2,1,0:T(8,128)(2,1)}, u32[]{:S(2)}, u32[]{:S(2)}) async-start(bf16[16,16,32,256]{3,2,1,0:T(8,128)(2,1)} %get-tuple-element.16), calls=%async_computation | async-start | bytes 8388608 | tf_op jit(solution)/shard_map/all_to_all | solution.py:291
  113.5 20.1 %shard_map.131 = (bf16[256,32,256]{2,1,0:T(8,128)(2,1)}, f32[32,256,256]{2,1,0:T(8,128)}) custom-call(bf16[256,32,256]{2,1,0:T(8,128)(2,1)} %bitcast.1.arrived, bf16[32,256,256]{2,1,0:T(8,128)(2,1)} %kernel.3, bf16[256,256]{1,0:T(8,128)(2,1)} %second.1, bf16[256,256]{1,0:T(8,128)(2,1)} %third.1, bf16[256,256]{1,0:T(8,128)(2,1)} %fusion.2.swap), custom_call_target="tpu_custom_call" | custom-call | flops 4300000256 | bytes 20971520 | tf_op jit(solution)/shard_map/pallas_call | solution.py:325
  133.5 56.8 %all-to-all-done = bf16[16,16,32,256]{3,2,1,0:T(8,128)(2,1)} async-done(((bf16[16,16,32,256]{3,2,1,0:T(8,128)(2,1)}), bf16[16,16,32,256]{3,2,1,0:T(8,128)(2,1)}, u32[]{:S(2)}, u32[]{:S(2)}) %all-to-all-start) | async-done | bytes 4194336 | tf_op jit(solution)/shard_map/all_to_all | solution.py:291
  190.4 19.8 %all-to-all-start.3 = ((bf16[16,16,32,256]{3,2,1,0:T(8,128)(2,1)}), bf16[16,16,32,256]{3,2,1,0:T(8,128)(2,1)}, u32[]{:S(2)}, u32[]{:S(2)}) async-start(bf16[16,16,32,256]{3,2,1,0:T(8,128)(2,1)} %bitcast.54), calls=%async_computation.3 | async-start | bytes 8388608 | tf_op jit(solution)/shard_map/all_to_all | solution.py:291
  211.7 20.6 %shard_map.132 = (bf16[256,32,256]{2,1,0:T(8,128)(2,1)}, bf16[32,256,256]{2,1,0:T(8,128)(2,1)}) custom-call(bf16[256,32,256]{2,1,0:T(8,128)(2,1)} %bitcast.arrived, bf16[32,256,256]{2,1,0:T(8,128)(2,1)} %kernel.3, f32[32,256,256]{2,1,0:T(8,128)} %get-tuple-element.17.spectrum, bf16[256,256]{1,0:T(8,128)(2,1)} %bitcast.70, bf16[256,256]{1,0:T(8,128)(2,1)} %bitcast.71, ...), custom_call_target="tpu_custom_call" | custom-call | flops 4300000256 | bytes 25165824 | tf_op jit(solution)/shard_map/pallas_call | solution.py:337
  232.4 55.5 %all-to-all-done.3.arrived = bf16[16,16,32,256]{3,2,1,0:T(8,128)(2,1)} async-done(((bf16[16,16,32,256]{3,2,1,0:T(8,128)(2,1)}), bf16[16,16,32,256]{3,2,1,0:T(8,128)(2,1)}, u32[]{:S(2)}, u32[]{:S(2)}) %all-to-all-start.3) | async-done | bytes 4194336 | tf_op jit(solution)/shard_map/all_to_all | solution.py:291
  287.9 19.8 %all-to-all-start.2 = ((bf16[16,16,32,256]{3,2,1,0:T(8,128)(2,1)}), bf16[16,16,32,256]{3,2,1,0:T(8,128)(2,1)}, u32[]{:S(2)}, u32[]{:S(2)}) async-start(bf16[16,16,32,256]{3,2,1,0:T(8,128)(2,1)} %bitcast.53), calls=%async_computation.2 | async-start | bytes 8388608 | tf_op jit(solution)/shard_map/all_to_all | solution.py:291
  308.7 13.3 %shard_map.133 = (f32[4096,512]{1,0:T(8,128)}, bf16[512,512]{1,0:T(8,128)(2,1)}) custom-call(bf16[16,16,32,256]{3,2,1,0:T(8,128)(2,1)} %all-to-all-done.3.arrived, bf16[512,4096]{1,0:T(8,128)(2,1)} %get-tuple-element.21.tokens_t, bf16[4096,512]{1,0:T(8,128)(2,1)} %get-tuple-element.22.value, bf16[4096,512]{1,0:T(8,128)(2,1)} %cotangent.3, ...), custom_call_target="tpu_custom_call" | custom-call | flops 5400000000 | bytes 26214400 | tf_op jit(solution)/shard_map/pallas_call | solution.py:356
  327.2 10.6 %collective-permute-done.1 = bf16[2,2,32,640]{3,2,0,1:T(8,128)(2,1)S(1)} collective-permute-done((bf16[2,2,32,640]{3,2,0,1:T(8,128)(2,1)S(1)}, bf16[2,2,32,640]{3,2,0,1:T(8,128)(2,1)S(1)}, u32[]{:S(2)}, u32[]{:S(2)}) %collective-permute-start.1) | collective-permute-done | bytes 163872 | tf_op jit(solution)/shard_map/ppermute | solution.py:219
  338.1 40.0 %collective-permute-done.2 = bf16[2,32,640]{2,1,0:T(8,128)(2,1)S(1)} collective-permute-done((bf16[2,32,640]{2,1,0:T(8,128)(2,1)S(1)}, bf16[2,32,640]{2,1,0:T(8,128)(2,1)S(1)}, u32[]{:S(2)}, u32[]{:S(2)}) %collective-permute-start.2) | collective-permute-done | bytes 81952 | tf_op jit(solution)/shard_map/ppermute | solution.py:219
  378.1 4.6 collective-permute-start.3
  383.5 19.9 %collective-permute-done.3 = bf16[32,640]{1,0:T(8,128)(2,1)S(1)} collective-permute-done((bf16[32,640]{1,0:T(8,128)(2,1)S(1)}, bf16[32,640]{1,0:T(8,128)(2,1)S(1)}, u32[]{:S(2)}, u32[]{:S(2)}) %collective-permute-start.3) | collective-permute-done | bytes 40992 | tf_op jit(solution)/shard_map/ppermute | solution.py:219
  404.1 9.1 %shard_map.135 = bf16[512,512]{1,0:T(8,128)(2,1)} custom-call(bf16[16,16,32,256]{3,2,1,0:T(8,128)(2,1)} %all-to-all-done.2.arrived, bf16[4096,512]{1,0:T(8,128)(2,1)} %tokens.5, bf16[512,4096]{1,0:T(8,128)(2,1)} %get-tuple-element.25.d_mix_t, bf16[256,256]{1,0:T(8,128)(2,1)} %first.3, f32[512,1]{1,0:T(8,128)} %copy.26.skip_column, ...), custom_call_target="tpu_custom_call" | custom-call | flops 3300000000 | bytes 13631488 | tf_op jit(solution)/shard_map/pallas_call | solution.py:371
  413.2 3.6 all-to-all-start.4
  418.6 2.8 collective-permute-start.4
  421.4 10.4 %shard_map.134._ = bf16[4096,512]{1,0:T(8,128)(2,1)} custom-call(bf16[16,16,32,256]{3,2,1,0:T(8,128)(2,1)} %all-to-all-done.2.arrived, bf16[4096,512]{1,0:T(8,128)(2,1)} %get-tuple-element.19.d_mix, f32[4096,512]{1,0:T(8,128)} %get-tuple-element.23.partial, bf16[256,256]{1,0:T(8,128)(2,1)} %bitcast.69, f32[1,512]{1,0:T(1,128)} %bitcast.79, ...), custom_call_target="tpu_custom_call" | custom-call | flops 3300000000 | bytes 20971520 | tf_op jit(solution)/shard_map/pallas_call | solution.py:383
  431.8 2.1 collective-permute-done.4
  434.0 4.4 collective-permute-done.5
  442.7 3.6 all-to-all-start.5
  449.1 11.7 %all-to-all-done.5 = bf16[16,32,512]{2,1,0:T(8,128)(2,1)S(1)} async-done(((bf16[16,32,512]{2,1,0:T(8,128)(2,1)}), bf16[16,32,512]{2,1,0:T(8,128)(2,1)S(1)}, u32[]{:S(2)}, u32[]{:S(2)}) %all-to-all-start.5) | async-done | bytes 524320 | tf_op jit(solution)/shard_map/all_to_all | solution.py:291
  (63 shorter events, 20.6 us)
Async XLA Ops:
  7.9 85.1 %all-to-all-start.1 = ((bf16[16,16,32,256]{3,2,1,0:T(8,128)(2,1)}), bf16[16,16,32,256]{3,2,1,0:T(8,128)(2,1)}, u32[]{:S(2)}, u32[]{:S(2)}) async-start(bf16[16,16,32,256]{3,2,1,0:T(8,128)(2,1)} %shard_map.130), calls=%async_computation.1 | async-start | bytes 8388608 | tf_op jit(solution)/shard_map/all_to_all | solution.py:291
  93.0 97.4 %all-to-all-start = ((bf16[16,16,32,256]{3,2,1,0:T(8,128)(2,1)}), bf16[16,16,32,256]{3,2,1,0:T(8,128)(2,1)}, u32[]{:S(2)}, u32[]{:S(2)}) async-start(bf16[16,16,32,256]{3,2,1,0:T(8,128)(2,1)} %get-tuple-element.16), calls=%async_computation | async-start | bytes 8388608 | tf_op jit(solution)/shard_map/all_to_all | solution.py:291
  190.4 19.8 %copy-start.5 = (bf16[256,256]{1,0:T(8,128)(2,1)S(1)}, bf16[256,256]{1,0:T(8,128)(2,1)}, u32[]{:S(2)}) copy-start(bf16[256,256]{1,0:T(8,128)(2,1)} %second.1) | copy-start | bytes 393220
  190.4 20.6 %copy-start.6 = (bf16[256,256]{1,0:T(8,128)(2,1)S(1)}, bf16[256,256]{1,0:T(8,128)(2,1)}, u32[]{:S(2)}) copy-start(bf16[256,256]{1,0:T(8,128)(2,1)} %third.1) | copy-start | bytes 393220
  190.4 97.5 %all-to-all-start.3 = ((bf16[16,16,32,256]{3,2,1,0:T(8,128)(2,1)}), bf16[16,16,32,256]{3,2,1,0:T(8,128)(2,1)}, u32[]{:S(2)}, u32[]{:S(2)}) async-start(bf16[16,16,32,256]{3,2,1,0:T(8,128)(2,1)} %bitcast.54), calls=%async_computation.3 | async-start | bytes 8388608 | tf_op jit(solution)/shard_map/all_to_all | solution.py:291
  287.9 19.8 %copy-start.3 = (bf16[512,512]{1,0:T(8,128)(2,1)S(1)}, bf16[512,512]{1,0:T(8,128)(2,1)}, u32[]{:S(2)}) copy-start(bf16[512,512]{1,0:T(8,128)(2,1)} %w_gate.1) | copy-start | bytes 1572868
  287.9 20.9 %copy-start.8 = (f32[1,512]{1,0:T(1,128)S(1)}, f32[1,512]{1,0:T(1,128)}, u32[]{:S(2)}) copy-start(f32[1,512]{1,0:T(1,128)} %get-tuple-element.27) | copy-start | bytes 6148
  287.9 116.2 %all-to-all-start.2 = ((bf16[16,16,32,256]{3,2,1,0:T(8,128)(2,1)}), bf16[16,16,32,256]{3,2,1,0:T(8,128)(2,1)}, u32[]{:S(2)}, u32[]{:S(2)}) async-start(bf16[16,16,32,256]{3,2,1,0:T(8,128)(2,1)} %bitcast.53), calls=%async_computation.2 | async-start | bytes 8388608 | tf_op jit(solution)/shard_map/all_to_all | solution.py:291
  322.0 60.6 %copy-start.7 = (f32[512]{0:T(512)S(1)}, f32[512]{0:T(512)}, u32[]{:S(2)}) copy-start(f32[512]{0:T(512)} %param.18) | copy-start | bytes 6148
  323.4 1.7 collective-permute-start
  325.2 12.5 %collective-permute-start.1 = (bf16[2,2,32,640]{3,2,0,1:T(8,128)(2,1)S(1)}, bf16[2,2,32,640]{3,2,0,1:T(8,128)(2,1)S(1)}, u32[]{:S(2)}, u32[]{:S(2)}) collective-permute-start(bf16[2,2,32,640]{3,2,0,1:T(8,128)(2,1)S(1)} %dynamic-slice_bitcast_fusion), channel_id=1, source_target_pairs={{0,2},{1,3},{2,0},{3,1},{4,6},{5,7},{6,4},{7,5},{8,10},{9,11},{10,... | collective-permute-start | bytes 491528 | tf_op jit(solution)/shard_map/ppermute | solution.py:219
  337.8 40.2 %collective-permute-start.2 = (bf16[2,32,640]{2,1,0:T(8,128)(2,1)S(1)}, bf16[2,32,640]{2,1,0:T(8,128)(2,1)S(1)}, u32[]{:S(2)}, u32[]{:S(2)}) collective-permute-start(bf16[2,32,640]{2,1,0:T(8,128)(2,1)S(1)} %dynamic-slice_bitcast_fusion.1), channel_id=1, source_target_pairs={{0,4},{1,5},{2,6},{3,7},{4,0},{5,1},{6,2},{7,3},{8,12},{9,13},{10,... | collective-permute-start | bytes 245768 | tf_op jit(solution)/shard_map/ppermute | solution.py:219
  378.1 25.4 %collective-permute-start.3 = (bf16[32,640]{1,0:T(8,128)(2,1)S(1)}, bf16[32,640]{1,0:T(8,128)(2,1)S(1)}, u32[]{:S(2)}, u32[]{:S(2)}) collective-permute-start(bf16[32,640]{1,0:T(8,128)(2,1)S(1)} %dynamic-slice_bitcast_fusion.2), channel_id=1, source_target_pairs={{0,8},{1,9},{2,10},{3,11},{4,12},{5,13},{6,14},{7,15},{8,0},{9,1},... | collective-permute-start | bytes 122888 | tf_op jit(solution)/shard_map/ppermute | solution.py:219
  404.1 12.7 %copy-start.2 = (bf16[256,256]{1,0:T(8,128)(2,1)S(1)}, bf16[256,256]{1,0:T(8,128)(2,1)}, u32[]{:S(2)}) copy-start(bf16[256,256]{1,0:T(8,128)(2,1)} %first.3) | copy-start | bytes 393220
  404.1 13.5 %copy-start.4 = (bf16[512,512]{1,0:T(8,128)(2,1)S(1)}, bf16[512,512]{1,0:T(8,128)(2,1)}, u32[]{:S(2)}) copy-start(bf16[512,512]{1,0:T(8,128)(2,1)} %w_value.3) | copy-start | bytes 1572868
  404.1 14.5 %copy-start.1 = (bf16[32,640]{1,0:T(8,128)(2,1)S(1)}, bf16[32,640]{1,0:T(8,128)(2,1)}, u32[]{:S(2)}) copy-start(bf16[32,640]{1,0:T(8,128)(2,1)} %fusion.4._) | copy-start | bytes 122884
  413.2 26.8 %all-to-all-start.4 = ((bf16[16,32,512]{2,1,0:T(8,128)(2,1)}), bf16[16,32,512]{2,1,0:T(8,128)(2,1)S(1)}, u32[]{:S(2)}, u32[]{:S(2)}) async-start(bf16[16,32,512]{2,1,0:T(8,128)(2,1)} %bitcast.58), calls=%async_computation.4 | async-start | bytes 1048576 | tf_op jit(solution)/shard_map/all_to_all | solution.py:291
  418.6 15.3 %collective-permute-start.4 = (bf16[32,640]{1,0:T(8,128)(2,1)S(1)}, bf16[32,640]{1,0:T(8,128)(2,1)S(1)}, u32[]{:S(2)}, u32[]{:S(2)}) collective-permute-start(bf16[32,640]{1,0:T(8,128)(2,1)S(1)} %copy-done.1), channel_id=1, source_target_pairs={{0,8},{1,9},{2,10},{3,11},{4,12},{5,13},{6,14},{7,15},{8,0},{9,1},... | collective-permute-start | bytes 122888 | tf_op jit(solution)/shard_map/ppermute | solution.py:219
  433.9 4.5 collective-permute-start.5
  438.4 7.9 %collective-permute-start.6 = (bf16[2,2,32,640]{3,2,0,1:T(8,128)(2,1)S(1)}, bf16[2,2,32,640]{3,2,0,1:T(8,128)(2,1)S(1)}, u32[]{:S(2)}, u32[]{:S(2)}) collective-permute-start(bf16[2,2,32,640]{3,2,0,1:T(8,128)(2,1)S(1)} %maximum_select_fusion.4), channel_id=1, source_target_pairs={{0,2},{1,3},{2,0},{3,1},{4,6},{5,7},{6,4},{7,5},{8,10},{9,11},{10,... | collective-permute-start | bytes 491528 | tf_op jit(solution)/shard_map/ppermute | solution.py:219
  440.0 0.8 copy-start
  442.7 18.0 %all-to-all-start.5 = ((bf16[16,32,512]{2,1,0:T(8,128)(2,1)}), bf16[16,32,512]{2,1,0:T(8,128)(2,1)S(1)}, u32[]{:S(2)}, u32[]{:S(2)}) async-start(bf16[16,32,512]{2,1,0:T(8,128)(2,1)} %shard_map.136), calls=%async_computation.5 | async-start | bytes 1048576 | tf_op jit(solution)/shard_map/all_to_all | solution.py:291
  446.4 1.7 collective-permute-start.7

commit v6 on v5

--- a/solution.py
+++ b/solution.py
@@ -1,3 +1,5 @@
+import functools
+
 import functools
 
 import jax
@@ -46,16 +48,45 @@
     return slice(r * N2, (r + 1) * N2)
 
 
-def section_one_kernel(tokens, w_value, first, out, first_turned):
-    @pl.when(pl.program_id(0) == 0)
-    def _():
-        first_turned[...] = first[...].T
-
-    n, per, chans, _ = out.shape
-    value = dot_nn(tokens[...], w_value[...]).astype(bf16)
-    for r in range(per):
-        section = dot_nn(value[row_slice(r)].T, first_turned[...]).astype(bf16)
-        out[:, r] = section.reshape(n, chans, N2)
+def section_one_kernel(
+    per, tokens, w_value, first, out, tokens_v, w_v, first_v, out_v, arrive, leave
+):
+    n, rows, chans, _ = out.shape
+    chunks = rows // per
+    in_first = pltpu.make_async_copy(first, first_v, arrive.at[chunks])
+    in_w = pltpu.make_async_copy(w_value, w_v, arrive.at[chunks + 1])
+    in_tokens = [
+        pltpu.make_async_copy(
+            tokens.at[pl.ds(i * per * N2, per * N2)],
+            tokens_v.at[pl.ds(i * per * N2, per * N2)],
+            arrive.at[i],
+        )
+        for i in range(chunks)
+    ]
+    outs = [
+        pltpu.make_async_copy(
+            out_v.at[:, pl.ds(i * per, per)], out.at[:, pl.ds(i * per, per)], leave.at[i]
+        )
+        for i in range(chunks)
+    ]
+    in_w.start()
+    in_tokens[0].start()
+    in_first.start()
+    for copy in in_tokens[1:]:
+        copy.start()
+    in_w.wait()
+    for i in range(chunks):
+        in_tokens[i].wait()
+        value = dot_nn(tokens_v[i * per * N2 : (i + 1) * per * N2], w_v[...]).astype(bf16)
+        if i == 0:
+            in_first.wait()
+            first_v[...] = first_v[...].T
+        for r in range(per):
+            section = dot_nn(value[row_slice(r)].T, first_v[...]).astype(bf16)
+            out_v[:, i * per + r] = section.reshape(n, chans, N2)
+        outs[i].start()
+    for copy in outs:
+        copy.wait()
 
 
 def d_three_kernel(
@@ -67,7 +98,6 @@
     out,
     value_out,
     d_mix_out,
-    d_mix_t_out,
     tokens_t_out,
     skip_out,
 ):
@@ -88,9 +118,7 @@
         skip_out[...] += jnp.sum(
             d_mix.astype(f32) * value.astype(f32), axis=0, keepdims=True
         )
-        d_mix_t = d_mix.T
-        d_mix_t_out[:, here] = d_mix_t
-        section = dot_nn(d_mix_t, fourth[...]).astype(bf16)
+        section = dot_nn(d_mix.T, fourth[...]).astype(bf16)
         out[:, r] = section.reshape(n, chans, N2)
 
 
@@ -187,19 +215,58 @@
 
 
 def value_kernel(
-    arrived, tokens, d_mix_t, first, skip_column, factor, _, grad_w, total, d_value_t
+    per,
+    arrived,
+    tokens_t,
+    d_mix,
+    first_t,
+    skip,
+    factor,
+    _,
+    grad_w,
+    arrived_v,
+    tokens_v,
+    d_mix_v,
+    d_value,
+    total,
+    arrive,
 ):
-    for r in range(arrived.shape[1]):
-        here = row_slice(r)
-        d_cube_t = dot_nn(arrived[:, r].reshape(D, N2), first[...])
-        d_value_t[:, here] = (
-            d_cube_t + skip_column[...] * d_mix_t[:, here].astype(f32)
-        ).astype(bf16)
-    accumulate(total, dot_nn(d_value_t[...], tokens[...]))
-
-    @pl.when(pl.program_id(0) == pl.num_programs(0) - 1)
-    def _():
-        grad_w[...] = (total[...] * factor[0, 0]).astype(bf16).T
+    rows = arrived.shape[1]
+    chunks = rows // per
+
+    def copies(i):
+        lines = pl.ds(i * per, per)
+        here = pl.ds(i * per * N2, per * N2)
+        return [
+            pltpu.make_async_copy(
+                arrived.at[:, lines], arrived_v.at[:, lines], arrive.at[i, 0]
+            ),
+            pltpu.make_async_copy(d_mix.at[here], d_mix_v.at[here], arrive.at[i, 1]),
+            pltpu.make_async_copy(
+                tokens_t.at[:, here], tokens_v.at[:, here], arrive.at[i, 2]
+            ),
+        ]
+
+    started = [copies(i) for i in range(chunks)]
+    for group in started:
+        for copy in group:
+            copy.start()
+    for i in range(chunks):
+        started[i][0].wait()
+        started[i][1].wait()
+        for r in range(i * per, (i + 1) * per):
+            here = row_slice(r)
+            d_cube = dot_nt(first_t[...], arrived_v[:, r].reshape(D, N2))
+            d_value[here] = (d_cube + skip[...] * d_mix_v[here].astype(f32)).astype(bf16)
+        started[i][2].wait()
+        here = slice(i * per * N2, (i + 1) * per * N2)
+        term = dot_nn(tokens_v[:, here], d_value[here])
+        if i == 0:
+            total[...] = term
+        elif i < chunks - 1:
+            total[...] += term
+        else:
+            grad_w[...] = ((total[...] + term) * factor[0, 0]).astype(bf16)
 
 
 def tokens_kernel(arrived, d_mix, partial, first_t, skip, w_value_t, grad_tokens):
@@ -210,9 +277,10 @@
         grad_tokens[here] = (partial[here] + dot_nn(d_value, w_value_t[...])).astype(bf16)
 
 
-def sum_kernel(parts, _, out):
+def sum_kernel(parts, early, _, out, early_out):
     total = jnp.sum(parts[...].astype(f32), axis=0, keepdims=True).astype(bf16)
     out[...] = jnp.broadcast_to(total, out.shape)
+    early_out[...] = early[...]
 
 
 def from_partner(array, b, n):
@@ -290,28 +358,34 @@
     def transfer(array):
         return lax.all_to_all(array, "seq", split_axis=0, concat_axis=0, tiled=True)
 
+    unread = pl.BlockSpec(memory_space=pl.ANY)
     one_sent = pl.pallas_call(
-        section_one_kernel,
-        grid=(rows // per,),
-        in_specs=[row, square, block],
-        out_specs=sent,
+        functools.partial(section_one_kernel, per),
+        in_specs=[unread] * 3,
+        out_specs=unread,
         out_shape=shape(sections),
-        scratch_shapes=[pltpu.VMEM((N2, N2), bf16)],
+        scratch_shapes=[
+            pltpu.VMEM((local_rows, D), bf16),
+            pltpu.VMEM((D, D), bf16),
+            pltpu.VMEM((N2, N2), bf16),
+            pltpu.VMEM(sections, bf16),
+            pltpu.SemaphoreType.DMA((rows // per + 2,)),
+            pltpu.SemaphoreType.DMA((rows // per,)),
+        ],
         compiler_params=params(),
         cost_estimate=cost(3.2, 9),
     )(tokens, w_value, first_block)
     one_home = transfer(one_sent)
 
-    three_sent, value, d_mix, d_mix_t, tokens_t, skip_term = pl.pallas_call(
+    three_sent, value, d_mix, tokens_t, skip_term = pl.pallas_call(
         d_three_kernel,
         grid=(rows // per,),
         in_specs=[row, row, square, square, block],
-        out_specs=[sent, row, row, column, column, line],
+        out_specs=[sent, row, row, column, line],
         out_shape=[
             shape(sections),
             shape((local_rows, D)),
             shape((local_rows, D)),
-            shape((D, local_rows)),
             shape((D, local_rows)),
             shape((1, D), f32),
         ],
@@ -367,17 +441,24 @@
     skip_lanes = jnp.broadcast_to((skip_term * factor[0, 0]).astype(bf16).T, (D, LANES))
     early = halve_over_seq(jnp.concatenate([gate_term, skip_lanes], axis=1), n)
 
-    unread = pl.BlockSpec(memory_space=pl.ANY)
+    first_t = first_block.T
+    in_vmem = pl.BlockSpec(memory_space=pltpu.VMEM)
     value_term = pl.pallas_call(
-        value_kernel,
-        grid=(rows // per,),
-        in_specs=[sent, row, column, block, whole((D, 1)), one, unread],
-        out_specs=square,
+        functools.partial(value_kernel, per),
+        in_specs=[unread, unread, unread, in_vmem, in_vmem, one, unread],
+        out_specs=in_vmem,
         out_shape=shape((D, D)),
-        scratch_shapes=[pltpu.VMEM((D, D), f32), pltpu.VMEM((D, per * N2), bf16)],
+        scratch_shapes=[
+            pltpu.VMEM(sections, bf16),
+            pltpu.VMEM((D, local_rows), bf16),
+            pltpu.VMEM((local_rows, D), bf16),
+            pltpu.VMEM((local_rows, D), bf16),
+            pltpu.VMEM((D, D), f32),
+            pltpu.SemaphoreType.DMA((rows // per, 3)),
+        ],
         compiler_params=params(),
         cost_estimate=cost(3.3, 13),
-    )(one_here, tokens, d_mix_t, first_block, skip_gain.reshape(D, 1), factor, early)
+    )(one_here, tokens_t, d_mix, first_t, skip, factor, early)
 
     parts = transfer(value_term.reshape(n, D // n, D))
     grad_tokens = pl.pallas_call(
@@ -388,16 +469,15 @@
         out_shape=shape((local_rows, D)),
         compiler_params=params(),
         cost_estimate=cost(3.3, 20),
-    )(one_here, d_mix, partial, first_block.T, skip, w_value.T)
-    own = pl.pallas_call(
+    )(one_here, d_mix, partial, first_t, skip, w_value.T)
+    own, early = pl.pallas_call(
         sum_kernel,
-        grid=(1,),
-        in_specs=[whole(parts.shape), unread],
-        out_specs=whole(parts.shape),
-        out_shape=shape(parts.shape),
+        in_specs=[in_vmem, in_vmem, unread],
+        out_specs=[in_vmem, in_vmem],
+        out_shape=[shape(parts.shape), shape(early.shape)],
         compiler_params=params(),
         cost_estimate=cost(0.001, 1),
-    )(parts, grad_tokens)
+    )(parts, early, grad_tokens)
     value_total = transfer(own).reshape(D, D)
     early = double_over_seq(early, n)
     gate_total, skip_total = early[:, :D], early[:, D]

time: 463 us -> 461 us (level)
    all_to_all x6, waiting for transfers between devices: 187 us -> 179 us  [transfer(): return lax.all_to_all(array, 'seq', split_axis=0, concat_axis=0, tiled=True)]
    ppermute x8, waiting for transfers between devices: 79.5 us -> 86.3 us  [from_partner(): return lax.ppermute(array, 'seq', [(i, i ^ 1 << b) for i in range(n)])]
  transfers between devices with their start and end apart: 14 -> 14, of which waited for: 11 -> 12; matrix products, arithmetic and copies ran while one was open for 2% -> 2% of each run, Pallas kernels for 17% -> 17%
where the time goes in v6:
time: 461 us; the launch traced here: 460 us
  waiting for transfers between devices  265 us (57%)
  Pallas kernels  94.8 us (21%)
  starting transfers between devices  86.1 us (19%)
  other arithmetic  7.73 us (2%)
  local copies, waits for them, and re-layouts  5.5 us (1%)
    all_to_all x6, waiting for transfers between devices, transfer(): return lax.all_to_all(array, 'seq', split_axis=0, concat_axis=0, tiled=True)  179 us
    ppermute x8, waiting for transfers between devices, from_partner(): return lax.ppermute(array, 'seq', [(i, i ^ 1 << b) for i in range(n)])  86.3 us
    all_to_all x6, starting transfers between devices, transfer(): return lax.all_to_all(array, 'seq', split_axis=0, concat_axis=0, tiled=True)  74 us
    pallas_call x1, Pallas kernels, on_device(): pl.pallas_call(home_backward_kernel, grid=(chans // GROUP,), in_specs=[at...  20.6 us
    pallas_call x1, Pallas kernels, on_device(): pl.pallas_call(home_forward_kernel, grid=(chans // GROUP,), in_specs=[at_...  20.1 us
    pallas_call x1, Pallas kernels, on_device(): pl.pallas_call(d_three_kernel, grid=(rows // per,), in_specs=[row, row, s...  14 us
    pallas_call x1, Pallas kernels, on_device(): pl.pallas_call(gate_kernel, grid=(rows // per,), in_specs=[sent, column,...  13.2 us
    ppermute x8, starting transfers between devices, from_partner(): return lax.ppermute(array, 'seq', [(i, i ^ 1 << b) for i in range(n)])  12 us
  transfers between devices with their start and end apart: 14, of which 12 were waited for; matrix products, arithmetic and copies ran while one was open for 2% of the time, Pallas kernels for 17%

profile of v6, /device:TPU:0, one launch (start us, length us, event | category | flops | bytes accessed | tf_op | source)
XLA Modules:
  0.0 460.3 jit_solution(18417983283857238487)
XLA Ops:
  0.6 6.7 %shard_map.130 = bf16[16,16,32,256]{3,2,1,0:T(8,128)(2,1)} custom-call(bf16[4096,512]{1,0:T(8,128)(2,1)} %tokens.3, bf16[512,512]{1,0:T(8,128)(2,1)} %w_value.3, bf16[256,256]{1,0:T(8,128)(2,1)} %first.1), custom_call_target="tpu_custom_call" | custom-call | flops 3200000000 | bytes 9437184 | tf_op jit(solution)/shard_map/pallas_call | solution.py:362
  7.4 7.5 %all-to-all-start.1 = ((bf16[16,16,32,256]{3,2,1,0:T(8,128)(2,1)}), bf16[16,16,32,256]{3,2,1,0:T(8,128)(2,1)}, u32[]{:S(2)}, u32[]{:S(2)}) async-start(bf16[16,16,32,256]{3,2,1,0:T(8,128)(2,1)} %shard_map.130), calls=%async_computation.1 | async-start | bytes 8388608 | tf_op jit(solution)/shard_map/all_to_all | solution.py:359
  14.8 14.0 %shard_map.129 = (bf16[16,16,32,256]{3,2,1,0:T(8,128)(2,1)}, bf16[4096,512]{1,0:T(8,128)(2,1)}, bf16[4096,512]{1,0:T(8,128)(2,1)}, bf16[512,4096]{1,0:T(8,128)(2,1)}, f32[1,512]{1,0:T(1,128)}) custom-call(bf16[4096,512]{1,0:T(8,128)(2,1)} %tokens.3, bf16[4096,512]{1,0:T(8,128)(2,1)} %cotangent.3, bf16[512,512]{1,0:T(8,128)(2,1)} %w_value.3, ...), custom_call_target="tpu_custom_call" | custom-call | flops 5400000000 | bytes 26214400 | tf_op jit(solution)/shard_map/pallas_call | solution.py:380
  28.9 63.6 %all-to-all-done.1 = bf16[16,16,32,256]{3,2,1,0:T(8,128)(2,1)} async-done(((bf16[16,16,32,256]{3,2,1,0:T(8,128)(2,1)}), bf16[16,16,32,256]{3,2,1,0:T(8,128)(2,1)}, u32[]{:S(2)}, u32[]{:S(2)}) %all-to-all-start.1) | async-done | bytes 4194336 | tf_op jit(solution)/shard_map/all_to_all | solution.py:359
  92.5 19.7 %all-to-all-start = ((bf16[16,16,32,256]{3,2,1,0:T(8,128)(2,1)}), bf16[16,16,32,256]{3,2,1,0:T(8,128)(2,1)}, u32[]{:S(2)}, u32[]{:S(2)}) async-start(bf16[16,16,32,256]{3,2,1,0:T(8,128)(2,1)} %get-tuple-element.17), calls=%async_computation | async-start | bytes 8388608 | tf_op jit(solution)/shard_map/all_to_all | solution.py:359
  113.0 20.1 %shard_map.131 = (bf16[256,32,256]{2,1,0:T(8,128)(2,1)}, f32[32,256,256]{2,1,0:T(8,128)}) custom-call(bf16[256,32,256]{2,1,0:T(8,128)(2,1)} %bitcast.1.arrived, bf16[32,256,256]{2,1,0:T(8,128)(2,1)} %kernel.3, bf16[256,256]{1,0:T(8,128)(2,1)} %second.1, bf16[256,256]{1,0:T(8,128)(2,1)} %third.1, bf16[256,256]{1,0:T(8,128)(2,1)} %fusion.2.swap), custom_call_target="tpu_custom_call" | custom-call | flops 4300000256 | bytes 20971520 | tf_op jit(solution)/shard_map/pallas_call | solution.py:399
  133.1 56.8 %all-to-all-done = bf16[16,16,32,256]{3,2,1,0:T(8,128)(2,1)} async-done(((bf16[16,16,32,256]{3,2,1,0:T(8,128)(2,1)}), bf16[16,16,32,256]{3,2,1,0:T(8,128)(2,1)}, u32[]{:S(2)}, u32[]{:S(2)}) %all-to-all-start) | async-done | bytes 4194336 | tf_op jit(solution)/shard_map/all_to_all | solution.py:359
  189.9 19.8 %all-to-all-start.3 = ((bf16[16,16,32,256]{3,2,1,0:T(8,128)(2,1)}), bf16[16,16,32,256]{3,2,1,0:T(8,128)(2,1)}, u32[]{:S(2)}, u32[]{:S(2)}) async-start(bf16[16,16,32,256]{3,2,1,0:T(8,128)(2,1)} %bitcast.53), calls=%async_computation.3 | async-start | bytes 8388608 | tf_op jit(solution)/shard_map/all_to_all | solution.py:359
  211.2 20.6 %shard_map.132 = (bf16[256,32,256]{2,1,0:T(8,128)(2,1)}, bf16[32,256,256]{2,1,0:T(8,128)(2,1)}) custom-call(bf16[256,32,256]{2,1,0:T(8,128)(2,1)} %bitcast.arrived, bf16[32,256,256]{2,1,0:T(8,128)(2,1)} %kernel.3, f32[32,256,256]{2,1,0:T(8,128)} %get-tuple-element.18.spectrum, bf16[256,256]{1,0:T(8,128)(2,1)} %bitcast.67, bf16[256,256]{1,0:T(8,128)(2,1)} %bitcast.68, ...), custom_call_target="tpu_custom_call" | custom-call | flops 4300000256 | bytes 25165824 | tf_op jit(solution)/shard_map/pallas_call | solution.py:411
  231.9 55.5 %all-to-all-done.3.arrived = bf16[16,16,32,256]{3,2,1,0:T(8,128)(2,1)} async-done(((bf16[16,16,32,256]{3,2,1,0:T(8,128)(2,1)}), bf16[16,16,32,256]{3,2,1,0:T(8,128)(2,1)}, u32[]{:S(2)}, u32[]{:S(2)}) %all-to-all-start.3) | async-done | bytes 4194336 | tf_op jit(solution)/shard_map/all_to_all | solution.py:359
  287.4 19.8 %all-to-all-start.2 = ((bf16[16,16,32,256]{3,2,1,0:T(8,128)(2,1)}), bf16[16,16,32,256]{3,2,1,0:T(8,128)(2,1)}, u32[]{:S(2)}, u32[]{:S(2)}) async-start(bf16[16,16,32,256]{3,2,1,0:T(8,128)(2,1)} %bitcast.52), calls=%async_computation.2 | async-start | bytes 8388608 | tf_op jit(solution)/shard_map/all_to_all | solution.py:359
  308.3 13.2 %shard_map.133 = (f32[4096,512]{1,0:T(8,128)}, bf16[512,512]{1,0:T(8,128)(2,1)}) custom-call(bf16[16,16,32,256]{3,2,1,0:T(8,128)(2,1)} %all-to-all-done.3.arrived, bf16[512,4096]{1,0:T(8,128)(2,1)} %get-tuple-element.22.tokens_t, bf16[4096,512]{1,0:T(8,128)(2,1)} %get-tuple-element.23.value, bf16[4096,512]{1,0:T(8,128)(2,1)} %cotangent.3, ...), custom_call_target="tpu_custom_call" | custom-call | flops 5400000000 | bytes 26214400 | tf_op jit(solution)/shard_map/pallas_call | solution.py:430
  326.6 10.7 %collective-permute-done.1 = bf16[2,2,32,640]{3,2,0,1:T(8,128)(2,1)S(1)} collective-permute-done((bf16[2,2,32,640]{3,2,0,1:T(8,128)(2,1)S(1)}, bf16[2,2,32,640]{3,2,0,1:T(8,128)(2,1)S(1)}, u32[]{:S(2)}, u32[]{:S(2)}) %collective-permute-start.1) | collective-permute-done | bytes 163872 | tf_op jit(solution)/shard_map/ppermute | solution.py:287
  337.5 40.0 %collective-permute-done.2 = bf16[2,32,640]{2,1,0:T(8,128)(2,1)S(1)} collective-permute-done((bf16[2,32,640]{2,1,0:T(8,128)(2,1)S(1)}, bf16[2,32,640]{2,1,0:T(8,128)(2,1)S(1)}, u32[]{:S(2)}, u32[]{:S(2)}) %collective-permute-start.2) | collective-permute-done | bytes 81952 | tf_op jit(solution)/shard_map/ppermute | solution.py:287
  377.6 4.6 collective-permute-start.3
  383.0 20.0 %collective-permute-done.3 = bf16[32,640]{1,0:T(8,128)(2,1)S(1)} collective-permute-done((bf16[32,640]{1,0:T(8,128)(2,1)S(1)}, bf16[32,640]{1,0:T(8,128)(2,1)S(1)}, u32[]{:S(2)}, u32[]{:S(2)}) %collective-permute-start.3) | collective-permute-done | bytes 40992 | tf_op jit(solution)/shard_map/ppermute | solution.py:287
  403.6 7.8 %shard_map.135 = bf16[512,512]{1,0:T(8,128)(2,1)} custom-call(bf16[16,16,32,256]{3,2,1,0:T(8,128)(2,1)} %all-to-all-done.2.arrived, bf16[512,4096]{1,0:T(8,128)(2,1)} %get-tuple-element.22.tokens_t, bf16[4096,512]{1,0:T(8,128)(2,1)} %get-tuple-element.20.d_mix, bf16[256,256]{1,0:T(8,128)(2,1)} %bitcast.60, f32[1,512]{1,0:T(1,128)} %bitcast.79, ...), custom_call_target="tpu_custom_call" | custom-call | flops 3300000000 | bytes 13631488 | tf_op jit(solution)/shard_map/pallas_call | solution.py:446
  411.4 3.7 all-to-all-start.4
  416.1 10.4 %shard_map.134._ = bf16[4096,512]{1,0:T(8,128)(2,1)} custom-call(bf16[16,16,32,256]{3,2,1,0:T(8,128)(2,1)} %all-to-all-done.2.arrived, bf16[4096,512]{1,0:T(8,128)(2,1)} %get-tuple-element.20.d_mix, f32[4096,512]{1,0:T(8,128)} %get-tuple-element.24.partial, bf16[256,256]{1,0:T(8,128)(2,1)} %bitcast.61, f32[1,512]{1,0:T(1,128)} %bitcast.80, ...), custom_call_target="tpu_custom_call" | custom-call | flops 3300000000 | bytes 20971520 | tf_op jit(solution)/shard_map/pallas_call | solution.py:464
  426.5 3.1 all-to-all-done.4.parts
  432.3 2.3 collective-permute-start.4
  434.6 3.6 all-to-all-start.5
  441.8 8.3 %collective-permute-done.5 = bf16[2,32,640]{2,1,0:T(8,128)(2,1)S(1)} collective-permute-done((bf16[2,32,640]{2,1,0:T(8,128)(2,1)S(1)}, bf16[2,32,640]{2,1,0:T(8,128)(2,1)S(1)}, u32[]{:S(2)}, u32[]{:S(2)}) %collective-permute-start.5) | collective-permute-done | bytes 81952 | tf_op jit(solution)/shard_map/ppermute | solution.py:287
  451.9 4.2 collective-permute-done.6
  (58 shorter events, 23.4 us)
Async XLA Ops:
  7.4 85.1 %all-to-all-start.1 = ((bf16[16,16,32,256]{3,2,1,0:T(8,128)(2,1)}), bf16[16,16,32,256]{3,2,1,0:T(8,128)(2,1)}, u32[]{:S(2)}, u32[]{:S(2)}) async-start(bf16[16,16,32,256]{3,2,1,0:T(8,128)(2,1)} %shard_map.130), calls=%async_computation.1 | async-start | bytes 8388608 | tf_op jit(solution)/shard_map/all_to_all | solution.py:359
  92.5 97.4 %all-to-all-start = ((bf16[16,16,32,256]{3,2,1,0:T(8,128)(2,1)}), bf16[16,16,32,256]{3,2,1,0:T(8,128)(2,1)}, u32[]{:S(2)}, u32[]{:S(2)}) async-start(bf16[16,16,32,256]{3,2,1,0:T(8,128)(2,1)} %get-tuple-element.17), calls=%async_computation | async-start | bytes 8388608 | tf_op jit(solution)/shard_map/all_to_all | solution.py:359
  189.9 19.8 %copy-start.3 = (bf16[256,256]{1,0:T(8,128)(2,1)S(1)}, bf16[256,256]{1,0:T(8,128)(2,1)}, u32[]{:S(2)}) copy-start(bf16[256,256]{1,0:T(8,128)(2,1)} %second.1) | copy-start | bytes 393220
  189.9 20.6 %copy-start.4 = (bf16[256,256]{1,0:T(8,128)(2,1)S(1)}, bf16[256,256]{1,0:T(8,128)(2,1)}, u32[]{:S(2)}) copy-start(bf16[256,256]{1,0:T(8,128)(2,1)} %third.1) | copy-start | bytes 393220
  189.9 97.5 %all-to-all-start.3 = ((bf16[16,16,32,256]{3,2,1,0:T(8,128)(2,1)}), bf16[16,16,32,256]{3,2,1,0:T(8,128)(2,1)}, u32[]{:S(2)}, u32[]{:S(2)}) async-start(bf16[16,16,32,256]{3,2,1,0:T(8,128)(2,1)} %bitcast.53), calls=%async_computation.3 | async-start | bytes 8388608 | tf_op jit(solution)/shard_map/all_to_all | solution.py:359
  287.4 19.8 %copy-start.1 = (bf16[512,512]{1,0:T(8,128)(2,1)S(1)}, bf16[512,512]{1,0:T(8,128)(2,1)}, u32[]{:S(2)}) copy-start(bf16[512,512]{1,0:T(8,128)(2,1)} %w_gate.1) | copy-start | bytes 1572868
  287.4 20.9 %copy-start.6 = (f32[1,512]{1,0:T(1,128)S(1)}, f32[1,512]{1,0:T(1,128)}, u32[]{:S(2)}) copy-start(f32[1,512]{1,0:T(1,128)} %get-tuple-element.27) | copy-start | bytes 6148
  287.4 116.2 %all-to-all-start.2 = ((bf16[16,16,32,256]{3,2,1,0:T(8,128)(2,1)}), bf16[16,16,32,256]{3,2,1,0:T(8,128)(2,1)}, u32[]{:S(2)}, u32[]{:S(2)}) async-start(bf16[16,16,32,256]{3,2,1,0:T(8,128)(2,1)} %bitcast.52), calls=%async_computation.2 | async-start | bytes 8388608 | tf_op jit(solution)/shard_map/all_to_all | solution.py:359
  321.4 60.8 %copy-start.5 = (bf16[256,256]{1,0:T(8,128)(2,1)S(1)}, bf16[256,256]{1,0:T(8,128)(2,1)}, u32[]{:S(2)}) copy-start(bf16[256,256]{1,0:T(8,128)(2,1)} %first.1) | copy-start | bytes 393220
  322.8 1.7 collective-permute-start
  324.6 12.7 %collective-permute-start.1 = (bf16[2,2,32,640]{3,2,0,1:T(8,128)(2,1)S(1)}, bf16[2,2,32,640]{3,2,0,1:T(8,128)(2,1)S(1)}, u32[]{:S(2)}, u32[]{:S(2)}) collective-permute-start(bf16[2,2,32,640]{3,2,0,1:T(8,128)(2,1)S(1)} %dynamic-slice_bitcast_fusion), channel_id=1, source_target_pairs={{0,2},{1,3},{2,0},{3,1},{4,6},{5,7},{6,4},{7,5},{8,10},{9,11},{10,... | collective-permute-start | bytes 491528 | tf_op jit(solution)/shard_map/ppermute | solution.py:287
  337.4 40.2 %collective-permute-start.2 = (bf16[2,32,640]{2,1,0:T(8,128)(2,1)S(1)}, bf16[2,32,640]{2,1,0:T(8,128)(2,1)S(1)}, u32[]{:S(2)}, u32[]{:S(2)}) collective-permute-start(bf16[2,32,640]{2,1,0:T(8,128)(2,1)S(1)} %dynamic-slice_bitcast_fusion.1), channel_id=1, source_target_pairs={{0,4},{1,5},{2,6},{3,7},{4,0},{5,1},{6,2},{7,3},{8,12},{9,13},{10,... | collective-permute-start | bytes 245768 | tf_op jit(solution)/shard_map/ppermute | solution.py:287
  377.6 25.4 %collective-permute-start.3 = (bf16[32,640]{1,0:T(8,128)(2,1)S(1)}, bf16[32,640]{1,0:T(8,128)(2,1)S(1)}, u32[]{:S(2)}, u32[]{:S(2)}) collective-permute-start(bf16[32,640]{1,0:T(8,128)(2,1)S(1)} %dynamic-slice_bitcast_fusion.2), channel_id=1, source_target_pairs={{0,8},{1,9},{2,10},{3,11},{4,12},{5,13},{6,14},{7,15},{8,0},{9,1},... | collective-permute-start | bytes 122888 | tf_op jit(solution)/shard_map/ppermute | solution.py:287
  403.6 11.5 %copy-start.2 = (bf16[512,512]{1,0:T(8,128)(2,1)S(1)}, bf16[512,512]{1,0:T(8,128)(2,1)}, u32[]{:S(2)}) copy-start(bf16[512,512]{1,0:T(8,128)(2,1)} %w_value.3) | copy-start | bytes 1572868
  411.4 18.1 %all-to-all-start.4 = ((bf16[16,32,512]{2,1,0:T(8,128)(2,1)}), bf16[16,32,512]{2,1,0:T(8,128)(2,1)S(1)}, u32[]{:S(2)}, u32[]{:S(2)}) async-start(bf16[16,32,512]{2,1,0:T(8,128)(2,1)} %bitcast.57), calls=%async_computation.4 | async-start | bytes 1048576 | tf_op jit(solution)/shard_map/all_to_all | solution.py:359
  429.6 0.8 copy-start
  432.3 6.0 %collective-permute-start.4 = (bf16[32,640]{1,0:T(8,128)(2,1)}, bf16[32,640]{1,0:T(8,128)(2,1)S(1)}, u32[]{:S(2)}, u32[]{:S(2)}) collective-permute-start(bf16[32,640]{1,0:T(8,128)(2,1)} %get-tuple-element.29), channel_id=1, source_target_pairs={{0,8},{1,9},{2,10},{3,11},{4,12},{5,13},{6,14},{7,15},{8,0},{9,1},... | collective-permute-start | bytes 122888 | tf_op jit(solution)/shard_map/ppermute | solution.py:287
  434.6 24.3 %all-to-all-start.5 = ((bf16[16,32,512]{2,1,0:T(8,128)(2,1)}), bf16[16,32,512]{2,1,0:T(8,128)(2,1)S(1)}, u32[]{:S(2)}, u32[]{:S(2)}) async-start(bf16[16,32,512]{2,1,0:T(8,128)(2,1)} %get-tuple-element.28), calls=%async_computation.5 | async-start | bytes 1048576 | tf_op jit(solution)/shard_map/all_to_all | solution.py:359
  439.2 10.9 %collective-permute-start.5 = (bf16[2,32,640]{2,1,0:T(8,128)(2,1)S(1)}, bf16[2,32,640]{2,1,0:T(8,128)(2,1)S(1)}, u32[]{:S(2)}, u32[]{:S(2)}) collective-permute-start(bf16[2,32,640]{2,1,0:T(8,128)(2,1)S(1)} %maximum_select_fusion.6), channel_id=1, source_target_pairs={{0,4},{1,5},{2,6},{3,7},{4,0},{5,1},{6,2},{7,3},{8,12},{9,13},{10,... | collective-permute-start | bytes 245768 | tf_op jit(solution)/shard_map/ppermute | solution.py:287
  450.1 6.0 %collective-permute-start.6 = (bf16[2,2,32,640]{3,2,0,1:T(8,128)(2,1)S(1)}, bf16[2,2,32,640]{3,2,0,1:T(8,128)(2,1)S(1)}, u32[]{:S(2)}, u32[]{:S(2)}) collective-permute-start(bf16[2,2,32,640]{3,2,0,1:T(8,128)(2,1)S(1)} %maximum_select_fusion.4), channel_id=1, source_target_pairs={{0,2},{1,3},{2,0},{3,1},{4,6},{5,7},{6,4},{7,5},{8,10},{9,11},{10,... | collective-permute-start | bytes 491528 | tf_op jit(solution)/shard_map/ppermute | solution.py:287
  456.2 1.7 collective-permute-start.7

commit v7 on v6

--- a/solution.py
+++ b/solution.py
@@ -4,6 +4,7 @@
 
 import jax
 import jax.numpy as jnp
+import numpy as np
 from jax import lax
 from jax.experimental import pallas as pl
 from jax.experimental.pallas import tpu as pltpu
@@ -44,12 +45,39 @@
     return pl.BlockSpec((n, per, chans, N2), lambda i: (0, i, 0, 0))
 
 
+def interleaved(n):
+    return [i // 2 + (i % 2) * (n // 2) for i in range(n)]
+
+
+def reversed_bits(n):
+    bits = n.bit_length() - 1
+    return [sum(((i >> b) & 1) << (bits - 1 - b) for b in range(bits)) for i in range(n)]
+
+
+def strided(n):
+    return [(i % 4) * (n // 4) + i // 4 for i in range(n)]
+
+
+def mirrored(n):
+    return [n - 1 - i // 2 if i % 2 else i // 2 for i in range(n)]
+
+
+def to_blocks(section, order, out, r):
+    chans = section.shape[0] // len(order)
+    for i, device in enumerate(order):
+        out[i, r] = section[device * chans : (device + 1) * chans]
+
+
+def from_blocks(arrived, order, r):
+    return jnp.concatenate([arrived[order.index(d), r] for d in range(len(order))])
+
+
 def row_slice(r):
     return slice(r * N2, (r + 1) * N2)
 
 
 def section_one_kernel(
-    per, tokens, w_value, first, out, tokens_v, w_v, first_v, out_v, arrive, leave
+    per, order, tokens, w_value, first, out, tokens_v, w_v, first_v, out_v, arrive, leave
 ):
     n, rows, chans, _ = out.shape
     chunks = rows // per
@@ -83,13 +111,14 @@
             first_v[...] = first_v[...].T
         for r in range(per):
             section = dot_nn(value[row_slice(r)].T, first_v[...]).astype(bf16)
-            out_v[:, i * per + r] = section.reshape(n, chans, N2)
+            to_blocks(section, order, out_v, i * per + r)
         outs[i].start()
     for copy in outs:
         copy.wait()
 
 
 def d_three_kernel(
+    order,
     tokens,
     cotangent,
     w_value,
@@ -101,13 +130,11 @@
     tokens_t_out,
     skip_out,
 ):
-    n, per, chans, _ = out.shape
-
     @pl.when(pl.program_id(0) == 0)
     def _():
         skip_out[...] = jnp.zeros_like(skip_out)
 
-    for r in range(per):
+    for r in range(out.shape[1]):
         here = row_slice(r)
         value = dot_nn(tokens[here], w_value[...]).astype(bf16)
         gate = dot_nn(tokens[here], w_gate[...]).astype(bf16)
@@ -119,7 +146,7 @@
             d_mix.astype(f32) * value.astype(f32), axis=0, keepdims=True
         )
         section = dot_nn(d_mix.T, fourth[...]).astype(bf16)
-        out[:, r] = section.reshape(n, chans, N2)
+        to_blocks(section, order, out, r)
 
 
 def turn_in(swap, arrived, by_channel):
@@ -191,6 +218,7 @@
 
 
 def gate_kernel(
+    order,
     arrived,
     tokens_t,
     value,
@@ -206,7 +234,7 @@
 ):
     for r in range(arrived.shape[1]):
         here = row_slice(r)
-        conv = dot_nt(fourth[...], arrived[:, r].reshape(D, N2))
+        conv = dot_nt(fourth[...], from_blocks(arrived, order, r))
         mixed = conv + skip[...] * value[here].astype(f32)
         d_gate[here] = (cotangent[here].astype(f32) * mixed).astype(bf16)
         partial[here] = dot_nn(d_gate[here], w_gate_t[...])
@@ -216,6 +244,7 @@
 
 def value_kernel(
     per,
+    order,
     arrived,
     tokens_t,
     d_mix,
@@ -256,7 +285,7 @@
         started[i][1].wait()
         for r in range(i * per, (i + 1) * per):
             here = row_slice(r)
-            d_cube = dot_nt(first_t[...], arrived_v[:, r].reshape(D, N2))
+            d_cube = dot_nt(first_t[...], from_blocks(arrived_v, order, r))
             d_value[here] = (d_cube + skip[...] * d_mix_v[here].astype(f32)).astype(bf16)
         started[i][2].wait()
         here = slice(i * per * N2, (i + 1) * per * N2)
@@ -269,10 +298,10 @@
             grad_w[...] = ((total[...] + term) * factor[0, 0]).astype(bf16)
 
 
-def tokens_kernel(arrived, d_mix, partial, first_t, skip, w_value_t, grad_tokens):
+def tokens_kernel(order, arrived, d_mix, partial, first_t, skip, w_value_t, grad_tokens):
     for r in range(arrived.shape[1]):
         here = row_slice(r)
-        d_cube = dot_nt(first_t[...], arrived[:, r].reshape(D, N2))
+        d_cube = dot_nt(first_t[...], from_blocks(arrived, order, r))
         d_value = (d_cube + skip[...] * d_mix[here].astype(f32)).astype(bf16)
         grad_tokens[here] = (partial[here] + dot_nn(d_value, w_value_t[...])).astype(bf16)
 
@@ -355,12 +384,20 @@
     def shape(dims, dtype=bf16):
         return jax.ShapeDtypeStruct(dims, dtype)
 
-    def transfer(array):
-        return lax.all_to_all(array, "seq", split_axis=0, concat_axis=0, tiled=True)
-
+    def transfer(array, order=None):
+        groups = None if order is None else [order]
+        return lax.all_to_all(
+            array, "seq", split_axis=0, concat_axis=0, tiled=True, axis_index_groups=groups
+        )
+
+    orders = [interleaved(n), reversed_bits(n), strided(n), mirrored(n)]
+    places = [np.concatenate([d * rows + np.arange(rows) for d in order]) for order in orders]
+    picks = [
+        (jnp.asarray(p)[:, None] == jnp.arange(N1)[None, :]).astype(bf16) for p in places
+    ]
     unread = pl.BlockSpec(memory_space=pl.ANY)
     one_sent = pl.pallas_call(
-        functools.partial(section_one_kernel, per),
+        functools.partial(section_one_kernel, per, orders[0]),
         in_specs=[unread] * 3,
         out_specs=unread,
         out_shape=shape(sections),
@@ -375,10 +412,10 @@
         compiler_params=params(),
         cost_estimate=cost(3.2, 9),
     )(tokens, w_value, first_block)
-    one_home = transfer(one_sent)
+    one_home = transfer(one_sent, orders[0])
 
     three_sent, value, d_mix, tokens_t, skip_term = pl.pallas_call(
-        d_three_kernel,
+        functools.partial(d_three_kernel, orders[1]),
         grid=(rows // per,),
         in_specs=[row, row, square, square, block],
         out_specs=[sent, row, row, column, line],
@@ -392,7 +429,7 @@
         compiler_params=params(),
         cost_estimate=cost(5.4, 25),
     )(tokens, cotangent, w_value, w_gate, fourth_block)
-    three_home = transfer(three_sent)
+    three_home = transfer(three_sent, orders[1])
 
     at_home = pl.BlockSpec((N1, GROUP, N2), lambda i: (0, i, 0))
     filters = pl.BlockSpec((GROUP, N1, N2), lambda i: (i, 0, 0))
@@ -405,8 +442,14 @@
         scratch_shapes=[pltpu.VMEM((GROUP, N1, N2), bf16)],
         compiler_params=params(),
         cost_estimate=cost(4.3, 20),
-    )(one_home.reshape(N1, chans, N2), kernel, second_block, third_block, swap)
-    three_here = transfer(three_back.reshape(sections))
+    )(
+        one_home.reshape(N1, chans, N2),
+        kernel,
+        dot_nt(second_block, picks[0]).astype(bf16),
+        dot_nn(picks[2], third_block).astype(bf16),
+        swap,
+    )
+    three_here = transfer(three_back.reshape(sections), orders[2])
 
     one_back, grad_kernel = pl.pallas_call(
         home_backward_kernel,
@@ -421,14 +464,14 @@
         three_home.reshape(N1, chans, N2),
         kernel,
         spectrum,
-        second_block.T,
-        third_block.T,
+        dot_nt(picks[3], second_block).astype(bf16),
+        dot_nn(picks[1], third_block).T.astype(bf16),
         swap,
     )
-    one_here = transfer(one_back.reshape(sections))
+    one_here = transfer(one_back.reshape(sections), orders[3])
 
     partial, gate_term = pl.pallas_call(
-        gate_kernel,
+        functools.partial(gate_kernel, orders[2]),
         grid=(rows // per,),
         in_specs=[sent, column, row, row, block, square, line, one],
         out_specs=[row, square],
@@ -444,7 +487,7 @@
     first_t = first_block.T
     in_vmem = pl.BlockSpec(memory_space=pltpu.VMEM)
     value_term = pl.pallas_call(
-        functools.partial(value_kernel, per),
+        functools.partial(value_kernel, per, orders[3]),
         in_specs=[unread, unread, unread, in_vmem, in_vmem, one, unread],
         out_specs=in_vmem,
         out_shape=shape((D, D)),
@@ -462,7 +505,7 @@
 
     parts = transfer(value_term.reshape(n, D // n, D))
     grad_tokens = pl.pallas_call(
-        tokens_kernel,
+        functools.partial(tokens_kernel, orders[3]),
         grid=(rows // per,),
         in_specs=[sent, row, row, block, line, square],
         out_specs=row,

time: 461 us -> 475 us (1.030)
  waiting for transfers between devices: 265 us -> 312 us
  starting transfers between devices: 86.1 us -> 50.9 us
    all_to_all x6, waiting for transfers between devices: 179 us -> 230 us  [transfer(): lax.all_to_all(array, 'seq', split_axis=0, concat_axis=0, tiled=True, axi...]
    all_to_all x6, starting transfers between devices: 74 us -> 34.4 us  [transfer(): lax.all_to_all(array, 'seq', split_axis=0, concat_axis=0, tiled=True, axi...]
    ppermute x8, waiting for transfers between devices: 86.3 us -> 81.5 us  [from_partner(): return lax.ppermute(array, 'seq', [(i, i ^ 1 << b) for i in range(n)])]
  transfers between devices with their start and end apart: 14 -> 14, of which waited for: 12 -> 12; matrix products, arithmetic and copies ran while one was open for 2% -> 3% of each run, Pallas kernels for 17% -> 17%
where the time goes in v7:
time: 475 us; the launch traced here: 474 us
  waiting for transfers between devices  312 us (66%)
  Pallas kernels  94.9 us (20%)
  starting transfers between devices  50.9 us (11%)
  other arithmetic  7.72 us (2%)
    all_to_all x6, waiting for transfers between devices, transfer(): lax.all_to_all(array, 'seq', split_axis=0, concat_axis=0, tiled=True, axi...  230 us
    ppermute x8, waiting for transfers between devices, from_partner(): return lax.ppermute(array, 'seq', [(i, i ^ 1 << b) for i in range(n)])  81.5 us
    all_to_all x6, starting transfers between devices, transfer(): lax.all_to_all(array, 'seq', split_axis=0, concat_axis=0, tiled=True, axi...  34.4 us
    pallas_call x1, Pallas kernels, on_device(): pl.pallas_call(home_backward_kernel, grid=(chans // GROUP,), in_specs=[at...  20.6 us
    pallas_call x1, Pallas kernels, on_device(): pl.pallas_call(home_forward_kernel, grid=(chans // GROUP,), in_specs=[at_...  20.1 us
    ppermute x8, starting transfers between devices, from_partner(): return lax.ppermute(array, 'seq', [(i, i ^ 1 << b) for i in range(n)])  16.5 us
    pallas_call x1, Pallas kernels, on_device(): pl.pallas_call(functools.partial(d_three_kernel, orders[1]), grid=(rows /...  14.1 us
    pallas_call x1, Pallas kernels, on_device(): pl.pallas_call(functools.partial(gate_kernel, orders[2]), grid=(rows // p...  13.1 us
  transfers between devices with their start and end apart: 14, of which 12 were waited for; matrix products, arithmetic and copies ran while one was open for 3% of the time, Pallas kernels for 17%

profile of v7, /device:TPU:0, one launch (start us, length us, event | category | flops | bytes accessed | tf_op | source)
XLA Modules:
  0.0 474.0 jit_solution(17292181447285834372)
XLA Ops:
  0.6 6.8 %shard_map.166 = bf16[16,16,32,256]{3,2,1,0:T(8,128)(2,1)} custom-call(bf16[4096,512]{1,0:T(8,128)(2,1)} %tokens.3, bf16[512,512]{1,0:T(8,128)(2,1)} %w_value.3, bf16[256,256]{1,0:T(8,128)(2,1)} %first.1), custom_call_target="tpu_custom_call" | custom-call | flops 3200000000 | bytes 9437184 | tf_op jit(solution)/shard_map/pallas_call | solution.py:399
  7.4 7.4 %all-to-all-start.1 = ((bf16[16,16,32,256]{3,2,1,0:T(8,128)(2,1)}), bf16[16,16,32,256]{3,2,1,0:T(8,128)(2,1)}, u32[]{:S(2)}, u32[]{:S(2)}) async-start(bf16[16,16,32,256]{3,2,1,0:T(8,128)(2,1)} %shard_map.166), calls=%async_computation.1 | async-start | bytes 8388608 | tf_op jit(solution)/shard_map/all_to_all | solution.py:389
  14.9 14.1 %shard_map.165 = (bf16[16,16,32,256]{3,2,1,0:T(8,128)(2,1)}, bf16[4096,512]{1,0:T(8,128)(2,1)}, bf16[4096,512]{1,0:T(8,128)(2,1)}, bf16[512,4096]{1,0:T(8,128)(2,1)}, f32[1,512]{1,0:T(1,128)}) custom-call(bf16[4096,512]{1,0:T(8,128)(2,1)} %tokens.3, bf16[4096,512]{1,0:T(8,128)(2,1)} %cotangent.3, bf16[512,512]{1,0:T(8,128)(2,1)} %w_value.3, ...), custom_call_target="tpu_custom_call" | custom-call | flops 5400000000 | bytes 26214400 | tf_op jit(solution)/shard_map/pallas_call | solution.py:417
  29.0 79.9 %all-to-all-done.1 = bf16[16,16,32,256]{3,2,1,0:T(8,128)(2,1)} async-done(((bf16[16,16,32,256]{3,2,1,0:T(8,128)(2,1)}), bf16[16,16,32,256]{3,2,1,0:T(8,128)(2,1)}, u32[]{:S(2)}, u32[]{:S(2)}) %all-to-all-start.1) | async-done | bytes 4194336 | tf_op jit(solution)/shard_map/all_to_all | solution.py:389
  108.9 7.6 %all-to-all-start = ((bf16[16,16,32,256]{3,2,1,0:T(8,128)(2,1)}), bf16[16,16,32,256]{3,2,1,0:T(8,128)(2,1)}, u32[]{:S(2)}, u32[]{:S(2)}) async-start(bf16[16,16,32,256]{3,2,1,0:T(8,128)(2,1)} %get-tuple-element.17), calls=%async_computation | async-start | bytes 8388608 | tf_op jit(solution)/shard_map/all_to_all | solution.py:389
  119.1 20.1 %shard_map.167 = (bf16[256,32,256]{2,1,0:T(8,128)(2,1)}, f32[32,256,256]{2,1,0:T(8,128)}) custom-call(bf16[256,32,256]{2,1,0:T(8,128)(2,1)} %bitcast.1.arrived, bf16[32,256,256]{2,1,0:T(8,128)(2,1)} %kernel.3, bf16[256,256]{1,0:T(8,128)(2,1)} %fusion.second, bf16[256,256]{1,0:T(8,128)(2,1)} %convolution_convert_fusion.2.third, bf16[256,256]{1,0:T(8,128)(2,1)} %fusion.4.swap), custom_call_target="tpu_custom_call" | custom-call | flops 4300000256 | bytes 20971520 | tf_op jit(solution)/shard_map/pallas_call | solution.py:436
  139.2 75.6 %all-to-all-done = bf16[16,16,32,256]{3,2,1,0:T(8,128)(2,1)} async-done(((bf16[16,16,32,256]{3,2,1,0:T(8,128)(2,1)}), bf16[16,16,32,256]{3,2,1,0:T(8,128)(2,1)}, u32[]{:S(2)}, u32[]{:S(2)}) %all-to-all-start) | async-done | bytes 4194336 | tf_op jit(solution)/shard_map/all_to_all | solution.py:389
  214.8 4.7 all-to-all-start.3
  221.3 20.6 %shard_map.168 = (bf16[256,32,256]{2,1,0:T(8,128)(2,1)}, bf16[32,256,256]{2,1,0:T(8,128)(2,1)}) custom-call(bf16[256,32,256]{2,1,0:T(8,128)(2,1)} %bitcast.arrived, bf16[32,256,256]{2,1,0:T(8,128)(2,1)} %kernel.3, f32[32,256,256]{2,1,0:T(8,128)} %get-tuple-element.18.spectrum, bf16[256,256]{1,0:T(8,128)(2,1)} %convolution_convert_fusion.1.second_t, ...), custom_call_target="tpu_custom_call" | custom-call | flops 4300000256 | bytes 25165824 | tf_op jit(solution)/shard_map/pallas_call | solution.py:454
  242.0 71.9 %all-to-all-done.3.arrived = bf16[16,16,32,256]{3,2,1,0:T(8,128)(2,1)} async-done(((bf16[16,16,32,256]{3,2,1,0:T(8,128)(2,1)}), bf16[16,16,32,256]{3,2,1,0:T(8,128)(2,1)}, u32[]{:S(2)}, u32[]{:S(2)}) %all-to-all-start.3) | async-done | bytes 4194336 | tf_op jit(solution)/shard_map/all_to_all | solution.py:389
  313.8 4.9 %all-to-all-start.2 = ((bf16[16,16,32,256]{3,2,1,0:T(8,128)(2,1)}), bf16[16,16,32,256]{3,2,1,0:T(8,128)(2,1)}, u32[]{:S(2)}, u32[]{:S(2)}) async-start(bf16[16,16,32,256]{3,2,1,0:T(8,128)(2,1)} %bitcast.58), calls=%async_computation.2 | async-start | bytes 8388608 | tf_op jit(solution)/shard_map/all_to_all | solution.py:389
  319.8 13.1 %shard_map.169 = (f32[4096,512]{1,0:T(8,128)}, bf16[512,512]{1,0:T(8,128)(2,1)}) custom-call(bf16[16,16,32,256]{3,2,1,0:T(8,128)(2,1)} %all-to-all-done.3.arrived, bf16[512,4096]{1,0:T(8,128)(2,1)} %get-tuple-element.22.tokens_t, bf16[4096,512]{1,0:T(8,128)(2,1)} %get-tuple-element.23.value, bf16[4096,512]{1,0:T(8,128)(2,1)} %cotangent.3, ...), custom_call_target="tpu_custom_call" | custom-call | flops 5400000000 | bytes 26214400 | tf_op jit(solution)/shard_map/pallas_call | solution.py:473
  337.7 18.9 %collective-permute-done.1 = bf16[2,2,32,640]{3,2,0,1:T(8,128)(2,1)S(1)} collective-permute-done((bf16[2,2,32,640]{3,2,0,1:T(8,128)(2,1)S(1)}, bf16[2,2,32,640]{3,2,0,1:T(8,128)(2,1)S(1)}, u32[]{:S(2)}, u32[]{:S(2)}) %collective-permute-start.1) | collective-permute-done | bytes 163872 | tf_op jit(solution)/shard_map/ppermute | solution.py:316
  356.8 31.8 %collective-permute-done.2 = bf16[2,32,640]{2,1,0:T(8,128)(2,1)S(1)} collective-permute-done((bf16[2,32,640]{2,1,0:T(8,128)(2,1)S(1)}, bf16[2,32,640]{2,1,0:T(8,128)(2,1)S(1)}, u32[]{:S(2)}, u32[]{:S(2)}) %collective-permute-start.2) | collective-permute-done | bytes 81952 | tf_op jit(solution)/shard_map/ppermute | solution.py:316
  388.7 9.7 %collective-permute-start.3 = (bf16[32,640]{1,0:T(8,128)(2,1)S(1)}, bf16[32,640]{1,0:T(8,128)(2,1)S(1)}, u32[]{:S(2)}, u32[]{:S(2)}) collective-permute-start(bf16[32,640]{1,0:T(8,128)(2,1)S(1)} %dynamic-slice_bitcast_fusion.2), channel_id=1, source_target_pairs={{0,8},{1,9},{2,10},{3,11},{4,12},{5,13},{6,14},{7,15},{8,0},{9,1},... | collective-permute-start | bytes 122888 | tf_op jit(solution)/shard_map/ppermute | solution.py:316
  399.1 15.0 %collective-permute-done.3 = bf16[32,640]{1,0:T(8,128)(2,1)S(1)} collective-permute-done((bf16[32,640]{1,0:T(8,128)(2,1)S(1)}, bf16[32,640]{1,0:T(8,128)(2,1)S(1)}, u32[]{:S(2)}, u32[]{:S(2)}) %collective-permute-start.3) | collective-permute-done | bytes 40992 | tf_op jit(solution)/shard_map/ppermute | solution.py:316
  414.7 7.8 %shard_map.171 = bf16[512,512]{1,0:T(8,128)(2,1)} custom-call(bf16[16,16,32,256]{3,2,1,0:T(8,128)(2,1)} %all-to-all-done.2.arrived, bf16[512,4096]{1,0:T(8,128)(2,1)} %get-tuple-element.22.tokens_t, bf16[4096,512]{1,0:T(8,128)(2,1)} %get-tuple-element.20.d_mix, bf16[256,256]{1,0:T(8,128)(2,1)} %bitcast.66, f32[1,512]{1,0:T(1,128)} %bitcast.83, ...), custom_call_target="tpu_custom_call" | custom-call | flops 3300000000 | bytes 13631488 | tf_op jit(solution)/shard_map/pallas_call | solution.py:489
  422.5 6.3 %all-to-all-start.4 = ((bf16[16,32,512]{2,1,0:T(8,128)(2,1)}), bf16[16,32,512]{2,1,0:T(8,128)(2,1)S(1)}, u32[]{:S(2)}, u32[]{:S(2)}) async-start(bf16[16,32,512]{2,1,0:T(8,128)(2,1)} %bitcast.63), calls=%async_computation.4 | async-start | bytes 1048576 | tf_op jit(solution)/shard_map/all_to_all | solution.py:389
  429.8 10.4 %shard_map.170._ = bf16[4096,512]{1,0:T(8,128)(2,1)} custom-call(bf16[16,16,32,256]{3,2,1,0:T(8,128)(2,1)} %all-to-all-done.2.arrived, bf16[4096,512]{1,0:T(8,128)(2,1)} %get-tuple-element.20.d_mix, f32[4096,512]{1,0:T(8,128)} %get-tuple-element.24.partial, bf16[256,256]{1,0:T(8,128)(2,1)} %bitcast.67, f32[1,512]{1,0:T(1,128)} %bitcast.84, ...), custom_call_target="tpu_custom_call" | custom-call | flops 3300000000 | bytes 20971520 | tf_op jit(solution)/shard_map/pallas_call | solution.py:507
  440.2 3.1 all-to-all-done.4.parts
  446.0 2.3 collective-permute-start.4
  448.3 3.6 all-to-all-start.5
  455.5 8.3 %collective-permute-done.5 = bf16[2,32,640]{2,1,0:T(8,128)(2,1)S(1)} collective-permute-done((bf16[2,32,640]{2,1,0:T(8,128)(2,1)S(1)}, bf16[2,32,640]{2,1,0:T(8,128)(2,1)S(1)}, u32[]{:S(2)}, u32[]{:S(2)}) %collective-permute-start.5) | collective-permute-done | bytes 81952 | tf_op jit(solution)/shard_map/ppermute | solution.py:316
  465.6 4.2 collective-permute-done.6
  (70 shorter events, 25.2 us)
Async XLA Ops:
  0.6 116.6 %copy-start = (bf16[256,256]{1,0:T(8,128)(2,1)S(1)}, bf16[256,256]{1,0:T(8,128)(2,1)}, u32[]{:S(2)}) copy-start(bf16[256,256]{1,0:T(8,128)(2,1)} %param.18) | copy-start | bytes 393220
  7.4 101.5 %all-to-all-start.1 = ((bf16[16,16,32,256]{3,2,1,0:T(8,128)(2,1)}), bf16[16,16,32,256]{3,2,1,0:T(8,128)(2,1)}, u32[]{:S(2)}, u32[]{:S(2)}) async-start(bf16[16,16,32,256]{3,2,1,0:T(8,128)(2,1)} %shard_map.166), calls=%async_computation.1 | async-start | bytes 8388608 | tf_op jit(solution)/shard_map/all_to_all | solution.py:389
  108.9 8.4 %copy-start.11 = (s32[256]{0:T(256)S(1)}, s32[256]{0:T(256)}, u32[]{:S(2)}) copy-start(s32[256]{0:T(256)} %constant.82.clone) | copy-start | bytes 3076
  108.9 9.3 %copy-start.5 = (bf16[256,256]{1,0:T(8,128)(2,1)S(1)}, bf16[256,256]{1,0:T(8,128)(2,1)}, u32[]{:S(2)}) copy-start(bf16[256,256]{1,0:T(8,128)(2,1)} %param.19) | copy-start | bytes 393220
  108.9 9.3 %copy-start.10 = (s32[256]{0:T(256)S(1)}, s32[256]{0:T(256)}, u32[]{:S(2)}) copy-start(s32[256]{0:T(256)} %constant.84.clone) | copy-start | bytes 3076
  108.9 105.9 %all-to-all-start = ((bf16[16,16,32,256]{3,2,1,0:T(8,128)(2,1)}), bf16[16,16,32,256]{3,2,1,0:T(8,128)(2,1)}, u32[]{:S(2)}, u32[]{:S(2)}) async-start(bf16[16,16,32,256]{3,2,1,0:T(8,128)(2,1)} %get-tuple-element.17), calls=%async_computation | async-start | bytes 8388608 | tf_op jit(solution)/shard_map/all_to_all | solution.py:389
  214.8 4.7 copy-start.9
  214.8 5.6 %copy-start.8 = (s32[256]{0:T(256)S(1)}, s32[256]{0:T(256)}, u32[]{:S(2)}) copy-start(s32[256]{0:T(256)} %constant.83.clone) | copy-start | bytes 3076
  214.8 99.1 %all-to-all-start.3 = ((bf16[16,16,32,256]{3,2,1,0:T(8,128)(2,1)}), bf16[16,16,32,256]{3,2,1,0:T(8,128)(2,1)}, u32[]{:S(2)}, u32[]{:S(2)}) async-start(bf16[16,16,32,256]{3,2,1,0:T(8,128)(2,1)} %bitcast.59), calls=%async_computation.3 | async-start | bytes 8388608 | tf_op jit(solution)/shard_map/all_to_all | solution.py:389
  313.8 4.9 %copy-start.3 = (bf16[512,512]{1,0:T(8,128)(2,1)S(1)}, bf16[512,512]{1,0:T(8,128)(2,1)}, u32[]{:S(2)}) copy-start(bf16[512,512]{1,0:T(8,128)(2,1)} %w_gate.1) | copy-start | bytes 1572868
  313.8 5.9 %copy-start.7 = (f32[1,512]{1,0:T(1,128)S(1)}, f32[1,512]{1,0:T(1,128)}, u32[]{:S(2)}) copy-start(f32[1,512]{1,0:T(1,128)} %get-tuple-element.27) | copy-start | bytes 6148
  313.8 100.9 %all-to-all-start.2 = ((bf16[16,16,32,256]{3,2,1,0:T(8,128)(2,1)}), bf16[16,16,32,256]{3,2,1,0:T(8,128)(2,1)}, u32[]{:S(2)}, u32[]{:S(2)}) async-start(bf16[16,16,32,256]{3,2,1,0:T(8,128)(2,1)} %bitcast.58), calls=%async_computation.2 | async-start | bytes 8388608 | tf_op jit(solution)/shard_map/all_to_all | solution.py:389
  332.9 65.5 %copy-start.6 = (bf16[256,256]{1,0:T(8,128)(2,1)S(1)}, bf16[256,256]{1,0:T(8,128)(2,1)}, u32[]{:S(2)}) copy-start(bf16[256,256]{1,0:T(8,128)(2,1)} %first.1) | copy-start | bytes 393220
  334.3 1.7 collective-permute-start
  336.1 20.5 %collective-permute-start.1 = (bf16[2,2,32,640]{3,2,0,1:T(8,128)(2,1)S(1)}, bf16[2,2,32,640]{3,2,0,1:T(8,128)(2,1)S(1)}, u32[]{:S(2)}, u32[]{:S(2)}) collective-permute-start(bf16[2,2,32,640]{3,2,0,1:T(8,128)(2,1)S(1)} %dynamic-slice_bitcast_fusion), channel_id=1, source_target_pairs={{0,2},{1,3},{2,0},{3,1},{4,6},{5,7},{6,4},{7,5},{8,10},{9,11},{10,... | collective-permute-start | bytes 491528 | tf_op jit(solution)/shard_map/ppermute | solution.py:316
  356.7 31.9 %collective-permute-start.2 = (bf16[2,32,640]{2,1,0:T(8,128)(2,1)S(1)}, bf16[2,32,640]{2,1,0:T(8,128)(2,1)S(1)}, u32[]{:S(2)}, u32[]{:S(2)}) collective-permute-start(bf16[2,32,640]{2,1,0:T(8,128)(2,1)S(1)} %dynamic-slice_bitcast_fusion.1), channel_id=1, source_target_pairs={{0,4},{1,5},{2,6},{3,7},{4,0},{5,1},{6,2},{7,3},{8,12},{9,13},{10,... | collective-permute-start | bytes 245768 | tf_op jit(solution)/shard_map/ppermute | solution.py:316
  388.7 25.4 %collective-permute-start.3 = (bf16[32,640]{1,0:T(8,128)(2,1)S(1)}, bf16[32,640]{1,0:T(8,128)(2,1)S(1)}, u32[]{:S(2)}, u32[]{:S(2)}) collective-permute-start(bf16[32,640]{1,0:T(8,128)(2,1)S(1)} %dynamic-slice_bitcast_fusion.2), channel_id=1, source_target_pairs={{0,8},{1,9},{2,10},{3,11},{4,12},{5,13},{6,14},{7,15},{8,0},{9,1},... | collective-permute-start | bytes 122888 | tf_op jit(solution)/shard_map/ppermute | solution.py:316
  414.7 14.1 %copy-start.4 = (bf16[512,512]{1,0:T(8,128)(2,1)S(1)}, bf16[512,512]{1,0:T(8,128)(2,1)}, u32[]{:S(2)}) copy-start(bf16[512,512]{1,0:T(8,128)(2,1)} %w_value.3) | copy-start | bytes 1572868
  422.5 20.7 %all-to-all-start.4 = ((bf16[16,32,512]{2,1,0:T(8,128)(2,1)}), bf16[16,32,512]{2,1,0:T(8,128)(2,1)S(1)}, u32[]{:S(2)}, u32[]{:S(2)}) async-start(bf16[16,32,512]{2,1,0:T(8,128)(2,1)} %bitcast.63), calls=%async_computation.4 | async-start | bytes 1048576 | tf_op jit(solution)/shard_map/all_to_all | solution.py:389
  446.0 6.0 %collective-permute-start.4 = (bf16[32,640]{1,0:T(8,128)(2,1)}, bf16[32,640]{1,0:T(8,128)(2,1)S(1)}, u32[]{:S(2)}, u32[]{:S(2)}) collective-permute-start(bf16[32,640]{1,0:T(8,128)(2,1)} %get-tuple-element.29), channel_id=1, source_target_pairs={{0,8},{1,9},{2,10},{3,11},{4,12},{5,13},{6,14},{7,15},{8,0},{9,1},... | collective-permute-start | bytes 122888 | tf_op jit(solution)/shard_map/ppermute | solution.py:316
  448.3 24.3 %all-to-all-start.5 = ((bf16[16,32,512]{2,1,0:T(8,128)(2,1)}), bf16[16,32,512]{2,1,0:T(8,128)(2,1)S(1)}, u32[]{:S(2)}, u32[]{:S(2)}) async-start(bf16[16,32,512]{2,1,0:T(8,128)(2,1)} %get-tuple-element.28), calls=%async_computation.5 | async-start | bytes 1048576 | tf_op jit(solution)/shard_map/all_to_all | solution.py:389
  452.9 10.9 %collective-permute-start.5 = (bf16[2,32,640]{2,1,0:T(8,128)(2,1)S(1)}, bf16[2,32,640]{2,1,0:T(8,128)(2,1)S(1)}, u32[]{:S(2)}, u32[]{:S(2)}) collective-permute-start(bf16[2,32,640]{2,1,0:T(8,128)(2,1)S(1)} %maximum_select_fusion.6), channel_id=1, source_target_pairs={{0,4},{1,5},{2,6},{3,7},{4,0},{5,1},{6,2},{7,3},{8,12},{9,13},{10,... | collective-permute-start | bytes 245768 | tf_op jit(solution)/shard_map/ppermute | solution.py:316
  463.8 6.0 %collective-permute-start.6 = (bf16[2,2,32,640]{3,2,0,1:T(8,128)(2,1)S(1)}, bf16[2,2,32,640]{3,2,0,1:T(8,128)(2,1)S(1)}, u32[]{:S(2)}, u32[]{:S(2)}) collective-permute-start(bf16[2,2,32,640]{3,2,0,1:T(8,128)(2,1)S(1)} %maximum_select_fusion.4), channel_id=1, source_target_pairs={{0,2},{1,3},{2,0},{3,1},{4,6},{5,7},{6,4},{7,5},{8,10},{9,11},{10,... | collective-permute-start | bytes 491528 | tf_op jit(solution)/shard_map/ppermute | solution.py:316
  469.9 1.7 collective-permute-start.7
  (2 other events, 5.0 us)

commit v8 on v6

--- a/solution.py
+++ b/solution.py
@@ -209,7 +209,7 @@
         conv = dot_nt(fourth[...], arrived[:, r].reshape(D, N2))
         mixed = conv + skip[...] * value[here].astype(f32)
         d_gate[here] = (cotangent[here].astype(f32) * mixed).astype(bf16)
-        partial[here] = dot_nn(d_gate[here], w_gate_t[...])
+        partial[here] = dot_nn(d_gate[here], w_gate_t[...]).astype(bf16)
     accumulate(total, dot_nn(tokens_t[...], d_gate[...]))
     finish(total, factor, grad_w)
 
@@ -269,49 +269,54 @@
             grad_w[...] = ((total[...] + term) * factor[0, 0]).astype(bf16)
 
 
-def tokens_kernel(arrived, d_mix, partial, first_t, skip, w_value_t, grad_tokens):
+def tokens_kernel(arrived, d_mix, partial, first_t, skip, w_value_t, *rest):
+    grad_tokens, zero = rest[-2:]
     for r in range(arrived.shape[1]):
         here = row_slice(r)
         d_cube = dot_nt(first_t[...], arrived[:, r].reshape(D, N2))
         d_value = (d_cube + skip[...] * d_mix[here].astype(f32)).astype(bf16)
-        grad_tokens[here] = (partial[here] + dot_nn(d_value, w_value_t[...])).astype(bf16)
-
-
-def sum_kernel(parts, early, _, out, early_out):
-    total = jnp.sum(parts[...].astype(f32), axis=0, keepdims=True).astype(bf16)
-    out[...] = jnp.broadcast_to(total, out.shape)
-    early_out[...] = early[...]
+        grad_tokens[here] = (
+            partial[here].astype(f32) + dot_nn(d_value, w_value_t[...])
+        ).astype(bf16)
+    zero[...] = jnp.zeros_like(zero)
+
+
+def place_kernel(values, offsets, me, *refs):
+    value_parts, gate_parts = refs[:values], refs[values : 2 * values]
+    out, skip_out, column = refs[2 * values :]
+    here = me[0, 0]
+    for distance, part in enumerate(value_parts):
+        size = part.shape[0]
+        start = pl.multiple_of((here % values ^ distance) * size, size)
+        out[0, pl.ds(start, size)] = part[...].astype(f32)
+    for distance, part in enumerate(gate_parts):
+        size = part.shape[0] // len(offsets)
+        for i, offset in enumerate(offsets):
+            start = pl.multiple_of((here ^ (distance | offset)) * size, size)
+            block = part[i * size : (i + 1) * size].astype(f32)
+            out[1, pl.ds(start, size)] = block[:, :D]
+            column[pl.ds(start, size)] = block[:, D:]
+    skip_out[...] = column[...].T[:1]
 
 
 def from_partner(array, b, n):
     return lax.ppermute(array, "seq", [(i, i ^ (1 << b)) for i in range(n)])
 
 
-def halve_over_seq(term, n):
-    me = lax.axis_index("seq")
-    bits = n.bit_length() - 1
-    part = term.reshape((2,) * bits + (term.shape[0] // n, term.shape[1]))
-    for b in range(bits):
-        axis = bits - 1 - b
-        bit = (me >> b) & 1
-        kept = lax.dynamic_index_in_dim(part, bit, axis, keepdims=False)
-        sent = lax.dynamic_index_in_dim(part, 1 - bit, axis, keepdims=False)
-        part = (kept.astype(f32) + from_partner(sent, b, n).astype(f32)).astype(bf16)
-    return part
-
-
-def double_over_seq(part, n):
-    me = lax.axis_index("seq")
-    bits = n.bit_length() - 1
-    lanes = part.shape[-1]
-    for b in reversed(range(bits)):
-        axis = bits - 1 - b
-        bit = (me >> b) & 1
-        other = from_partner(part, b, n)
-        part = jnp.where(
-            bit == 0, jnp.stack([part, other], axis), jnp.stack([other, part], axis)
-        )
-    return part.reshape(-1, lanes)
+def halves(part, axis, b):
+    bit = (lax.axis_index("seq") >> b) & 1
+    kept = lax.dynamic_index_in_dim(part, bit, axis, keepdims=False)
+    sent = lax.dynamic_index_in_dim(part, 1 - bit, axis, keepdims=False)
+    return kept, sent
+
+
+def added(kept, got, zero=0.0):
+    return (kept.astype(f32) + got.astype(f32) + zero).astype(bf16)
+
+
+def doubled(part, n):
+    other = from_partner(part, 1, n)
+    return [part, from_partner(part, 0, n), other, from_partner(other, 0, n)]
 
 
 def on_device(
@@ -432,14 +437,20 @@
         grid=(rows // per,),
         in_specs=[sent, column, row, row, block, square, line, one],
         out_specs=[row, square],
-        out_shape=[shape((local_rows, D), f32), shape((D, D))],
+        out_shape=[shape((local_rows, D)), shape((D, D))],
         scratch_shapes=[pltpu.VMEM((D, D), f32), pltpu.VMEM((per * N2, D), bf16)],
         compiler_params=params(),
         cost_estimate=cost(5.4, 25),
     )(three_here, tokens_t, value, cotangent, fourth_block, w_gate.T, skip, factor)
 
     skip_lanes = jnp.broadcast_to((skip_term * factor[0, 0]).astype(bf16).T, (D, LANES))
-    early = halve_over_seq(jnp.concatenate([gate_term, skip_lanes], axis=1), n)
+    gate_term = jnp.concatenate([gate_term, skip_lanes], axis=1)
+    bits = n.bit_length() - 1
+    gate_part = gate_term.reshape((2,) * bits + (D // n, D + LANES))
+    for b in range(bits):
+        early = gate_part
+        kept, sent_half = halves(gate_part, bits - 1 - b, b)
+        gate_part = added(kept, from_partner(sent_half, b, n))
 
     first_t = first_block.T
     in_vmem = pl.BlockSpec(memory_space=pltpu.VMEM)
@@ -460,33 +471,67 @@
         cost_estimate=cost(3.3, 13),
     )(one_here, tokens_t, d_mix, first_t, skip, factor, early)
 
-    parts = transfer(value_term.reshape(n, D // n, D))
-    grad_tokens = pl.pallas_call(
-        tokens_kernel,
-        grid=(rows // per,),
-        in_specs=[sent, row, row, block, line, square],
-        out_specs=row,
-        out_shape=shape((local_rows, D)),
-        compiler_params=params(),
-        cost_estimate=cost(3.3, 20),
-    )(one_here, d_mix, partial, first_t, skip, w_value.T)
-    own, early = pl.pallas_call(
-        sum_kernel,
-        in_specs=[in_vmem, in_vmem, unread],
+    offsets = [0]
+    for b in reversed(range(2, bits)):
+        gate_part = jnp.concatenate([gate_part, from_partner(gate_part, b, n)])
+        offsets += [offset | (1 << b) for offset in offsets]
+    gate_parts = doubled(gate_part, n)
+
+    quarters = 4
+    pair = rows // quarters // 2 if rows > quarters else 1
+    steps = rows // quarters // pair
+    w_value_t = w_value.T
+
+    def quarter(i, grad_tokens, after):
+        turn = lambda g: g + i * steps
+        lines = pl.BlockSpec((pair * N2, D), lambda g: (turn(g), 0))
+        held = [] if grad_tokens is None else [grad_tokens]
+        return pl.pallas_call(
+            tokens_kernel,
+            grid=(steps,),
+            in_specs=[
+                pl.BlockSpec((n, pair, chans, N2), lambda g: (0, turn(g), 0, 0)),
+                lines,
+                lines,
+                block,
+                line,
+                square,
+                unread,
+            ]
+            + [unread] * len(held),
+            out_specs=[lines, whole((1, LANES))],
+            out_shape=[shape((local_rows, D)), shape((1, LANES), f32)],
+            input_output_aliases={7: 0} if held else {},
+            compiler_params=params(),
+            cost_estimate=cost(0.8, 4),
+        )(one_here, d_mix, partial, first_t, skip, w_value_t, after, *held)
+
+    value_part = value_term.reshape(2, 2, D // 4, D)
+    grad_tokens = None
+    for i, b in enumerate(range(bits)):
+        if b < 2:
+            kept, sent_half = halves(value_part, 1 - b, b)
+        else:
+            kept, sent_half = value_part, value_part
+        got = from_partner(sent_half, b, n)
+        zero = 0.0
+        if i < quarters:
+            grad_tokens, zeros = quarter(i, grad_tokens, value_part)
+            zero = zeros[0, 0]
+        value_part = added(kept, got, zero)
+    value_parts = doubled(value_part, n)
+
+    vmem_specs = [in_vmem] * 8
+    grad_weights, skip_total = pl.pallas_call(
+        functools.partial(place_kernel, 4, offsets),
+        in_specs=[one] + vmem_specs,
         out_specs=[in_vmem, in_vmem],
-        out_shape=[shape(parts.shape), shape(early.shape)],
-        compiler_params=params(),
-        cost_estimate=cost(0.001, 1),
-    )(parts, early, grad_tokens)
-    value_total = transfer(own).reshape(D, D)
-    early = double_over_seq(early, n)
-    gate_total, skip_total = early[:, :D], early[:, D]
-    return (
-        grad_tokens,
-        grad_kernel,
-        jnp.stack([value_total, gate_total]).astype(f32),
-        skip_total.astype(f32),
-    )
+        out_shape=[shape((2, D, D), f32), shape((1, D), f32)],
+        scratch_shapes=[pltpu.VMEM((D, LANES), f32)],
+        compiler_params=params(),
+        cost_estimate=cost(0.001, 3),
+    )(lax.axis_index("seq").reshape(1, 1), *value_parts, *gate_parts)
+    return grad_tokens, grad_kernel, grad_weights, skip_total.reshape(D)
 
 
 def solution(mesh):

time: 461 us -> 453 us (0.983)
  waiting for transfers between devices: 265 us -> 241 us
  starting transfers between devices: 86.1 us -> 94.4 us
  Pallas kernels: 94.8 us -> 100 us
    ppermute x8 -> x16, waiting for transfers between devices: 86.3 us -> 58.8 us  [from_partner(): return lax.ppermute(array, 'seq', [(i, i ^ 1 << b) for i in range(n)])]
    ppermute x8 -> x16, starting transfers between devices: 12 us -> 27.6 us  [from_partner(): return lax.ppermute(array, 'seq', [(i, i ^ 1 << b) for i in range(n)])]
    all_to_all x6 -> x4, starting transfers between devices: 74 us -> 66.8 us  [transfer(): return lax.all_to_all(array, 'seq', split_axis=0, concat_axis=0, tiled=True)]
    pallas_call x2 -> x5, Pallas kernels: 12.3 us -> 18.5 us  [the longest x4 15.7 us: quarter(): pl.pallas_call(tokens_kernel, grid=(steps,), in_specs=[pl.BlockSpec((n, p...]
    all_to_all x6 -> x4, waiting for transfers between devices: 179 us -> 183 us  [transfer(): return lax.all_to_all(array, 'seq', split_axis=0, concat_axis=0, tiled=True)]
  transfers between devices with their start and end apart: 14 -> 20, of which waited for: 12 -> 11; matrix products, arithmetic and copies ran while one was open for 2% -> 3% of each run, Pallas kernels for 17% -> 18%
where the time goes in v8:
time: 453 us; the launch traced here: 452 us
  waiting for transfers between devices  241 us (53%)
  Pallas kernels  100 us (22%)
  starting transfers between devices  94.4 us (21%)
  other arithmetic  8.24 us (2%)
  local copies, waits for them, and re-layouts  6.72 us (1%)
    all_to_all x4, waiting for transfers between devices, transfer(): return lax.all_to_all(array, 'seq', split_axis=0, concat_axis=0, tiled=True)  183 us
    all_to_all x4, starting transfers between devices, transfer(): return lax.all_to_all(array, 'seq', split_axis=0, concat_axis=0, tiled=True)  66.8 us
    ppermute x16, waiting for transfers between devices, from_partner(): return lax.ppermute(array, 'seq', [(i, i ^ 1 << b) for i in range(n)])  58.8 us
    ppermute x16, starting transfers between devices, from_partner(): return lax.ppermute(array, 'seq', [(i, i ^ 1 << b) for i in range(n)])  27.6 us
    pallas_call x1, Pallas kernels, on_device(): pl.pallas_call(home_backward_kernel, grid=(chans // GROUP,), in_specs=[at...  20.6 us
    pallas_call x1, Pallas kernels, on_device(): pl.pallas_call(home_forward_kernel, grid=(chans // GROUP,), in_specs=[at_...  20.1 us
    pallas_call x4, Pallas kernels, quarter(): pl.pallas_call(tokens_kernel, grid=(steps,), in_specs=[pl.BlockSpec((n, p...  15.7 us
    pallas_call x1, Pallas kernels, on_device(): pl.pallas_call(d_three_kernel, grid=(rows // per,), in_specs=[row, row, s...  14 us
  transfers between devices with their start and end apart: 20, of which 11 were waited for; matrix products, arithmetic and copies ran while one was open for 3% of the time, Pallas kernels for 18%

profile of v8, /device:TPU:0, one launch (start us, length us, event | category | flops | bytes accessed | tf_op | source)
XLA Modules:
  0.0 451.9 jit_solution(310616157360406735)
XLA Ops:
  0.6 6.7 %shard_map.130 = bf16[16,16,32,256]{3,2,1,0:T(8,128)(2,1)} custom-call(bf16[4096,512]{1,0:T(8,128)(2,1)} %tokens.3, bf16[512,512]{1,0:T(8,128)(2,1)} %w_value.3, bf16[256,256]{1,0:T(8,128)(2,1)} %first.1), custom_call_target="tpu_custom_call" | custom-call | flops 3200000000 | bytes 9437184 | tf_op jit(solution)/shard_map/pallas_call | solution.py:367
  7.4 7.5 %all-to-all-start.1 = ((bf16[16,16,32,256]{3,2,1,0:T(8,128)(2,1)}), bf16[16,16,32,256]{3,2,1,0:T(8,128)(2,1)}, u32[]{:S(2)}, u32[]{:S(2)}) async-start(bf16[16,16,32,256]{3,2,1,0:T(8,128)(2,1)} %shard_map.130), calls=%async_computation.1 | async-start | bytes 8388608 | tf_op jit(solution)/shard_map/all_to_all | solution.py:364
  14.8 14.0 %shard_map.129 = (bf16[16,16,32,256]{3,2,1,0:T(8,128)(2,1)}, bf16[4096,512]{1,0:T(8,128)(2,1)}, bf16[4096,512]{1,0:T(8,128)(2,1)}, bf16[512,4096]{1,0:T(8,128)(2,1)}, f32[1,512]{1,0:T(1,128)}) custom-call(bf16[4096,512]{1,0:T(8,128)(2,1)} %tokens.3, bf16[4096,512]{1,0:T(8,128)(2,1)} %cotangent.3, bf16[512,512]{1,0:T(8,128)(2,1)} %w_value.3, ...), custom_call_target="tpu_custom_call" | custom-call | flops 5400000000 | bytes 26214400 | tf_op jit(solution)/shard_map/pallas_call | solution.py:385
  28.9 63.6 %all-to-all-done.1 = bf16[16,16,32,256]{3,2,1,0:T(8,128)(2,1)} async-done(((bf16[16,16,32,256]{3,2,1,0:T(8,128)(2,1)}), bf16[16,16,32,256]{3,2,1,0:T(8,128)(2,1)}, u32[]{:S(2)}, u32[]{:S(2)}) %all-to-all-start.1) | async-done | bytes 4194336 | tf_op jit(solution)/shard_map/all_to_all | solution.py:364
  92.5 19.7 %all-to-all-start = ((bf16[16,16,32,256]{3,2,1,0:T(8,128)(2,1)}), bf16[16,16,32,256]{3,2,1,0:T(8,128)(2,1)}, u32[]{:S(2)}, u32[]{:S(2)}) async-start(bf16[16,16,32,256]{3,2,1,0:T(8,128)(2,1)} %get-tuple-element.25), calls=%async_computation | async-start | bytes 8388608 | tf_op jit(solution)/shard_map/all_to_all | solution.py:364
  113.0 20.1 %shard_map.131 = (bf16[256,32,256]{2,1,0:T(8,128)(2,1)}, f32[32,256,256]{2,1,0:T(8,128)}) custom-call(bf16[256,32,256]{2,1,0:T(8,128)(2,1)} %bitcast.1.arrived, bf16[32,256,256]{2,1,0:T(8,128)(2,1)} %kernel.3, bf16[256,256]{1,0:T(8,128)(2,1)} %second.1, bf16[256,256]{1,0:T(8,128)(2,1)} %third.1, bf16[256,256]{1,0:T(8,128)(2,1)} %fusion.6.swap), custom_call_target="tpu_custom_call" | custom-call | flops 4300000256 | bytes 20971520 | tf_op jit(solution)/shard_map/pallas_call | solution.py:404
  133.1 56.8 %all-to-all-done = bf16[16,16,32,256]{3,2,1,0:T(8,128)(2,1)} async-done(((bf16[16,16,32,256]{3,2,1,0:T(8,128)(2,1)}), bf16[16,16,32,256]{3,2,1,0:T(8,128)(2,1)}, u32[]{:S(2)}, u32[]{:S(2)}) %all-to-all-start) | async-done | bytes 4194336 | tf_op jit(solution)/shard_map/all_to_all | solution.py:364
  189.9 19.8 %all-to-all-start.3 = ((bf16[16,16,32,256]{3,2,1,0:T(8,128)(2,1)}), bf16[16,16,32,256]{3,2,1,0:T(8,128)(2,1)}, u32[]{:S(2)}, u32[]{:S(2)}) async-start(bf16[16,16,32,256]{3,2,1,0:T(8,128)(2,1)} %bitcast.70), calls=%async_computation.3 | async-start | bytes 8388608 | tf_op jit(solution)/shard_map/all_to_all | solution.py:364
  211.3 20.6 %shard_map.132 = (bf16[256,32,256]{2,1,0:T(8,128)(2,1)}, bf16[32,256,256]{2,1,0:T(8,128)(2,1)}) custom-call(bf16[256,32,256]{2,1,0:T(8,128)(2,1)} %bitcast.arrived, bf16[32,256,256]{2,1,0:T(8,128)(2,1)} %kernel.3, f32[32,256,256]{2,1,0:T(8,128)} %get-tuple-element.26.spectrum, bf16[256,256]{1,0:T(8,128)(2,1)} %bitcast.72, bf16[256,256]{1,0:T(8,128)(2,1)} %bitcast.73, ...), custom_call_target="tpu_custom_call" | custom-call | flops 4300000256 | bytes 25165824 | tf_op jit(solution)/shard_map/pallas_call | solution.py:416
  231.9 55.5 %all-to-all-done.3.arrived = bf16[16,16,32,256]{3,2,1,0:T(8,128)(2,1)} async-done(((bf16[16,16,32,256]{3,2,1,0:T(8,128)(2,1)}), bf16[16,16,32,256]{3,2,1,0:T(8,128)(2,1)}, u32[]{:S(2)}, u32[]{:S(2)}) %all-to-all-start.3) | async-done | bytes 4194336 | tf_op jit(solution)/shard_map/all_to_all | solution.py:364
  287.4 19.8 %all-to-all-start.2 = ((bf16[16,16,32,256]{3,2,1,0:T(8,128)(2,1)}), bf16[16,16,32,256]{3,2,1,0:T(8,128)(2,1)}, u32[]{:S(2)}, u32[]{:S(2)}) async-start(bf16[16,16,32,256]{3,2,1,0:T(8,128)(2,1)} %bitcast.69), calls=%async_computation.2 | async-start | bytes 8388608 | tf_op jit(solution)/shard_map/all_to_all | solution.py:364
  308.3 12.3 %shard_map.133 = (bf16[4096,512]{1,0:T(8,128)(2,1)}, bf16[512,512]{1,0:T(8,128)(2,1)}) custom-call(bf16[16,16,32,256]{3,2,1,0:T(8,128)(2,1)} %all-to-all-done.3.arrived, bf16[512,4096]{1,0:T(8,128)(2,1)} %get-tuple-element.30.tokens_t, bf16[4096,512]{1,0:T(8,128)(2,1)} %get-tuple-element.31.value, bf16[4096,512]{1,0:T(8,128)(2,1)} %cotangent.3, ...), custom_call_target="tpu_custom_call" | custom-call | flops 5400000000 | bytes 26214400 | tf_op jit(solution)/shard_map/pallas_call | solution.py:435
  323.8 1.9 collective-permute-start.1
  325.7 11.6 %collective-permute-done.1 = bf16[2,2,32,640]{3,2,0,1:T(8,128)(2,1)S(1)} collective-permute-done((bf16[2,2,32,640]{3,2,0,1:T(8,128)(2,1)S(1)}, bf16[2,2,32,640]{3,2,0,1:T(8,128)(2,1)S(1)}, u32[]{:S(2)}, u32[]{:S(2)}) %collective-permute-start.1) | collective-permute-done | bytes 163872 | tf_op jit(solution)/shard_map/ppermute | solution.py:303
  338.2 39.3 %collective-permute-done.2 = bf16[2,32,640]{2,1,0:T(8,128)(2,1)S(1)} collective-permute-done((bf16[2,32,640]{2,1,0:T(8,128)(2,1)S(1)}, bf16[2,32,640]{2,1,0:T(8,128)(2,1)S(1)}, u32[]{:S(2)}, u32[]{:S(2)}) %collective-permute-start.2) | collective-permute-done | bytes 81952 | tf_op jit(solution)/shard_map/ppermute | solution.py:303
  378.3 6.7 %all-to-all-done.2.arrived = bf16[16,16,32,256]{3,2,1,0:T(8,128)(2,1)} async-done(((bf16[16,16,32,256]{3,2,1,0:T(8,128)(2,1)}), bf16[16,16,32,256]{3,2,1,0:T(8,128)(2,1)}, u32[]{:S(2)}, u32[]{:S(2)}) %all-to-all-start.2) | async-done | bytes 4194336 | tf_op jit(solution)/shard_map/all_to_all | solution.py:364
  385.0 7.8 %shard_map.134 = bf16[512,512]{1,0:T(8,128)(2,1)} custom-call(bf16[16,16,32,256]{3,2,1,0:T(8,128)(2,1)} %all-to-all-done.2.arrived, bf16[512,4096]{1,0:T(8,128)(2,1)} %get-tuple-element.30.tokens_t, bf16[4096,512]{1,0:T(8,128)(2,1)} %get-tuple-element.28.d_mix, bf16[256,256]{1,0:T(8,128)(2,1)} %bitcast.61, f32[1,512]{1,0:T(1,128)} %bitcast.77, ...), custom_call_target="tpu_custom_call" | custom-call | flops 3300000000 | bytes 13631488 | tf_op jit(solution)/shard_map/pallas_call | solution.py:457
  395.6 17.0 %collective-permute-start.10 = (bf16[32,640]{1,0:T(8,128)(2,1)S(1)}, bf16[32,640]{1,0:T(8,128)(2,1)S(1)}, u32[]{:S(2)}, u32[]{:S(2)}) collective-permute-start(bf16[32,640]{1,0:T(8,128)(2,1)S(1)} %dynamic-slice_bitcast_fusion.4), channel_id=1, source_target_pairs={{0,8},{1,9},{2,10},{3,11},{4,12},{5,13},{6,14},{7,15},{8,0},{9,1},... | collective-permute-start | bytes 122888 | tf_op jit(solution)/shard_map/ppermute | solution.py:303
  412.6 4.0 shard_map.135
  418.0 3.9 shard_map.136
  426.8 3.9 shard_map.137
  435.9 3.9 shard_map.138
  443.6 3.5 collective-permute-done.8.refs_2_
  449.1 2.8 shard_map.139
  (92 shorter events, 28.0 us)
Async XLA Ops:
  7.4 85.1 %all-to-all-start.1 = ((bf16[16,16,32,256]{3,2,1,0:T(8,128)(2,1)}), bf16[16,16,32,256]{3,2,1,0:T(8,128)(2,1)}, u32[]{:S(2)}, u32[]{:S(2)}) async-start(bf16[16,16,32,256]{3,2,1,0:T(8,128)(2,1)} %shard_map.130), calls=%async_computation.1 | async-start | bytes 8388608 | tf_op jit(solution)/shard_map/all_to_all | solution.py:364
  92.5 97.4 %all-to-all-start = ((bf16[16,16,32,256]{3,2,1,0:T(8,128)(2,1)}), bf16[16,16,32,256]{3,2,1,0:T(8,128)(2,1)}, u32[]{:S(2)}, u32[]{:S(2)}) async-start(bf16[16,16,32,256]{3,2,1,0:T(8,128)(2,1)} %get-tuple-element.25), calls=%async_computation | async-start | bytes 8388608 | tf_op jit(solution)/shard_map/all_to_all | solution.py:364
  189.9 19.8 %copy-start.15 = (bf16[256,256]{1,0:T(8,128)(2,1)S(1)}, bf16[256,256]{1,0:T(8,128)(2,1)}, u32[]{:S(2)}) copy-start(bf16[256,256]{1,0:T(8,128)(2,1)} %second.1) | copy-start | bytes 393220
  189.9 20.6 %copy-start.16 = (bf16[256,256]{1,0:T(8,128)(2,1)S(1)}, bf16[256,256]{1,0:T(8,128)(2,1)}, u32[]{:S(2)}) copy-start(bf16[256,256]{1,0:T(8,128)(2,1)} %third.1) | copy-start | bytes 393220
  189.9 97.5 %all-to-all-start.3 = ((bf16[16,16,32,256]{3,2,1,0:T(8,128)(2,1)}), bf16[16,16,32,256]{3,2,1,0:T(8,128)(2,1)}, u32[]{:S(2)}, u32[]{:S(2)}) async-start(bf16[16,16,32,256]{3,2,1,0:T(8,128)(2,1)} %bitcast.70), calls=%async_computation.3 | async-start | bytes 8388608 | tf_op jit(solution)/shard_map/all_to_all | solution.py:364
  287.4 19.9 %copy-start.7 = (bf16[512,512]{1,0:T(8,128)(2,1)S(1)}, bf16[512,512]{1,0:T(8,128)(2,1)}, u32[]{:S(2)}) copy-start(bf16[512,512]{1,0:T(8,128)(2,1)} %w_gate.1) | copy-start | bytes 1572868
  287.4 20.9 %copy-start.18 = (f32[1,512]{1,0:T(1,128)S(1)}, f32[1,512]{1,0:T(1,128)}, u32[]{:S(2)}) copy-start(f32[1,512]{1,0:T(1,128)} %get-tuple-element.34) | copy-start | bytes 6148
  287.4 97.6 %all-to-all-start.2 = ((bf16[16,16,32,256]{3,2,1,0:T(8,128)(2,1)}), bf16[16,16,32,256]{3,2,1,0:T(8,128)(2,1)}, u32[]{:S(2)}, u32[]{:S(2)}) async-start(bf16[16,16,32,256]{3,2,1,0:T(8,128)(2,1)} %bitcast.69), calls=%async_computation.2 | async-start | bytes 8388608 | tf_op jit(solution)/shard_map/all_to_all | solution.py:364
  322.0 1.7 collective-permute-start
  323.8 13.5 %collective-permute-start.1 = (bf16[2,2,32,640]{3,2,0,1:T(8,128)(2,1)S(1)}, bf16[2,2,32,640]{3,2,0,1:T(8,128)(2,1)S(1)}, u32[]{:S(2)}, u32[]{:S(2)}) collective-permute-start(bf16[2,2,32,640]{3,2,0,1:T(8,128)(2,1)S(1)} %dynamic-slice_bitcast_fusion.1), channel_id=1, source_target_pairs={{0,2},{1,3},{2,0},{3,1},{4,6},{5,7},{6,4},{7,5},{8,10},{9,11},{10,... | collective-permute-start | bytes 491528 | tf_op jit(solution)/shard_map/ppermute | solution.py:303
  337.4 40.2 %collective-permute-start.2 = (bf16[2,32,640]{2,1,0:T(8,128)(2,1)S(1)}, bf16[2,32,640]{2,1,0:T(8,128)(2,1)S(1)}, u32[]{:S(2)}, u32[]{:S(2)}) collective-permute-start(bf16[2,32,640]{2,1,0:T(8,128)(2,1)S(1)} %dynamic-slice_bitcast_fusion.3), channel_id=1, source_target_pairs={{0,4},{1,5},{2,6},{3,7},{4,0},{5,1},{6,2},{7,3},{8,12},{9,13},{10,... | collective-permute-start | bytes 245768 | tf_op jit(solution)/shard_map/ppermute | solution.py:303
  393.7 22.8 %collective-permute-start.3 = (bf16[2,128,512]{2,1,0:T(8,128)(2,1)S(1)}, bf16[2,128,512]{2,1,0:T(8,128)(2,1)S(1)}, u32[]{:S(2)}, u32[]{:S(2)}) collective-permute-start(bf16[2,128,512]{2,1,0:T(8,128)(2,1)S(1)} %dynamic-slice_bitcast_fusion), channel_id=1, source_target_pairs={{0,1},{1,0},{2,3},{3,2},{4,5},{5,4},{6,7},{7,6},{8,9},{9,8},{10,11... | collective-permute-start | bytes 786440 | tf_op jit(solution)/shard_map/ppermute | solution.py:303
  395.6 21.8 %collective-permute-start.10 = (bf16[32,640]{1,0:T(8,128)(2,1)S(1)}, bf16[32,640]{1,0:T(8,128)(2,1)S(1)}, u32[]{:S(2)}, u32[]{:S(2)}) collective-permute-start(bf16[32,640]{1,0:T(8,128)(2,1)S(1)} %dynamic-slice_bitcast_fusion.4), channel_id=1, source_target_pairs={{0,8},{1,9},{2,10},{3,11},{4,12},{5,13},{6,14},{7,15},{8,0},{9,1},... | collective-permute-start | bytes 122888 | tf_op jit(solution)/shard_map/ppermute | solution.py:303
  417.4 5.7 %collective-permute-start.4 = (bf16[128,512]{1,0:T(8,128)(2,1)S(1)}, bf16[128,512]{1,0:T(8,128)(2,1)S(1)}, u32[]{:S(2)}, u32[]{:S(2)}) collective-permute-start(bf16[128,512]{1,0:T(8,128)(2,1)S(1)} %dynamic-slice_bitcast_fusion.2), channel_id=1, source_target_pairs={{0,2},{1,3},{2,0},{3,1},{4,6},{5,7},{6,4},{7,5},{8,10},{9,11},{10,... | collective-permute-start | bytes 393224 | tf_op jit(solution)/shard_map/ppermute | solution.py:303
  417.5 9.0 %collective-permute-start.11 = (bf16[32,640]{1,0:T(8,128)(2,1)S(1)}, bf16[32,640]{1,0:T(8,128)(2,1)S(1)}, u32[]{:S(2)}, u32[]{:S(2)}) collective-permute-start(bf16[32,640]{1,0:T(8,128)(2,1)S(1)} %fusion.8), channel_id=1, source_target_pairs={{0,8},{1,9},{2,10},{3,11},{4,12},{5,13},{6,14},{7,15},{8,0},{9,1},... | collective-permute-start | bytes 122888 | tf_op jit(solution)/shard_map/ppermute | solution.py:303
  424.6 6.1 %collective-permute-start.5 = (bf16[128,512]{1,0:T(8,128)(2,1)S(1)}, bf16[128,512]{1,0:T(8,128)(2,1)S(1)}, u32[]{:S(2)}, u32[]{:S(2)}) collective-permute-start(bf16[128,512]{1,0:T(8,128)(2,1)S(1)} %fusion.5.rest_0_), channel_id=1, source_target_pairs={{0,4},{1,5},{2,6},{3,7},{4,0},{5,1},{6,2},{7,3},{8,12},{9,13},{10,... | collective-permute-start | bytes 393224 | tf_op jit(solution)/shard_map/ppermute | solution.py:303
  426.5 7.4 %collective-permute-start.12 = (bf16[64,640]{1,0:T(8,128)(2,1)S(1)}, bf16[64,640]{1,0:T(8,128)(2,1)S(1)}, u32[]{:S(2)}, u32[]{:S(2)}) collective-permute-start(bf16[64,640]{1,0:T(8,128)(2,1)S(1)} %pad_maximum_fusion.2), channel_id=1, source_target_pairs={{0,4},{1,5},{2,6},{3,7},{4,0},{5,1},{6,2},{7,3},{8,12},{9,13},{10,... | collective-permute-start | bytes 245768 | tf_op jit(solution)/shard_map/ppermute | solution.py:303
  432.3 8.1 %collective-permute-start.6 = (bf16[128,512]{1,0:T(8,128)(2,1)S(1)}, bf16[128,512]{1,0:T(8,128)(2,1)S(1)}, u32[]{:S(2)}, u32[]{:S(2)}) collective-permute-start(bf16[128,512]{1,0:T(8,128)(2,1)S(1)} %add_convert_fusion.1.rest_0_), channel_id=1, source_target_pairs={{0,8},{1,9},{2,10},{3,11},{4,12},{5,13},{6,14},{7,15},{8,0},{9,1},... | collective-permute-start | bytes 393224 | tf_op jit(solution)/shard_map/ppermute | solution.py:303
  433.9 9.1 %collective-permute-start.14 = (bf16[128,640]{1,0:T(8,128)(2,1)S(1)}, bf16[128,640]{1,0:T(8,128)(2,1)S(1)}, u32[]{:S(2)}, u32[]{:S(2)}) collective-permute-start(bf16[128,640]{1,0:T(8,128)(2,1)S(1)} %pad_maximum_fusion.1.refs_4_), channel_id=1, source_target_pairs={{0,2},{1,3},{2,0},{3,1},{4,6},{5,7},{6,4},{7,5},{8,10},{9,11},{10,... | collective-permute-start | bytes 491528 | tf_op jit(solution)/shard_map/ppermute | solution.py:303
  442.1 5.0 %collective-permute-start.8 = (bf16[128,512]{1,0:T(8,128)(2,1)S(1)}, bf16[128,512]{1,0:T(8,128)(2,1)S(1)}, u32[]{:S(2)}, u32[]{:S(2)}) collective-permute-start(bf16[128,512]{1,0:T(8,128)(2,1)S(1)} %add_convert_fusion.refs_0_), channel_id=1, source_target_pairs={{0,2},{1,3},{2,0},{3,1},{4,6},{5,7},{6,4},{7,5},{8,10},{9,11},{10,... | collective-permute-start | bytes 393224 | tf_op jit(solution)/shard_map/ppermute | solution.py:303
  443.0 4.1 collective-permute-start.13
  443.0 4.1 collective-permute-start.15
  443.5 3.6 collective-permute-start.7
  447.1 1.3 collective-permute-start.9
  (15 other events, 74.5 us)

commit v9 on v8

--- a/solution.py
+++ b/solution.py
@@ -100,12 +100,16 @@
     d_mix_out,
     tokens_t_out,
     skip_out,
+    w_value_t,
+    w_gate_t,
 ):
     n, per, chans, _ = out.shape
 
     @pl.when(pl.program_id(0) == 0)
     def _():
         skip_out[...] = jnp.zeros_like(skip_out)
+        w_value_t[...] = w_value[...].T
+        w_gate_t[...] = w_gate[...].T
 
     for r in range(per):
         here = row_slice(r)
@@ -222,14 +226,18 @@
     first_t,
     skip,
     factor,
+    bit,
     _,
-    grad_w,
+    kept,
+    given,
+    d_value_out,
     arrived_v,
     tokens_v,
     d_mix_v,
     d_value,
     total,
     arrive,
+    leave,
 ):
     rows = arrived.shape[1]
     chunks = rows // per
@@ -251,6 +259,7 @@
     for group in started:
         for copy in group:
             copy.start()
+    outs = []
     for i in range(chunks):
         started[i][0].wait()
         started[i][1].wait()
@@ -258,45 +267,75 @@
             here = row_slice(r)
             d_cube = dot_nt(first_t[...], arrived_v[:, r].reshape(D, N2))
             d_value[here] = (d_cube + skip[...] * d_mix_v[here].astype(f32)).astype(bf16)
+        here = pl.ds(i * per * N2, per * N2)
+        outs.append(pltpu.make_async_copy(d_value.at[here], d_value_out.at[here], leave.at[i]))
+        outs[i].start()
         started[i][2].wait()
         here = slice(i * per * N2, (i + 1) * per * N2)
         term = dot_nn(tokens_v[:, here], d_value[here])
         if i == 0:
             total[...] = term
-        elif i < chunks - 1:
+        else:
             total[...] += term
-        else:
-            grad_w[...] = ((total[...] + term) * factor[0, 0]).astype(bf16)
-
-
-def tokens_kernel(arrived, d_mix, partial, first_t, skip, w_value_t, *rest):
+    size = kept.shape[1]
+    for high in range(2):
+        for part, low in ((kept, bit[0, 0]), (given, 1 - bit[0, 0])):
+            start = pl.multiple_of((2 * high + low) * size, size)
+            part[high] = (total[pl.ds(start, size)] * factor[0, 0]).astype(bf16)
+    for copy in outs:
+        copy.wait()
+
+
+def tokens_kernel(d_value, partial, w_value_t, *rest):
     grad_tokens, zero = rest[-2:]
-    for r in range(arrived.shape[1]):
+    for r in range(d_value.shape[0] // N2):
         here = row_slice(r)
-        d_cube = dot_nt(first_t[...], arrived[:, r].reshape(D, N2))
-        d_value = (d_cube + skip[...] * d_mix[here].astype(f32)).astype(bf16)
         grad_tokens[here] = (
-            partial[here].astype(f32) + dot_nn(d_value, w_value_t[...])
+            partial[here].astype(f32) + dot_nn(d_value[here], w_value_t[...])
         ).astype(bf16)
     zero[...] = jnp.zeros_like(zero)
 
 
-def place_kernel(values, offsets, me, *refs):
-    value_parts, gate_parts = refs[:values], refs[values : 2 * values]
-    out, skip_out, column = refs[2 * values :]
-    here = me[0, 0]
-    for distance, part in enumerate(value_parts):
-        size = part.shape[0]
-        start = pl.multiple_of((here % values ^ distance) * size, size)
-        out[0, pl.ds(start, size)] = part[...].astype(f32)
-    for distance, part in enumerate(gate_parts):
-        size = part.shape[0] // len(offsets)
+def place_gate_kernel(offsets, me, *refs):
+    parts, (out, skip_out), held = refs[:4], refs[4:6], refs[6:10]
+    wide, column, arrive, leave = refs[10:]
+    copies = [
+        pltpu.make_async_copy(parts[i], held[i], arrive.at[i]) for i in range(4)
+    ]
+    for copy in copies:
+        copy.start()
+    for distance in range(4):
+        copies[distance].wait()
+        size = held[distance].shape[0] // len(offsets)
         for i, offset in enumerate(offsets):
-            start = pl.multiple_of((here ^ (distance | offset)) * size, size)
-            block = part[i * size : (i + 1) * size].astype(f32)
-            out[1, pl.ds(start, size)] = block[:, :D]
+            start = pl.multiple_of((me[0, 0] ^ (distance | offset)) * size, size)
+            block = held[distance][i * size : (i + 1) * size].astype(f32)
+            wide[pl.ds(start, size)] = block[:, :D]
             column[pl.ds(start, size)] = block[:, D:]
+    copy = pltpu.make_async_copy(wide, out.at[1], leave)
+    copy.start()
     skip_out[...] = column[...].T[:1]
+    copy.wait()
+
+
+def place_value_kernel(me, *refs):
+    parts, out, held, wide = refs[:4], refs[5], refs[6:10], refs[10:14]
+    arrive, leave = refs[14:]
+    ins = [pltpu.make_async_copy(parts[i], held[i], arrive.at[i]) for i in range(4)]
+    for copy in ins:
+        copy.start()
+    outs = []
+    for i in range(4):
+        ins[i].wait()
+        wide[i][...] = held[i][...].astype(f32)
+        size = D // 4
+        start = pl.multiple_of(((me[0, 0] % 4) ^ i) * size, size)
+        outs.append(
+            pltpu.make_async_copy(wide[i], out.at[0, pl.ds(start, size)], leave.at[i])
+        )
+        outs[i].start()
+    for copy in outs:
+        copy.wait()
 
 
 def from_partner(array, b, n):
@@ -382,17 +421,19 @@
     )(tokens, w_value, first_block)
     one_home = transfer(one_sent)
 
-    three_sent, value, d_mix, tokens_t, skip_term = pl.pallas_call(
+    three_sent, value, d_mix, tokens_t, skip_term, w_value_t, w_gate_t = pl.pallas_call(
         d_three_kernel,
         grid=(rows // per,),
         in_specs=[row, row, square, square, block],
-        out_specs=[sent, row, row, column, line],
+        out_specs=[sent, row, row, column, line, square, square],
         out_shape=[
             shape(sections),
             shape((local_rows, D)),
             shape((local_rows, D)),
             shape((D, local_rows)),
             shape((1, D), f32),
+            shape((D, D)),
+            shape((D, D)),
         ],
         compiler_params=params(),
         cost_estimate=cost(5.4, 25),
@@ -441,24 +482,25 @@
         scratch_shapes=[pltpu.VMEM((D, D), f32), pltpu.VMEM((per * N2, D), bf16)],
         compiler_params=params(),
         cost_estimate=cost(5.4, 25),
-    )(three_here, tokens_t, value, cotangent, fourth_block, w_gate.T, skip, factor)
+    )(three_here, tokens_t, value, cotangent, fourth_block, w_gate_t, skip, factor)
 
     skip_lanes = jnp.broadcast_to((skip_term * factor[0, 0]).astype(bf16).T, (D, LANES))
     gate_term = jnp.concatenate([gate_term, skip_lanes], axis=1)
     bits = n.bit_length() - 1
     gate_part = gate_term.reshape((2,) * bits + (D // n, D + LANES))
     for b in range(bits):
-        early = gate_part
-        kept, sent_half = halves(gate_part, bits - 1 - b, b)
-        gate_part = added(kept, from_partner(sent_half, b, n))
+        kept, given = halves(gate_part, bits - 1 - b, b)
+        gate_part = added(kept, from_partner(given, b, n))
 
     first_t = first_block.T
     in_vmem = pl.BlockSpec(memory_space=pltpu.VMEM)
-    value_term = pl.pallas_call(
+    me = lax.axis_index("seq").reshape(1, 1)
+    half = (2, D // 4, D)
+    kept, given, d_value = pl.pallas_call(
         functools.partial(value_kernel, per),
-        in_specs=[unread, unread, unread, in_vmem, in_vmem, one, unread],
-        out_specs=in_vmem,
-        out_shape=shape((D, D)),
+        in_specs=[unread, unread, unread, in_vmem, in_vmem, one, one, unread],
+        out_specs=[in_vmem, in_vmem, unread],
+        out_shape=[shape(half), shape(half), shape((local_rows, D))],
         scratch_shapes=[
             pltpu.VMEM(sections, bf16),
             pltpu.VMEM((D, local_rows), bf16),
@@ -466,71 +508,81 @@
             pltpu.VMEM((local_rows, D), bf16),
             pltpu.VMEM((D, D), f32),
             pltpu.SemaphoreType.DMA((rows // per, 3)),
+            pltpu.SemaphoreType.DMA((rows // per,)),
         ],
         compiler_params=params(),
-        cost_estimate=cost(3.3, 13),
-    )(one_here, tokens_t, d_mix, first_t, skip, factor, early)
+        cost_estimate=cost(3.3, 17),
+    )(one_here, tokens_t, d_mix, first_t, skip, factor, me & 1, gate_part)
 
     offsets = [0]
+    gate_after = []
     for b in reversed(range(2, bits)):
         gate_part = jnp.concatenate([gate_part, from_partner(gate_part, b, n)])
+        gate_after.append(gate_part)
         offsets += [offset | (1 << b) for offset in offsets]
     gate_parts = doubled(gate_part, n)
+    gate_after = gate_after[-2:] + gate_parts[2:]
 
     quarters = 4
-    pair = rows // quarters // 2 if rows > quarters else 1
+    pair = max(rows // quarters // 2, 1)
     steps = rows // quarters // pair
-    w_value_t = w_value.T
 
     def quarter(i, grad_tokens, after):
-        turn = lambda g: g + i * steps
-        lines = pl.BlockSpec((pair * N2, D), lambda g: (turn(g), 0))
+        lines = pl.BlockSpec((pair * N2, D), lambda g: (g + i * steps, 0))
         held = [] if grad_tokens is None else [grad_tokens]
         return pl.pallas_call(
             tokens_kernel,
             grid=(steps,),
-            in_specs=[
-                pl.BlockSpec((n, pair, chans, N2), lambda g: (0, turn(g), 0, 0)),
-                lines,
-                lines,
-                block,
-                line,
-                square,
-                unread,
-            ]
-            + [unread] * len(held),
-            out_specs=[lines, whole((1, LANES))],
-            out_shape=[shape((local_rows, D)), shape((1, LANES), f32)],
-            input_output_aliases={7: 0} if held else {},
+            in_specs=[lines, lines, square, unread, unread] + [unread] * len(held),
+            out_specs=[lines, line],
+            out_shape=[shape((local_rows, D)), shape((1, D), f32)],
+            input_output_aliases={5: 0} if held else {},
             compiler_params=params(),
-            cost_estimate=cost(0.8, 4),
-        )(one_here, d_mix, partial, first_t, skip, w_value_t, after, *held)
-
-    value_part = value_term.reshape(2, 2, D // 4, D)
+            cost_estimate=cost(0.53, 3.5),
+        )(d_value, partial, w_value_t, after, gate_after[i], *held)
+
     grad_tokens = None
-    for i, b in enumerate(range(bits)):
-        if b < 2:
-            kept, sent_half = halves(value_part, 1 - b, b)
-        else:
-            kept, sent_half = value_part, value_part
-        got = from_partner(sent_half, b, n)
-        zero = 0.0
-        if i < quarters:
-            grad_tokens, zeros = quarter(i, grad_tokens, value_part)
-            zero = zeros[0, 0]
-        value_part = added(kept, got, zero)
+    for b in range(bits):
+        if b == 1:
+            kept, given = halves(value_part, 0, b)
+        elif b > 1:
+            kept, given = value_part, value_part
+        got = from_partner(given, b, n)
+        zeros = 0.0
+        if b < quarters:
+            grad_tokens, zeros = quarter(b, grad_tokens, given)
+        value_part = added(kept, got, zeros)
     value_parts = doubled(value_part, n)
 
-    vmem_specs = [in_vmem] * 8
+    placed = shape((2, D, D), f32)
+    gate_block = (D // 4, D + LANES)
     grad_weights, skip_total = pl.pallas_call(
-        functools.partial(place_kernel, 4, offsets),
-        in_specs=[one] + vmem_specs,
-        out_specs=[in_vmem, in_vmem],
-        out_shape=[shape((2, D, D), f32), shape((1, D), f32)],
-        scratch_shapes=[pltpu.VMEM((D, LANES), f32)],
-        compiler_params=params(),
-        cost_estimate=cost(0.001, 3),
-    )(lax.axis_index("seq").reshape(1, 1), *value_parts, *gate_parts)
+        functools.partial(place_gate_kernel, offsets),
+        in_specs=[one] + [unread] * 4,
+        out_specs=[unread, in_vmem],
+        out_shape=[placed, shape((1, D), f32)],
+        scratch_shapes=[pltpu.VMEM(gate_block, bf16)] * 4
+        + [
+            pltpu.VMEM((D, D), f32),
+            pltpu.VMEM((D, LANES), f32),
+            pltpu.SemaphoreType.DMA((4,)),
+            pltpu.SemaphoreType.DMA,
+        ],
+        compiler_params=params(),
+        cost_estimate=cost(0.001, 2),
+    )(me, *gate_parts)
+    grad_weights = pl.pallas_call(
+        place_value_kernel,
+        in_specs=[one] + [unread] * 5,
+        out_specs=unread,
+        out_shape=placed,
+        input_output_aliases={5: 0},
+        scratch_shapes=[pltpu.VMEM((D // 4, D), bf16)] * 4
+        + [pltpu.VMEM((D // 4, D), f32)] * 4
+        + [pltpu.SemaphoreType.DMA((4,)), pltpu.SemaphoreType.DMA((4,))],
+        compiler_params=params(),
+        cost_estimate=cost(0.001, 2),
+    )(me, *value_parts, grad_weights)
     return grad_tokens, grad_kernel, grad_weights, skip_total.reshape(D)
 
 

time: 453 us -> 457 us (level)
  waiting for transfers between devices: 241 us -> 261 us
  starting transfers between devices: 94.4 us -> 82.2 us
    ppermute x16, waiting for transfers between devices: 58.8 us -> 85.7 us  [from_partner(): return lax.ppermute(array, 'seq', [(i, i ^ 1 << b) for i in range(n)])]
    ppermute x16, starting transfers between devices: 27.6 us -> 15.4 us  [from_partner(): return lax.ppermute(array, 'seq', [(i, i ^ 1 << b) for i in range(n)])]
    all_to_all x4, waiting for transfers between devices: 183 us -> 175 us  [transfer(): return lax.all_to_all(array, 'seq', split_axis=0, concat_axis=0, tiled=True)]
    pallas_call x5 -> x6, Pallas kernels: 18.5 us -> 17 us  [the longest x4 12.3 us: quarter(): pl.pallas_call(tokens_kernel, grid=(steps,), in_specs=[lines, lines, squa...]
  transfers between devices with their start and end apart: 20 -> 20, of which waited for: 11 -> 11; matrix products, arithmetic and copies ran while one was open for 3% -> 2% of each run, Pallas kernels for 18% -> 18%
where the time goes in v9:
time: 457 us; the launch traced here: 456 us
  waiting for transfers between devices  261 us (57%)
  Pallas kernels  99.9 us (22%)
  starting transfers between devices  82.2 us (18%)
  other arithmetic  6.06 us (1%)
  local copies, waits for them, and re-layouts  5.91 us (1%)
    all_to_all x4, waiting for transfers between devices, transfer(): return lax.all_to_all(array, 'seq', split_axis=0, concat_axis=0, tiled=True)  175 us
    ppermute x16, waiting for transfers between devices, from_partner(): return lax.ppermute(array, 'seq', [(i, i ^ 1 << b) for i in range(n)])  85.7 us
    all_to_all x4, starting transfers between devices, transfer(): return lax.all_to_all(array, 'seq', split_axis=0, concat_axis=0, tiled=True)  66.8 us
    pallas_call x1, Pallas kernels, on_device(): pl.pallas_call(home_backward_kernel, grid=(chans // GROUP,), in_specs=[at...  20.6 us
    pallas_call x1, Pallas kernels, on_device(): pl.pallas_call(home_forward_kernel, grid=(chans // GROUP,), in_specs=[at_...  20.1 us
    ppermute x16, starting transfers between devices, from_partner(): return lax.ppermute(array, 'seq', [(i, i ^ 1 << b) for i in range(n)])  15.4 us
    pallas_call x1, Pallas kernels, on_device(): pl.pallas_call(d_three_kernel, grid=(rows // per,), in_specs=[row, row, s...  14.7 us
    pallas_call x4, Pallas kernels, quarter(): pl.pallas_call(tokens_kernel, grid=(steps,), in_specs=[lines, lines, squa...  12.3 us
  transfers between devices with their start and end apart: 20, of which 11 were waited for; matrix products, arithmetic and copies ran while one was open for 2% of the time, Pallas kernels for 18%

profile of v9, /device:TPU:0, one launch (start us, length us, event | category | flops | bytes accessed | tf_op | source)
XLA Modules:
  0.0 456.3 jit_solution(5693704882420574372)
XLA Ops:
  0.6 6.7 %shard_map.130 = bf16[16,16,32,256]{3,2,1,0:T(8,128)(2,1)} custom-call(bf16[4096,512]{1,0:T(8,128)(2,1)} %tokens.3, bf16[512,512]{1,0:T(8,128)(2,1)} %w_value.3, bf16[256,256]{1,0:T(8,128)(2,1)} %first.1), custom_call_target="tpu_custom_call" | custom-call | flops 3200000000 | bytes 9437184 | tf_op jit(solution)/shard_map/pallas_call | solution.py:406
  7.4 7.5 %all-to-all-start.1 = ((bf16[16,16,32,256]{3,2,1,0:T(8,128)(2,1)}), bf16[16,16,32,256]{3,2,1,0:T(8,128)(2,1)}, u32[]{:S(2)}, u32[]{:S(2)}) async-start(bf16[16,16,32,256]{3,2,1,0:T(8,128)(2,1)} %shard_map.130), calls=%async_computation.1 | async-start | bytes 8388608 | tf_op jit(solution)/shard_map/all_to_all | solution.py:403
  14.8 14.7 %shard_map.129 = (bf16[16,16,32,256]{3,2,1,0:T(8,128)(2,1)}, bf16[4096,512]{1,0:T(8,128)(2,1)}, bf16[4096,512]{1,0:T(8,128)(2,1)}, bf16[512,4096]{1,0:T(8,128)(2...) custom-call(bf16[4096,512]{1,0:T(8,128)(2,1)} %tokens.3, bf16[4096,512]{1,0:T(8,128)(2,1)} %cotangent.3, ...), custom_call_target="tpu_custom_call" | custom-call | flops 5400000000 | bytes 26214400 | tf_op jit(solution)/shard_map/pallas_call | solution.py:424
  29.5 63.0 %all-to-all-done.1 = bf16[16,16,32,256]{3,2,1,0:T(8,128)(2,1)} async-done(((bf16[16,16,32,256]{3,2,1,0:T(8,128)(2,1)}), bf16[16,16,32,256]{3,2,1,0:T(8,128)(2,1)}, u32[]{:S(2)}, u32[]{:S(2)}) %all-to-all-start.1) | async-done | bytes 4194336 | tf_op jit(solution)/shard_map/all_to_all | solution.py:403
  92.5 19.7 %all-to-all-start = ((bf16[16,16,32,256]{3,2,1,0:T(8,128)(2,1)}), bf16[16,16,32,256]{3,2,1,0:T(8,128)(2,1)}, u32[]{:S(2)}, u32[]{:S(2)}) async-start(bf16[16,16,32,256]{3,2,1,0:T(8,128)(2,1)} %get-tuple-element.30), calls=%async_computation | async-start | bytes 8388608 | tf_op jit(solution)/shard_map/all_to_all | solution.py:403
  113.0 20.1 %shard_map.131 = (bf16[256,32,256]{2,1,0:T(8,128)(2,1)}, f32[32,256,256]{2,1,0:T(8,128)}) custom-call(bf16[256,32,256]{2,1,0:T(8,128)(2,1)} %bitcast.1.arrived, bf16[32,256,256]{2,1,0:T(8,128)(2,1)} %kernel.3, bf16[256,256]{1,0:T(8,128)(2,1)} %second.1, bf16[256,256]{1,0:T(8,128)(2,1)} %third.1, bf16[256,256]{1,0:T(8,128)(2,1)} %fusion.4.swap), custom_call_target="tpu_custom_call" | custom-call | flops 4300000256 | bytes 20971520 | tf_op jit(solution)/shard_map/pallas_call | solution.py:445
  133.1 56.8 %all-to-all-done = bf16[16,16,32,256]{3,2,1,0:T(8,128)(2,1)} async-done(((bf16[16,16,32,256]{3,2,1,0:T(8,128)(2,1)}), bf16[16,16,32,256]{3,2,1,0:T(8,128)(2,1)}, u32[]{:S(2)}, u32[]{:S(2)}) %all-to-all-start) | async-done | bytes 4194336 | tf_op jit(solution)/shard_map/all_to_all | solution.py:403
  189.9 19.8 %all-to-all-start.3 = ((bf16[16,16,32,256]{3,2,1,0:T(8,128)(2,1)}), bf16[16,16,32,256]{3,2,1,0:T(8,128)(2,1)}, u32[]{:S(2)}, u32[]{:S(2)}) async-start(bf16[16,16,32,256]{3,2,1,0:T(8,128)(2,1)} %bitcast.44), calls=%async_computation.3 | async-start | bytes 8388608 | tf_op jit(solution)/shard_map/all_to_all | solution.py:403
  211.2 20.6 %shard_map.132 = (bf16[256,32,256]{2,1,0:T(8,128)(2,1)}, bf16[32,256,256]{2,1,0:T(8,128)(2,1)}) custom-call(bf16[256,32,256]{2,1,0:T(8,128)(2,1)} %bitcast.arrived, bf16[32,256,256]{2,1,0:T(8,128)(2,1)} %kernel.3, f32[32,256,256]{2,1,0:T(8,128)} %get-tuple-element.31.spectrum, bf16[256,256]{1,0:T(8,128)(2,1)} %bitcast.47, bf16[256,256]{1,0:T(8,128)(2,1)} %bitcast.48, ...), custom_call_target="tpu_custom_call" | custom-call | flops 4300000256 | bytes 25165824 | tf_op jit(solution)/shard_map/pallas_call | solution.py:457
  231.9 55.5 %all-to-all-done.3.arrived = bf16[16,16,32,256]{3,2,1,0:T(8,128)(2,1)} async-done(((bf16[16,16,32,256]{3,2,1,0:T(8,128)(2,1)}), bf16[16,16,32,256]{3,2,1,0:T(8,128)(2,1)}, u32[]{:S(2)}, u32[]{:S(2)}) %all-to-all-start.3) | async-done | bytes 4194336 | tf_op jit(solution)/shard_map/all_to_all | solution.py:403
  287.4 19.8 %all-to-all-start.2 = ((bf16[16,16,32,256]{3,2,1,0:T(8,128)(2,1)}), bf16[16,16,32,256]{3,2,1,0:T(8,128)(2,1)}, u32[]{:S(2)}, u32[]{:S(2)}) async-start(bf16[16,16,32,256]{3,2,1,0:T(8,128)(2,1)} %bitcast.43), calls=%async_computation.2 | async-start | bytes 8388608 | tf_op jit(solution)/shard_map/all_to_all | solution.py:403
  307.3 12.2 %shard_map.133 = (bf16[4096,512]{1,0:T(8,128)(2,1)}, bf16[512,512]{1,0:T(8,128)(2,1)}) custom-call(bf16[16,16,32,256]{3,2,1,0:T(8,128)(2,1)} %all-to-all-done.3.arrived, bf16[512,4096]{1,0:T(8,128)(2,1)} %get-tuple-element.33.tokens_t, bf16[4096,512]{1,0:T(8,128)(2,1)} %get-tuple-element.36.value, bf16[4096,512]{1,0:T(8,128)(2,1)} %cotangent.3, ...), custom_call_target="tpu_custom_call" | custom-call | flops 5400000000 | bytes 26214400 | tf_op jit(solution)/shard_map/pallas_call | solution.py:476
  324.7 12.6 %collective-permute-done.1 = bf16[2,2,32,640]{3,2,0,1:T(8,128)(2,1)S(1)} collective-permute-done((bf16[2,2,32,640]{3,2,0,1:T(8,128)(2,1)S(1)}, bf16[2,2,32,640]{3,2,0,1:T(8,128)(2,1)S(1)}, u32[]{:S(2)}, u32[]{:S(2)}) %collective-permute-start.1) | collective-permute-done | bytes 163872 | tf_op jit(solution)/shard_map/ppermute | solution.py:342
  337.5 40.1 %collective-permute-done.2 = bf16[2,32,640]{2,1,0:T(8,128)(2,1)S(1)} collective-permute-done((bf16[2,32,640]{2,1,0:T(8,128)(2,1)S(1)}, bf16[2,32,640]{2,1,0:T(8,128)(2,1)S(1)}, u32[]{:S(2)}, u32[]{:S(2)}) %collective-permute-start.2) | collective-permute-done | bytes 81952 | tf_op jit(solution)/shard_map/ppermute | solution.py:342
  377.6 4.6 %collective-permute-start.3 = (bf16[32,640]{1,0:T(8,128)(2,1)S(1)}, bf16[32,640]{1,0:T(8,128)(2,1)S(1)}, u32[]{:S(2)}, u32[]{:S(2)}) collective-permute-start(bf16[32,640]{1,0:T(8,128)(2,1)S(1)} %dynamic-slice_bitcast_fusion.3), channel_id=1, source_target_pairs={{0,8},{1,9},{2,10},{3,11},{4,12},{5,13},{6,14},{7,15},{8,0},{9,1},... | collective-permute-start | bytes 122888 | tf_op jit(solution)/shard_map/ppermute | solution.py:342
  383.0 20.0 %collective-permute-done.3 = bf16[32,640]{1,0:T(8,128)(2,1)S(1)} collective-permute-done((bf16[32,640]{1,0:T(8,128)(2,1)S(1)}, bf16[32,640]{1,0:T(8,128)(2,1)S(1)}, u32[]{:S(2)}, u32[]{:S(2)}) %collective-permute-start.3) | collective-permute-done | bytes 40992 | tf_op jit(solution)/shard_map/ppermute | solution.py:342
  403.6 8.4 %shard_map.134 = (bf16[2,128,512]{2,1,0:T(8,128)(2,1)}, bf16[2,128,512]{2,1,0:T(8,128)(2,1)}, bf16[4096,512]{1,0:T(8,128)(2,1)}) custom-call(bf16[16,16,32,256]{3,2,1,0:T(8,128)(2,1)} %all-to-all-done.2.arrived, bf16[512,4096]{1,0:T(8,128)(2,1)} %get-tuple-element.33.tokens_t, bf16[4096,512]{1,0:T(8,128)(2,1)} %get-tuple-element.34.d_mix, ...), custom_call_target="tpu_custom_call" | custom-call | flops 3300000000 | bytes 17825792 | tf_op jit(solution)/shard_map/pallas_call | solution.py:499
  412.6 4.5 collective-permute-done.5
  417.8 3.1 shard_map.135
  423.9 3.1 shard_map.136
  430.8 3.1 shard_map.137
  437.9 3.1 shard_map.138
  441.0 2.9 collective-permute-done.11
  447.0 3.0 collective-permute-done.13.refs_2_
  (90 shorter events, 30.1 us)
Async XLA Ops:
  7.4 85.1 %all-to-all-start.1 = ((bf16[16,16,32,256]{3,2,1,0:T(8,128)(2,1)}), bf16[16,16,32,256]{3,2,1,0:T(8,128)(2,1)}, u32[]{:S(2)}, u32[]{:S(2)}) async-start(bf16[16,16,32,256]{3,2,1,0:T(8,128)(2,1)} %shard_map.130), calls=%async_computation.1 | async-start | bytes 8388608 | tf_op jit(solution)/shard_map/all_to_all | solution.py:403
  92.5 97.4 %all-to-all-start = ((bf16[16,16,32,256]{3,2,1,0:T(8,128)(2,1)}), bf16[16,16,32,256]{3,2,1,0:T(8,128)(2,1)}, u32[]{:S(2)}, u32[]{:S(2)}) async-start(bf16[16,16,32,256]{3,2,1,0:T(8,128)(2,1)} %get-tuple-element.30), calls=%async_computation | async-start | bytes 8388608 | tf_op jit(solution)/shard_map/all_to_all | solution.py:403
  189.9 19.8 %copy-start.15 = (bf16[256,256]{1,0:T(8,128)(2,1)S(1)}, bf16[256,256]{1,0:T(8,128)(2,1)}, u32[]{:S(2)}) copy-start(bf16[256,256]{1,0:T(8,128)(2,1)} %second.1) | copy-start | bytes 393220
  189.9 20.6 %copy-start.16 = (bf16[256,256]{1,0:T(8,128)(2,1)S(1)}, bf16[256,256]{1,0:T(8,128)(2,1)}, u32[]{:S(2)}) copy-start(bf16[256,256]{1,0:T(8,128)(2,1)} %third.1) | copy-start | bytes 393220
  189.9 97.5 %all-to-all-start.3 = ((bf16[16,16,32,256]{3,2,1,0:T(8,128)(2,1)}), bf16[16,16,32,256]{3,2,1,0:T(8,128)(2,1)}, u32[]{:S(2)}, u32[]{:S(2)}) async-start(bf16[16,16,32,256]{3,2,1,0:T(8,128)(2,1)} %bitcast.44), calls=%async_computation.3 | async-start | bytes 8388608 | tf_op jit(solution)/shard_map/all_to_all | solution.py:403
  287.4 19.9 %copy-start.18 = (f32[1,512]{1,0:T(1,128)S(1)}, f32[1,512]{1,0:T(1,128)}, u32[]{:S(2)}) copy-start(f32[1,512]{1,0:T(1,128)} %get-tuple-element.39) | copy-start | bytes 6148
  287.4 116.2 %all-to-all-start.2 = ((bf16[16,16,32,256]{3,2,1,0:T(8,128)(2,1)}), bf16[16,16,32,256]{3,2,1,0:T(8,128)(2,1)}, u32[]{:S(2)}, u32[]{:S(2)}) async-start(bf16[16,16,32,256]{3,2,1,0:T(8,128)(2,1)} %bitcast.43), calls=%async_computation.2 | async-start | bytes 8388608 | tf_op jit(solution)/shard_map/all_to_all | solution.py:403
  319.5 62.7 %copy-start.17 = (bf16[256,256]{1,0:T(8,128)(2,1)S(1)}, bf16[256,256]{1,0:T(8,128)(2,1)}, u32[]{:S(2)}) copy-start(bf16[256,256]{1,0:T(8,128)(2,1)} %first.1) | copy-start | bytes 393220
  320.9 1.7 collective-permute-start
  322.7 14.6 %collective-permute-start.1 = (bf16[2,2,32,640]{3,2,0,1:T(8,128)(2,1)S(1)}, bf16[2,2,32,640]{3,2,0,1:T(8,128)(2,1)S(1)}, u32[]{:S(2)}, u32[]{:S(2)}) collective-permute-start(bf16[2,2,32,640]{3,2,0,1:T(8,128)(2,1)S(1)} %dynamic-slice_bitcast_fusion), channel_id=1, source_target_pairs={{0,2},{1,3},{2,0},{3,1},{4,6},{5,7},{6,4},{7,5},{8,10},{9,11},{10,... | collective-permute-start | bytes 491528 | tf_op jit(solution)/shard_map/ppermute | solution.py:342
  337.4 40.2 %collective-permute-start.2 = (bf16[2,32,640]{2,1,0:T(8,128)(2,1)S(1)}, bf16[2,32,640]{2,1,0:T(8,128)(2,1)S(1)}, u32[]{:S(2)}, u32[]{:S(2)}) collective-permute-start(bf16[2,32,640]{2,1,0:T(8,128)(2,1)S(1)} %dynamic-slice_bitcast_fusion.2), channel_id=1, source_target_pairs={{0,4},{1,5},{2,6},{3,7},{4,0},{5,1},{6,2},{7,3},{8,12},{9,13},{10,... | collective-permute-start | bytes 245768 | tf_op jit(solution)/shard_map/ppermute | solution.py:342
  377.6 25.4 %collective-permute-start.3 = (bf16[32,640]{1,0:T(8,128)(2,1)S(1)}, bf16[32,640]{1,0:T(8,128)(2,1)S(1)}, u32[]{:S(2)}, u32[]{:S(2)}) collective-permute-start(bf16[32,640]{1,0:T(8,128)(2,1)S(1)} %dynamic-slice_bitcast_fusion.3), channel_id=1, source_target_pairs={{0,8},{1,9},{2,10},{3,11},{4,12},{5,13},{6,14},{7,15},{8,0},{9,1},... | collective-permute-start | bytes 122888 | tf_op jit(solution)/shard_map/ppermute | solution.py:342
  412.0 8.8 %collective-permute-start.4 = (bf16[2,128,512]{2,1,0:T(8,128)(2,1)}, bf16[2,128,512]{2,1,0:T(8,128)(2,1)S(1)}, u32[]{:S(2)}, u32[]{:S(2)}) collective-permute-start(bf16[2,128,512]{2,1,0:T(8,128)(2,1)} %get-tuple-element.44.rest_0_), channel_id=1, source_target_pairs={{0,1},{1,0},{2,3},{3,2},{4,5},{5,4},{6,7},{7,6},{8,9},{9,8},{10,11... | collective-permute-start | bytes 786440 | tf_op jit(solution)/shard_map/ppermute | solution.py:342
  412.1 5.0 %collective-permute-start.5 = (bf16[32,640]{1,0:T(8,128)(2,1)S(1)}, bf16[32,640]{1,0:T(8,128)(2,1)S(1)}, u32[]{:S(2)}, u32[]{:S(2)}) collective-permute-start(bf16[32,640]{1,0:T(8,128)(2,1)S(1)} %copy-done.4), channel_id=1, source_target_pairs={{0,8},{1,9},{2,10},{3,11},{4,12},{5,13},{6,14},{7,15},{8,0},{9,1},... | collective-permute-start | bytes 122888 | tf_op jit(solution)/shard_map/ppermute | solution.py:342
  417.1 6.1 %collective-permute-start.7 = (bf16[64,640]{1,0:T(8,128)(2,1)S(1)}, bf16[64,640]{1,0:T(8,128)(2,1)S(1)}, u32[]{:S(2)}, u32[]{:S(2)}) collective-permute-start(bf16[64,640]{1,0:T(8,128)(2,1)S(1)} %pad_maximum_fusion.2.rest_1_), channel_id=1, source_target_pairs={{0,4},{1,5},{2,6},{3,7},{4,0},{5,1},{6,2},{7,3},{8,12},{9,13},{10,... | collective-permute-start | bytes 245768 | tf_op jit(solution)/shard_map/ppermute | solution.py:342
  421.7 6.5 %collective-permute-start.6 = (bf16[128,512]{1,0:T(8,128)(2,1)S(1)}, bf16[128,512]{1,0:T(8,128)(2,1)S(1)}, u32[]{:S(2)}, u32[]{:S(2)}) collective-permute-start(bf16[128,512]{1,0:T(8,128)(2,1)S(1)} %dynamic-slice_bitcast_fusion.1.rest_0_), channel_id=1, source_target_pairs={{0,2},{1,3},{2,0},{3,1},{4,6},{5,7},{6,4},{7,5},{8,10},{9,11},{10,... | collective-permute-start | bytes 393224 | tf_op jit(solution)/shard_map/ppermute | solution.py:342
  423.3 6.9 %collective-permute-start.9 = (bf16[128,640]{1,0:T(8,128)(2,1)S(1)}, bf16[128,640]{1,0:T(8,128)(2,1)S(1)}, u32[]{:S(2)}, u32[]{:S(2)}) collective-permute-start(bf16[128,640]{1,0:T(8,128)(2,1)S(1)} %pad_maximum_fusion.1.rest_1_.refs_0_), channel_id=1, source_target_pairs={{0,2},{1,3},{2,0},{3,1},{4,6},{5,7},{6,4},{7,5},{8,10},{9,11},{10,... | collective-permute-start | bytes 491528 | tf_op jit(solution)/shard_map/ppermute | solution.py:342
  428.9 5.0 %collective-permute-start.8 = (bf16[128,512]{1,0:T(8,128)(2,1)S(1)}, bf16[128,512]{1,0:T(8,128)(2,1)S(1)}, u32[]{:S(2)}, u32[]{:S(2)}) collective-permute-start(bf16[128,512]{1,0:T(8,128)(2,1)S(1)} %fusion.3.rest_0_), channel_id=1, source_target_pairs={{0,4},{1,5},{2,6},{3,7},{4,0},{5,1},{6,2},{7,3},{8,12},{9,13},{10,... | collective-permute-start | bytes 393224 | tf_op jit(solution)/shard_map/ppermute | solution.py:342
  430.2 7.1 %collective-permute-start.10 = (bf16[128,640]{1,0:T(8,128)(2,1)S(1)}, bf16[128,640]{1,0:T(8,128)(2,1)S(1)}, u32[]{:S(2)}, u32[]{:S(2)}) collective-permute-start(bf16[128,640]{1,0:T(8,128)(2,1)S(1)} %collective-permute-done.9.rest_1_.refs_2_), channel_id=1, source_target_pairs={{0,1},{1,0},{2,3},{3,2},{4,5},{5,4},{6,7},{7,6},{8,9},{9,8},{10,11... | collective-permute-start | bytes 491528 | tf_op jit(solution)/shard_map/ppermute | solution.py:342
  434.9 9.0 %collective-permute-start.11 = (bf16[128,512]{1,0:T(8,128)(2,1)S(1)}, bf16[128,512]{1,0:T(8,128)(2,1)S(1)}, u32[]{:S(2)}, u32[]{:S(2)}) collective-permute-start(bf16[128,512]{1,0:T(8,128)(2,1)S(1)} %add_convert_fusion.2.rest_0_), channel_id=1, source_target_pairs={{0,8},{1,9},{2,10},{3,11},{4,12},{5,13},{6,14},{7,15},{8,0},{9,1},... | collective-permute-start | bytes 393224 | tf_op jit(solution)/shard_map/ppermute | solution.py:342
  444.9 5.1 %collective-permute-start.13 = (bf16[128,512]{1,0:T(8,128)(2,1)S(1)}, bf16[128,512]{1,0:T(8,128)(2,1)S(1)}, u32[]{:S(2)}, u32[]{:S(2)}) collective-permute-start(bf16[128,512]{1,0:T(8,128)(2,1)S(1)} %add_convert_fusion.1.refs_0_), channel_id=1, source_target_pairs={{0,2},{1,3},{2,0},{3,1},{4,6},{5,7},{6,4},{7,5},{8,10},{9,11},{10,... | collective-permute-start | bytes 393224 | tf_op jit(solution)/shard_map/ppermute | solution.py:342
  446.4 3.5 collective-permute-start.15
  446.4 7.0 %collective-permute-start.12 = (bf16[128,512]{1,0:T(8,128)(2,1)S(1)}, bf16[128,512]{1,0:T(8,128)(2,1)S(1)}, u32[]{:S(2)}, u32[]{:S(2)}) collective-permute-start(bf16[128,512]{1,0:T(8,128)(2,1)S(1)} %add_convert_fusion.1.refs_0_), channel_id=1, source_target_pairs={{0,1},{1,0},{2,3},{3,2},{4,5},{5,4},{6,7},{7,6},{8,9},{9,8},{10,11... | collective-permute-start | bytes 393224 | tf_op jit(solution)/shard_map/ppermute | solution.py:342
  449.9 3.5 collective-permute-start.14
  (15 other events, 42.8 us)

commit v10 on v9

--- a/solution.py
+++ b/solution.py
@@ -296,44 +296,34 @@
     zero[...] = jnp.zeros_like(zero)
 
 
-def place_gate_kernel(offsets, me, *refs):
-    parts, (out, skip_out), held = refs[:4], refs[4:6], refs[6:10]
-    wide, column, arrive, leave = refs[10:]
-    copies = [
-        pltpu.make_async_copy(parts[i], held[i], arrive.at[i]) for i in range(4)
-    ]
-    for copy in copies:
-        copy.start()
-    for distance in range(4):
-        copies[distance].wait()
-        size = held[distance].shape[0] // len(offsets)
-        for i, offset in enumerate(offsets):
-            start = pl.multiple_of((me[0, 0] ^ (distance | offset)) * size, size)
-            block = held[distance][i * size : (i + 1) * size].astype(f32)
-            wide[pl.ds(start, size)] = block[:, :D]
-            column[pl.ds(start, size)] = block[:, D:]
-    copy = pltpu.make_async_copy(wide, out.at[1], leave)
-    copy.start()
-    skip_out[...] = column[...].T[:1]
-    copy.wait()
-
-
-def place_value_kernel(me, *refs):
-    parts, out, held, wide = refs[:4], refs[5], refs[6:10], refs[10:14]
-    arrive, leave = refs[14:]
-    ins = [pltpu.make_async_copy(parts[i], held[i], arrive.at[i]) for i in range(4)]
+def place_kernel(distances, me, *refs):
+    count = len(distances)
+    parts, refs = refs[:count], refs[count:]
+    out, skip_out, *refs = refs[-(2 + 3 * count + 2) :]
+    held, wides, columns = refs[:count], refs[count : 2 * count], refs[2 * count : 3 * count]
+    arrive, leave = refs[-2:]
+    size = D // 4
+    ins = [pltpu.make_async_copy(parts[i], held[i], arrive.at[i]) for i in range(count)]
     for copy in ins:
         copy.start()
     outs = []
-    for i in range(4):
+    for i, distance in enumerate(distances):
         ins[i].wait()
-        wide[i][...] = held[i][...].astype(f32)
-        size = D // 4
-        start = pl.multiple_of(((me[0, 0] % 4) ^ i) * size, size)
-        outs.append(
-            pltpu.make_async_copy(wide[i], out.at[0, pl.ds(start, size)], leave.at[i])
-        )
-        outs[i].start()
+        start = pl.multiple_of(((me[0, 0] % 4) ^ distance) * size, size)
+        wides[i][0] = held[i][:, :D].astype(f32)
+        wides[i][1] = held[i][:, D : 2 * D].astype(f32)
+        columns[i][...] = held[i][:, 2 * D :].astype(f32)
+        columns[i][...] = columns[i][...].T
+        outs += [
+            pltpu.make_async_copy(wides[i], out.at[:, pl.ds(start, size)], leave.at[i, 0]),
+            pltpu.make_async_copy(
+                columns[i].at[pl.ds(0, 8)],
+                skip_out.at[:, pl.ds(start, size)],
+                leave.at[i, 1],
+            ),
+        ]
+        outs[-2].start()
+        outs[-1].start()
     for copy in outs:
         copy.wait()
 
@@ -351,11 +341,6 @@
 
 def added(kept, got, zero=0.0):
     return (kept.astype(f32) + got.astype(f32) + zero).astype(bf16)
-
-
-def doubled(part, n):
-    other = from_partner(part, 1, n)
-    return [part, from_partner(part, 0, n), other, from_partner(other, 0, n)]
 
 
 def on_device(
@@ -487,9 +472,9 @@
     skip_lanes = jnp.broadcast_to((skip_term * factor[0, 0]).astype(bf16).T, (D, LANES))
     gate_term = jnp.concatenate([gate_term, skip_lanes], axis=1)
     bits = n.bit_length() - 1
-    gate_part = gate_term.reshape((2,) * bits + (D // n, D + LANES))
+    gate_part = gate_term.reshape(2, 2, D // 4, D + LANES)
     for b in range(bits):
-        kept, given = halves(gate_part, bits - 1 - b, b)
+        kept, given = halves(gate_part, 1 - b, b) if b < 2 else (gate_part, gate_part)
         gate_part = added(kept, from_partner(given, b, n))
 
     first_t = first_block.T
@@ -514,15 +499,6 @@
         cost_estimate=cost(3.3, 17),
     )(one_here, tokens_t, d_mix, first_t, skip, factor, me & 1, gate_part)
 
-    offsets = [0]
-    gate_after = []
-    for b in reversed(range(2, bits)):
-        gate_part = jnp.concatenate([gate_part, from_partner(gate_part, b, n)])
-        gate_after.append(gate_part)
-        offsets += [offset | (1 << b) for offset in offsets]
-    gate_parts = doubled(gate_part, n)
-    gate_after = gate_after[-2:] + gate_parts[2:]
-
     quarters = 4
     pair = max(rows // quarters // 2, 1)
     steps = rows // quarters // pair
@@ -533,13 +509,13 @@
         return pl.pallas_call(
             tokens_kernel,
             grid=(steps,),
-            in_specs=[lines, lines, square, unread, unread] + [unread] * len(held),
+            in_specs=[lines, lines, square, unread] + [unread] * len(held),
             out_specs=[lines, line],
             out_shape=[shape((local_rows, D)), shape((1, D), f32)],
-            input_output_aliases={5: 0} if held else {},
+            input_output_aliases={4: 0} if held else {},
             compiler_params=params(),
             cost_estimate=cost(0.53, 3.5),
-        )(d_value, partial, w_value_t, after, gate_after[i], *held)
+        )(d_value, partial, w_value_t, after, *held)
 
     grad_tokens = None
     for b in range(bits):
@@ -552,38 +528,31 @@
         if b < quarters:
             grad_tokens, zeros = quarter(b, grad_tokens, given)
         value_part = added(kept, got, zeros)
-    value_parts = doubled(value_part, n)
-
-    placed = shape((2, D, D), f32)
-    gate_block = (D // 4, D + LANES)
-    grad_weights, skip_total = pl.pallas_call(
-        functools.partial(place_gate_kernel, offsets),
-        in_specs=[one] + [unread] * 4,
-        out_specs=[unread, in_vmem],
-        out_shape=[placed, shape((1, D), f32)],
-        scratch_shapes=[pltpu.VMEM(gate_block, bf16)] * 4
-        + [
-            pltpu.VMEM((D, D), f32),
-            pltpu.VMEM((D, LANES), f32),
-            pltpu.SemaphoreType.DMA((4,)),
-            pltpu.SemaphoreType.DMA,
-        ],
-        compiler_params=params(),
-        cost_estimate=cost(0.001, 2),
-    )(me, *gate_parts)
-    grad_weights = pl.pallas_call(
-        place_value_kernel,
-        in_specs=[one] + [unread] * 5,
-        out_specs=unread,
-        out_shape=placed,
-        input_output_aliases={5: 0},
-        scratch_shapes=[pltpu.VMEM((D // 4, D), bf16)] * 4
-        + [pltpu.VMEM((D // 4, D), f32)] * 4
-        + [pltpu.SemaphoreType.DMA((4,)), pltpu.SemaphoreType.DMA((4,))],
-        compiler_params=params(),
-        cost_estimate=cost(0.001, 2),
-    )(me, *value_parts, grad_weights)
-    return grad_tokens, grad_kernel, grad_weights, skip_total.reshape(D)
+    both = jnp.concatenate([value_part, gate_part], axis=1)
+    other = from_partner(both, 1, n)
+    near = from_partner(both, 0, n)
+    far = from_partner(other, 0, n)
+
+    def place(parts, distances, held):
+        count = len(parts)
+        block = (D // 4, 2 * D + LANES)
+        return pl.pallas_call(
+            functools.partial(place_kernel, distances),
+            in_specs=[one] + [unread] * (count + len(held)),
+            out_specs=[unread, unread],
+            out_shape=[shape((2, D, D), f32), shape((8, D), f32)],
+            input_output_aliases={1 + count: 0, 2 + count: 1} if held else {},
+            scratch_shapes=[pltpu.VMEM(block, bf16)] * count
+            + [pltpu.VMEM((2, D // 4, D), f32)] * count
+            + [pltpu.VMEM((LANES, D // 4), f32)] * count
+            + [pltpu.SemaphoreType.DMA((count,)), pltpu.SemaphoreType.DMA((count, 2))],
+            compiler_params=params(),
+            cost_estimate=cost(0.001, count),
+        )(me, *parts, *held)
+
+    placed = place([both, near, other], [0, 1, 2], [])
+    grad_weights, skip_total = place([far], [3], placed)
+    return grad_tokens, grad_kernel, grad_weights, skip_total[0]
 
 
 def solution(mesh):

time: 457 us -> 460 us (level)
  waiting for transfers between devices: 261 us -> 269 us
  starting transfers between devices: 82.2 us -> 77.4 us
    ppermute x16 -> x11, waiting for transfers between devices: 85.7 us -> 93.3 us  [from_partner(): return lax.ppermute(array, 'seq', [(i, i ^ 1 << b) for i in range(n)])]
    ppermute x16 -> x11, starting transfers between devices: 15.4 us -> 10.6 us  [from_partner(): return lax.ppermute(array, 'seq', [(i, i ^ 1 << b) for i in range(n)])]
  transfers between devices with their start and end apart: 20 -> 15, of which waited for: 11 -> 11; matrix products, arithmetic and copies ran while one was open for 2% -> 1% of each run, Pallas kernels for 18% -> 18%
where the time goes in v10:
time: 460 us; the launch traced here: 459 us
  waiting for transfers between devices  269 us (58%)
  Pallas kernels  99.3 us (22%)
  starting transfers between devices  77.4 us (17%)
  local copies, waits for them, and re-layouts  6.84 us (1%)
  other arithmetic  6.18 us (1%)
    all_to_all x4, waiting for transfers between devices, transfer(): return lax.all_to_all(array, 'seq', split_axis=0, concat_axis=0, tiled=True)  175 us
    ppermute x11, waiting for transfers between devices, from_partner(): return lax.ppermute(array, 'seq', [(i, i ^ 1 << b) for i in range(n)])  93.3 us
    all_to_all x4, starting transfers between devices, transfer(): return lax.all_to_all(array, 'seq', split_axis=0, concat_axis=0, tiled=True)  66.8 us
    pallas_call x1, Pallas kernels, on_device(): pl.pallas_call(home_backward_kernel, grid=(chans // GROUP,), in_specs=[at...  20.6 us
    pallas_call x1, Pallas kernels, on_device(): pl.pallas_call(home_forward_kernel, grid=(chans // GROUP,), in_specs=[at_...  20.1 us
    pallas_call x1, Pallas kernels, on_device(): pl.pallas_call(d_three_kernel, grid=(rows // per,), in_specs=[row, row, s...  14.7 us
    pallas_call x1, Pallas kernels, on_device(): pl.pallas_call(gate_kernel, grid=(rows // per,), in_specs=[sent, column,...  12.3 us
    pallas_call x4, Pallas kernels, quarter(): pl.pallas_call(tokens_kernel, grid=(steps,), in_specs=[lines, lines, squa...  12.3 us
  transfers between devices with their start and end apart: 15, of which 11 were waited for; matrix products, arithmetic and copies ran while one was open for 1% of the time, Pallas kernels for 18%

profile of v10, /device:TPU:0, one launch (start us, length us, event | category | flops | bytes accessed | tf_op | source)
XLA Modules:
  0.0 459.2 jit_solution(10068259082783905235)
XLA Ops:
  0.6 6.7 %shard_map.130 = bf16[16,16,32,256]{3,2,1,0:T(8,128)(2,1)} custom-call(bf16[4096,512]{1,0:T(8,128)(2,1)} %tokens.3, bf16[512,512]{1,0:T(8,128)(2,1)} %w_value.3, bf16[256,256]{1,0:T(8,128)(2,1)} %first.1), custom_call_target="tpu_custom_call" | custom-call | flops 3200000000 | bytes 9437184 | tf_op jit(solution)/shard_map/pallas_call | solution.py:391
  7.4 7.5 %all-to-all-start.1 = ((bf16[16,16,32,256]{3,2,1,0:T(8,128)(2,1)}), bf16[16,16,32,256]{3,2,1,0:T(8,128)(2,1)}, u32[]{:S(2)}, u32[]{:S(2)}) async-start(bf16[16,16,32,256]{3,2,1,0:T(8,128)(2,1)} %shard_map.130), calls=%async_computation.1 | async-start | bytes 8388608 | tf_op jit(solution)/shard_map/all_to_all | solution.py:388
  14.8 14.7 %shard_map.129 = (bf16[16,16,32,256]{3,2,1,0:T(8,128)(2,1)}, bf16[4096,512]{1,0:T(8,128)(2,1)}, bf16[4096,512]{1,0:T(8,128)(2,1)}, bf16[512,4096]{1,0:T(8,128)(2...) custom-call(bf16[4096,512]{1,0:T(8,128)(2,1)} %tokens.3, bf16[4096,512]{1,0:T(8,128)(2,1)} %cotangent.3, ...), custom_call_target="tpu_custom_call" | custom-call | flops 5400000000 | bytes 26214400 | tf_op jit(solution)/shard_map/pallas_call | solution.py:409
  29.6 63.0 %all-to-all-done.1 = bf16[16,16,32,256]{3,2,1,0:T(8,128)(2,1)} async-done(((bf16[16,16,32,256]{3,2,1,0:T(8,128)(2,1)}), bf16[16,16,32,256]{3,2,1,0:T(8,128)(2,1)}, u32[]{:S(2)}, u32[]{:S(2)}) %all-to-all-start.1) | async-done | bytes 4194336 | tf_op jit(solution)/shard_map/all_to_all | solution.py:388
  92.5 19.7 %all-to-all-start = ((bf16[16,16,32,256]{3,2,1,0:T(8,128)(2,1)}), bf16[16,16,32,256]{3,2,1,0:T(8,128)(2,1)}, u32[]{:S(2)}, u32[]{:S(2)}) async-start(bf16[16,16,32,256]{3,2,1,0:T(8,128)(2,1)} %get-tuple-element.32), calls=%async_computation | async-start | bytes 8388608 | tf_op jit(solution)/shard_map/all_to_all | solution.py:388
  113.0 20.1 %shard_map.131 = (bf16[256,32,256]{2,1,0:T(8,128)(2,1)}, f32[32,256,256]{2,1,0:T(8,128)}) custom-call(bf16[256,32,256]{2,1,0:T(8,128)(2,1)} %bitcast.1.arrived, bf16[32,256,256]{2,1,0:T(8,128)(2,1)} %kernel.3, bf16[256,256]{1,0:T(8,128)(2,1)} %second.1, bf16[256,256]{1,0:T(8,128)(2,1)} %third.1, bf16[256,256]{1,0:T(8,128)(2,1)} %fusion.4.swap), custom_call_target="tpu_custom_call" | custom-call | flops 4300000256 | bytes 20971520 | tf_op jit(solution)/shard_map/pallas_call | solution.py:430
  133.1 56.8 %all-to-all-done = bf16[16,16,32,256]{3,2,1,0:T(8,128)(2,1)} async-done(((bf16[16,16,32,256]{3,2,1,0:T(8,128)(2,1)}), bf16[16,16,32,256]{3,2,1,0:T(8,128)(2,1)}, u32[]{:S(2)}, u32[]{:S(2)}) %all-to-all-start) | async-done | bytes 4194336 | tf_op jit(solution)/shard_map/all_to_all | solution.py:388
  189.9 19.8 %all-to-all-start.3 = ((bf16[16,16,32,256]{3,2,1,0:T(8,128)(2,1)}), bf16[16,16,32,256]{3,2,1,0:T(8,128)(2,1)}, u32[]{:S(2)}, u32[]{:S(2)}) async-start(bf16[16,16,32,256]{3,2,1,0:T(8,128)(2,1)} %bitcast.33), calls=%async_computation.3 | async-start | bytes 8388608 | tf_op jit(solution)/shard_map/all_to_all | solution.py:388
  211.3 20.6 %shard_map.132 = (bf16[256,32,256]{2,1,0:T(8,128)(2,1)}, bf16[32,256,256]{2,1,0:T(8,128)(2,1)}) custom-call(bf16[256,32,256]{2,1,0:T(8,128)(2,1)} %bitcast.arrived, bf16[32,256,256]{2,1,0:T(8,128)(2,1)} %kernel.3, f32[32,256,256]{2,1,0:T(8,128)} %get-tuple-element.33.spectrum, bf16[256,256]{1,0:T(8,128)(2,1)} %bitcast.37, bf16[256,256]{1,0:T(8,128)(2,1)} %bitcast.38, ...), custom_call_target="tpu_custom_call" | custom-call | flops 4300000256 | bytes 25165824 | tf_op jit(solution)/shard_map/pallas_call | solution.py:442
  231.9 55.5 %all-to-all-done.3.arrived = bf16[16,16,32,256]{3,2,1,0:T(8,128)(2,1)} async-done(((bf16[16,16,32,256]{3,2,1,0:T(8,128)(2,1)}), bf16[16,16,32,256]{3,2,1,0:T(8,128)(2,1)}, u32[]{:S(2)}, u32[]{:S(2)}) %all-to-all-start.3) | async-done | bytes 4194336 | tf_op jit(solution)/shard_map/all_to_all | solution.py:388
  287.4 19.8 %all-to-all-start.2 = ((bf16[16,16,32,256]{3,2,1,0:T(8,128)(2,1)}), bf16[16,16,32,256]{3,2,1,0:T(8,128)(2,1)}, u32[]{:S(2)}, u32[]{:S(2)}) async-start(bf16[16,16,32,256]{3,2,1,0:T(8,128)(2,1)} %bitcast.32), calls=%async_computation.2 | async-start | bytes 8388608 | tf_op jit(solution)/shard_map/all_to_all | solution.py:388
  307.3 12.3 %shard_map.133 = (bf16[4096,512]{1,0:T(8,128)(2,1)}, bf16[512,512]{1,0:T(8,128)(2,1)}) custom-call(bf16[16,16,32,256]{3,2,1,0:T(8,128)(2,1)} %all-to-all-done.3.arrived, bf16[512,4096]{1,0:T(8,128)(2,1)} %get-tuple-element.35.tokens_t, bf16[4096,512]{1,0:T(8,128)(2,1)} %get-tuple-element.38.value, bf16[4096,512]{1,0:T(8,128)(2,1)} %cotangent.3, ...), custom_call_target="tpu_custom_call" | custom-call | flops 5400000000 | bytes 26214400 | tf_op jit(solution)/shard_map/pallas_call | solution.py:461
  324.7 12.6 %collective-permute-done.1 = bf16[128,640]{1,0:T(8,128)(2,1)S(1)} collective-permute-done((bf16[128,640]{1,0:T(8,128)(2,1)S(1)}, bf16[128,640]{1,0:T(8,128)(2,1)S(1)}, u32[]{:S(2)}, u32[]{:S(2)}) %collective-permute-start.1) | collective-permute-done | bytes 163872 | tf_op jit(solution)/shard_map/ppermute | solution.py:332
  337.4 41.9 %collective-permute-done.2 = bf16[128,640]{1,0:T(8,128)(2,1)S(1)} collective-permute-done((bf16[128,640]{1,0:T(8,128)(2,1)S(1)}, bf16[128,640]{1,0:T(8,128)(2,1)S(1)}, u32[]{:S(2)}, u32[]{:S(2)}) %collective-permute-start.2) | collective-permute-done | bytes 163872 | tf_op jit(solution)/shard_map/ppermute | solution.py:332
  379.4 4.6 collective-permute-start.3
  384.7 23.5 %collective-permute-done.3 = bf16[128,640]{1,0:T(8,128)(2,1)S(1)} collective-permute-done((bf16[128,640]{1,0:T(8,128)(2,1)S(1)}, bf16[128,640]{1,0:T(8,128)(2,1)S(1)}, u32[]{:S(2)}, u32[]{:S(2)}) %collective-permute-start.3) | collective-permute-done | bytes 163872 | tf_op jit(solution)/shard_map/ppermute | solution.py:332
  409.0 8.4 %shard_map.134 = (bf16[2,128,512]{2,1,0:T(8,128)(2,1)}, bf16[2,128,512]{2,1,0:T(8,128)(2,1)}, bf16[4096,512]{1,0:T(8,128)(2,1)}) custom-call(bf16[16,16,32,256]{3,2,1,0:T(8,128)(2,1)} %all-to-all-done.2.arrived, bf16[512,4096]{1,0:T(8,128)(2,1)} %get-tuple-element.35.tokens_t, bf16[4096,512]{1,0:T(8,128)(2,1)} %get-tuple-element.36.d_mix, ...), custom_call_target="tpu_custom_call" | custom-call | flops 3300000000 | bytes 17825792 | tf_op jit(solution)/shard_map/pallas_call | solution.py:484
  417.5 3.1 shard_map.135
  423.0 3.1 shard_map.136
  428.7 3.1 shard_map.137
  434.9 3.1 shard_map.138
  437.9 4.2 collective-permute-done.7
  444.8 7.0 %collective-permute-done.8.refs_2_ = bf16[128,1152]{1,0:T(8,128)(2,1)S(1)} collective-permute-done((bf16[128,1152]{1,0:T(8,128)(2,1)S(1)}, bf16[128,1152]{1,0:T(8,128)(2,1)S(1)}, u32[]{:S(2)}, u32[]{:S(2)}) %collective-permute-start.8) | collective-permute-done | bytes 294944 | tf_op jit(solution)/shard_map/ppermute | solution.py:332
  453.2 2.2 shard_map.139
  (65 shorter events, 24.9 us)
Async XLA Ops:
  7.4 85.1 %all-to-all-start.1 = ((bf16[16,16,32,256]{3,2,1,0:T(8,128)(2,1)}), bf16[16,16,32,256]{3,2,1,0:T(8,128)(2,1)}, u32[]{:S(2)}, u32[]{:S(2)}) async-start(bf16[16,16,32,256]{3,2,1,0:T(8,128)(2,1)} %shard_map.130), calls=%async_computation.1 | async-start | bytes 8388608 | tf_op jit(solution)/shard_map/all_to_all | solution.py:388
  92.5 97.4 %all-to-all-start = ((bf16[16,16,32,256]{3,2,1,0:T(8,128)(2,1)}), bf16[16,16,32,256]{3,2,1,0:T(8,128)(2,1)}, u32[]{:S(2)}, u32[]{:S(2)}) async-start(bf16[16,16,32,256]{3,2,1,0:T(8,128)(2,1)} %get-tuple-element.32), calls=%async_computation | async-start | bytes 8388608 | tf_op jit(solution)/shard_map/all_to_all | solution.py:388
  189.9 19.8 %copy-start.9 = (bf16[256,256]{1,0:T(8,128)(2,1)S(1)}, bf16[256,256]{1,0:T(8,128)(2,1)}, u32[]{:S(2)}) copy-start(bf16[256,256]{1,0:T(8,128)(2,1)} %second.1) | copy-start | bytes 393220
  189.9 20.6 %copy-start.10 = (bf16[256,256]{1,0:T(8,128)(2,1)S(1)}, bf16[256,256]{1,0:T(8,128)(2,1)}, u32[]{:S(2)}) copy-start(bf16[256,256]{1,0:T(8,128)(2,1)} %third.1) | copy-start | bytes 393220
  189.9 97.5 %all-to-all-start.3 = ((bf16[16,16,32,256]{3,2,1,0:T(8,128)(2,1)}), bf16[16,16,32,256]{3,2,1,0:T(8,128)(2,1)}, u32[]{:S(2)}, u32[]{:S(2)}) async-start(bf16[16,16,32,256]{3,2,1,0:T(8,128)(2,1)} %bitcast.33), calls=%async_computation.3 | async-start | bytes 8388608 | tf_op jit(solution)/shard_map/all_to_all | solution.py:388
  287.4 19.9 %copy-start.12 = (f32[1,512]{1,0:T(1,128)S(1)}, f32[1,512]{1,0:T(1,128)}, u32[]{:S(2)}) copy-start(f32[1,512]{1,0:T(1,128)} %get-tuple-element.41) | copy-start | bytes 6148
  287.4 121.6 %all-to-all-start.2 = ((bf16[16,16,32,256]{3,2,1,0:T(8,128)(2,1)}), bf16[16,16,32,256]{3,2,1,0:T(8,128)(2,1)}, u32[]{:S(2)}, u32[]{:S(2)}) async-start(bf16[16,16,32,256]{3,2,1,0:T(8,128)(2,1)} %bitcast.32), calls=%async_computation.2 | async-start | bytes 8388608 | tf_op jit(solution)/shard_map/all_to_all | solution.py:388
  319.6 64.3 %copy-start.11 = (bf16[256,256]{1,0:T(8,128)(2,1)S(1)}, bf16[256,256]{1,0:T(8,128)(2,1)}, u32[]{:S(2)}) copy-start(bf16[256,256]{1,0:T(8,128)(2,1)} %first.1) | copy-start | bytes 393220
  320.9 1.7 collective-permute-start
  322.7 14.6 %collective-permute-start.1 = (bf16[128,640]{1,0:T(8,128)(2,1)S(1)}, bf16[128,640]{1,0:T(8,128)(2,1)S(1)}, u32[]{:S(2)}, u32[]{:S(2)}) collective-permute-start(bf16[128,640]{1,0:T(8,128)(2,1)S(1)} %dynamic-slice_bitcast_fusion.1), channel_id=1, source_target_pairs={{0,2},{1,3},{2,0},{3,1},{4,6},{5,7},{6,4},{7,5},{8,10},{9,11},{10,... | collective-permute-start | bytes 491528 | tf_op jit(solution)/shard_map/ppermute | solution.py:332
  337.3 42.0 %collective-permute-start.2 = (bf16[128,640]{1,0:T(8,128)(2,1)S(1)}, bf16[128,640]{1,0:T(8,128)(2,1)S(1)}, u32[]{:S(2)}, u32[]{:S(2)}) collective-permute-start(bf16[128,640]{1,0:T(8,128)(2,1)S(1)} %fusion.1), channel_id=1, source_target_pairs={{0,4},{1,5},{2,6},{3,7},{4,0},{5,1},{6,2},{7,3},{8,12},{9,13},{10,... | collective-permute-start | bytes 491528 | tf_op jit(solution)/shard_map/ppermute | solution.py:332
  379.4 28.9 %collective-permute-start.3 = (bf16[128,640]{1,0:T(8,128)(2,1)S(1)}, bf16[128,640]{1,0:T(8,128)(2,1)S(1)}, u32[]{:S(2)}, u32[]{:S(2)}) collective-permute-start(bf16[128,640]{1,0:T(8,128)(2,1)S(1)} %add_convert_fusion.2), channel_id=1, source_target_pairs={{0,8},{1,9},{2,10},{3,11},{4,12},{5,13},{6,14},{7,15},{8,0},{9,1},... | collective-permute-start | bytes 491528 | tf_op jit(solution)/shard_map/ppermute | solution.py:332
  417.4 3.2 collective-permute-start.4
  417.5 3.1 copy-start.8
  421.4 1.6 copy-start.4
  421.4 5.9 %collective-permute-start.5 = (bf16[128,512]{1,0:T(8,128)(2,1)S(1)}, bf16[128,512]{1,0:T(8,128)(2,1)S(1)}, u32[]{:S(2)}, u32[]{:S(2)}) collective-permute-start(bf16[128,512]{1,0:T(8,128)(2,1)S(1)} %dynamic-slice_bitcast_fusion.2.rest_0_), channel_id=1, source_target_pairs={{0,2},{1,3},{2,0},{3,1},{4,6},{5,7},{6,4},{7,5},{8,10},{9,11},{10,... | collective-permute-start | bytes 393224 | tf_op jit(solution)/shard_map/ppermute | solution.py:332
  428.1 5.2 %collective-permute-start.6 = (bf16[128,512]{1,0:T(8,128)(2,1)S(1)}, bf16[128,512]{1,0:T(8,128)(2,1)S(1)}, u32[]{:S(2)}, u32[]{:S(2)}) collective-permute-start(bf16[128,512]{1,0:T(8,128)(2,1)S(1)} %fusion.3.rest_0_), channel_id=1, source_target_pairs={{0,4},{1,5},{2,6},{3,7},{4,0},{5,1},{6,2},{7,3},{8,12},{9,13},{10,... | collective-permute-start | bytes 393224 | tf_op jit(solution)/shard_map/ppermute | solution.py:332
  434.2 8.0 %collective-permute-start.7 = (bf16[128,512]{1,0:T(8,128)(2,1)S(1)}, bf16[128,512]{1,0:T(8,128)(2,1)S(1)}, u32[]{:S(2)}, u32[]{:S(2)}) collective-permute-start(bf16[128,512]{1,0:T(8,128)(2,1)S(1)} %add_convert_fusion.4.rest_0_), channel_id=1, source_target_pairs={{0,8},{1,9},{2,10},{3,11},{4,12},{5,13},{6,14},{7,15},{8,0},{9,1},... | collective-permute-start | bytes 393224 | tf_op jit(solution)/shard_map/ppermute | solution.py:332
  434.9 8.3 %copy-start = (bf16[128,640]{1,0:T(8,128)(2,1)S(1)}, bf16[128,640]{1,0:T(8,128)(2,1)}, u32[]{:S(2)}) copy-start(bf16[128,640]{1,0:T(8,128)(2,1)} %add_convert_fusion.1._) | copy-start | bytes 491524
  443.2 8.6 %copy-start.3 = (bf16[128,1152]{1,0:T(8,128)(2,1)}, bf16[128,1152]{1,0:T(8,128)(2,1)S(1)}, u32[]{:S(2)}) copy-start(bf16[128,1152]{1,0:T(8,128)(2,1)S(1)} %pad_maximum_fusion.1.refs_0_) | copy-start | bytes 884740
  443.2 8.5 %collective-permute-start.8 = (bf16[128,1152]{1,0:T(8,128)(2,1)S(1)}, bf16[128,1152]{1,0:T(8,128)(2,1)S(1)}, u32[]{:S(2)}, u32[]{:S(2)}) collective-permute-start(bf16[128,1152]{1,0:T(8,128)(2,1)S(1)} %pad_maximum_fusion.1.refs_0_), channel_id=1, source_target_pairs={{0,2},{1,3},{2,0},{3,1},{4,6},{5,7},{6,4},{7,5},{8,10},{9,11},{10,... | collective-permute-start | bytes 884744 | tf_op jit(solution)/shard_map/ppermute | solution.py:332
  444.7 7.0 %collective-permute-start.10 = (bf16[128,1152]{1,0:T(8,128)(2,1)S(1)}, bf16[128,1152]{1,0:T(8,128)(2,1)S(1)}, u32[]{:S(2)}, u32[]{:S(2)}) collective-permute-start(bf16[128,1152]{1,0:T(8,128)(2,1)S(1)} %pad_maximum_fusion.1.refs_0_), channel_id=1, source_target_pairs={{0,1},{1,0},{2,3},{3,2},{4,5},{5,4},{6,7},{7,6},{8,9},{9,8},{10,11... | collective-permute-start | bytes 884744 | tf_op jit(solution)/shard_map/ppermute | solution.py:332
  451.7 0.7 copy-start.5
  451.7 3.7 collective-permute-start.9
  (4 other events, 2.8 us)

commit v11 on v10

--- a/solution.py
+++ b/solution.py
@@ -287,45 +287,12 @@
 
 
 def tokens_kernel(d_value, partial, w_value_t, *rest):
-    grad_tokens, zero = rest[-2:]
+    grad_tokens = rest[-1]
     for r in range(d_value.shape[0] // N2):
         here = row_slice(r)
         grad_tokens[here] = (
             partial[here].astype(f32) + dot_nn(d_value[here], w_value_t[...])
         ).astype(bf16)
-    zero[...] = jnp.zeros_like(zero)
-
-
-def place_kernel(distances, me, *refs):
-    count = len(distances)
-    parts, refs = refs[:count], refs[count:]
-    out, skip_out, *refs = refs[-(2 + 3 * count + 2) :]
-    held, wides, columns = refs[:count], refs[count : 2 * count], refs[2 * count : 3 * count]
-    arrive, leave = refs[-2:]
-    size = D // 4
-    ins = [pltpu.make_async_copy(parts[i], held[i], arrive.at[i]) for i in range(count)]
-    for copy in ins:
-        copy.start()
-    outs = []
-    for i, distance in enumerate(distances):
-        ins[i].wait()
-        start = pl.multiple_of(((me[0, 0] % 4) ^ distance) * size, size)
-        wides[i][0] = held[i][:, :D].astype(f32)
-        wides[i][1] = held[i][:, D : 2 * D].astype(f32)
-        columns[i][...] = held[i][:, 2 * D :].astype(f32)
-        columns[i][...] = columns[i][...].T
-        outs += [
-            pltpu.make_async_copy(wides[i], out.at[:, pl.ds(start, size)], leave.at[i, 0]),
-            pltpu.make_async_copy(
-                columns[i].at[pl.ds(0, 8)],
-                skip_out.at[:, pl.ds(start, size)],
-                leave.at[i, 1],
-            ),
-        ]
-        outs[-2].start()
-        outs[-1].start()
-    for copy in outs:
-        copy.wait()
 
 
 def from_partner(array, b, n):
@@ -339,8 +306,16 @@
     return kept, sent
 
 
-def added(kept, got, zero=0.0):
-    return (kept.astype(f32) + got.astype(f32) + zero).astype(bf16)
+def added(kept, got):
+    return (kept.astype(f32) + got.astype(f32)).astype(bf16)
+
+
+def doubled(part, axis, b, n):
+    bit = (lax.axis_index("seq") >> b) & 1
+    mine = jnp.expand_dims(part, axis)
+    other = jnp.expand_dims(from_partner(part, b, n), axis)
+    around = jnp.concatenate([mine, other, mine], axis)
+    return lax.dynamic_slice_in_dim(around, bit, 2, axis)
 
 
 def on_device(
@@ -472,9 +447,9 @@
     skip_lanes = jnp.broadcast_to((skip_term * factor[0, 0]).astype(bf16).T, (D, LANES))
     gate_term = jnp.concatenate([gate_term, skip_lanes], axis=1)
     bits = n.bit_length() - 1
-    gate_part = gate_term.reshape(2, 2, D // 4, D + LANES)
+    gate_part = gate_term.reshape((2,) * bits + (D // n, D + LANES))
     for b in range(bits):
-        kept, given = halves(gate_part, 1 - b, b) if b < 2 else (gate_part, gate_part)
+        kept, given = halves(gate_part, bits - 1 - b, b)
         gate_part = added(kept, from_partner(given, b, n))
 
     first_t = first_block.T
@@ -499,6 +474,10 @@
         cost_estimate=cost(3.3, 17),
     )(one_here, tokens_t, d_mix, first_t, skip, factor, me & 1, gate_part)
 
+    for b in reversed(range(bits)):
+        gate_part = doubled(gate_part, bits - 1 - b, b, n)
+    gate_total = gate_part.reshape(D, D + LANES)
+
     quarters = 4
     pair = max(rows // quarters // 2, 1)
     steps = rows // quarters // pair
@@ -510,8 +489,8 @@
             tokens_kernel,
             grid=(steps,),
             in_specs=[lines, lines, square, unread] + [unread] * len(held),
-            out_specs=[lines, line],
-            out_shape=[shape((local_rows, D)), shape((1, D), f32)],
+            out_specs=lines,
+            out_shape=shape((local_rows, D)),
             input_output_aliases={4: 0} if held else {},
             compiler_params=params(),
             cost_estimate=cost(0.53, 3.5),
@@ -524,35 +503,13 @@
         elif b > 1:
             kept, given = value_part, value_part
         got = from_partner(given, b, n)
-        zeros = 0.0
         if b < quarters:
-            grad_tokens, zeros = quarter(b, grad_tokens, given)
-        value_part = added(kept, got, zeros)
-    both = jnp.concatenate([value_part, gate_part], axis=1)
-    other = from_partner(both, 1, n)
-    near = from_partner(both, 0, n)
-    far = from_partner(other, 0, n)
-
-    def place(parts, distances, held):
-        count = len(parts)
-        block = (D // 4, 2 * D + LANES)
-        return pl.pallas_call(
-            functools.partial(place_kernel, distances),
-            in_specs=[one] + [unread] * (count + len(held)),
-            out_specs=[unread, unread],
-            out_shape=[shape((2, D, D), f32), shape((8, D), f32)],
-            input_output_aliases={1 + count: 0, 2 + count: 1} if held else {},
-            scratch_shapes=[pltpu.VMEM(block, bf16)] * count
-            + [pltpu.VMEM((2, D // 4, D), f32)] * count
-            + [pltpu.VMEM((LANES, D // 4), f32)] * count
-            + [pltpu.SemaphoreType.DMA((count,)), pltpu.SemaphoreType.DMA((count, 2))],
-            compiler_params=params(),
-            cost_estimate=cost(0.001, count),
-        )(me, *parts, *held)
-
-    placed = place([both, near, other], [0, 1, 2], [])
-    grad_weights, skip_total = place([far], [3], placed)
-    return grad_tokens, grad_kernel, grad_weights, skip_total[0]
+            grad_tokens = quarter(b, grad_tokens, given)
+        value_part = added(kept, got)
+    for b in (1, 0):
+        value_part = doubled(value_part, 1 - b, b, n)
+    grad_weights = jnp.stack([value_part.reshape(D, D), gate_total[:, :D]]).astype(f32)
+    return grad_tokens, grad_kernel, grad_weights, gate_total[:, D].astype(f32)
 
 
 def solution(mesh):

time: 460 us -> 446 us (0.970)
  waiting for transfers between devices: 269 us -> 257 us
  starting transfers between devices: 77.4 us -> 82.6 us
    ppermute x11 -> x14, waiting for transfers between devices: 93.3 us -> 81.8 us  [from_partner(): return lax.ppermute(array, 'seq', [(i, i ^ 1 << b) for i in range(n)])]
    ppermute x11 -> x14, starting transfers between devices: 10.6 us -> 15.7 us  [from_partner(): return lax.ppermute(array, 'seq', [(i, i ^ 1 << b) for i in range(n)])]
  transfers between devices with their start and end apart: 15 -> 18, of which waited for: 11 -> 12; matrix products, arithmetic and copies ran while one was open for 1% -> 2% of each run, Pallas kernels for 18% -> 20%
where the time goes in v11:
time: 446 us; the launch traced here: 445 us
  waiting for transfers between devices  257 us (58%)
  Pallas kernels  95.2 us (21%)
  starting transfers between devices  82.6 us (19%)
  other arithmetic  5.97 us (1%)
    all_to_all x4, waiting for transfers between devices, transfer(): return lax.all_to_all(array, 'seq', split_axis=0, concat_axis=0, tiled=True)  175 us
    ppermute x14, waiting for transfers between devices, from_partner(): return lax.ppermute(array, 'seq', [(i, i ^ 1 << b) for i in range(n)])  81.8 us
    all_to_all x4, starting transfers between devices, transfer(): return lax.all_to_all(array, 'seq', split_axis=0, concat_axis=0, tiled=True)  66.8 us
    pallas_call x1, Pallas kernels, on_device(): pl.pallas_call(home_backward_kernel, grid=(chans // GROUP,), in_specs=[at...  20.6 us
    pallas_call x1, Pallas kernels, on_device(): pl.pallas_call(home_forward_kernel, grid=(chans // GROUP,), in_specs=[at_...  20.1 us
    ppermute x14, starting transfers between devices, from_partner(): return lax.ppermute(array, 'seq', [(i, i ^ 1 << b) for i in range(n)])  15.7 us
    pallas_call x1, Pallas kernels, on_device(): pl.pallas_call(d_three_kernel, grid=(rows // per,), in_specs=[row, row, s...  14.7 us
    pallas_call x1, Pallas kernels, on_device(): pl.pallas_call(gate_kernel, grid=(rows // per,), in_specs=[sent, column,...  12.3 us
  transfers between devices with their start and end apart: 18, of which 12 were waited for; matrix products, arithmetic and copies ran while one was open for 2% of the time, Pallas kernels for 20%

profile of v11, /device:TPU:0, one launch (start us, length us, event | category | flops | bytes accessed | tf_op | source)
XLA Modules:
  0.0 445.1 jit_solution(1083246718114919723)
XLA Ops:
  0.6 6.7 %shard_map.130 = bf16[16,16,32,256]{3,2,1,0:T(8,128)(2,1)} custom-call(bf16[4096,512]{1,0:T(8,128)(2,1)} %tokens.3, bf16[512,512]{1,0:T(8,128)(2,1)} %w_value.3, bf16[256,256]{1,0:T(8,128)(2,1)} %first.1), custom_call_target="tpu_custom_call" | custom-call | flops 3200000000 | bytes 9437184 | tf_op jit(solution)/shard_map/pallas_call | solution.py:366
  7.4 7.5 %all-to-all-start.1 = ((bf16[16,16,32,256]{3,2,1,0:T(8,128)(2,1)}), bf16[16,16,32,256]{3,2,1,0:T(8,128)(2,1)}, u32[]{:S(2)}, u32[]{:S(2)}) async-start(bf16[16,16,32,256]{3,2,1,0:T(8,128)(2,1)} %shard_map.130), calls=%async_computation.1 | async-start | bytes 8388608 | tf_op jit(solution)/shard_map/all_to_all | solution.py:363
  14.8 14.7 %shard_map.129 = (bf16[16,16,32,256]{3,2,1,0:T(8,128)(2,1)}, bf16[4096,512]{1,0:T(8,128)(2,1)}, bf16[4096,512]{1,0:T(8,128)(2,1)}, bf16[512,4096]{1,0:T(8,128)(2...) custom-call(bf16[4096,512]{1,0:T(8,128)(2,1)} %tokens.3, bf16[4096,512]{1,0:T(8,128)(2,1)} %cotangent.3, ...), custom_call_target="tpu_custom_call" | custom-call | flops 5400000000 | bytes 26214400 | tf_op jit(solution)/shard_map/pallas_call | solution.py:384
  29.5 63.0 %all-to-all-done.1 = bf16[16,16,32,256]{3,2,1,0:T(8,128)(2,1)} async-done(((bf16[16,16,32,256]{3,2,1,0:T(8,128)(2,1)}), bf16[16,16,32,256]{3,2,1,0:T(8,128)(2,1)}, u32[]{:S(2)}, u32[]{:S(2)}) %all-to-all-start.1) | async-done | bytes 4194336 | tf_op jit(solution)/shard_map/all_to_all | solution.py:363
  92.5 19.7 %all-to-all-start = ((bf16[16,16,32,256]{3,2,1,0:T(8,128)(2,1)}), bf16[16,16,32,256]{3,2,1,0:T(8,128)(2,1)}, u32[]{:S(2)}, u32[]{:S(2)}) async-start(bf16[16,16,32,256]{3,2,1,0:T(8,128)(2,1)} %get-tuple-element.20), calls=%async_computation | async-start | bytes 8388608 | tf_op jit(solution)/shard_map/all_to_all | solution.py:363
  113.0 20.1 %shard_map.131 = (bf16[256,32,256]{2,1,0:T(8,128)(2,1)}, f32[32,256,256]{2,1,0:T(8,128)}) custom-call(bf16[256,32,256]{2,1,0:T(8,128)(2,1)} %bitcast.1.arrived, bf16[32,256,256]{2,1,0:T(8,128)(2,1)} %kernel.3, bf16[256,256]{1,0:T(8,128)(2,1)} %second.1, bf16[256,256]{1,0:T(8,128)(2,1)} %third.1, bf16[256,256]{1,0:T(8,128)(2,1)} %fusion.11.swap), custom_call_target="tpu_custom_call" | custom-call | flops 4300000256 | bytes 20971520 | tf_op jit(solution)/shard_map/pallas_call | solution.py:405
  133.1 56.8 %all-to-all-done = bf16[16,16,32,256]{3,2,1,0:T(8,128)(2,1)} async-done(((bf16[16,16,32,256]{3,2,1,0:T(8,128)(2,1)}), bf16[16,16,32,256]{3,2,1,0:T(8,128)(2,1)}, u32[]{:S(2)}, u32[]{:S(2)}) %all-to-all-start) | async-done | bytes 4194336 | tf_op jit(solution)/shard_map/all_to_all | solution.py:363
  189.9 19.8 %all-to-all-start.3 = ((bf16[16,16,32,256]{3,2,1,0:T(8,128)(2,1)}), bf16[16,16,32,256]{3,2,1,0:T(8,128)(2,1)}, u32[]{:S(2)}, u32[]{:S(2)}) async-start(bf16[16,16,32,256]{3,2,1,0:T(8,128)(2,1)} %bitcast.59), calls=%async_computation.3 | async-start | bytes 8388608 | tf_op jit(solution)/shard_map/all_to_all | solution.py:363
  211.3 20.6 %shard_map.132 = (bf16[256,32,256]{2,1,0:T(8,128)(2,1)}, bf16[32,256,256]{2,1,0:T(8,128)(2,1)}) custom-call(bf16[256,32,256]{2,1,0:T(8,128)(2,1)} %bitcast.arrived, bf16[32,256,256]{2,1,0:T(8,128)(2,1)} %kernel.3, f32[32,256,256]{2,1,0:T(8,128)} %get-tuple-element.21.spectrum, bf16[256,256]{1,0:T(8,128)(2,1)} %bitcast.71, bf16[256,256]{1,0:T(8,128)(2,1)} %bitcast.72, ...), custom_call_target="tpu_custom_call" | custom-call | flops 4300000256 | bytes 25165824 | tf_op jit(solution)/shard_map/pallas_call | solution.py:417
  231.9 55.5 %all-to-all-done.3.arrived = bf16[16,16,32,256]{3,2,1,0:T(8,128)(2,1)} async-done(((bf16[16,16,32,256]{3,2,1,0:T(8,128)(2,1)}), bf16[16,16,32,256]{3,2,1,0:T(8,128)(2,1)}, u32[]{:S(2)}, u32[]{:S(2)}) %all-to-all-start.3) | async-done | bytes 4194336 | tf_op jit(solution)/shard_map/all_to_all | solution.py:363
  287.4 19.8 %all-to-all-start.2 = ((bf16[16,16,32,256]{3,2,1,0:T(8,128)(2,1)}), bf16[16,16,32,256]{3,2,1,0:T(8,128)(2,1)}, u32[]{:S(2)}, u32[]{:S(2)}) async-start(bf16[16,16,32,256]{3,2,1,0:T(8,128)(2,1)} %bitcast.58), calls=%async_computation.2 | async-start | bytes 8388608 | tf_op jit(solution)/shard_map/all_to_all | solution.py:363
  307.3 12.3 %shard_map.133 = (bf16[4096,512]{1,0:T(8,128)(2,1)}, bf16[512,512]{1,0:T(8,128)(2,1)}) custom-call(bf16[16,16,32,256]{3,2,1,0:T(8,128)(2,1)} %all-to-all-done.3.arrived, bf16[512,4096]{1,0:T(8,128)(2,1)} %get-tuple-element.23.tokens_t, bf16[4096,512]{1,0:T(8,128)(2,1)} %get-tuple-element.26.value, bf16[4096,512]{1,0:T(8,128)(2,1)} %cotangent.3, ...), custom_call_target="tpu_custom_call" | custom-call | flops 5400000000 | bytes 26214400 | tf_op jit(solution)/shard_map/pallas_call | solution.py:436
  322.8 1.9 collective-permute-start.1
  324.7 12.6 %collective-permute-done.1 = bf16[2,2,32,640]{3,2,0,1:T(8,128)(2,1)S(1)} collective-permute-done((bf16[2,2,32,640]{3,2,0,1:T(8,128)(2,1)S(1)}, bf16[2,2,32,640]{3,2,0,1:T(8,128)(2,1)S(1)}, u32[]{:S(2)}, u32[]{:S(2)}) %collective-permute-start.1) | collective-permute-done | bytes 163872 | tf_op jit(solution)/shard_map/ppermute | solution.py:299
  337.5 40.1 %collective-permute-done.2 = bf16[2,32,640]{2,1,0:T(8,128)(2,1)S(1)} collective-permute-done((bf16[2,32,640]{2,1,0:T(8,128)(2,1)S(1)}, bf16[2,32,640]{2,1,0:T(8,128)(2,1)S(1)}, u32[]{:S(2)}, u32[]{:S(2)}) %collective-permute-start.2) | collective-permute-done | bytes 81952 | tf_op jit(solution)/shard_map/ppermute | solution.py:299
  377.6 4.6 %collective-permute-start.3 = (bf16[32,640]{1,0:T(8,128)(2,1)S(1)}, bf16[32,640]{1,0:T(8,128)(2,1)S(1)}, u32[]{:S(2)}, u32[]{:S(2)}) collective-permute-start(bf16[32,640]{1,0:T(8,128)(2,1)S(1)} %dynamic-slice_bitcast_fusion.3), channel_id=1, source_target_pairs={{0,8},{1,9},{2,10},{3,11},{4,12},{5,13},{6,14},{7,15},{8,0},{9,1},... | collective-permute-start | bytes 122888 | tf_op jit(solution)/shard_map/ppermute | solution.py:299
  383.0 20.0 %collective-permute-done.3 = bf16[32,640]{1,0:T(8,128)(2,1)S(1)} collective-permute-done((bf16[32,640]{1,0:T(8,128)(2,1)S(1)}, bf16[32,640]{1,0:T(8,128)(2,1)S(1)}, u32[]{:S(2)}, u32[]{:S(2)}) %collective-permute-start.3) | collective-permute-done | bytes 40992 | tf_op jit(solution)/shard_map/ppermute | solution.py:299
  403.6 8.4 %shard_map.134 = (bf16[2,128,512]{2,1,0:T(8,128)(2,1)}, bf16[2,128,512]{2,1,0:T(8,128)(2,1)}, bf16[4096,512]{1,0:T(8,128)(2,1)}) custom-call(bf16[16,16,32,256]{3,2,1,0:T(8,128)(2,1)} %all-to-all-done.2.arrived, bf16[512,4096]{1,0:T(8,128)(2,1)} %get-tuple-element.23.tokens_t, bf16[4096,512]{1,0:T(8,128)(2,1)} %get-tuple-element.24.d_mix, ...), custom_call_target="tpu_custom_call" | custom-call | flops 3300000000 | bytes 17825792 | tf_op jit(solution)/shard_map/pallas_call | solution.py:459
  412.1 3.1 shard_map.135.rest_1_
  423.5 3.1 shard_map.136.rest_1_
  427.8 1.8 collective-permute-start.7
  429.8 3.1 shard_map.137.rest_1_
  432.9 3.7 collective-permute-done.7
  438.0 3.1 shard_map.138
  (79 shorter events, 22.2 us)
Async XLA Ops:
  7.4 85.1 %all-to-all-start.1 = ((bf16[16,16,32,256]{3,2,1,0:T(8,128)(2,1)}), bf16[16,16,32,256]{3,2,1,0:T(8,128)(2,1)}, u32[]{:S(2)}, u32[]{:S(2)}) async-start(bf16[16,16,32,256]{3,2,1,0:T(8,128)(2,1)} %shard_map.130), calls=%async_computation.1 | async-start | bytes 8388608 | tf_op jit(solution)/shard_map/all_to_all | solution.py:363
  92.5 97.4 %all-to-all-start = ((bf16[16,16,32,256]{3,2,1,0:T(8,128)(2,1)}), bf16[16,16,32,256]{3,2,1,0:T(8,128)(2,1)}, u32[]{:S(2)}, u32[]{:S(2)}) async-start(bf16[16,16,32,256]{3,2,1,0:T(8,128)(2,1)} %get-tuple-element.20), calls=%async_computation | async-start | bytes 8388608 | tf_op jit(solution)/shard_map/all_to_all | solution.py:363
  189.9 19.8 %copy-start.6 = (bf16[256,256]{1,0:T(8,128)(2,1)S(1)}, bf16[256,256]{1,0:T(8,128)(2,1)}, u32[]{:S(2)}) copy-start(bf16[256,256]{1,0:T(8,128)(2,1)} %second.1) | copy-start | bytes 393220
  189.9 20.6 %copy-start.7 = (bf16[256,256]{1,0:T(8,128)(2,1)S(1)}, bf16[256,256]{1,0:T(8,128)(2,1)}, u32[]{:S(2)}) copy-start(bf16[256,256]{1,0:T(8,128)(2,1)} %third.1) | copy-start | bytes 393220
  189.9 97.5 %all-to-all-start.3 = ((bf16[16,16,32,256]{3,2,1,0:T(8,128)(2,1)}), bf16[16,16,32,256]{3,2,1,0:T(8,128)(2,1)}, u32[]{:S(2)}, u32[]{:S(2)}) async-start(bf16[16,16,32,256]{3,2,1,0:T(8,128)(2,1)} %bitcast.59), calls=%async_computation.3 | async-start | bytes 8388608 | tf_op jit(solution)/shard_map/all_to_all | solution.py:363
  287.4 19.9 %copy-start.9 = (f32[1,512]{1,0:T(1,128)S(1)}, f32[1,512]{1,0:T(1,128)}, u32[]{:S(2)}) copy-start(f32[1,512]{1,0:T(1,128)} %get-tuple-element.29) | copy-start | bytes 6148
  287.4 115.7 %all-to-all-start.2 = ((bf16[16,16,32,256]{3,2,1,0:T(8,128)(2,1)}), bf16[16,16,32,256]{3,2,1,0:T(8,128)(2,1)}, u32[]{:S(2)}, u32[]{:S(2)}) async-start(bf16[16,16,32,256]{3,2,1,0:T(8,128)(2,1)} %bitcast.58), calls=%async_computation.2 | async-start | bytes 8388608 | tf_op jit(solution)/shard_map/all_to_all | solution.py:363
  319.6 62.6 %copy-start.8 = (bf16[256,256]{1,0:T(8,128)(2,1)S(1)}, bf16[256,256]{1,0:T(8,128)(2,1)}, u32[]{:S(2)}) copy-start(bf16[256,256]{1,0:T(8,128)(2,1)} %first.1) | copy-start | bytes 393220
  321.0 1.7 collective-permute-start
  322.8 14.5 %collective-permute-start.1 = (bf16[2,2,32,640]{3,2,0,1:T(8,128)(2,1)S(1)}, bf16[2,2,32,640]{3,2,0,1:T(8,128)(2,1)S(1)}, u32[]{:S(2)}, u32[]{:S(2)}) collective-permute-start(bf16[2,2,32,640]{3,2,0,1:T(8,128)(2,1)S(1)} %dynamic-slice_bitcast_fusion), channel_id=1, source_target_pairs={{0,2},{1,3},{2,0},{3,1},{4,6},{5,7},{6,4},{7,5},{8,10},{9,11},{10,... | collective-permute-start | bytes 491528 | tf_op jit(solution)/shard_map/ppermute | solution.py:299
  337.4 40.2 %collective-permute-start.2 = (bf16[2,32,640]{2,1,0:T(8,128)(2,1)S(1)}, bf16[2,32,640]{2,1,0:T(8,128)(2,1)S(1)}, u32[]{:S(2)}, u32[]{:S(2)}) collective-permute-start(bf16[2,32,640]{2,1,0:T(8,128)(2,1)S(1)} %dynamic-slice_bitcast_fusion.2), channel_id=1, source_target_pairs={{0,4},{1,5},{2,6},{3,7},{4,0},{5,1},{6,2},{7,3},{8,12},{9,13},{10,... | collective-permute-start | bytes 245768 | tf_op jit(solution)/shard_map/ppermute | solution.py:299
  377.6 25.4 %collective-permute-start.3 = (bf16[32,640]{1,0:T(8,128)(2,1)S(1)}, bf16[32,640]{1,0:T(8,128)(2,1)S(1)}, u32[]{:S(2)}, u32[]{:S(2)}) collective-permute-start(bf16[32,640]{1,0:T(8,128)(2,1)S(1)} %dynamic-slice_bitcast_fusion.3), channel_id=1, source_target_pairs={{0,8},{1,9},{2,10},{3,11},{4,12},{5,13},{6,14},{7,15},{8,0},{9,1},... | collective-permute-start | bytes 122888 | tf_op jit(solution)/shard_map/ppermute | solution.py:299
  403.0 12.2 %collective-permute-start.10 = (bf16[32,640]{1,0:T(8,128)(2,1)S(1)}, bf16[32,640]{1,0:T(8,128)(2,1)S(1)}, u32[]{:S(2)}, u32[]{:S(2)}) collective-permute-start(bf16[32,640]{1,0:T(8,128)(2,1)S(1)} %fusion.17._), channel_id=1, source_target_pairs={{0,8},{1,9},{2,10},{3,11},{4,12},{5,13},{6,14},{7,15},{8,0},{9,1},... | collective-permute-start | bytes 122888 | tf_op jit(solution)/shard_map/ppermute | solution.py:299
  412.0 4.9 %collective-permute-start.4 = (bf16[2,128,512]{2,1,0:T(8,128)(2,1)}, bf16[2,128,512]{2,1,0:T(8,128)(2,1)S(1)}, u32[]{:S(2)}, u32[]{:S(2)}) collective-permute-start(bf16[2,128,512]{2,1,0:T(8,128)(2,1)} %get-tuple-element.34.rest_0_), channel_id=1, source_target_pairs={{0,1},{1,0},{2,3},{3,2},{4,5},{5,4},{6,7},{7,6},{8,9},{9,8},{10,11... | collective-permute-start | bytes 786440 | tf_op jit(solution)/shard_map/ppermute | solution.py:299
  415.3 4.9 %collective-permute-start.11 = (bf16[2,32,640]{2,1,0:T(8,128)(2,1)S(1)}, bf16[2,32,640]{2,1,0:T(8,128)(2,1)S(1)}, u32[]{:S(2)}, u32[]{:S(2)}) collective-permute-start(bf16[2,32,640]{2,1,0:T(8,128)(2,1)S(1)} %fusion.16), channel_id=1, source_target_pairs={{0,4},{1,5},{2,6},{3,7},{4,0},{5,1},{6,2},{7,3},{8,12},{9,13},{10,... | collective-permute-start | bytes 245768 | tf_op jit(solution)/shard_map/ppermute | solution.py:299
  417.0 6.5 %copy-start.4 = (bf16[128,512]{1,0:T(8,128)(2,1)}, bf16[128,512]{1,0:T(8,128)(2,1)S(1)}, u32[]{:S(2)}) copy-start(bf16[128,512]{1,0:T(8,128)(2,1)S(1)} %dynamic-slice_bitcast_fusion.1.rest_0_) | copy-start | bytes 393220
  417.0 5.7 %collective-permute-start.5 = (bf16[128,512]{1,0:T(8,128)(2,1)S(1)}, bf16[128,512]{1,0:T(8,128)(2,1)S(1)}, u32[]{:S(2)}, u32[]{:S(2)}) collective-permute-start(bf16[128,512]{1,0:T(8,128)(2,1)S(1)} %dynamic-slice_bitcast_fusion.1.rest_0_), channel_id=1, source_target_pairs={{0,2},{1,3},{2,0},{3,1},{4,6},{5,7},{6,4},{7,5},{8,10},{9,11},{10,... | collective-permute-start | bytes 393224 | tf_op jit(solution)/shard_map/ppermute | solution.py:299
  420.3 6.2 %collective-permute-start.12 = (bf16[2,2,32,640]{3,2,0,1:T(8,128)(2,1)S(1)}, bf16[2,2,32,640]{3,2,0,1:T(8,128)(2,1)S(1)}, u32[]{:S(2)}, u32[]{:S(2)}) collective-permute-start(bf16[2,2,32,640]{3,2,0,1:T(8,128)(2,1)S(1)} %fusion.13), channel_id=1, source_target_pairs={{0,2},{1,3},{2,0},{3,1},{4,6},{5,7},{6,4},{7,5},{8,10},{9,11},{10,... | collective-permute-start | bytes 491528 | tf_op jit(solution)/shard_map/ppermute | solution.py:299
  422.8 5.0 %collective-permute-start.6 = (bf16[128,512]{1,0:T(8,128)(2,1)S(1)}, bf16[128,512]{1,0:T(8,128)(2,1)S(1)}, u32[]{:S(2)}, u32[]{:S(2)}) collective-permute-start(bf16[128,512]{1,0:T(8,128)(2,1)S(1)} %fusion.10.rest_0_), channel_id=1, source_target_pairs={{0,4},{1,5},{2,6},{3,7},{4,0},{5,1},{6,2},{7,3},{8,12},{9,13},{10,... | collective-permute-start | bytes 393224 | tf_op jit(solution)/shard_map/ppermute | solution.py:299
  426.7 14.4 %collective-permute-start.13 = (bf16[2,2,2,32,640]{4,3,0,1,2:T(8,128)(2,1)S(1)}, bf16[2,2,2,32,640]{4,3,0,1,2:T(8,128)(2,1)S(1)}, u32[]{:S(2)}, u32[]{:S(2)}) collective-permute-start(bf16[2,2,2,32,640]{4,3,0,1,2:T(8,128)(2,1)S(1)} %fusion.6), channel_id=1, source_target_pairs={{0,1},{1,0},{2,3},{3,2},{4,5},{5,4},{6,7},{7,6},{8,9},{9,8},{10,11... | collective-permute-start | bytes 983048 | tf_op jit(solution)/shard_map/ppermute | solution.py:299
  427.8 8.7 %copy-start = (bf16[128,512]{1,0:T(8,128)(2,1)}, bf16[128,512]{1,0:T(8,128)(2,1)S(1)}, u32[]{:S(2)}) copy-start(bf16[128,512]{1,0:T(8,128)(2,1)S(1)} %add_convert_fusion.2.rest_0_) | copy-start | bytes 393220
  427.8 8.7 %collective-permute-start.7 = (bf16[128,512]{1,0:T(8,128)(2,1)S(1)}, bf16[128,512]{1,0:T(8,128)(2,1)S(1)}, u32[]{:S(2)}, u32[]{:S(2)}) collective-permute-start(bf16[128,512]{1,0:T(8,128)(2,1)S(1)} %add_convert_fusion.2.rest_0_), channel_id=1, source_target_pairs={{0,8},{1,9},{2,10},{3,11},{4,12},{5,13},{6,14},{7,15},{8,0},{9,1},... | collective-permute-start | bytes 393224 | tf_op jit(solution)/shard_map/ppermute | solution.py:299
  436.6 5.0 %collective-permute-start.8 = (bf16[128,512]{1,0:T(8,128)(2,1)S(1)}, bf16[128,512]{1,0:T(8,128)(2,1)S(1)}, u32[]{:S(2)}, u32[]{:S(2)}) collective-permute-start(bf16[128,512]{1,0:T(8,128)(2,1)S(1)} %add_convert_fusion.1), channel_id=1, source_target_pairs={{0,2},{1,3},{2,0},{3,1},{4,6},{5,7},{6,4},{7,5},{8,10},{9,11},{10,... | collective-permute-start | bytes 393224 | tf_op jit(solution)/shard_map/ppermute | solution.py:299
  441.7 1.6 collective-permute-start.9
  (4 other events, 13.6 us)

commit v12 on v11

--- a/solution.py
+++ b/solution.py
@@ -271,12 +271,7 @@
         outs.append(pltpu.make_async_copy(d_value.at[here], d_value_out.at[here], leave.at[i]))
         outs[i].start()
         started[i][2].wait()
-        here = slice(i * per * N2, (i + 1) * per * N2)
-        term = dot_nn(tokens_v[:, here], d_value[here])
-        if i == 0:
-            total[...] = term
-        else:
-            total[...] += term
+    total[...] = dot_nn(tokens_v[...], d_value[...])
     size = kept.shape[1]
     for high in range(2):
         for part, low in ((kept, bit[0, 0]), (given, 1 - bit[0, 0])):
@@ -449,6 +444,7 @@
     bits = n.bit_length() - 1
     gate_part = gate_term.reshape((2,) * bits + (D // n, D + LANES))
     for b in range(bits):
+        early = gate_part
         kept, given = halves(gate_part, bits - 1 - b, b)
         gate_part = added(kept, from_partner(given, b, n))
 
@@ -472,7 +468,7 @@
         ],
         compiler_params=params(),
         cost_estimate=cost(3.3, 17),
-    )(one_here, tokens_t, d_mix, first_t, skip, factor, me & 1, gate_part)
+    )(one_here, tokens_t, d_mix, first_t, skip, factor, me & 1, early)
 
     for b in reversed(range(bits)):
         gate_part = doubled(gate_part, bits - 1 - b, b, n)
@@ -503,12 +499,16 @@
         elif b > 1:
             kept, given = value_part, value_part
         got = from_partner(given, b, n)
-        if b < quarters:
-            grad_tokens = quarter(b, grad_tokens, given)
+        if 0 < b < quarters:
+            grad_tokens = quarter(b - 1, grad_tokens, given)
         value_part = added(kept, got)
+    grad_tokens = quarter(quarters - 1, grad_tokens, value_part)
     for b in (1, 0):
         value_part = doubled(value_part, 1 - b, b, n)
-    grad_weights = jnp.stack([value_part.reshape(D, D), gate_total[:, :D]]).astype(f32)
+    grad_weights = jnp.broadcast_to(gate_total[None, :, :D].astype(f32), (2, D, D))
+    grad_weights = lax.dynamic_update_slice(
+        grad_weights, value_part.reshape(1, D, D).astype(f32), (0, 0, 0)
+    )
     return grad_tokens, grad_kernel, grad_weights, gate_total[:, D].astype(f32)
 
 

time: 446 us -> 452 us (1.013)
  transfers between devices with their start and end apart: 18 -> 18, of which waited for: 12 -> 11; matrix products, arithmetic and copies ran while one was open for 2% -> 2% of each run, Pallas kernels for 20% -> 20%
where the time goes in v12:
time: 452 us; the launch traced here: 451 us
  waiting for transfers between devices  257 us (57%)
  Pallas kernels  96.7 us (21%)
  starting transfers between devices  84.7 us (19%)
  other arithmetic  7.53 us (2%)
    all_to_all x4, waiting for transfers between devices, transfer(): return lax.all_to_all(array, 'seq', split_axis=0, concat_axis=0, tiled=True)  175 us
    ppermute x14, waiting for transfers between devices, from_partner(): return lax.ppermute(array, 'seq', [(i, i ^ 1 << b) for i in range(n)])  81.4 us
    all_to_all x4, starting transfers between devices, transfer(): return lax.all_to_all(array, 'seq', split_axis=0, concat_axis=0, tiled=True)  66.8 us
    pallas_call x1, Pallas kernels, on_device(): pl.pallas_call(home_backward_kernel, grid=(chans // GROUP,), in_specs=[at...  20.6 us
    pallas_call x1, Pallas kernels, on_device(): pl.pallas_call(home_forward_kernel, grid=(chans // GROUP,), in_specs=[at_...  20.1 us
    ppermute x14, starting transfers between devices, from_partner(): return lax.ppermute(array, 'seq', [(i, i ^ 1 << b) for i in range(n)])  17.9 us
    pallas_call x1, Pallas kernels, on_device(): pl.pallas_call(d_three_kernel, grid=(rows // per,), in_specs=[row, row, s...  14.7 us
    pallas_call x4, Pallas kernels, quarter(): pl.pallas_call(tokens_kernel, grid=(steps,), in_specs=[lines, lines, squa...  12.3 us
  transfers between devices with their start and end apart: 18, of which 11 were waited for; matrix products, arithmetic and copies ran while one was open for 2% of the time, Pallas kernels for 20%

profile of v12, /device:TPU:0, one launch (start us, length us, event | category | flops | bytes accessed | tf_op | source)
XLA Modules:
  0.0 451.0 jit_solution(7522607320340653688)
XLA Ops:
  0.6 6.7 %shard_map.130 = bf16[16,16,32,256]{3,2,1,0:T(8,128)(2,1)} custom-call(bf16[4096,512]{1,0:T(8,128)(2,1)} %tokens.3, bf16[512,512]{1,0:T(8,128)(2,1)} %w_value.3, bf16[256,256]{1,0:T(8,128)(2,1)} %first.1), custom_call_target="tpu_custom_call" | custom-call | flops 3200000000 | bytes 9437184 | tf_op jit(solution)/shard_map/pallas_call | solution.py:361
  7.4 7.5 %all-to-all-start.1 = ((bf16[16,16,32,256]{3,2,1,0:T(8,128)(2,1)}), bf16[16,16,32,256]{3,2,1,0:T(8,128)(2,1)}, u32[]{:S(2)}, u32[]{:S(2)}) async-start(bf16[16,16,32,256]{3,2,1,0:T(8,128)(2,1)} %shard_map.130), calls=%async_computation.1 | async-start | bytes 8388608 | tf_op jit(solution)/shard_map/all_to_all | solution.py:358
  14.8 14.7 %shard_map.129 = (bf16[16,16,32,256]{3,2,1,0:T(8,128)(2,1)}, bf16[4096,512]{1,0:T(8,128)(2,1)}, bf16[4096,512]{1,0:T(8,128)(2,1)}, bf16[512,4096]{1,0:T(8,128)(2...) custom-call(bf16[4096,512]{1,0:T(8,128)(2,1)} %tokens.3, bf16[4096,512]{1,0:T(8,128)(2,1)} %cotangent.3, ...), custom_call_target="tpu_custom_call" | custom-call | flops 5400000000 | bytes 26214400 | tf_op jit(solution)/shard_map/pallas_call | solution.py:379
  29.5 63.0 %all-to-all-done.1 = bf16[16,16,32,256]{3,2,1,0:T(8,128)(2,1)} async-done(((bf16[16,16,32,256]{3,2,1,0:T(8,128)(2,1)}), bf16[16,16,32,256]{3,2,1,0:T(8,128)(2,1)}, u32[]{:S(2)}, u32[]{:S(2)}) %all-to-all-start.1) | async-done | bytes 4194336 | tf_op jit(solution)/shard_map/all_to_all | solution.py:358
  92.5 19.7 %all-to-all-start = ((bf16[16,16,32,256]{3,2,1,0:T(8,128)(2,1)}), bf16[16,16,32,256]{3,2,1,0:T(8,128)(2,1)}, u32[]{:S(2)}, u32[]{:S(2)}) async-start(bf16[16,16,32,256]{3,2,1,0:T(8,128)(2,1)} %get-tuple-element.20), calls=%async_computation | async-start | bytes 8388608 | tf_op jit(solution)/shard_map/all_to_all | solution.py:358
  113.0 20.1 %shard_map.131 = (bf16[256,32,256]{2,1,0:T(8,128)(2,1)}, f32[32,256,256]{2,1,0:T(8,128)}) custom-call(bf16[256,32,256]{2,1,0:T(8,128)(2,1)} %bitcast.1.arrived, bf16[32,256,256]{2,1,0:T(8,128)(2,1)} %kernel.3, bf16[256,256]{1,0:T(8,128)(2,1)} %second.1, bf16[256,256]{1,0:T(8,128)(2,1)} %third.1, bf16[256,256]{1,0:T(8,128)(2,1)} %fusion.12.swap), custom_call_target="tpu_custom_call" | custom-call | flops 4300000256 | bytes 20971520 | tf_op jit(solution)/shard_map/pallas_call | solution.py:400
  133.1 56.8 %all-to-all-done = bf16[16,16,32,256]{3,2,1,0:T(8,128)(2,1)} async-done(((bf16[16,16,32,256]{3,2,1,0:T(8,128)(2,1)}), bf16[16,16,32,256]{3,2,1,0:T(8,128)(2,1)}, u32[]{:S(2)}, u32[]{:S(2)}) %all-to-all-start) | async-done | bytes 4194336 | tf_op jit(solution)/shard_map/all_to_all | solution.py:358
  189.9 19.8 %all-to-all-start.3 = ((bf16[16,16,32,256]{3,2,1,0:T(8,128)(2,1)}), bf16[16,16,32,256]{3,2,1,0:T(8,128)(2,1)}, u32[]{:S(2)}, u32[]{:S(2)}) async-start(bf16[16,16,32,256]{3,2,1,0:T(8,128)(2,1)} %bitcast.57), calls=%async_computation.3 | async-start | bytes 8388608 | tf_op jit(solution)/shard_map/all_to_all | solution.py:358
  211.3 20.6 %shard_map.132 = (bf16[256,32,256]{2,1,0:T(8,128)(2,1)}, bf16[32,256,256]{2,1,0:T(8,128)(2,1)}) custom-call(bf16[256,32,256]{2,1,0:T(8,128)(2,1)} %bitcast.arrived, bf16[32,256,256]{2,1,0:T(8,128)(2,1)} %kernel.3, f32[32,256,256]{2,1,0:T(8,128)} %get-tuple-element.21.spectrum, bf16[256,256]{1,0:T(8,128)(2,1)} %bitcast.67, bf16[256,256]{1,0:T(8,128)(2,1)} %bitcast.68, ...), custom_call_target="tpu_custom_call" | custom-call | flops 4300000256 | bytes 25165824 | tf_op jit(solution)/shard_map/pallas_call | solution.py:412
  231.9 55.5 %all-to-all-done.3.arrived = bf16[16,16,32,256]{3,2,1,0:T(8,128)(2,1)} async-done(((bf16[16,16,32,256]{3,2,1,0:T(8,128)(2,1)}), bf16[16,16,32,256]{3,2,1,0:T(8,128)(2,1)}, u32[]{:S(2)}, u32[]{:S(2)}) %all-to-all-start.3) | async-done | bytes 4194336 | tf_op jit(solution)/shard_map/all_to_all | solution.py:358
  287.4 19.8 %all-to-all-start.2 = ((bf16[16,16,32,256]{3,2,1,0:T(8,128)(2,1)}), bf16[16,16,32,256]{3,2,1,0:T(8,128)(2,1)}, u32[]{:S(2)}, u32[]{:S(2)}) async-start(bf16[16,16,32,256]{3,2,1,0:T(8,128)(2,1)} %bitcast.56), calls=%async_computation.2 | async-start | bytes 8388608 | tf_op jit(solution)/shard_map/all_to_all | solution.py:358
  307.3 12.2 %shard_map.133 = (bf16[4096,512]{1,0:T(8,128)(2,1)}, bf16[512,512]{1,0:T(8,128)(2,1)}) custom-call(bf16[16,16,32,256]{3,2,1,0:T(8,128)(2,1)} %all-to-all-done.3.arrived, bf16[512,4096]{1,0:T(8,128)(2,1)} %get-tuple-element.23.tokens_t, bf16[4096,512]{1,0:T(8,128)(2,1)} %get-tuple-element.26.value, bf16[4096,512]{1,0:T(8,128)(2,1)} %cotangent.3, ...), custom_call_target="tpu_custom_call" | custom-call | flops 5400000000 | bytes 26214400 | tf_op jit(solution)/shard_map/pallas_call | solution.py:431
  324.7 12.6 %collective-permute-done.1 = bf16[2,2,32,640]{3,2,0,1:T(8,128)(2,1)S(1)} collective-permute-done((bf16[2,2,32,640]{3,2,0,1:T(8,128)(2,1)S(1)}, bf16[2,2,32,640]{3,2,0,1:T(8,128)(2,1)S(1)}, u32[]{:S(2)}, u32[]{:S(2)}) %collective-permute-start.1) | collective-permute-done | bytes 163872 | tf_op jit(solution)/shard_map/ppermute | solution.py:294
  337.5 40.1 %collective-permute-done.2 = bf16[2,32,640]{2,1,0:T(8,128)(2,1)S(1)} collective-permute-done((bf16[2,32,640]{2,1,0:T(8,128)(2,1)S(1)}, bf16[2,32,640]{2,1,0:T(8,128)(2,1)S(1)}, u32[]{:S(2)}, u32[]{:S(2)}) %collective-permute-start.2) | collective-permute-done | bytes 81952 | tf_op jit(solution)/shard_map/ppermute | solution.py:294
  377.6 4.6 %collective-permute-start.7 = (bf16[32,640]{1,0:T(8,128)(2,1)S(1)}, bf16[32,640]{1,0:T(8,128)(2,1)S(1)}, u32[]{:S(2)}, u32[]{:S(2)}) collective-permute-start(bf16[32,640]{1,0:T(8,128)(2,1)S(1)} %dynamic-slice_bitcast_fusion.3), channel_id=1, source_target_pairs={{0,8},{1,9},{2,10},{3,11},{4,12},{5,13},{6,14},{7,15},{8,0},{9,1},... | collective-permute-start | bytes 122888 | tf_op jit(solution)/shard_map/ppermute | solution.py:294
  383.0 20.0 %collective-permute-done.7 = bf16[32,640]{1,0:T(8,128)(2,1)S(1)} collective-permute-done((bf16[32,640]{1,0:T(8,128)(2,1)S(1)}, bf16[32,640]{1,0:T(8,128)(2,1)S(1)}, u32[]{:S(2)}, u32[]{:S(2)}) %collective-permute-start.7) | collective-permute-done | bytes 40992 | tf_op jit(solution)/shard_map/ppermute | solution.py:294
  403.1 10.0 %shard_map.134 = (bf16[2,128,512]{2,1,0:T(8,128)(2,1)}, bf16[2,128,512]{2,1,0:T(8,128)(2,1)}, bf16[4096,512]{1,0:T(8,128)(2,1)}) custom-call(bf16[16,16,32,256]{3,2,1,0:T(8,128)(2,1)} %all-to-all-done.2.arrived, bf16[512,4096]{1,0:T(8,128)(2,1)} %get-tuple-element.23.tokens_t, bf16[4096,512]{1,0:T(8,128)(2,1)} %get-tuple-element.24.d_mix, ...), custom_call_target="tpu_custom_call" | custom-call | flops 3300000000 | bytes 17825792 | tf_op jit(solution)/shard_map/pallas_call | solution.py:455
  420.0 2.8 collective-permute-done.4
  424.5 3.1 shard_map.135.rest_1_
  428.0 2.5 collective-permute-start.6
  430.7 3.1 shard_map.136.rest_1_
  433.8 3.1 shard_map.137.rest_1_
  440.0 3.8 collective-permute-done.12
  444.0 3.1 shard_map.138
  (80 shorter events, 24.7 us)
Async XLA Ops:
  7.4 85.1 %all-to-all-start.1 = ((bf16[16,16,32,256]{3,2,1,0:T(8,128)(2,1)}), bf16[16,16,32,256]{3,2,1,0:T(8,128)(2,1)}, u32[]{:S(2)}, u32[]{:S(2)}) async-start(bf16[16,16,32,256]{3,2,1,0:T(8,128)(2,1)} %shard_map.130), calls=%async_computation.1 | async-start | bytes 8388608 | tf_op jit(solution)/shard_map/all_to_all | solution.py:358
  92.5 97.4 %all-to-all-start = ((bf16[16,16,32,256]{3,2,1,0:T(8,128)(2,1)}), bf16[16,16,32,256]{3,2,1,0:T(8,128)(2,1)}, u32[]{:S(2)}, u32[]{:S(2)}) async-start(bf16[16,16,32,256]{3,2,1,0:T(8,128)(2,1)} %get-tuple-element.20), calls=%async_computation | async-start | bytes 8388608 | tf_op jit(solution)/shard_map/all_to_all | solution.py:358
  189.9 19.8 %copy-start.6 = (bf16[256,256]{1,0:T(8,128)(2,1)S(1)}, bf16[256,256]{1,0:T(8,128)(2,1)}, u32[]{:S(2)}) copy-start(bf16[256,256]{1,0:T(8,128)(2,1)} %second.1) | copy-start | bytes 393220
  189.9 20.6 %copy-start.7 = (bf16[256,256]{1,0:T(8,128)(2,1)S(1)}, bf16[256,256]{1,0:T(8,128)(2,1)}, u32[]{:S(2)}) copy-start(bf16[256,256]{1,0:T(8,128)(2,1)} %third.1) | copy-start | bytes 393220
  189.9 97.5 %all-to-all-start.3 = ((bf16[16,16,32,256]{3,2,1,0:T(8,128)(2,1)}), bf16[16,16,32,256]{3,2,1,0:T(8,128)(2,1)}, u32[]{:S(2)}, u32[]{:S(2)}) async-start(bf16[16,16,32,256]{3,2,1,0:T(8,128)(2,1)} %bitcast.57), calls=%async_computation.3 | async-start | bytes 8388608 | tf_op jit(solution)/shard_map/all_to_all | solution.py:358
  287.4 19.9 %copy-start.9 = (f32[1,512]{1,0:T(1,128)S(1)}, f32[1,512]{1,0:T(1,128)}, u32[]{:S(2)}) copy-start(f32[1,512]{1,0:T(1,128)} %get-tuple-element.29) | copy-start | bytes 6148
  287.4 115.7 %all-to-all-start.2 = ((bf16[16,16,32,256]{3,2,1,0:T(8,128)(2,1)}), bf16[16,16,32,256]{3,2,1,0:T(8,128)(2,1)}, u32[]{:S(2)}, u32[]{:S(2)}) async-start(bf16[16,16,32,256]{3,2,1,0:T(8,128)(2,1)} %bitcast.56), calls=%async_computation.2 | async-start | bytes 8388608 | tf_op jit(solution)/shard_map/all_to_all | solution.py:358
  319.5 62.7 %copy-start.8 = (bf16[256,256]{1,0:T(8,128)(2,1)S(1)}, bf16[256,256]{1,0:T(8,128)(2,1)}, u32[]{:S(2)}) copy-start(bf16[256,256]{1,0:T(8,128)(2,1)} %first.1) | copy-start | bytes 393220
  320.9 1.7 collective-permute-start
  322.7 14.6 %collective-permute-start.1 = (bf16[2,2,32,640]{3,2,0,1:T(8,128)(2,1)S(1)}, bf16[2,2,32,640]{3,2,0,1:T(8,128)(2,1)S(1)}, u32[]{:S(2)}, u32[]{:S(2)}) collective-permute-start(bf16[2,2,32,640]{3,2,0,1:T(8,128)(2,1)S(1)} %dynamic-slice_bitcast_fusion), channel_id=1, source_target_pairs={{0,2},{1,3},{2,0},{3,1},{4,6},{5,7},{6,4},{7,5},{8,10},{9,11},{10,... | collective-permute-start | bytes 491528 | tf_op jit(solution)/shard_map/ppermute | solution.py:294
  337.4 40.2 %collective-permute-start.2 = (bf16[2,32,640]{2,1,0:T(8,128)(2,1)S(1)}, bf16[2,32,640]{2,1,0:T(8,128)(2,1)S(1)}, u32[]{:S(2)}, u32[]{:S(2)}) collective-permute-start(bf16[2,32,640]{2,1,0:T(8,128)(2,1)S(1)} %dynamic-slice_bitcast_fusion.2), channel_id=1, source_target_pairs={{0,4},{1,5},{2,6},{3,7},{4,0},{5,1},{6,2},{7,3},{8,12},{9,13},{10,... | collective-permute-start | bytes 245768 | tf_op jit(solution)/shard_map/ppermute | solution.py:294
  377.6 25.5 %copy-start.4 = (bf16[2,32,640]{2,1,0:T(8,128)(2,1)}, bf16[2,32,640]{2,1,0:T(8,128)(2,1)S(1)}, u32[]{:S(2)}) copy-start(bf16[2,32,640]{2,1,0:T(8,128)(2,1)S(1)} %fusion.15._) | copy-start | bytes 245764
  377.6 25.4 %collective-permute-start.7 = (bf16[32,640]{1,0:T(8,128)(2,1)S(1)}, bf16[32,640]{1,0:T(8,128)(2,1)S(1)}, u32[]{:S(2)}, u32[]{:S(2)}) collective-permute-start(bf16[32,640]{1,0:T(8,128)(2,1)S(1)} %dynamic-slice_bitcast_fusion.3), channel_id=1, source_target_pairs={{0,8},{1,9},{2,10},{3,11},{4,12},{5,13},{6,14},{7,15},{8,0},{9,1},... | collective-permute-start | bytes 122888 | tf_op jit(solution)/shard_map/ppermute | solution.py:294
  403.0 10.2 %collective-permute-start.8 = (bf16[32,640]{1,0:T(8,128)(2,1)S(1)}, bf16[32,640]{1,0:T(8,128)(2,1)S(1)}, u32[]{:S(2)}, u32[]{:S(2)}) collective-permute-start(bf16[32,640]{1,0:T(8,128)(2,1)S(1)} %fusion.18), channel_id=1, source_target_pairs={{0,8},{1,9},{2,10},{3,11},{4,12},{5,13},{6,14},{7,15},{8,0},{9,1},... | collective-permute-start | bytes 122888 | tf_op jit(solution)/shard_map/ppermute | solution.py:294
  413.1 2.3 collective-permute-start.3
  413.2 5.1 %collective-permute-start.9 = (bf16[2,32,640]{2,1,0:T(8,128)(2,1)S(1)}, bf16[2,32,640]{2,1,0:T(8,128)(2,1)S(1)}, u32[]{:S(2)}, u32[]{:S(2)}) collective-permute-start(bf16[2,32,640]{2,1,0:T(8,128)(2,1)S(1)} %fusion.17), channel_id=1, source_target_pairs={{0,4},{1,5},{2,6},{3,7},{4,0},{5,1},{6,2},{7,3},{8,12},{9,13},{10,... | collective-permute-start | bytes 245768 | tf_op jit(solution)/shard_map/ppermute | solution.py:294
  416.4 8.1 %copy-start.5 = (bf16[128,512]{1,0:T(8,128)(2,1)}, bf16[128,512]{1,0:T(8,128)(2,1)S(1)}, u32[]{:S(2)}) copy-start(bf16[128,512]{1,0:T(8,128)(2,1)S(1)} %dynamic-slice_bitcast_fusion.1.rest_0_) | copy-start | bytes 393220
  416.4 6.4 %collective-permute-start.4 = (bf16[128,512]{1,0:T(8,128)(2,1)S(1)}, bf16[128,512]{1,0:T(8,128)(2,1)S(1)}, u32[]{:S(2)}, u32[]{:S(2)}) collective-permute-start(bf16[128,512]{1,0:T(8,128)(2,1)S(1)} %dynamic-slice_bitcast_fusion.1.rest_0_), channel_id=1, source_target_pairs={{0,2},{1,3},{2,0},{3,1},{4,6},{5,7},{6,4},{7,5},{8,10},{9,11},{10,... | collective-permute-start | bytes 393224 | tf_op jit(solution)/shard_map/ppermute | solution.py:294
  418.5 9.1 %collective-permute-start.10 = (bf16[2,2,32,640]{3,2,0,1:T(8,128)(2,1)S(1)}, bf16[2,2,32,640]{3,2,0,1:T(8,128)(2,1)S(1)}, u32[]{:S(2)}, u32[]{:S(2)}) collective-permute-start(bf16[2,2,32,640]{3,2,0,1:T(8,128)(2,1)S(1)} %fusion.14), channel_id=1, source_target_pairs={{0,2},{1,3},{2,0},{3,1},{4,6},{5,7},{6,4},{7,5},{8,10},{9,11},{10,... | collective-permute-start | bytes 491528 | tf_op jit(solution)/shard_map/ppermute | solution.py:294
  422.9 5.0 %collective-permute-start.5 = (bf16[128,512]{1,0:T(8,128)(2,1)S(1)}, bf16[128,512]{1,0:T(8,128)(2,1)S(1)}, u32[]{:S(2)}, u32[]{:S(2)}) collective-permute-start(bf16[128,512]{1,0:T(8,128)(2,1)S(1)} %fusion.11.rest_0_), channel_id=1, source_target_pairs={{0,4},{1,5},{2,6},{3,7},{4,0},{5,1},{6,2},{7,3},{8,12},{9,13},{10,... | collective-permute-start | bytes 393224 | tf_op jit(solution)/shard_map/ppermute | solution.py:294
  428.0 8.9 %collective-permute-start.6 = (bf16[128,512]{1,0:T(8,128)(2,1)S(1)}, bf16[128,512]{1,0:T(8,128)(2,1)S(1)}, u32[]{:S(2)}, u32[]{:S(2)}) collective-permute-start(bf16[128,512]{1,0:T(8,128)(2,1)S(1)} %add_convert_fusion.2.rest_0_), channel_id=1, source_target_pairs={{0,8},{1,9},{2,10},{3,11},{4,12},{5,13},{6,14},{7,15},{8,0},{9,1},... | collective-permute-start | bytes 393224 | tf_op jit(solution)/shard_map/ppermute | solution.py:294
  430.7 8.8 %collective-permute-start.11 = (bf16[2,2,2,32,640]{4,3,0,1,2:T(8,128)(2,1)S(1)}, bf16[2,2,2,32,640]{4,3,0,1,2:T(8,128)(2,1)S(1)}, u32[]{:S(2)}, u32[]{:S(2)}) collective-permute-start(bf16[2,2,2,32,640]{4,3,0,1,2:T(8,128)(2,1)S(1)} %fusion.7), channel_id=1, source_target_pairs={{0,1},{1,0},{2,3},{3,2},{4,5},{5,4},{6,7},{7,6},{8,9},{9,8},{10,11... | collective-permute-start | bytes 983048 | tf_op jit(solution)/shard_map/ppermute | solution.py:294
  437.8 5.9 %collective-permute-start.12 = (bf16[128,512]{1,0:T(8,128)(2,1)S(1)}, bf16[128,512]{1,0:T(8,128)(2,1)S(1)}, u32[]{:S(2)}, u32[]{:S(2)}) collective-permute-start(bf16[128,512]{1,0:T(8,128)(2,1)S(1)} %add_convert_fusion.1.rest_0_), channel_id=1, source_target_pairs={{0,2},{1,3},{2,0},{3,1},{4,6},{5,7},{6,4},{7,5},{8,10},{9,11},{10,... | collective-permute-start | bytes 393224 | tf_op jit(solution)/shard_map/ppermute | solution.py:294
  443.9 5.0 %collective-permute-start.13 = (bf16[2,128,512]{2,1,0:T(8,128)(2,1)S(1)}, bf16[2,128,512]{2,1,0:T(8,128)(2,1)S(1)}, u32[]{:S(2)}, u32[]{:S(2)}) collective-permute-start(bf16[2,128,512]{2,1,0:T(8,128)(2,1)S(1)} %fusion.10), channel_id=1, source_target_pairs={{0,1},{1,0},{2,3},{3,2},{4,5},{5,4},{6,7},{7,6},{8,9},{9,8},{10,11... | collective-permute-start | bytes 786440 | tf_op jit(solution)/shard_map/ppermute | solution.py:294
  (4 other events, 18.4 us)

commit v13 on v11

--- a/solution.py
+++ b/solution.py
@@ -72,11 +72,12 @@
     in_w.start()
     in_tokens[0].start()
     in_first.start()
-    for copy in in_tokens[1:]:
-        copy.start()
+    in_tokens[1].start()
     in_w.wait()
     for i in range(chunks):
         in_tokens[i].wait()
+        if i + 2 < chunks:
+            in_tokens[i + 2].start()
         value = dot_nn(tokens_v[i * per * N2 : (i + 1) * per * N2], w_v[...]).astype(bf16)
         if i == 0:
             in_first.wait()
@@ -227,10 +228,11 @@
     skip,
     factor,
     bit,
-    _,
+    gate_part,
     kept,
     given,
     d_value_out,
+    gate_out,
     arrived_v,
     tokens_v,
     d_mix_v,
@@ -238,9 +240,11 @@
     total,
     arrive,
     leave,
+    hand_on,
 ):
     rows = arrived.shape[1]
     chunks = rows // per
+    gate_copy = pltpu.make_async_copy(gate_part, gate_out, hand_on)
 
     def copies(i):
         lines = pl.ds(i * per, per)
@@ -256,13 +260,20 @@
         ]
 
     started = [copies(i) for i in range(chunks)]
-    for group in started:
-        for copy in group:
-            copy.start()
+
+    def start(i):
+        if i < chunks:
+            for copy in started[i]:
+                copy.start()
+
+    start(0)
+    start(1)
+    gate_copy.start()
     outs = []
     for i in range(chunks):
         started[i][0].wait()
         started[i][1].wait()
+        start(i + 2)
         for r in range(i * per, (i + 1) * per):
             here = row_slice(r)
             d_cube = dot_nt(first_t[...], arrived_v[:, r].reshape(D, N2))
@@ -280,10 +291,11 @@
     size = kept.shape[1]
     for high in range(2):
         for part, low in ((kept, bit[0, 0]), (given, 1 - bit[0, 0])):
-            start = pl.multiple_of((2 * high + low) * size, size)
-            part[high] = (total[pl.ds(start, size)] * factor[0, 0]).astype(bf16)
+            place = pl.multiple_of((2 * high + low) * size, size)
+            part[high] = (total[pl.ds(place, size)] * factor[0, 0]).astype(bf16)
     for copy in outs:
         copy.wait()
+    gate_copy.wait()
 
 
 def tokens_kernel(d_value, partial, w_value_t, *rest):
@@ -456,11 +468,11 @@
     in_vmem = pl.BlockSpec(memory_space=pltpu.VMEM)
     me = lax.axis_index("seq").reshape(1, 1)
     half = (2, D // 4, D)
-    kept, given, d_value = pl.pallas_call(
+    kept, given, d_value, gate_part = pl.pallas_call(
         functools.partial(value_kernel, per),
         in_specs=[unread, unread, unread, in_vmem, in_vmem, one, one, unread],
-        out_specs=[in_vmem, in_vmem, unread],
-        out_shape=[shape(half), shape(half), shape((local_rows, D))],
+        out_specs=[in_vmem, in_vmem, unread, unread],
+        out_shape=[shape(half), shape(half), shape((local_rows, D)), shape(gate_part.shape)],
         scratch_shapes=[
             pltpu.VMEM(sections, bf16),
             pltpu.VMEM((D, local_rows), bf16),
@@ -469,6 +481,7 @@
             pltpu.VMEM((D, D), f32),
             pltpu.SemaphoreType.DMA((rows // per, 3)),
             pltpu.SemaphoreType.DMA((rows // per,)),
+            pltpu.SemaphoreType.DMA,
         ],
         compiler_params=params(),
         cost_estimate=cost(3.3, 17),
@@ -478,22 +491,22 @@
         gate_part = doubled(gate_part, bits - 1 - b, b, n)
     gate_total = gate_part.reshape(D, D + LANES)
 
-    quarters = 4
-    pair = max(rows // quarters // 2, 1)
-    steps = rows // quarters // pair
-
-    def quarter(i, grad_tokens, after):
-        lines = pl.BlockSpec((pair * N2, D), lambda g: (g + i * steps, 0))
+    unit = rows // 8
+    pieces = [1, 2, 3, 2]
+
+    def piece(i, grad_tokens, after):
+        first = sum(pieces[:i])
+        lines = pl.BlockSpec((unit * N2, D), lambda g: (g + first, 0))
         held = [] if grad_tokens is None else [grad_tokens]
         return pl.pallas_call(
             tokens_kernel,
-            grid=(steps,),
+            grid=(pieces[i],),
             in_specs=[lines, lines, square, unread] + [unread] * len(held),
             out_specs=lines,
             out_shape=shape((local_rows, D)),
             input_output_aliases={4: 0} if held else {},
             compiler_params=params(),
-            cost_estimate=cost(0.53, 3.5),
+            cost_estimate=cost(0.265 * pieces[i], 1.5 * pieces[i]),
         )(d_value, partial, w_value_t, after, *held)
 
     grad_tokens = None
@@ -503,8 +516,8 @@
         elif b > 1:
             kept, given = value_part, value_part
         got = from_partner(given, b, n)
-        if b < quarters:
-            grad_tokens = quarter(b, grad_tokens, given)
+        if b < len(pieces):
+            grad_tokens = piece(b, grad_tokens, given)
         value_part = added(kept, got)
     for b in (1, 0):
         value_part = doubled(value_part, 1 - b, b, n)

time: 446 us -> 446 us (level)
  transfers between devices with their start and end apart: 18 -> 18, of which waited for: 12 -> 11; matrix products, arithmetic and copies ran while one was open for 2% -> 2% of each run, Pallas kernels for 20% -> 18%
where the time goes in v13:
time: 446 us
  waiting for transfers between devices  256 us (57%)
  Pallas kernels  96.6 us (22%)
  starting transfers between devices  82.3 us (18%)
  other arithmetic  6.6 us (1%)
    all_to_all x4, waiting for transfers between devices, transfer(): return lax.all_to_all(array, 'seq', split_axis=0, concat_axis=0, tiled=True)  175 us
    ppermute x14, waiting for transfers between devices, from_partner(): return lax.ppermute(array, 'seq', [(i, i ^ 1 << b) for i in range(n)])  81 us
    all_to_all x4, starting transfers between devices, transfer(): return lax.all_to_all(array, 'seq', split_axis=0, concat_axis=0, tiled=True)  66.8 us
    pallas_call x1, Pallas kernels, on_device(): pl.pallas_call(home_backward_kernel, grid=(chans // GROUP,), in_specs=[at...  20.6 us
    pallas_call x1, Pallas kernels, on_device(): pl.pallas_call(home_forward_kernel, grid=(chans // GROUP,), in_specs=[at_...  20.1 us
    ppermute x14, starting transfers between devices, from_partner(): return lax.ppermute(array, 'seq', [(i, i ^ 1 << b) for i in range(n)])  15.5 us
    pallas_call x1, Pallas kernels, on_device(): pl.pallas_call(d_three_kernel, grid=(rows // per,), in_specs=[row, row, s...  14.7 us
    pallas_call x4, Pallas kernels, piece(): pl.pallas_call(tokens_kernel, grid=(pieces[i],), in_specs=[lines, lines,...  13.6 us
  transfers between devices with their start and end apart: 18, of which 11 were waited for; matrix products, arithmetic and copies ran while one was open for 2% of the time, Pallas kernels for 18%

profile of v13, /device:TPU:0, one launch (start us, length us, event | category | flops | bytes accessed | tf_op | source)
XLA Modules:
  0.0 445.5 jit_solution(15818046327710106114)
XLA Ops:
  0.6 6.7 %shard_map.130 = bf16[16,16,32,256]{3,2,1,0:T(8,128)(2,1)} custom-call(bf16[4096,512]{1,0:T(8,128)(2,1)} %tokens.3, bf16[512,512]{1,0:T(8,128)(2,1)} %w_value.3, bf16[256,256]{1,0:T(8,128)(2,1)} %first.1), custom_call_target="tpu_custom_call" | custom-call | flops 3200000000 | bytes 9437184 | tf_op jit(solution)/shard_map/pallas_call | solution.py:378
  7.4 7.4 %all-to-all-start.1 = ((bf16[16,16,32,256]{3,2,1,0:T(8,128)(2,1)}), bf16[16,16,32,256]{3,2,1,0:T(8,128)(2,1)}, u32[]{:S(2)}, u32[]{:S(2)}) async-start(bf16[16,16,32,256]{3,2,1,0:T(8,128)(2,1)} %shard_map.130), calls=%async_computation.1 | async-start | bytes 8388608 | tf_op jit(solution)/shard_map/all_to_all | solution.py:375
  14.8 14.7 %shard_map.129 = (bf16[16,16,32,256]{3,2,1,0:T(8,128)(2,1)}, bf16[4096,512]{1,0:T(8,128)(2,1)}, bf16[4096,512]{1,0:T(8,128)(2,1)}, bf16[512,4096]{1,0:T(8,128)(2...) custom-call(bf16[4096,512]{1,0:T(8,128)(2,1)} %tokens.3, bf16[4096,512]{1,0:T(8,128)(2,1)} %cotangent.3, ...), custom_call_target="tpu_custom_call" | custom-call | flops 5400000000 | bytes 26214400 | tf_op jit(solution)/shard_map/pallas_call | solution.py:396
  29.5 63.0 %all-to-all-done.1 = bf16[16,16,32,256]{3,2,1,0:T(8,128)(2,1)} async-done(((bf16[16,16,32,256]{3,2,1,0:T(8,128)(2,1)}), bf16[16,16,32,256]{3,2,1,0:T(8,128)(2,1)}, u32[]{:S(2)}, u32[]{:S(2)}) %all-to-all-start.1) | async-done | bytes 4194336 | tf_op jit(solution)/shard_map/all_to_all | solution.py:375
  92.5 19.7 %all-to-all-start = ((bf16[16,16,32,256]{3,2,1,0:T(8,128)(2,1)}), bf16[16,16,32,256]{3,2,1,0:T(8,128)(2,1)}, u32[]{:S(2)}, u32[]{:S(2)}) async-start(bf16[16,16,32,256]{3,2,1,0:T(8,128)(2,1)} %get-tuple-element.21), calls=%async_computation | async-start | bytes 8388608 | tf_op jit(solution)/shard_map/all_to_all | solution.py:375
  113.0 20.1 %shard_map.131 = (bf16[256,32,256]{2,1,0:T(8,128)(2,1)}, f32[32,256,256]{2,1,0:T(8,128)}) custom-call(bf16[256,32,256]{2,1,0:T(8,128)(2,1)} %bitcast.1.arrived, bf16[32,256,256]{2,1,0:T(8,128)(2,1)} %kernel.3, bf16[256,256]{1,0:T(8,128)(2,1)} %second.1, bf16[256,256]{1,0:T(8,128)(2,1)} %third.1, bf16[256,256]{1,0:T(8,128)(2,1)} %fusion.11.swap), custom_call_target="tpu_custom_call" | custom-call | flops 4300000256 | bytes 20971520 | tf_op jit(solution)/shard_map/pallas_call | solution.py:417
  133.1 56.8 %all-to-all-done = bf16[16,16,32,256]{3,2,1,0:T(8,128)(2,1)} async-done(((bf16[16,16,32,256]{3,2,1,0:T(8,128)(2,1)}), bf16[16,16,32,256]{3,2,1,0:T(8,128)(2,1)}, u32[]{:S(2)}, u32[]{:S(2)}) %all-to-all-start) | async-done | bytes 4194336 | tf_op jit(solution)/shard_map/all_to_all | solution.py:375
  189.9 19.8 %all-to-all-start.3 = ((bf16[16,16,32,256]{3,2,1,0:T(8,128)(2,1)}), bf16[16,16,32,256]{3,2,1,0:T(8,128)(2,1)}, u32[]{:S(2)}, u32[]{:S(2)}) async-start(bf16[16,16,32,256]{3,2,1,0:T(8,128)(2,1)} %bitcast.59), calls=%async_computation.3 | async-start | bytes 8388608 | tf_op jit(solution)/shard_map/all_to_all | solution.py:375
  211.2 20.6 %shard_map.132 = (bf16[256,32,256]{2,1,0:T(8,128)(2,1)}, bf16[32,256,256]{2,1,0:T(8,128)(2,1)}) custom-call(bf16[256,32,256]{2,1,0:T(8,128)(2,1)} %bitcast.arrived, bf16[32,256,256]{2,1,0:T(8,128)(2,1)} %kernel.3, f32[32,256,256]{2,1,0:T(8,128)} %get-tuple-element.22.spectrum, bf16[256,256]{1,0:T(8,128)(2,1)} %bitcast.69, bf16[256,256]{1,0:T(8,128)(2,1)} %bitcast.70, ...), custom_call_target="tpu_custom_call" | custom-call | flops 4300000256 | bytes 25165824 | tf_op jit(solution)/shard_map/pallas_call | solution.py:429
  231.9 55.5 %all-to-all-done.3.arrived = bf16[16,16,32,256]{3,2,1,0:T(8,128)(2,1)} async-done(((bf16[16,16,32,256]{3,2,1,0:T(8,128)(2,1)}), bf16[16,16,32,256]{3,2,1,0:T(8,128)(2,1)}, u32[]{:S(2)}, u32[]{:S(2)}) %all-to-all-start.3) | async-done | bytes 4194336 | tf_op jit(solution)/shard_map/all_to_all | solution.py:375
  287.4 19.8 %all-to-all-start.2 = ((bf16[16,16,32,256]{3,2,1,0:T(8,128)(2,1)}), bf16[16,16,32,256]{3,2,1,0:T(8,128)(2,1)}, u32[]{:S(2)}, u32[]{:S(2)}) async-start(bf16[16,16,32,256]{3,2,1,0:T(8,128)(2,1)} %bitcast.58), calls=%async_computation.2 | async-start | bytes 8388608 | tf_op jit(solution)/shard_map/all_to_all | solution.py:375
  307.3 12.3 %shard_map.133 = (bf16[4096,512]{1,0:T(8,128)(2,1)}, bf16[512,512]{1,0:T(8,128)(2,1)}) custom-call(bf16[16,16,32,256]{3,2,1,0:T(8,128)(2,1)} %all-to-all-done.3.arrived, bf16[512,4096]{1,0:T(8,128)(2,1)} %get-tuple-element.24.tokens_t, bf16[4096,512]{1,0:T(8,128)(2,1)} %get-tuple-element.27.value, bf16[4096,512]{1,0:T(8,128)(2,1)} %cotangent.3, ...), custom_call_target="tpu_custom_call" | custom-call | flops 5400000000 | bytes 26214400 | tf_op jit(solution)/shard_map/pallas_call | solution.py:448
  324.7 12.6 %collective-permute-done.1 = bf16[2,2,32,640]{3,2,0,1:T(8,128)(2,1)S(1)} collective-permute-done((bf16[2,2,32,640]{3,2,0,1:T(8,128)(2,1)S(1)}, bf16[2,2,32,640]{3,2,0,1:T(8,128)(2,1)S(1)}, u32[]{:S(2)}, u32[]{:S(2)}) %collective-permute-start.1) | collective-permute-done | bytes 163872 | tf_op jit(solution)/shard_map/ppermute | solution.py:311
  337.5 40.1 %collective-permute-done.2 = bf16[2,32,640]{2,1,0:T(8,128)(2,1)S(1)} collective-permute-done((bf16[2,32,640]{2,1,0:T(8,128)(2,1)S(1)}, bf16[2,32,640]{2,1,0:T(8,128)(2,1)S(1)}, u32[]{:S(2)}, u32[]{:S(2)}) %collective-permute-start.2) | collective-permute-done | bytes 81952 | tf_op jit(solution)/shard_map/ppermute | solution.py:311
  377.6 4.6 %collective-permute-start.3 = (bf16[32,640]{1,0:T(8,128)(2,1)S(1)}, bf16[32,640]{1,0:T(8,128)(2,1)S(1)}, u32[]{:S(2)}, u32[]{:S(2)}) collective-permute-start(bf16[32,640]{1,0:T(8,128)(2,1)S(1)} %dynamic-slice_bitcast_fusion.3), channel_id=1, source_target_pairs={{0,8},{1,9},{2,10},{3,11},{4,12},{5,13},{6,14},{7,15},{8,0},{9,1},... | collective-permute-start | bytes 122888 | tf_op jit(solution)/shard_map/ppermute | solution.py:311
  382.9 20.0 %collective-permute-done.3 = bf16[32,640]{1,0:T(8,128)(2,1)S(1)} collective-permute-done((bf16[32,640]{1,0:T(8,128)(2,1)S(1)}, bf16[32,640]{1,0:T(8,128)(2,1)S(1)}, u32[]{:S(2)}, u32[]{:S(2)}) %collective-permute-start.3) | collective-permute-done | bytes 40992 | tf_op jit(solution)/shard_map/ppermute | solution.py:311
  403.6 8.5 %shard_map.134 = (bf16[2,128,512]{2,1,0:T(8,128)(2,1)}, bf16[2,128,512]{2,1,0:T(8,128)(2,1)}, bf16[4096,512]{1,0:T(8,128)(2,1)}, bf16[32,640]{1,0:T(8,128)(2,1)}) custom-call(bf16[16,16,32,256]{3,2,1,0:T(8,128)(2,1)} %all-to-all-done.2.arrived, bf16[512,4096]{1,0:T(8,128)(2,1)} %get-tuple-element.24.tokens_t, bf16[4096,512]{1,0:T(8,128)(2,1)} %get-tuple-element.25.d_mix, ...), custom_call_target="tpu_custom_call" | custom-call | flops 3300000000 | bytes 17825792 | tf_op jit(solution)/shard_map/pallas_call | solution.py:471
  412.6 2.6 shard_map.135.rest_1_
  415.2 2.1 collective-permute-done.10
  419.2 2.7 collective-permute-done.11
  423.7 2.2 collective-permute-start.6
  425.9 3.2 shard_map.136.rest_1_
  430.4 4.7 %shard_map.137.rest_1_ = bf16[4096,512]{1,0:T(8,128)(2,1)} custom-call(bf16[4096,512]{1,0:T(8,128)(2,1)} %get-tuple-element.31.d_value, bf16[4096,512]{1,0:T(8,128)(2,1)} %get-tuple-element.32.partial, bf16[512,512]{1,0:T(8,128)(2,1)} %get-tuple-element.33.w_value_t, bf16[128,512]{1,0:T(8,128)(2,1)} %copy-done.1, ...), custom_call_target="tpu_custom_call", output_to_operand_aliasing={{}: (4, {})} | custom-call | flops 795000000 | bytes 4718592 | tf_op jit(solution)/shard_map/pallas_call | solution.py:501
  438.4 3.1 shard_map.138
  (77 shorter events, 21.6 us)
Async XLA Ops:
  7.4 85.1 %all-to-all-start.1 = ((bf16[16,16,32,256]{3,2,1,0:T(8,128)(2,1)}), bf16[16,16,32,256]{3,2,1,0:T(8,128)(2,1)}, u32[]{:S(2)}, u32[]{:S(2)}) async-start(bf16[16,16,32,256]{3,2,1,0:T(8,128)(2,1)} %shard_map.130), calls=%async_computation.1 | async-start | bytes 8388608 | tf_op jit(solution)/shard_map/all_to_all | solution.py:375
  92.5 97.4 %all-to-all-start = ((bf16[16,16,32,256]{3,2,1,0:T(8,128)(2,1)}), bf16[16,16,32,256]{3,2,1,0:T(8,128)(2,1)}, u32[]{:S(2)}, u32[]{:S(2)}) async-start(bf16[16,16,32,256]{3,2,1,0:T(8,128)(2,1)} %get-tuple-element.21), calls=%async_computation | async-start | bytes 8388608 | tf_op jit(solution)/shard_map/all_to_all | solution.py:375
  189.9 19.8 %copy-start.5 = (bf16[256,256]{1,0:T(8,128)(2,1)S(1)}, bf16[256,256]{1,0:T(8,128)(2,1)}, u32[]{:S(2)}) copy-start(bf16[256,256]{1,0:T(8,128)(2,1)} %second.1) | copy-start | bytes 393220
  189.9 20.6 %copy-start.6 = (bf16[256,256]{1,0:T(8,128)(2,1)S(1)}, bf16[256,256]{1,0:T(8,128)(2,1)}, u32[]{:S(2)}) copy-start(bf16[256,256]{1,0:T(8,128)(2,1)} %third.1) | copy-start | bytes 393220
  189.9 97.5 %all-to-all-start.3 = ((bf16[16,16,32,256]{3,2,1,0:T(8,128)(2,1)}), bf16[16,16,32,256]{3,2,1,0:T(8,128)(2,1)}, u32[]{:S(2)}, u32[]{:S(2)}) async-start(bf16[16,16,32,256]{3,2,1,0:T(8,128)(2,1)} %bitcast.59), calls=%async_computation.3 | async-start | bytes 8388608 | tf_op jit(solution)/shard_map/all_to_all | solution.py:375
  287.4 19.9 %copy-start.8 = (f32[1,512]{1,0:T(1,128)S(1)}, f32[1,512]{1,0:T(1,128)}, u32[]{:S(2)}) copy-start(f32[1,512]{1,0:T(1,128)} %get-tuple-element.30) | copy-start | bytes 6148
  287.4 116.2 %all-to-all-start.2 = ((bf16[16,16,32,256]{3,2,1,0:T(8,128)(2,1)}), bf16[16,16,32,256]{3,2,1,0:T(8,128)(2,1)}, u32[]{:S(2)}, u32[]{:S(2)}) async-start(bf16[16,16,32,256]{3,2,1,0:T(8,128)(2,1)} %bitcast.58), calls=%async_computation.2 | async-start | bytes 8388608 | tf_op jit(solution)/shard_map/all_to_all | solution.py:375
  319.6 62.6 %copy-start.7 = (bf16[256,256]{1,0:T(8,128)(2,1)S(1)}, bf16[256,256]{1,0:T(8,128)(2,1)}, u32[]{:S(2)}) copy-start(bf16[256,256]{1,0:T(8,128)(2,1)} %first.1) | copy-start | bytes 393220
  321.0 1.7 collective-permute-start
  322.8 14.5 %collective-permute-start.1 = (bf16[2,2,32,640]{3,2,0,1:T(8,128)(2,1)S(1)}, bf16[2,2,32,640]{3,2,0,1:T(8,128)(2,1)S(1)}, u32[]{:S(2)}, u32[]{:S(2)}) collective-permute-start(bf16[2,2,32,640]{3,2,0,1:T(8,128)(2,1)S(1)} %dynamic-slice_bitcast_fusion), channel_id=1, source_target_pairs={{0,2},{1,3},{2,0},{3,1},{4,6},{5,7},{6,4},{7,5},{8,10},{9,11},{10,... | collective-permute-start | bytes 491528 | tf_op jit(solution)/shard_map/ppermute | solution.py:311
  337.4 40.2 %collective-permute-start.2 = (bf16[2,32,640]{2,1,0:T(8,128)(2,1)S(1)}, bf16[2,32,640]{2,1,0:T(8,128)(2,1)S(1)}, u32[]{:S(2)}, u32[]{:S(2)}) collective-permute-start(bf16[2,32,640]{2,1,0:T(8,128)(2,1)S(1)} %dynamic-slice_bitcast_fusion.2), channel_id=1, source_target_pairs={{0,4},{1,5},{2,6},{3,7},{4,0},{5,1},{6,2},{7,3},{8,12},{9,13},{10,... | collective-permute-start | bytes 245768 | tf_op jit(solution)/shard_map/ppermute | solution.py:311
  377.6 25.4 %collective-permute-start.3 = (bf16[32,640]{1,0:T(8,128)(2,1)S(1)}, bf16[32,640]{1,0:T(8,128)(2,1)S(1)}, u32[]{:S(2)}, u32[]{:S(2)}) collective-permute-start(bf16[32,640]{1,0:T(8,128)(2,1)S(1)} %dynamic-slice_bitcast_fusion.3), channel_id=1, source_target_pairs={{0,8},{1,9},{2,10},{3,11},{4,12},{5,13},{6,14},{7,15},{8,0},{9,1},... | collective-permute-start | bytes 122888 | tf_op jit(solution)/shard_map/ppermute | solution.py:311
  412.1 5.2 %collective-permute-start.10 = (bf16[32,640]{1,0:T(8,128)(2,1)}, bf16[32,640]{1,0:T(8,128)(2,1)S(1)}, u32[]{:S(2)}, u32[]{:S(2)}) collective-permute-start(bf16[32,640]{1,0:T(8,128)(2,1)} %get-tuple-element.37), channel_id=1, source_target_pairs={{0,8},{1,9},{2,10},{3,11},{4,12},{5,13},{6,14},{7,15},{8,0},{9,1},... | collective-permute-start | bytes 122888 | tf_op jit(solution)/shard_map/ppermute | solution.py:311
  412.6 4.9 %collective-permute-start.4 = (bf16[2,128,512]{2,1,0:T(8,128)(2,1)}, bf16[2,128,512]{2,1,0:T(8,128)(2,1)S(1)}, u32[]{:S(2)}, u32[]{:S(2)}) collective-permute-start(bf16[2,128,512]{2,1,0:T(8,128)(2,1)} %get-tuple-element.35.rest_0_), channel_id=1, source_target_pairs={{0,1},{1,0},{2,3},{3,2},{4,5},{5,4},{6,7},{7,6},{8,9},{9,8},{10,11... | collective-permute-start | bytes 786440 | tf_op jit(solution)/shard_map/ppermute | solution.py:311
  417.3 4.5 %collective-permute-start.11 = (bf16[2,32,640]{2,1,0:T(8,128)(2,1)S(1)}, bf16[2,32,640]{2,1,0:T(8,128)(2,1)S(1)}, u32[]{:S(2)}, u32[]{:S(2)}) collective-permute-start(bf16[2,32,640]{2,1,0:T(8,128)(2,1)S(1)} %fusion.16), channel_id=1, source_target_pairs={{0,4},{1,5},{2,6},{3,7},{4,0},{5,1},{6,2},{7,3},{8,12},{9,13},{10,... | collective-permute-start | bytes 245768 | tf_op jit(solution)/shard_map/ppermute | solution.py:311
  417.6 8.3 %copy-start.2 = (bf16[128,512]{1,0:T(8,128)(2,1)}, bf16[128,512]{1,0:T(8,128)(2,1)S(1)}, u32[]{:S(2)}) copy-start(bf16[128,512]{1,0:T(8,128)(2,1)S(1)} %dynamic-slice_bitcast_fusion.1.rest_0_) | copy-start | bytes 393220
  417.6 6.0 %collective-permute-start.5 = (bf16[128,512]{1,0:T(8,128)(2,1)S(1)}, bf16[128,512]{1,0:T(8,128)(2,1)S(1)}, u32[]{:S(2)}, u32[]{:S(2)}) collective-permute-start(bf16[128,512]{1,0:T(8,128)(2,1)S(1)} %dynamic-slice_bitcast_fusion.1.rest_0_), channel_id=1, source_target_pairs={{0,2},{1,3},{2,0},{3,1},{4,6},{5,7},{6,4},{7,5},{8,10},{9,11},{10,... | collective-permute-start | bytes 393224 | tf_op jit(solution)/shard_map/ppermute | solution.py:311
  421.9 7.1 %collective-permute-start.12 = (bf16[2,2,32,640]{3,2,0,1:T(8,128)(2,1)S(1)}, bf16[2,2,32,640]{3,2,0,1:T(8,128)(2,1)S(1)}, u32[]{:S(2)}, u32[]{:S(2)}) collective-permute-start(bf16[2,2,32,640]{3,2,0,1:T(8,128)(2,1)S(1)} %fusion.13), channel_id=1, source_target_pairs={{0,2},{1,3},{2,0},{3,1},{4,6},{5,7},{6,4},{7,5},{8,10},{9,11},{10,... | collective-permute-start | bytes 491528 | tf_op jit(solution)/shard_map/ppermute | solution.py:311
  423.7 5.6 %collective-permute-start.6 = (bf16[128,512]{1,0:T(8,128)(2,1)S(1)}, bf16[128,512]{1,0:T(8,128)(2,1)S(1)}, u32[]{:S(2)}, u32[]{:S(2)}) collective-permute-start(bf16[128,512]{1,0:T(8,128)(2,1)S(1)} %fusion.10.rest_0_), channel_id=1, source_target_pairs={{0,4},{1,5},{2,6},{3,7},{4,0},{5,1},{6,2},{7,3},{8,12},{9,13},{10,... | collective-permute-start | bytes 393224 | tf_op jit(solution)/shard_map/ppermute | solution.py:311
  429.3 7.3 %copy-start = (bf16[128,512]{1,0:T(8,128)(2,1)}, bf16[128,512]{1,0:T(8,128)(2,1)S(1)}, u32[]{:S(2)}) copy-start(bf16[128,512]{1,0:T(8,128)(2,1)S(1)} %add_convert_fusion.2.rest_0_) | copy-start | bytes 393220
  429.4 7.3 %collective-permute-start.7 = (bf16[128,512]{1,0:T(8,128)(2,1)S(1)}, bf16[128,512]{1,0:T(8,128)(2,1)S(1)}, u32[]{:S(2)}, u32[]{:S(2)}) collective-permute-start(bf16[128,512]{1,0:T(8,128)(2,1)S(1)} %add_convert_fusion.2.rest_0_), channel_id=1, source_target_pairs={{0,8},{1,9},{2,10},{3,11},{4,12},{5,13},{6,14},{7,15},{8,0},{9,1},... | collective-permute-start | bytes 393224 | tf_op jit(solution)/shard_map/ppermute | solution.py:311
  430.3 11.2 %collective-permute-start.13 = (bf16[2,2,2,32,640]{4,3,0,1,2:T(8,128)(2,1)S(1)}, bf16[2,2,2,32,640]{4,3,0,1,2:T(8,128)(2,1)S(1)}, u32[]{:S(2)}, u32[]{:S(2)}) collective-permute-start(bf16[2,2,2,32,640]{4,3,0,1,2:T(8,128)(2,1)S(1)} %fusion.6), channel_id=1, source_target_pairs={{0,1},{1,0},{2,3},{3,2},{4,5},{5,4},{6,7},{7,6},{8,9},{9,8},{10,11... | collective-permute-start | bytes 983048 | tf_op jit(solution)/shard_map/ppermute | solution.py:311
  436.7 5.2 %collective-permute-start.8 = (bf16[128,512]{1,0:T(8,128)(2,1)S(1)}, bf16[128,512]{1,0:T(8,128)(2,1)S(1)}, u32[]{:S(2)}, u32[]{:S(2)}) collective-permute-start(bf16[128,512]{1,0:T(8,128)(2,1)S(1)} %add_convert_fusion.1), channel_id=1, source_target_pairs={{0,2},{1,3},{2,0},{3,1},{4,6},{5,7},{6,4},{7,5},{8,10},{9,11},{10,... | collective-permute-start | bytes 393224 | tf_op jit(solution)/shard_map/ppermute | solution.py:311
  442.1 1.6 collective-permute-start.9
  (3 other events, 15.2 us)

commit v14 on v11

--- a/solution.py
+++ b/solution.py
@@ -94,11 +94,15 @@
     cotangent,
     w_value,
     w_gate,
+    first,
     fourth,
+    skip,
     out,
     value_out,
     d_mix_out,
     tokens_t_out,
+    turned_out,
+    direct_out,
     skip_out,
     w_value_t,
     w_gate_t,
@@ -108,6 +112,7 @@
     @pl.when(pl.program_id(0) == 0)
     def _():
         skip_out[...] = jnp.zeros_like(skip_out)
+        direct_out[...] = jnp.zeros_like(direct_out)
         w_value_t[...] = w_value[...].T
         w_gate_t[...] = w_gate[...].T
 
@@ -119,11 +124,17 @@
         value_out[here] = value
         d_mix_out[here] = d_mix
         tokens_t_out[:, here] = tokens[here].T
+        turned_out[here] = dot_nn(first[...], tokens[here]).astype(bf16)
         skip_out[...] += jnp.sum(
             d_mix.astype(f32) * value.astype(f32), axis=0, keepdims=True
         )
         section = dot_nn(d_mix.T, fourth[...]).astype(bf16)
         out[:, r] = section.reshape(n, chans, N2)
+    direct_out[...] += dot_nn(tokens_t_out[...], d_mix_out[...])
+
+    @pl.when(pl.program_id(0) == pl.num_programs(0) - 1)
+    def _():
+        direct_out[...] = direct_out[...] * skip[...]
 
 
 def turn_in(swap, arrived, by_channel):
@@ -199,8 +210,10 @@
     tokens_t,
     value,
     cotangent,
+    d_mix,
     fourth,
     w_gate_t,
+    w_value_t,
     skip,
     factor,
     partial,
@@ -213,7 +226,10 @@
         conv = dot_nt(fourth[...], arrived[:, r].reshape(D, N2))
         mixed = conv + skip[...] * value[here].astype(f32)
         d_gate[here] = (cotangent[here].astype(f32) * mixed).astype(bf16)
-        partial[here] = dot_nn(d_gate[here], w_gate_t[...]).astype(bf16)
+        direct = (skip[...] * d_mix[here].astype(f32)).astype(bf16)
+        partial[here] = (
+            dot_nn(d_gate[here], w_gate_t[...]) + dot_nn(direct, w_value_t[...])
+        ).astype(bf16)
     accumulate(total, dot_nn(tokens_t[...], d_gate[...]))
     finish(total, factor, grad_w)
 
@@ -221,26 +237,22 @@
 def value_kernel(
     per,
     arrived,
-    tokens_t,
-    d_mix,
-    first_t,
-    skip,
+    turned,
+    direct,
     factor,
     bit,
     _,
     kept,
     given,
-    d_value_out,
     arrived_v,
-    tokens_v,
-    d_mix_v,
-    d_value,
+    turned_v,
+    direct_v,
     total,
     arrive,
-    leave,
 ):
     rows = arrived.shape[1]
     chunks = rows // per
+    in_direct = pltpu.make_async_copy(direct, direct_v, arrive.at[chunks, 0])
 
     def copies(i):
         lines = pl.ds(i * per, per)
@@ -249,49 +261,41 @@
             pltpu.make_async_copy(
                 arrived.at[:, lines], arrived_v.at[:, lines], arrive.at[i, 0]
             ),
-            pltpu.make_async_copy(d_mix.at[here], d_mix_v.at[here], arrive.at[i, 1]),
-            pltpu.make_async_copy(
-                tokens_t.at[:, here], tokens_v.at[:, here], arrive.at[i, 2]
-            ),
+            pltpu.make_async_copy(turned.at[here], turned_v.at[here], arrive.at[i, 1]),
         ]
 
     started = [copies(i) for i in range(chunks)]
     for group in started:
         for copy in group:
             copy.start()
-    outs = []
+    in_direct.start()
     for i in range(chunks):
-        started[i][0].wait()
-        started[i][1].wait()
-        for r in range(i * per, (i + 1) * per):
-            here = row_slice(r)
-            d_cube = dot_nt(first_t[...], arrived_v[:, r].reshape(D, N2))
-            d_value[here] = (d_cube + skip[...] * d_mix_v[here].astype(f32)).astype(bf16)
-        here = pl.ds(i * per * N2, per * N2)
-        outs.append(pltpu.make_async_copy(d_value.at[here], d_value_out.at[here], leave.at[i]))
-        outs[i].start()
-        started[i][2].wait()
-        here = slice(i * per * N2, (i + 1) * per * N2)
-        term = dot_nn(tokens_v[:, here], d_value[here])
+        for copy in started[i]:
+            copy.wait()
+        side = jnp.concatenate(
+            [arrived_v[:, r].reshape(D, N2) for r in range(i * per, (i + 1) * per)], axis=1
+        )
+        term = dot_nn(side, turned_v[i * per * N2 : (i + 1) * per * N2])
         if i == 0:
             total[...] = term
         else:
             total[...] += term
+    in_direct.wait()
     size = kept.shape[1]
+    total[...] = total[...].T
     for high in range(2):
         for part, low in ((kept, bit[0, 0]), (given, 1 - bit[0, 0])):
-            start = pl.multiple_of((2 * high + low) * size, size)
-            part[high] = (total[pl.ds(start, size)] * factor[0, 0]).astype(bf16)
-    for copy in outs:
-        copy.wait()
-
-
-def tokens_kernel(d_value, partial, w_value_t, *rest):
+            place = pl.ds(pl.multiple_of((2 * high + low) * size, size), size)
+            part[high] = ((total[place] + direct_v[place]) * factor[0, 0]).astype(bf16)
+
+
+def tokens_kernel(arrived, partial, first_t, w_value_t, *rest):
     grad_tokens = rest[-1]
-    for r in range(d_value.shape[0] // N2):
+    for r in range(arrived.shape[1]):
         here = row_slice(r)
+        d_cube = dot_nt(first_t[...], arrived[:, r].reshape(D, N2)).astype(bf16)
         grad_tokens[here] = (
-            partial[here].astype(f32) + dot_nn(d_value[here], w_value_t[...])
+            partial[here].astype(f32) + dot_nn(d_cube, w_value_t[...])
         ).astype(bf16)
 
 
@@ -381,23 +385,25 @@
     )(tokens, w_value, first_block)
     one_home = transfer(one_sent)
 
-    three_sent, value, d_mix, tokens_t, skip_term, w_value_t, w_gate_t = pl.pallas_call(
+    three_sent, value, d_mix, tokens_t, turned, direct, skip_term, w_value_t, w_gate_t = pl.pallas_call(
         d_three_kernel,
         grid=(rows // per,),
-        in_specs=[row, row, square, square, block],
-        out_specs=[sent, row, row, column, line, square, square],
+        in_specs=[row, row, square, square, block, block, line],
+        out_specs=[sent, row, row, column, row, square, line, square, square],
         out_shape=[
             shape(sections),
             shape((local_rows, D)),
             shape((local_rows, D)),
             shape((D, local_rows)),
+            shape((local_rows, D)),
+            shape((D, D), f32),
             shape((1, D), f32),
             shape((D, D)),
             shape((D, D)),
         ],
         compiler_params=params(),
-        cost_estimate=cost(5.4, 25),
-    )(tokens, cotangent, w_value, w_gate, fourth_block)
+        cost_estimate=cost(8.6, 30),
+    )(tokens, cotangent, w_value, w_gate, first_block, fourth_block, skip)
     three_home = transfer(three_sent)
 
     at_home = pl.BlockSpec((N1, GROUP, N2), lambda i: (0, i, 0))
@@ -436,13 +442,24 @@
     partial, gate_term = pl.pallas_call(
         gate_kernel,
         grid=(rows // per,),
-        in_specs=[sent, column, row, row, block, square, line, one],
+        in_specs=[sent, column, row, row, row, block, square, square, line, one],
         out_specs=[row, square],
         out_shape=[shape((local_rows, D)), shape((D, D))],
         scratch_shapes=[pltpu.VMEM((D, D), f32), pltpu.VMEM((per * N2, D), bf16)],
         compiler_params=params(),
         cost_estimate=cost(5.4, 25),
-    )(three_here, tokens_t, value, cotangent, fourth_block, w_gate_t, skip, factor)
+    )(
+        three_here,
+        tokens_t,
+        value,
+        cotangent,
+        d_mix,
+        fourth_block,
+        w_gate_t,
+        w_value_t,
+        skip,
+        factor,
+    )
 
     skip_lanes = jnp.broadcast_to((skip_term * factor[0, 0]).astype(bf16).T, (D, LANES))
     gate_term = jnp.concatenate([gate_term, skip_lanes], axis=1)
@@ -456,45 +473,50 @@
     in_vmem = pl.BlockSpec(memory_space=pltpu.VMEM)
     me = lax.axis_index("seq").reshape(1, 1)
     half = (2, D // 4, D)
-    kept, given, d_value = pl.pallas_call(
+    kept, given = pl.pallas_call(
         functools.partial(value_kernel, per),
-        in_specs=[unread, unread, unread, in_vmem, in_vmem, one, one, unread],
-        out_specs=[in_vmem, in_vmem, unread],
-        out_shape=[shape(half), shape(half), shape((local_rows, D))],
+        in_specs=[unread, unread, unread, one, one, unread],
+        out_specs=[in_vmem, in_vmem],
+        out_shape=[shape(half), shape(half)],
         scratch_shapes=[
             pltpu.VMEM(sections, bf16),
-            pltpu.VMEM((D, local_rows), bf16),
-            pltpu.VMEM((local_rows, D), bf16),
             pltpu.VMEM((local_rows, D), bf16),
             pltpu.VMEM((D, D), f32),
-            pltpu.SemaphoreType.DMA((rows // per, 3)),
-            pltpu.SemaphoreType.DMA((rows // per,)),
+            pltpu.VMEM((D, D), f32),
+            pltpu.SemaphoreType.DMA((rows // per + 1, 2)),
         ],
         compiler_params=params(),
-        cost_estimate=cost(3.3, 17),
-    )(one_here, tokens_t, d_mix, first_t, skip, factor, me & 1, gate_part)
+        cost_estimate=cost(2.2, 9.5),
+    )(one_here, turned, direct, factor, me & 1, gate_part)
 
     for b in reversed(range(bits)):
         gate_part = doubled(gate_part, bits - 1 - b, b, n)
     gate_total = gate_part.reshape(D, D + LANES)
 
-    quarters = 4
-    pair = max(rows // quarters // 2, 1)
-    steps = rows // quarters // pair
-
-    def quarter(i, grad_tokens, after):
-        lines = pl.BlockSpec((pair * N2, D), lambda g: (g + i * steps, 0))
+    unit = rows // 8
+    pieces = [1, 2, 3, 2]
+
+    def piece(i, grad_tokens, after):
+        first = sum(pieces[:i])
+        lines = pl.BlockSpec((unit * N2, D), lambda g: (g + first, 0))
         held = [] if grad_tokens is None else [grad_tokens]
         return pl.pallas_call(
             tokens_kernel,
-            grid=(steps,),
-            in_specs=[lines, lines, square, unread] + [unread] * len(held),
+            grid=(pieces[i],),
+            in_specs=[
+                pl.BlockSpec((n, unit, chans, N2), lambda g: (0, g + first, 0, 0)),
+                lines,
+                block,
+                square,
+                unread,
+            ]
+            + [unread] * len(held),
             out_specs=lines,
             out_shape=shape((local_rows, D)),
-            input_output_aliases={4: 0} if held else {},
+            input_output_aliases={5: 0} if held else {},
             compiler_params=params(),
-            cost_estimate=cost(0.53, 3.5),
-        )(d_value, partial, w_value_t, after, *held)
+            cost_estimate=cost(0.4 * pieces[i], 1.5 * pieces[i]),
+        )(one_here, partial, first_t, w_value_t, after, *held)
 
     grad_tokens = None
     for b in range(bits):
@@ -503,8 +525,8 @@
         elif b > 1:
             kept, given = value_part, value_part
         got = from_partner(given, b, n)
-        if b < quarters:
-            grad_tokens = quarter(b, grad_tokens, given)
+        if b < len(pieces):
+            grad_tokens = piece(b, grad_tokens, given)
         value_part = added(kept, got)
     for b in (1, 0):
         value_part = doubled(value_part, 1 - b, b, n)

time: 446 us -> 443 us (level)
  waiting for transfers between devices: 257 us -> 249 us
    ppermute x14, waiting for transfers between devices: 81.8 us -> 76.3 us  [from_partner(): return lax.ppermute(array, 'seq', [(i, i ^ 1 << b) for i in range(n)])]
  transfers between devices with their start and end apart: 18 -> 18, of which waited for: 12 -> 12; matrix products, arithmetic and copies ran while one was open for 2% -> 2% of each run, Pallas kernels for 20% -> 21%
where the time goes in v14:
time: 443 us; the launch traced here: 442 us
  waiting for transfers between devices  249 us (56%)
  Pallas kernels  99.6 us (22%)
  starting transfers between devices  82.8 us (19%)
  other arithmetic  5.97 us (1%)
    all_to_all x4, waiting for transfers between devices, transfer(): return lax.all_to_all(array, 'seq', split_axis=0, concat_axis=0, tiled=True)  173 us
    ppermute x14, waiting for transfers between devices, from_partner(): return lax.ppermute(array, 'seq', [(i, i ^ 1 << b) for i in range(n)])  76.3 us
    all_to_all x4, starting transfers between devices, transfer(): return lax.all_to_all(array, 'seq', split_axis=0, concat_axis=0, tiled=True)  66.8 us
    pallas_call x1, Pallas kernels, on_device(): pl.pallas_call(home_backward_kernel, grid=(chans // GROUP,), in_specs=[at...  20.6 us
    pallas_call x1, Pallas kernels, on_device(): pl.pallas_call(home_forward_kernel, grid=(chans // GROUP,), in_specs=[at_...  20.1 us
    pallas_call x1, Pallas kernels, on_device(): pl.pallas_call(d_three_kernel, grid=(rows // per,), in_specs=[row, row, s...  17.1 us
    ppermute x14, starting transfers between devices, from_partner(): return lax.ppermute(array, 'seq', [(i, i ^ 1 << b) for i in range(n)])  16 us
    pallas_call x4, Pallas kernels, piece(): pl.pallas_call(tokens_kernel, grid=(pieces[i],), in_specs=[pl.BlockSpec((...  15.6 us
  transfers between devices with their start and end apart: 18, of which 12 were waited for; matrix products, arithmetic and copies ran while one was open for 2% of the time, Pallas kernels for 21%

profile of v14, /device:TPU:0, one launch (start us, length us, event | category | flops | bytes accessed | tf_op | source)
XLA Modules:
  0.0 441.9 jit_solution(15234326512196805032)
XLA Ops:
  0.6 6.7 %shard_map.130 = bf16[16,16,32,256]{3,2,1,0:T(8,128)(2,1)} custom-call(bf16[4096,512]{1,0:T(8,128)(2,1)} %tokens.3, bf16[512,512]{1,0:T(8,128)(2,1)} %w_value.3, bf16[256,256]{1,0:T(8,128)(2,1)} %first.3), custom_call_target="tpu_custom_call" | custom-call | flops 3200000000 | bytes 9437184 | tf_op jit(solution)/shard_map/pallas_call | solution.py:370
  7.4 7.5 %all-to-all-start.1 = ((bf16[16,16,32,256]{3,2,1,0:T(8,128)(2,1)}), bf16[16,16,32,256]{3,2,1,0:T(8,128)(2,1)}, u32[]{:S(2)}, u32[]{:S(2)}) async-start(bf16[16,16,32,256]{3,2,1,0:T(8,128)(2,1)} %shard_map.130), calls=%async_computation.1 | async-start | bytes 8388608 | tf_op jit(solution)/shard_map/all_to_all | solution.py:367
  14.8 17.1 %shard_map.129 = (bf16[16,16,32,256]{3,2,1,0:T(8,128)(2,1)}, bf16[4096,512]{1,0:T(8,128)(2,1)}, bf16[4096,512]{1,0:T(8,128)(2,1)}, bf16[512,4096]{1,0:T(8,128)(2...) custom-call(bf16[4096,512]{1,0:T(8,128)(2,1)} %tokens.3, ...), custom_call_target="tpu_custom_call" | custom-call | flops 8600000512 | bytes 31457280 | tf_op jit(solution)/shard_map/pallas_call | solution.py:388
  31.9 60.6 %all-to-all-done.1 = bf16[16,16,32,256]{3,2,1,0:T(8,128)(2,1)} async-done(((bf16[16,16,32,256]{3,2,1,0:T(8,128)(2,1)}), bf16[16,16,32,256]{3,2,1,0:T(8,128)(2,1)}, u32[]{:S(2)}, u32[]{:S(2)}) %all-to-all-start.1) | async-done | bytes 4194336 | tf_op jit(solution)/shard_map/all_to_all | solution.py:367
  92.5 19.7 %all-to-all-start = ((bf16[16,16,32,256]{3,2,1,0:T(8,128)(2,1)}), bf16[16,16,32,256]{3,2,1,0:T(8,128)(2,1)}, u32[]{:S(2)}, u32[]{:S(2)}) async-start(bf16[16,16,32,256]{3,2,1,0:T(8,128)(2,1)} %get-tuple-element.21), calls=%async_computation | async-start | bytes 8388608 | tf_op jit(solution)/shard_map/all_to_all | solution.py:367
  113.0 20.1 %shard_map.131 = (bf16[256,32,256]{2,1,0:T(8,128)(2,1)}, f32[32,256,256]{2,1,0:T(8,128)}) custom-call(bf16[256,32,256]{2,1,0:T(8,128)(2,1)} %bitcast.2.arrived, bf16[32,256,256]{2,1,0:T(8,128)(2,1)} %kernel.3, bf16[256,256]{1,0:T(8,128)(2,1)} %second.1, bf16[256,256]{1,0:T(8,128)(2,1)} %third.1, bf16[256,256]{1,0:T(8,128)(2,1)} %fusion.11.swap), custom_call_target="tpu_custom_call" | custom-call | flops 4300000256 | bytes 20971520 | tf_op jit(solution)/shard_map/pallas_call | solution.py:411
  133.0 56.9 %all-to-all-done = bf16[16,16,32,256]{3,2,1,0:T(8,128)(2,1)} async-done(((bf16[16,16,32,256]{3,2,1,0:T(8,128)(2,1)}), bf16[16,16,32,256]{3,2,1,0:T(8,128)(2,1)}, u32[]{:S(2)}, u32[]{:S(2)}) %all-to-all-start) | async-done | bytes 4194336 | tf_op jit(solution)/shard_map/all_to_all | solution.py:367
  189.9 19.8 %all-to-all-start.3 = ((bf16[16,16,32,256]{3,2,1,0:T(8,128)(2,1)}), bf16[16,16,32,256]{3,2,1,0:T(8,128)(2,1)}, u32[]{:S(2)}, u32[]{:S(2)}) async-start(bf16[16,16,32,256]{3,2,1,0:T(8,128)(2,1)} %bitcast.59), calls=%async_computation.3 | async-start | bytes 8388608 | tf_op jit(solution)/shard_map/all_to_all | solution.py:367
  211.2 20.6 %shard_map.132 = (bf16[256,32,256]{2,1,0:T(8,128)(2,1)}, bf16[32,256,256]{2,1,0:T(8,128)(2,1)}) custom-call(bf16[256,32,256]{2,1,0:T(8,128)(2,1)} %bitcast.1.arrived, bf16[32,256,256]{2,1,0:T(8,128)(2,1)} %kernel.3, f32[32,256,256]{2,1,0:T(8,128)} %get-tuple-element.22.spectrum, bf16[256,256]{1,0:T(8,128)(2,1)} %bitcast.74, bf16[256,256]{1,0:T(8,128)(2,1)} %bitcast.75, ...), custom_call_target="tpu_custom_call" | custom-call | flops 4300000256 | bytes 25165824 | tf_op jit(solution)/shard_map/pallas_call | solution.py:423
  231.9 55.5 %all-to-all-done.3.arrived = bf16[16,16,32,256]{3,2,1,0:T(8,128)(2,1)} async-done(((bf16[16,16,32,256]{3,2,1,0:T(8,128)(2,1)}), bf16[16,16,32,256]{3,2,1,0:T(8,128)(2,1)}, u32[]{:S(2)}, u32[]{:S(2)}) %all-to-all-start.3) | async-done | bytes 4194336 | tf_op jit(solution)/shard_map/all_to_all | solution.py:367
  287.4 19.8 %all-to-all-start.2 = ((bf16[16,16,32,256]{3,2,1,0:T(8,128)(2,1)}), bf16[16,16,32,256]{3,2,1,0:T(8,128)(2,1)}, u32[]{:S(2)}, u32[]{:S(2)}) async-start(bf16[16,16,32,256]{3,2,1,0:T(8,128)(2,1)} %bitcast.58), calls=%async_computation.2 | async-start | bytes 8388608 | tf_op jit(solution)/shard_map/all_to_all | solution.py:367
  307.3 14.1 %shard_map.133 = (bf16[4096,512]{1,0:T(8,128)(2,1)}, bf16[512,512]{1,0:T(8,128)(2,1)}) custom-call(bf16[16,16,32,256]{3,2,1,0:T(8,128)(2,1)} %all-to-all-done.3.arrived, bf16[512,4096]{1,0:T(8,128)(2,1)} %get-tuple-element.25.tokens_t, bf16[4096,512]{1,0:T(8,128)(2,1)} %get-tuple-element.26.value, bf16[4096,512]{1,0:T(8,128)(2,1)} %cotangent.3, ...), custom_call_target="tpu_custom_call" | custom-call | flops 5400000000 | bytes 26214400 | tf_op jit(solution)/shard_map/pallas_call | solution.py:442
  324.6 1.9 collective-permute-start.1
  326.5 10.8 %collective-permute-done.1 = bf16[2,2,32,640]{3,2,0,1:T(8,128)(2,1)S(1)} collective-permute-done((bf16[2,2,32,640]{3,2,0,1:T(8,128)(2,1)S(1)}, bf16[2,2,32,640]{3,2,0,1:T(8,128)(2,1)S(1)}, u32[]{:S(2)}, u32[]{:S(2)}) %collective-permute-start.1) | collective-permute-done | bytes 163872 | tf_op jit(solution)/shard_map/ppermute | solution.py:303
  337.5 40.1 %collective-permute-done.2 = bf16[2,32,640]{2,1,0:T(8,128)(2,1)S(1)} collective-permute-done((bf16[2,32,640]{2,1,0:T(8,128)(2,1)S(1)}, bf16[2,32,640]{2,1,0:T(8,128)(2,1)S(1)}, u32[]{:S(2)}, u32[]{:S(2)}) %collective-permute-start.2) | collective-permute-done | bytes 81952 | tf_op jit(solution)/shard_map/ppermute | solution.py:303
  377.6 4.6 %collective-permute-start.3 = (bf16[32,640]{1,0:T(8,128)(2,1)S(1)}, bf16[32,640]{1,0:T(8,128)(2,1)S(1)}, u32[]{:S(2)}, u32[]{:S(2)}) collective-permute-start(bf16[32,640]{1,0:T(8,128)(2,1)S(1)} %dynamic-slice_bitcast_fusion.3), channel_id=1, source_target_pairs={{0,8},{1,9},{2,10},{3,11},{4,12},{5,13},{6,14},{7,15},{8,0},{9,1},... | collective-permute-start | bytes 122888 | tf_op jit(solution)/shard_map/ppermute | solution.py:303
  383.0 20.0 %collective-permute-done.3 = bf16[32,640]{1,0:T(8,128)(2,1)S(1)} collective-permute-done((bf16[32,640]{1,0:T(8,128)(2,1)S(1)}, bf16[32,640]{1,0:T(8,128)(2,1)S(1)}, u32[]{:S(2)}, u32[]{:S(2)}) %collective-permute-start.3) | collective-permute-done | bytes 40992 | tf_op jit(solution)/shard_map/ppermute | solution.py:303
  403.6 5.4 %shard_map.134 = (bf16[2,128,512]{2,1,0:T(8,128)(2,1)}, bf16[2,128,512]{2,1,0:T(8,128)(2,1)}) custom-call(bf16[16,16,32,256]{3,2,1,0:T(8,128)(2,1)} %all-to-all-done.2.arrived, bf16[4096,512]{1,0:T(8,128)(2,1)} %get-tuple-element.31.turned, f32[512,512]{1,0:T(8,128)} %get-tuple-element.32.direct, f32[1,1]{1,0:T(1,128)} %constant.77.clone.1.factor, ...), custom_call_target="tpu_custom_call" | custom-call | flops 2200000000 | bytes 9961472 | tf_op jit(solution)/shard_map/pallas_call | solution.py:476
  409.2 3.0 shard_map.135.rest_1_
  415.4 1.7 collective-permute-done.11
  420.4 3.7 shard_map.136.rest_1_
  424.8 2.0 collective-permute-start.7
  427.0 5.1 %shard_map.137.rest_1_ = bf16[4096,512]{1,0:T(8,128)(2,1)} custom-call(bf16[16,16,32,256]{3,2,1,0:T(8,128)(2,1)} %all-to-all-done.2.arrived, bf16[4096,512]{1,0:T(8,128)(2,1)} %get-tuple-element.30.partial, bf16[256,256]{1,0:T(8,128)(2,1)} %bitcast.62, bf16[512,512]{1,0:T(8,128)(2,1)} %get-tuple-element.29.w_value_t, ...), custom_call_target="tpu_custom_call", output_to_operand_aliasing={{}: (5, {})} | custom-call | flops 1200000000 | bytes 4718592 | tf_op jit(solution)/shard_map/pallas_call | solution.py:503
  434.2 3.7 shard_map.138
  (79 shorter events, 20.3 us)
Async XLA Ops:
  7.4 85.1 %all-to-all-start.1 = ((bf16[16,16,32,256]{3,2,1,0:T(8,128)(2,1)}), bf16[16,16,32,256]{3,2,1,0:T(8,128)(2,1)}, u32[]{:S(2)}, u32[]{:S(2)}) async-start(bf16[16,16,32,256]{3,2,1,0:T(8,128)(2,1)} %shard_map.130), calls=%async_computation.1 | async-start | bytes 8388608 | tf_op jit(solution)/shard_map/all_to_all | solution.py:367
  92.5 97.4 %all-to-all-start = ((bf16[16,16,32,256]{3,2,1,0:T(8,128)(2,1)}), bf16[16,16,32,256]{3,2,1,0:T(8,128)(2,1)}, u32[]{:S(2)}, u32[]{:S(2)}) async-start(bf16[16,16,32,256]{3,2,1,0:T(8,128)(2,1)} %get-tuple-element.21), calls=%async_computation | async-start | bytes 8388608 | tf_op jit(solution)/shard_map/all_to_all | solution.py:367
  189.9 19.8 %copy-start.6 = (bf16[256,256]{1,0:T(8,128)(2,1)S(1)}, bf16[256,256]{1,0:T(8,128)(2,1)}, u32[]{:S(2)}) copy-start(bf16[256,256]{1,0:T(8,128)(2,1)} %second.1) | copy-start | bytes 393220
  189.9 20.6 %copy-start.7 = (bf16[256,256]{1,0:T(8,128)(2,1)S(1)}, bf16[256,256]{1,0:T(8,128)(2,1)}, u32[]{:S(2)}) copy-start(bf16[256,256]{1,0:T(8,128)(2,1)} %third.1) | copy-start | bytes 393220
  189.9 97.5 %all-to-all-start.3 = ((bf16[16,16,32,256]{3,2,1,0:T(8,128)(2,1)}), bf16[16,16,32,256]{3,2,1,0:T(8,128)(2,1)}, u32[]{:S(2)}, u32[]{:S(2)}) async-start(bf16[16,16,32,256]{3,2,1,0:T(8,128)(2,1)} %bitcast.59), calls=%async_computation.3 | async-start | bytes 8388608 | tf_op jit(solution)/shard_map/all_to_all | solution.py:367
  287.4 19.9 %copy-start.9 = (f32[1,512]{1,0:T(1,128)S(1)}, f32[1,512]{1,0:T(1,128)}, u32[]{:S(2)}) copy-start(f32[1,512]{1,0:T(1,128)} %get-tuple-element.34) | copy-start | bytes 6148
  287.4 115.7 %all-to-all-start.2 = ((bf16[16,16,32,256]{3,2,1,0:T(8,128)(2,1)}), bf16[16,16,32,256]{3,2,1,0:T(8,128)(2,1)}, u32[]{:S(2)}, u32[]{:S(2)}) async-start(bf16[16,16,32,256]{3,2,1,0:T(8,128)(2,1)} %bitcast.58), calls=%async_computation.2 | async-start | bytes 8388608 | tf_op jit(solution)/shard_map/all_to_all | solution.py:367
  321.4 60.8 %copy-start.8 = (bf16[256,256]{1,0:T(8,128)(2,1)S(1)}, bf16[256,256]{1,0:T(8,128)(2,1)}, u32[]{:S(2)}) copy-start(bf16[256,256]{1,0:T(8,128)(2,1)} %first.3) | copy-start | bytes 393220
  322.7 1.7 collective-permute-start
  324.6 12.7 %collective-permute-start.1 = (bf16[2,2,32,640]{3,2,0,1:T(8,128)(2,1)S(1)}, bf16[2,2,32,640]{3,2,0,1:T(8,128)(2,1)S(1)}, u32[]{:S(2)}, u32[]{:S(2)}) collective-permute-start(bf16[2,2,32,640]{3,2,0,1:T(8,128)(2,1)S(1)} %dynamic-slice_bitcast_fusion), channel_id=1, source_target_pairs={{0,2},{1,3},{2,0},{3,1},{4,6},{5,7},{6,4},{7,5},{8,10},{9,11},{10,... | collective-permute-start | bytes 491528 | tf_op jit(solution)/shard_map/ppermute | solution.py:303
  337.4 40.2 %collective-permute-start.2 = (bf16[2,32,640]{2,1,0:T(8,128)(2,1)S(1)}, bf16[2,32,640]{2,1,0:T(8,128)(2,1)S(1)}, u32[]{:S(2)}, u32[]{:S(2)}) collective-permute-start(bf16[2,32,640]{2,1,0:T(8,128)(2,1)S(1)} %dynamic-slice_bitcast_fusion.2), channel_id=1, source_target_pairs={{0,4},{1,5},{2,6},{3,7},{4,0},{5,1},{6,2},{7,3},{8,12},{9,13},{10,... | collective-permute-start | bytes 245768 | tf_op jit(solution)/shard_map/ppermute | solution.py:303
  377.6 25.4 %collective-permute-start.3 = (bf16[32,640]{1,0:T(8,128)(2,1)S(1)}, bf16[32,640]{1,0:T(8,128)(2,1)S(1)}, u32[]{:S(2)}, u32[]{:S(2)}) collective-permute-start(bf16[32,640]{1,0:T(8,128)(2,1)S(1)} %dynamic-slice_bitcast_fusion.3), channel_id=1, source_target_pairs={{0,8},{1,9},{2,10},{3,11},{4,12},{5,13},{6,14},{7,15},{8,0},{9,1},... | collective-permute-start | bytes 122888 | tf_op jit(solution)/shard_map/ppermute | solution.py:303
  403.0 9.2 %collective-permute-start.10 = (bf16[32,640]{1,0:T(8,128)(2,1)S(1)}, bf16[32,640]{1,0:T(8,128)(2,1)S(1)}, u32[]{:S(2)}, u32[]{:S(2)}) collective-permute-start(bf16[32,640]{1,0:T(8,128)(2,1)S(1)} %fusion.17._), channel_id=1, source_target_pairs={{0,8},{1,9},{2,10},{3,11},{4,12},{5,13},{6,14},{7,15},{8,0},{9,1},... | collective-permute-start | bytes 122888 | tf_op jit(solution)/shard_map/ppermute | solution.py:303
  409.1 4.8 %collective-permute-start.4 = (bf16[2,128,512]{2,1,0:T(8,128)(2,1)}, bf16[2,128,512]{2,1,0:T(8,128)(2,1)S(1)}, u32[]{:S(2)}, u32[]{:S(2)}) collective-permute-start(bf16[2,128,512]{2,1,0:T(8,128)(2,1)} %get-tuple-element.36.rest_0_), channel_id=1, source_target_pairs={{0,1},{1,0},{2,3},{3,2},{4,5},{5,4},{6,7},{7,6},{8,9},{9,8},{10,11... | collective-permute-start | bytes 786440 | tf_op jit(solution)/shard_map/ppermute | solution.py:303
  412.2 4.9 %collective-permute-start.11 = (bf16[2,32,640]{2,1,0:T(8,128)(2,1)S(1)}, bf16[2,32,640]{2,1,0:T(8,128)(2,1)S(1)}, u32[]{:S(2)}, u32[]{:S(2)}) collective-permute-start(bf16[2,32,640]{2,1,0:T(8,128)(2,1)S(1)} %fusion.16), channel_id=1, source_target_pairs={{0,4},{1,5},{2,6},{3,7},{4,0},{5,1},{6,2},{7,3},{8,12},{9,13},{10,... | collective-permute-start | bytes 245768 | tf_op jit(solution)/shard_map/ppermute | solution.py:303
  414.0 6.4 %copy-start.4 = (bf16[128,512]{1,0:T(8,128)(2,1)}, bf16[128,512]{1,0:T(8,128)(2,1)S(1)}, u32[]{:S(2)}) copy-start(bf16[128,512]{1,0:T(8,128)(2,1)S(1)} %dynamic-slice_bitcast_fusion.1.rest_0_) | copy-start | bytes 393220
  414.0 5.7 %collective-permute-start.5 = (bf16[128,512]{1,0:T(8,128)(2,1)S(1)}, bf16[128,512]{1,0:T(8,128)(2,1)S(1)}, u32[]{:S(2)}, u32[]{:S(2)}) collective-permute-start(bf16[128,512]{1,0:T(8,128)(2,1)S(1)} %dynamic-slice_bitcast_fusion.1.rest_0_), channel_id=1, source_target_pairs={{0,2},{1,3},{2,0},{3,1},{4,6},{5,7},{6,4},{7,5},{8,10},{9,11},{10,... | collective-permute-start | bytes 393224 | tf_op jit(solution)/shard_map/ppermute | solution.py:303
  417.2 6.9 %collective-permute-start.12 = (bf16[2,2,32,640]{3,2,0,1:T(8,128)(2,1)S(1)}, bf16[2,2,32,640]{3,2,0,1:T(8,128)(2,1)S(1)}, u32[]{:S(2)}, u32[]{:S(2)}) collective-permute-start(bf16[2,2,32,640]{3,2,0,1:T(8,128)(2,1)S(1)} %fusion.13), channel_id=1, source_target_pairs={{0,2},{1,3},{2,0},{3,1},{4,6},{5,7},{6,4},{7,5},{8,10},{9,11},{10,... | collective-permute-start | bytes 491528 | tf_op jit(solution)/shard_map/ppermute | solution.py:303
  419.7 5.0 %collective-permute-start.6 = (bf16[128,512]{1,0:T(8,128)(2,1)S(1)}, bf16[128,512]{1,0:T(8,128)(2,1)S(1)}, u32[]{:S(2)}, u32[]{:S(2)}) collective-permute-start(bf16[128,512]{1,0:T(8,128)(2,1)S(1)} %fusion.10.rest_0_), channel_id=1, source_target_pairs={{0,4},{1,5},{2,6},{3,7},{4,0},{5,1},{6,2},{7,3},{8,12},{9,13},{10,... | collective-permute-start | bytes 393224 | tf_op jit(solution)/shard_map/ppermute | solution.py:303
  424.8 7.9 %copy-start = (bf16[128,512]{1,0:T(8,128)(2,1)}, bf16[128,512]{1,0:T(8,128)(2,1)S(1)}, u32[]{:S(2)}) copy-start(bf16[128,512]{1,0:T(8,128)(2,1)S(1)} %add_convert_fusion.2.rest_0_) | copy-start | bytes 393220
  424.8 7.9 %collective-permute-start.7 = (bf16[128,512]{1,0:T(8,128)(2,1)S(1)}, bf16[128,512]{1,0:T(8,128)(2,1)S(1)}, u32[]{:S(2)}, u32[]{:S(2)}) collective-permute-start(bf16[128,512]{1,0:T(8,128)(2,1)S(1)} %add_convert_fusion.2.rest_0_), channel_id=1, source_target_pairs={{0,8},{1,9},{2,10},{3,11},{4,12},{5,13},{6,14},{7,15},{8,0},{9,1},... | collective-permute-start | bytes 393224 | tf_op jit(solution)/shard_map/ppermute | solution.py:303
  427.0 10.9 %collective-permute-start.13 = (bf16[2,2,2,32,640]{4,3,0,1,2:T(8,128)(2,1)S(1)}, bf16[2,2,2,32,640]{4,3,0,1,2:T(8,128)(2,1)S(1)}, u32[]{:S(2)}, u32[]{:S(2)}) collective-permute-start(bf16[2,2,2,32,640]{4,3,0,1,2:T(8,128)(2,1)S(1)} %fusion.6), channel_id=1, source_target_pairs={{0,1},{1,0},{2,3},{3,2},{4,5},{5,4},{6,7},{7,6},{8,9},{9,8},{10,11... | collective-permute-start | bytes 983048 | tf_op jit(solution)/shard_map/ppermute | solution.py:303
  432.7 5.6 %collective-permute-start.8 = (bf16[128,512]{1,0:T(8,128)(2,1)S(1)}, bf16[128,512]{1,0:T(8,128)(2,1)S(1)}, u32[]{:S(2)}, u32[]{:S(2)}) collective-permute-start(bf16[128,512]{1,0:T(8,128)(2,1)S(1)} %add_convert_fusion.1), channel_id=1, source_target_pairs={{0,2},{1,3},{2,0},{3,1},{4,6},{5,7},{6,4},{7,5},{8,10},{9,11},{10,... | collective-permute-start | bytes 393224 | tf_op jit(solution)/shard_map/ppermute | solution.py:303
  438.5 1.6 collective-permute-start.9
  (4 other events, 13.4 us)

commit v15 on v14

--- a/solution.py
+++ b/solution.py
@@ -48,13 +48,11 @@
     return slice(r * N2, (r + 1) * N2)
 
 
-def section_one_kernel(
-    per, tokens, w_value, first, out, tokens_v, w_v, first_v, out_v, arrive, leave
-):
-    n, rows, chans, _ = out.shape
+def send_value_kernel(per, tokens, w_value, out, tokens_v, w_v, out_v, arrive, leave):
+    rows = out.shape[1]
+    n, _, chans, _ = out.shape
     chunks = rows // per
-    in_first = pltpu.make_async_copy(first, first_v, arrive.at[chunks])
-    in_w = pltpu.make_async_copy(w_value, w_v, arrive.at[chunks + 1])
+    in_w = pltpu.make_async_copy(w_value, w_v, arrive.at[chunks])
     in_tokens = [
         pltpu.make_async_copy(
             tokens.at[pl.ds(i * per * N2, per * N2)],
@@ -70,20 +68,14 @@
         for i in range(chunks)
     ]
     in_w.start()
-    in_tokens[0].start()
-    in_first.start()
-    for copy in in_tokens[1:]:
+    for copy in in_tokens:
         copy.start()
     in_w.wait()
     for i in range(chunks):
         in_tokens[i].wait()
         value = dot_nn(tokens_v[i * per * N2 : (i + 1) * per * N2], w_v[...]).astype(bf16)
-        if i == 0:
-            in_first.wait()
-            first_v[...] = first_v[...].T
         for r in range(per):
-            section = dot_nn(value[row_slice(r)].T, first_v[...]).astype(bf16)
-            out_v[:, i * per + r] = section.reshape(n, chans, N2)
+            out_v[:, i * per + r] = value[row_slice(r)].T.reshape(n, chans, N2)
         outs[i].start()
     for copy in outs:
         copy.wait()
@@ -159,11 +151,14 @@
     lax.fori_loop(0, N1 // GROUP, body, 0, unroll=2)
 
 
-def home_forward_kernel(arrived, kernel, second, third, swap, out, spectrum_out, by_channel):
+def home_forward_kernel(
+    arrived, kernel, first_t, second, third, swap, out, spectrum_out, by_channel
+):
     turn_in(swap, arrived, by_channel)
 
     def body(c, _):
-        spectrum = dot_nn(second[...], by_channel[c])
+        section = dot_nn(by_channel[c], first_t[...]).astype(bf16)
+        spectrum = dot_nn(second[...], section)
         spectrum_out[c] = spectrum
         filtered = (spectrum * kernel[c].astype(f32)).astype(bf16)
         by_channel[c] = dot_nn(third[...], filtered).astype(bf16)
@@ -368,21 +363,20 @@
 
     unread = pl.BlockSpec(memory_space=pl.ANY)
     one_sent = pl.pallas_call(
-        functools.partial(section_one_kernel, per),
-        in_specs=[unread] * 3,
+        functools.partial(send_value_kernel, per),
+        in_specs=[unread] * 2,
         out_specs=unread,
         out_shape=shape(sections),
         scratch_shapes=[
             pltpu.VMEM((local_rows, D), bf16),
             pltpu.VMEM((D, D), bf16),
-            pltpu.VMEM((N2, N2), bf16),
             pltpu.VMEM(sections, bf16),
-            pltpu.SemaphoreType.DMA((rows // per + 2,)),
+            pltpu.SemaphoreType.DMA((rows // per + 1,)),
             pltpu.SemaphoreType.DMA((rows // per,)),
         ],
         compiler_params=params(),
-        cost_estimate=cost(3.2, 9),
-    )(tokens, w_value, first_block)
+        cost_estimate=cost(2.1, 9),
+    )(tokens, w_value)
     one_home = transfer(one_sent)
 
     three_sent, value, d_mix, tokens_t, turned, direct, skip_term, w_value_t, w_gate_t = pl.pallas_call(
@@ -406,18 +400,26 @@
     )(tokens, cotangent, w_value, w_gate, first_block, fourth_block, skip)
     three_home = transfer(three_sent)
 
+    first_t = first_block.T
     at_home = pl.BlockSpec((N1, GROUP, N2), lambda i: (0, i, 0))
     filters = pl.BlockSpec((GROUP, N1, N2), lambda i: (i, 0, 0))
     three_back, spectrum = pl.pallas_call(
         home_forward_kernel,
         grid=(chans // GROUP,),
-        in_specs=[at_home, filters, block, block, block],
+        in_specs=[at_home, filters, block, block, block, block],
         out_specs=[at_home, filters],
         out_shape=[shape((N1, chans, N2)), shape((chans, N1, N2), f32)],
         scratch_shapes=[pltpu.VMEM((GROUP, N1, N2), bf16)],
         compiler_params=params(),
-        cost_estimate=cost(4.3, 20),
-    )(one_home.reshape(N1, chans, N2), kernel, second_block, third_block, swap)
+        cost_estimate=cost(5.4, 20),
+    )(
+        one_home.reshape(N1, chans, N2),
+        kernel,
+        first_t,
+        second_block,
+        third_block,
+        swap,
+    )
     three_here = transfer(three_back.reshape(sections))
 
     one_back, grad_kernel = pl.pallas_call(
@@ -469,7 +471,6 @@
         kept, given = halves(gate_part, bits - 1 - b, b)
         gate_part = added(kept, from_partner(given, b, n))
 
-    first_t = first_block.T
     in_vmem = pl.BlockSpec(memory_space=pltpu.VMEM)
     me = lax.axis_index("seq").reshape(1, 1)
     half = (2, D // 4, D)
@@ -494,7 +495,7 @@
     gate_total = gate_part.reshape(D, D + LANES)
 
     unit = rows // 8
-    pieces = [1, 2, 3, 2]
+    pieces = [3, 3, 2]
 
     def piece(i, grad_tokens, after):
         first = sum(pieces[:i])
@@ -525,8 +526,8 @@
         elif b > 1:
             kept, given = value_part, value_part
         got = from_partner(given, b, n)
-        if b < len(pieces):
-            grad_tokens = piece(b, grad_tokens, given)
+        if 0 < b <= len(pieces):
+            grad_tokens = piece(b - 1, grad_tokens, given)
         value_part = added(kept, got)
     for b in (1, 0):
         value_part = doubled(value_part, 1 - b, b, n)

time: 443 us -> 443 us (level)
  waiting for transfers between devices: 249 us -> 244 us
    all_to_all x4, waiting for transfers between devices: 173 us -> 166 us  [transfer(): return lax.all_to_all(array, 'seq', split_axis=0, concat_axis=0, tiled=True)]
    pallas_call x1, Pallas kernels: 20.1 us -> 26 us  [on_device(): pl.pallas_call(home_forward_kernel, grid=(chans // GROUP,), in_specs=[at_...]
    pallas_call x4 -> x3, Pallas kernels: 15.6 us -> 14 us  [piece(): pl.pallas_call(tokens_kernel, grid=(pieces[i],), in_specs=[pl.BlockSpec((...]
  transfers between devices with their start and end apart: 18 -> 18, of which waited for: 12 -> 10; matrix products, arithmetic and copies ran while one was open for 2% -> 2% of each run, Pallas kernels for 21% -> 22%
where the time goes in v15:
time: 443 us; the launch traced here: 442 us
  waiting for transfers between devices  244 us (55%)
  Pallas kernels  103 us (23%)
  starting transfers between devices  83.2 us (19%)
  other arithmetic  8.64 us (2%)
    all_to_all x4, waiting for transfers between devices, transfer(): return lax.all_to_all(array, 'seq', split_axis=0, concat_axis=0, tiled=True)  166 us
    ppermute x14, waiting for transfers between devices, from_partner(): return lax.ppermute(array, 'seq', [(i, i ^ 1 << b) for i in range(n)])  77.2 us
    all_to_all x4, starting transfers between devices, transfer(): return lax.all_to_all(array, 'seq', split_axis=0, concat_axis=0, tiled=True)  66.9 us
    pallas_call x1, Pallas kernels, on_device(): pl.pallas_call(home_forward_kernel, grid=(chans // GROUP,), in_specs=[at_...  26 us
    pallas_call x1, Pallas kernels, on_device(): pl.pallas_call(home_backward_kernel, grid=(chans // GROUP,), in_specs=[at...  20.6 us
    pallas_call x1, Pallas kernels, on_device(): pl.pallas_call(d_three_kernel, grid=(rows // per,), in_specs=[row, row, s...  17.1 us
    ppermute x14, starting transfers between devices, from_partner(): return lax.ppermute(array, 'seq', [(i, i ^ 1 << b) for i in range(n)])  16.2 us
    pallas_call x1, Pallas kernels, on_device(): pl.pallas_call(gate_kernel, grid=(rows // per,), in_specs=[sent, column,...  14 us
  transfers between devices with their start and end apart: 18, of which 10 were waited for; matrix products, arithmetic and copies ran while one was open for 2% of the time, Pallas kernels for 22%

profile of v15, /device:TPU:0, one launch (start us, length us, event | category | flops | bytes accessed | tf_op | source)
XLA Modules:
  0.0 442.2 jit_solution(8859079043368495552)
XLA Ops:
  0.6 5.6 %shard_map.130 = bf16[16,16,32,256]{3,2,1,0:T(8,128)(2,1)} custom-call(bf16[4096,512]{1,0:T(8,128)(2,1)} %tokens.3, bf16[512,512]{1,0:T(8,128)(2,1)} %w_value.3), custom_call_target="tpu_custom_call" | custom-call | flops 2100000000 | bytes 9437184 | tf_op jit(solution)/shard_map/pallas_call | solution.py:365
  6.2 7.5 %all-to-all-start.1 = ((bf16[16,16,32,256]{3,2,1,0:T(8,128)(2,1)}), bf16[16,16,32,256]{3,2,1,0:T(8,128)(2,1)}, u32[]{:S(2)}, u32[]{:S(2)}) async-start(bf16[16,16,32,256]{3,2,1,0:T(8,128)(2,1)} %shard_map.130), calls=%async_computation.1 | async-start | bytes 8388608 | tf_op jit(solution)/shard_map/all_to_all | solution.py:362
  13.7 17.1 %shard_map.129 = (bf16[16,16,32,256]{3,2,1,0:T(8,128)(2,1)}, bf16[4096,512]{1,0:T(8,128)(2,1)}, bf16[4096,512]{1,0:T(8,128)(2,1)}, bf16[512,4096]{1,0:T(8,128)(2...) custom-call(bf16[4096,512]{1,0:T(8,128)(2,1)} %tokens.3, ...), custom_call_target="tpu_custom_call" | custom-call | flops 8600000512 | bytes 31457280 | tf_op jit(solution)/shard_map/pallas_call | solution.py:382
  30.7 60.6 %all-to-all-done.1 = bf16[16,16,32,256]{3,2,1,0:T(8,128)(2,1)} async-done(((bf16[16,16,32,256]{3,2,1,0:T(8,128)(2,1)}), bf16[16,16,32,256]{3,2,1,0:T(8,128)(2,1)}, u32[]{:S(2)}, u32[]{:S(2)}) %all-to-all-start.1) | async-done | bytes 4194336 | tf_op jit(solution)/shard_map/all_to_all | solution.py:362
  91.3 19.8 %all-to-all-start = ((bf16[16,16,32,256]{3,2,1,0:T(8,128)(2,1)}), bf16[16,16,32,256]{3,2,1,0:T(8,128)(2,1)}, u32[]{:S(2)}, u32[]{:S(2)}) async-start(bf16[16,16,32,256]{3,2,1,0:T(8,128)(2,1)} %get-tuple-element.21), calls=%async_computation | async-start | bytes 8388608 | tf_op jit(solution)/shard_map/all_to_all | solution.py:362
  112.7 26.0 %shard_map.131 = (bf16[256,32,256]{2,1,0:T(8,128)(2,1)}, f32[32,256,256]{2,1,0:T(8,128)}) custom-call(bf16[256,32,256]{2,1,0:T(8,128)(2,1)} %bitcast.2.arrived, bf16[32,256,256]{2,1,0:T(8,128)(2,1)} %kernel.3, bf16[256,256]{1,0:T(8,128)(2,1)} %bitcast.63, bf16[256,256]{1,0:T(8,128)(2,1)} %second.1, bf16[256,256]{1,0:T(8,128)(2,1)} %third.1, ...), custom_call_target="tpu_custom_call" | custom-call | flops 5400000000 | bytes 20971520 | tf_op jit(solution)/shard_map/pallas_call | solution.py:406
  138.7 50.2 %all-to-all-done = bf16[16,16,32,256]{3,2,1,0:T(8,128)(2,1)} async-done(((bf16[16,16,32,256]{3,2,1,0:T(8,128)(2,1)}), bf16[16,16,32,256]{3,2,1,0:T(8,128)(2,1)}, u32[]{:S(2)}, u32[]{:S(2)}) %all-to-all-start) | async-done | bytes 4194336 | tf_op jit(solution)/shard_map/all_to_all | solution.py:362
  188.9 19.8 %all-to-all-start.3 = ((bf16[16,16,32,256]{3,2,1,0:T(8,128)(2,1)}), bf16[16,16,32,256]{3,2,1,0:T(8,128)(2,1)}, u32[]{:S(2)}, u32[]{:S(2)}) async-start(bf16[16,16,32,256]{3,2,1,0:T(8,128)(2,1)} %bitcast.59), calls=%async_computation.3 | async-start | bytes 8388608 | tf_op jit(solution)/shard_map/all_to_all | solution.py:362
  210.2 20.6 %shard_map.132 = (bf16[256,32,256]{2,1,0:T(8,128)(2,1)}, bf16[32,256,256]{2,1,0:T(8,128)(2,1)}) custom-call(bf16[256,32,256]{2,1,0:T(8,128)(2,1)} %bitcast.1.arrived, bf16[32,256,256]{2,1,0:T(8,128)(2,1)} %kernel.3, f32[32,256,256]{2,1,0:T(8,128)} %get-tuple-element.22.spectrum, bf16[256,256]{1,0:T(8,128)(2,1)} %bitcast.74, bf16[256,256]{1,0:T(8,128)(2,1)} %bitcast.75, ...), custom_call_target="tpu_custom_call" | custom-call | flops 4300000256 | bytes 25165824 | tf_op jit(solution)/shard_map/pallas_call | solution.py:425
  230.8 55.5 %all-to-all-done.3.arrived = bf16[16,16,32,256]{3,2,1,0:T(8,128)(2,1)} async-done(((bf16[16,16,32,256]{3,2,1,0:T(8,128)(2,1)}), bf16[16,16,32,256]{3,2,1,0:T(8,128)(2,1)}, u32[]{:S(2)}, u32[]{:S(2)}) %all-to-all-start.3) | async-done | bytes 4194336 | tf_op jit(solution)/shard_map/all_to_all | solution.py:362
  286.4 19.8 %all-to-all-start.2 = ((bf16[16,16,32,256]{3,2,1,0:T(8,128)(2,1)}), bf16[16,16,32,256]{3,2,1,0:T(8,128)(2,1)}, u32[]{:S(2)}, u32[]{:S(2)}) async-start(bf16[16,16,32,256]{3,2,1,0:T(8,128)(2,1)} %bitcast.58), calls=%async_computation.2 | async-start | bytes 8388608 | tf_op jit(solution)/shard_map/all_to_all | solution.py:362
  306.2 14.0 %shard_map.133 = (bf16[4096,512]{1,0:T(8,128)(2,1)}, bf16[512,512]{1,0:T(8,128)(2,1)}) custom-call(bf16[16,16,32,256]{3,2,1,0:T(8,128)(2,1)} %all-to-all-done.3.arrived, bf16[512,4096]{1,0:T(8,128)(2,1)} %get-tuple-element.25.tokens_t, bf16[4096,512]{1,0:T(8,128)(2,1)} %get-tuple-element.26.value, bf16[4096,512]{1,0:T(8,128)(2,1)} %cotangent.3, ...), custom_call_target="tpu_custom_call" | custom-call | flops 5400000000 | bytes 26214400 | tf_op jit(solution)/shard_map/pallas_call | solution.py:444
  323.4 1.9 collective-permute-start.1
  325.4 10.9 %collective-permute-done.1 = bf16[2,2,32,640]{3,2,0,1:T(8,128)(2,1)S(1)} collective-permute-done((bf16[2,2,32,640]{3,2,0,1:T(8,128)(2,1)S(1)}, bf16[2,2,32,640]{3,2,0,1:T(8,128)(2,1)S(1)}, u32[]{:S(2)}, u32[]{:S(2)}) %collective-permute-start.1) | collective-permute-done | bytes 163872 | tf_op jit(solution)/shard_map/ppermute | solution.py:298
  336.4 40.1 %collective-permute-done.2 = bf16[2,32,640]{2,1,0:T(8,128)(2,1)S(1)} collective-permute-done((bf16[2,32,640]{2,1,0:T(8,128)(2,1)S(1)}, bf16[2,32,640]{2,1,0:T(8,128)(2,1)S(1)}, u32[]{:S(2)}, u32[]{:S(2)}) %collective-permute-start.2) | collective-permute-done | bytes 81952 | tf_op jit(solution)/shard_map/ppermute | solution.py:298
  376.6 4.6 %collective-permute-start.3 = (bf16[32,640]{1,0:T(8,128)(2,1)S(1)}, bf16[32,640]{1,0:T(8,128)(2,1)S(1)}, u32[]{:S(2)}, u32[]{:S(2)}) collective-permute-start(bf16[32,640]{1,0:T(8,128)(2,1)S(1)} %dynamic-slice_bitcast_fusion.3), channel_id=1, source_target_pairs={{0,8},{1,9},{2,10},{3,11},{4,12},{5,13},{6,14},{7,15},{8,0},{9,1},... | collective-permute-start | bytes 122888 | tf_op jit(solution)/shard_map/ppermute | solution.py:298
  381.2 20.8 %collective-permute-done.3 = bf16[32,640]{1,0:T(8,128)(2,1)S(1)} collective-permute-done((bf16[32,640]{1,0:T(8,128)(2,1)S(1)}, bf16[32,640]{1,0:T(8,128)(2,1)S(1)}, u32[]{:S(2)}, u32[]{:S(2)}) %collective-permute-start.3) | collective-permute-done | bytes 40992 | tf_op jit(solution)/shard_map/ppermute | solution.py:298
  402.6 5.4 %shard_map.134 = (bf16[2,128,512]{2,1,0:T(8,128)(2,1)}, bf16[2,128,512]{2,1,0:T(8,128)(2,1)}) custom-call(bf16[16,16,32,256]{3,2,1,0:T(8,128)(2,1)} %all-to-all-done.2.arrived, bf16[4096,512]{1,0:T(8,128)(2,1)} %get-tuple-element.31.turned, f32[512,512]{1,0:T(8,128)} %get-tuple-element.32.direct, f32[1,1]{1,0:T(1,128)} %constant.77.clone.1.factor, ...), custom_call_target="tpu_custom_call" | custom-call | flops 2200000000 | bytes 9961472 | tf_op jit(solution)/shard_map/pallas_call | solution.py:477
  415.7 3.3 collective-permute-done.5
  419.6 5.1 %shard_map.135.rest_1_ = bf16[4096,512]{1,0:T(8,128)(2,1)} custom-call(bf16[16,16,32,256]{3,2,1,0:T(8,128)(2,1)} %all-to-all-done.2.arrived, bf16[4096,512]{1,0:T(8,128)(2,1)} %get-tuple-element.30.partial, bf16[256,256]{1,0:T(8,128)(2,1)} %bitcast.64, bf16[512,512]{1,0:T(8,128)(2,1)} %get-tuple-element.29.w_value_t, bf16[128,512]{1,0:T(8,128)(2,1)} %copy-done.3), custom_call_target="tpu_custom_call" | custom-call | flops 1200000000 | bytes 4718592 | tf_op jit(solution)/shard_map/pallas_call | solution.py:504
  425.0 2.3 collective-permute-start.7
  427.6 5.1 %shard_map.136.rest_1_ = bf16[4096,512]{1,0:T(8,128)(2,1)} custom-call(bf16[16,16,32,256]{3,2,1,0:T(8,128)(2,1)} %all-to-all-done.2.arrived, bf16[4096,512]{1,0:T(8,128)(2,1)} %get-tuple-element.30.partial, bf16[256,256]{1,0:T(8,128)(2,1)} %bitcast.65, bf16[512,512]{1,0:T(8,128)(2,1)} %get-tuple-element.29.w_value_t, ...), custom_call_target="tpu_custom_call", output_to_operand_aliasing={{}: (5, {})} | custom-call | flops 1200000000 | bytes 4718592 | tf_op jit(solution)/shard_map/pallas_call | solution.py:504
  432.8 1.6 collective-permute-start.8
  434.3 3.7 shard_map.137
  (74 shorter events, 19.9 us)
Async XLA Ops:
  6.2 85.1 %all-to-all-start.1 = ((bf16[16,16,32,256]{3,2,1,0:T(8,128)(2,1)}), bf16[16,16,32,256]{3,2,1,0:T(8,128)(2,1)}, u32[]{:S(2)}, u32[]{:S(2)}) async-start(bf16[16,16,32,256]{3,2,1,0:T(8,128)(2,1)} %shard_map.130), calls=%async_computation.1 | async-start | bytes 8388608 | tf_op jit(solution)/shard_map/all_to_all | solution.py:362
  91.3 19.8 %copy-start.4 = (bf16[256,256]{1,0:T(8,128)(2,1)S(1)}, bf16[256,256]{1,0:T(8,128)(2,1)}, u32[]{:S(2)}) copy-start(bf16[256,256]{1,0:T(8,128)(2,1)} %first.1) | copy-start | bytes 393220
  91.3 97.5 %all-to-all-start = ((bf16[16,16,32,256]{3,2,1,0:T(8,128)(2,1)}), bf16[16,16,32,256]{3,2,1,0:T(8,128)(2,1)}, u32[]{:S(2)}, u32[]{:S(2)}) async-start(bf16[16,16,32,256]{3,2,1,0:T(8,128)(2,1)} %get-tuple-element.21), calls=%async_computation | async-start | bytes 8388608 | tf_op jit(solution)/shard_map/all_to_all | solution.py:362
  188.9 19.8 %copy-start.5 = (bf16[256,256]{1,0:T(8,128)(2,1)S(1)}, bf16[256,256]{1,0:T(8,128)(2,1)}, u32[]{:S(2)}) copy-start(bf16[256,256]{1,0:T(8,128)(2,1)} %second.1) | copy-start | bytes 393220
  188.9 20.6 %copy-start.6 = (bf16[256,256]{1,0:T(8,128)(2,1)S(1)}, bf16[256,256]{1,0:T(8,128)(2,1)}, u32[]{:S(2)}) copy-start(bf16[256,256]{1,0:T(8,128)(2,1)} %third.1) | copy-start | bytes 393220
  188.9 97.5 %all-to-all-start.3 = ((bf16[16,16,32,256]{3,2,1,0:T(8,128)(2,1)}), bf16[16,16,32,256]{3,2,1,0:T(8,128)(2,1)}, u32[]{:S(2)}, u32[]{:S(2)}) async-start(bf16[16,16,32,256]{3,2,1,0:T(8,128)(2,1)} %bitcast.59), calls=%async_computation.3 | async-start | bytes 8388608 | tf_op jit(solution)/shard_map/all_to_all | solution.py:362
  286.4 19.9 %copy-start.7 = (f32[1,512]{1,0:T(1,128)S(1)}, f32[1,512]{1,0:T(1,128)}, u32[]{:S(2)}) copy-start(f32[1,512]{1,0:T(1,128)} %get-tuple-element.34) | copy-start | bytes 6148
  286.4 115.7 %all-to-all-start.2 = ((bf16[16,16,32,256]{3,2,1,0:T(8,128)(2,1)}), bf16[16,16,32,256]{3,2,1,0:T(8,128)(2,1)}, u32[]{:S(2)}, u32[]{:S(2)}) async-start(bf16[16,16,32,256]{3,2,1,0:T(8,128)(2,1)} %bitcast.58), calls=%async_computation.2 | async-start | bytes 8388608 | tf_op jit(solution)/shard_map/all_to_all | solution.py:362
  321.6 1.7 collective-permute-start
  323.4 12.8 %collective-permute-start.1 = (bf16[2,2,32,640]{3,2,0,1:T(8,128)(2,1)S(1)}, bf16[2,2,32,640]{3,2,0,1:T(8,128)(2,1)S(1)}, u32[]{:S(2)}, u32[]{:S(2)}) collective-permute-start(bf16[2,2,32,640]{3,2,0,1:T(8,128)(2,1)S(1)} %dynamic-slice_bitcast_fusion), channel_id=1, source_target_pairs={{0,2},{1,3},{2,0},{3,1},{4,6},{5,7},{6,4},{7,5},{8,10},{9,11},{10,... | collective-permute-start | bytes 491528 | tf_op jit(solution)/shard_map/ppermute | solution.py:298
  336.3 40.2 %collective-permute-start.2 = (bf16[2,32,640]{2,1,0:T(8,128)(2,1)S(1)}, bf16[2,32,640]{2,1,0:T(8,128)(2,1)S(1)}, u32[]{:S(2)}, u32[]{:S(2)}) collective-permute-start(bf16[2,32,640]{2,1,0:T(8,128)(2,1)S(1)} %dynamic-slice_bitcast_fusion.2), channel_id=1, source_target_pairs={{0,4},{1,5},{2,6},{3,7},{4,0},{5,1},{6,2},{7,3},{8,12},{9,13},{10,... | collective-permute-start | bytes 245768 | tf_op jit(solution)/shard_map/ppermute | solution.py:298
  376.6 25.4 %collective-permute-start.3 = (bf16[32,640]{1,0:T(8,128)(2,1)S(1)}, bf16[32,640]{1,0:T(8,128)(2,1)S(1)}, u32[]{:S(2)}, u32[]{:S(2)}) collective-permute-start(bf16[32,640]{1,0:T(8,128)(2,1)S(1)} %dynamic-slice_bitcast_fusion.3), channel_id=1, source_target_pairs={{0,8},{1,9},{2,10},{3,11},{4,12},{5,13},{6,14},{7,15},{8,0},{9,1},... | collective-permute-start | bytes 122888 | tf_op jit(solution)/shard_map/ppermute | solution.py:298
  402.0 6.1 %collective-permute-start.10 = (bf16[32,640]{1,0:T(8,128)(2,1)S(1)}, bf16[32,640]{1,0:T(8,128)(2,1)S(1)}, u32[]{:S(2)}, u32[]{:S(2)}) collective-permute-start(bf16[32,640]{1,0:T(8,128)(2,1)S(1)} %fusion.17._), channel_id=1, source_target_pairs={{0,8},{1,9},{2,10},{3,11},{4,12},{5,13},{6,14},{7,15},{8,0},{9,1},... | collective-permute-start | bytes 122888 | tf_op jit(solution)/shard_map/ppermute | solution.py:298
  408.0 3.4 collective-permute-start.4
  409.0 5.0 %collective-permute-start.11 = (bf16[2,32,640]{2,1,0:T(8,128)(2,1)S(1)}, bf16[2,32,640]{2,1,0:T(8,128)(2,1)S(1)}, u32[]{:S(2)}, u32[]{:S(2)}) collective-permute-start(bf16[2,32,640]{2,1,0:T(8,128)(2,1)S(1)} %fusion.16), channel_id=1, source_target_pairs={{0,4},{1,5},{2,6},{3,7},{4,0},{5,1},{6,2},{7,3},{8,12},{9,13},{10,... | collective-permute-start | bytes 245768 | tf_op jit(solution)/shard_map/ppermute | solution.py:298
  412.5 7.1 %copy-start.3 = (bf16[128,512]{1,0:T(8,128)(2,1)}, bf16[128,512]{1,0:T(8,128)(2,1)S(1)}, u32[]{:S(2)}) copy-start(bf16[128,512]{1,0:T(8,128)(2,1)S(1)} %dynamic-slice_bitcast_fusion.1.rest_0_) | copy-start | bytes 393220
  412.5 6.4 %collective-permute-start.5 = (bf16[128,512]{1,0:T(8,128)(2,1)S(1)}, bf16[128,512]{1,0:T(8,128)(2,1)S(1)}, u32[]{:S(2)}, u32[]{:S(2)}) collective-permute-start(bf16[128,512]{1,0:T(8,128)(2,1)S(1)} %dynamic-slice_bitcast_fusion.1.rest_0_), channel_id=1, source_target_pairs={{0,2},{1,3},{2,0},{3,1},{4,6},{5,7},{6,4},{7,5},{8,10},{9,11},{10,... | collective-permute-start | bytes 393224 | tf_op jit(solution)/shard_map/ppermute | solution.py:298
  414.1 10.6 %collective-permute-start.12 = (bf16[2,2,32,640]{3,2,0,1:T(8,128)(2,1)S(1)}, bf16[2,2,32,640]{3,2,0,1:T(8,128)(2,1)S(1)}, u32[]{:S(2)}, u32[]{:S(2)}) collective-permute-start(bf16[2,2,32,640]{3,2,0,1:T(8,128)(2,1)S(1)} %fusion.13), channel_id=1, source_target_pairs={{0,2},{1,3},{2,0},{3,1},{4,6},{5,7},{6,4},{7,5},{8,10},{9,11},{10,... | collective-permute-start | bytes 491528 | tf_op jit(solution)/shard_map/ppermute | solution.py:298
  419.0 5.9 %collective-permute-start.6 = (bf16[128,512]{1,0:T(8,128)(2,1)S(1)}, bf16[128,512]{1,0:T(8,128)(2,1)S(1)}, u32[]{:S(2)}, u32[]{:S(2)}) collective-permute-start(bf16[128,512]{1,0:T(8,128)(2,1)S(1)} %fusion.10.rest_0_), channel_id=1, source_target_pairs={{0,4},{1,5},{2,6},{3,7},{4,0},{5,1},{6,2},{7,3},{8,12},{9,13},{10,... | collective-permute-start | bytes 393224 | tf_op jit(solution)/shard_map/ppermute | solution.py:298
  425.0 7.7 %copy-start = (bf16[128,512]{1,0:T(8,128)(2,1)}, bf16[128,512]{1,0:T(8,128)(2,1)S(1)}, u32[]{:S(2)}) copy-start(bf16[128,512]{1,0:T(8,128)(2,1)S(1)} %add_convert_fusion.2.rest_0_) | copy-start | bytes 393220
  425.0 7.7 %collective-permute-start.7 = (bf16[128,512]{1,0:T(8,128)(2,1)S(1)}, bf16[128,512]{1,0:T(8,128)(2,1)S(1)}, u32[]{:S(2)}, u32[]{:S(2)}) collective-permute-start(bf16[128,512]{1,0:T(8,128)(2,1)S(1)} %add_convert_fusion.2.rest_0_), channel_id=1, source_target_pairs={{0,8},{1,9},{2,10},{3,11},{4,12},{5,13},{6,14},{7,15},{8,0},{9,1},... | collective-permute-start | bytes 393224 | tf_op jit(solution)/shard_map/ppermute | solution.py:298
  427.5 10.6 %collective-permute-start.13 = (bf16[2,2,2,32,640]{4,3,0,1,2:T(8,128)(2,1)S(1)}, bf16[2,2,2,32,640]{4,3,0,1,2:T(8,128)(2,1)S(1)}, u32[]{:S(2)}, u32[]{:S(2)}) collective-permute-start(bf16[2,2,2,32,640]{4,3,0,1,2:T(8,128)(2,1)S(1)} %fusion.6), channel_id=1, source_target_pairs={{0,1},{1,0},{2,3},{3,2},{4,5},{5,4},{6,7},{7,6},{8,9},{9,8},{10,11... | collective-permute-start | bytes 983048 | tf_op jit(solution)/shard_map/ppermute | solution.py:298
  432.8 5.9 %collective-permute-start.8 = (bf16[128,512]{1,0:T(8,128)(2,1)S(1)}, bf16[128,512]{1,0:T(8,128)(2,1)S(1)}, u32[]{:S(2)}, u32[]{:S(2)}) collective-permute-start(bf16[128,512]{1,0:T(8,128)(2,1)S(1)} %add_convert_fusion.1), channel_id=1, source_target_pairs={{0,2},{1,3},{2,0},{3,1},{4,6},{5,7},{6,4},{7,5},{8,10},{9,11},{10,... | collective-permute-start | bytes 393224 | tf_op jit(solution)/shard_map/ppermute | solution.py:298
  438.8 1.6 collective-permute-start.9
  (2 other events, 6.6 us)

commit v16 on v15

--- a/solution.py
+++ b/solution.py
@@ -363,7 +363,7 @@
 
     unread = pl.BlockSpec(memory_space=pl.ANY)
     one_sent = pl.pallas_call(
-        functools.partial(send_value_kernel, per),
+        functools.partial(send_value_kernel, min(2, rows)),
         in_specs=[unread] * 2,
         out_specs=unread,
         out_shape=shape(sections),
@@ -371,8 +371,8 @@
             pltpu.VMEM((local_rows, D), bf16),
             pltpu.VMEM((D, D), bf16),
             pltpu.VMEM(sections, bf16),
-            pltpu.SemaphoreType.DMA((rows // per + 1,)),
-            pltpu.SemaphoreType.DMA((rows // per,)),
+            pltpu.SemaphoreType.DMA((rows // min(2, rows) + 1,)),
+            pltpu.SemaphoreType.DMA((rows // min(2, rows),)),
         ],
         compiler_params=params(),
         cost_estimate=cost(2.1, 9),
@@ -495,7 +495,7 @@
     gate_total = gate_part.reshape(D, D + LANES)
 
     unit = rows // 8
-    pieces = [3, 3, 2]
+    pieces = [2, 2, 2, 2]
 
     def piece(i, grad_tokens, after):
         first = sum(pieces[:i])
@@ -526,8 +526,8 @@
         elif b > 1:
             kept, given = value_part, value_part
         got = from_partner(given, b, n)
-        if 0 < b <= len(pieces):
-            grad_tokens = piece(b - 1, grad_tokens, given)
+        if b < len(pieces):
+            grad_tokens = piece(b, grad_tokens, given)
         value_part = added(kept, got)
     for b in (1, 0):
         value_part = doubled(value_part, 1 - b, b, n)

time: 443 us -> 443 us (level)
    pallas_call x3 -> x4, Pallas kernels: 14 us -> 15 us  [piece(): pl.pallas_call(tokens_kernel, grid=(pieces[i],), in_specs=[pl.BlockSpec((...]
  transfers between devices with their start and end apart: 18 -> 18, of which waited for: 10 -> 12; matrix products, arithmetic and copies ran while one was open for 2% -> 2% of each run, Pallas kernels for 22% -> 22%
where the time goes in v16:
time: 443 us; the launch traced here: 442 us
  waiting for transfers between devices  245 us (55%)
  Pallas kernels  104 us (23%)
  starting transfers between devices  82.9 us (19%)
  other arithmetic  5.98 us (1%)
    all_to_all x4, waiting for transfers between devices, transfer(): return lax.all_to_all(array, 'seq', split_axis=0, concat_axis=0, tiled=True)  166 us
    ppermute x14, waiting for transfers between devices, from_partner(): return lax.ppermute(array, 'seq', [(i, i ^ 1 << b) for i in range(n)])  78.4 us
    all_to_all x4, starting transfers between devices, transfer(): return lax.all_to_all(array, 'seq', split_axis=0, concat_axis=0, tiled=True)  66.9 us
    pallas_call x1, Pallas kernels, on_device(): pl.pallas_call(home_forward_kernel, grid=(chans // GROUP,), in_specs=[at_...  26 us
    pallas_call x1, Pallas kernels, on_device(): pl.pallas_call(home_backward_kernel, grid=(chans // GROUP,), in_specs=[at...  20.6 us
    pallas_call x1, Pallas kernels, on_device(): pl.pallas_call(d_three_kernel, grid=(rows // per,), in_specs=[row, row, s...  17.1 us
    ppermute x14, starting transfers between devices, from_partner(): return lax.ppermute(array, 'seq', [(i, i ^ 1 << b) for i in range(n)])  16 us
    pallas_call x4, Pallas kernels, piece(): pl.pallas_call(tokens_kernel, grid=(pieces[i],), in_specs=[pl.BlockSpec((...  15 us
  transfers between devices with their start and end apart: 18, of which 12 were waited for; matrix products, arithmetic and copies ran while one was open for 2% of the time, Pallas kernels for 22%

profile of v16, /device:TPU:0, one launch (start us, length us, event | category | flops | bytes accessed | tf_op | source)
XLA Modules:
  0.0 442.3 jit_solution(12612612172170925187)
XLA Ops:
  0.6 6.3 %shard_map.130 = bf16[16,16,32,256]{3,2,1,0:T(8,128)(2,1)} custom-call(bf16[4096,512]{1,0:T(8,128)(2,1)} %tokens.3, bf16[512,512]{1,0:T(8,128)(2,1)} %w_value.3), custom_call_target="tpu_custom_call" | custom-call | flops 2100000000 | bytes 9437184 | tf_op jit(solution)/shard_map/pallas_call | solution.py:365
  6.9 7.4 %all-to-all-start.1 = ((bf16[16,16,32,256]{3,2,1,0:T(8,128)(2,1)}), bf16[16,16,32,256]{3,2,1,0:T(8,128)(2,1)}, u32[]{:S(2)}, u32[]{:S(2)}) async-start(bf16[16,16,32,256]{3,2,1,0:T(8,128)(2,1)} %shard_map.130), calls=%async_computation.1 | async-start | bytes 8388608 | tf_op jit(solution)/shard_map/all_to_all | solution.py:362
  14.4 17.1 %shard_map.129 = (bf16[16,16,32,256]{3,2,1,0:T(8,128)(2,1)}, bf16[4096,512]{1,0:T(8,128)(2,1)}, bf16[4096,512]{1,0:T(8,128)(2,1)}, bf16[512,4096]{1,0:T(8,128)(2...) custom-call(bf16[4096,512]{1,0:T(8,128)(2,1)} %tokens.3, ...), custom_call_target="tpu_custom_call" | custom-call | flops 8600000512 | bytes 31457280 | tf_op jit(solution)/shard_map/pallas_call | solution.py:382
  31.4 60.6 %all-to-all-done.1 = bf16[16,16,32,256]{3,2,1,0:T(8,128)(2,1)} async-done(((bf16[16,16,32,256]{3,2,1,0:T(8,128)(2,1)}), bf16[16,16,32,256]{3,2,1,0:T(8,128)(2,1)}, u32[]{:S(2)}, u32[]{:S(2)}) %all-to-all-start.1) | async-done | bytes 4194336 | tf_op jit(solution)/shard_map/all_to_all | solution.py:362
  92.0 19.8 %all-to-all-start = ((bf16[16,16,32,256]{3,2,1,0:T(8,128)(2,1)}), bf16[16,16,32,256]{3,2,1,0:T(8,128)(2,1)}, u32[]{:S(2)}, u32[]{:S(2)}) async-start(bf16[16,16,32,256]{3,2,1,0:T(8,128)(2,1)} %get-tuple-element.21), calls=%async_computation | async-start | bytes 8388608 | tf_op jit(solution)/shard_map/all_to_all | solution.py:362
  113.4 26.0 %shard_map.131 = (bf16[256,32,256]{2,1,0:T(8,128)(2,1)}, f32[32,256,256]{2,1,0:T(8,128)}) custom-call(bf16[256,32,256]{2,1,0:T(8,128)(2,1)} %bitcast.2.arrived, bf16[32,256,256]{2,1,0:T(8,128)(2,1)} %kernel.3, bf16[256,256]{1,0:T(8,128)(2,1)} %bitcast.60, bf16[256,256]{1,0:T(8,128)(2,1)} %second.1, bf16[256,256]{1,0:T(8,128)(2,1)} %third.1, ...), custom_call_target="tpu_custom_call" | custom-call | flops 5400000000 | bytes 20971520 | tf_op jit(solution)/shard_map/pallas_call | solution.py:406
  139.3 50.2 %all-to-all-done = bf16[16,16,32,256]{3,2,1,0:T(8,128)(2,1)} async-done(((bf16[16,16,32,256]{3,2,1,0:T(8,128)(2,1)}), bf16[16,16,32,256]{3,2,1,0:T(8,128)(2,1)}, u32[]{:S(2)}, u32[]{:S(2)}) %all-to-all-start) | async-done | bytes 4194336 | tf_op jit(solution)/shard_map/all_to_all | solution.py:362
  189.6 19.8 %all-to-all-start.3 = ((bf16[16,16,32,256]{3,2,1,0:T(8,128)(2,1)}), bf16[16,16,32,256]{3,2,1,0:T(8,128)(2,1)}, u32[]{:S(2)}, u32[]{:S(2)}) async-start(bf16[16,16,32,256]{3,2,1,0:T(8,128)(2,1)} %bitcast.59), calls=%async_computation.3 | async-start | bytes 8388608 | tf_op jit(solution)/shard_map/all_to_all | solution.py:362
  210.9 20.6 %shard_map.132 = (bf16[256,32,256]{2,1,0:T(8,128)(2,1)}, bf16[32,256,256]{2,1,0:T(8,128)(2,1)}) custom-call(bf16[256,32,256]{2,1,0:T(8,128)(2,1)} %bitcast.1.arrived, bf16[32,256,256]{2,1,0:T(8,128)(2,1)} %kernel.3, f32[32,256,256]{2,1,0:T(8,128)} %get-tuple-element.22.spectrum, bf16[256,256]{1,0:T(8,128)(2,1)} %bitcast.75, bf16[256,256]{1,0:T(8,128)(2,1)} %bitcast.76, ...), custom_call_target="tpu_custom_call" | custom-call | flops 4300000256 | bytes 25165824 | tf_op jit(solution)/shard_map/pallas_call | solution.py:425
  231.5 55.5 %all-to-all-done.3.arrived = bf16[16,16,32,256]{3,2,1,0:T(8,128)(2,1)} async-done(((bf16[16,16,32,256]{3,2,1,0:T(8,128)(2,1)}), bf16[16,16,32,256]{3,2,1,0:T(8,128)(2,1)}, u32[]{:S(2)}, u32[]{:S(2)}) %all-to-all-start.3) | async-done | bytes 4194336 | tf_op jit(solution)/shard_map/all_to_all | solution.py:362
  287.1 19.8 %all-to-all-start.2 = ((bf16[16,16,32,256]{3,2,1,0:T(8,128)(2,1)}), bf16[16,16,32,256]{3,2,1,0:T(8,128)(2,1)}, u32[]{:S(2)}, u32[]{:S(2)}) async-start(bf16[16,16,32,256]{3,2,1,0:T(8,128)(2,1)} %bitcast.58), calls=%async_computation.2 | async-start | bytes 8388608 | tf_op jit(solution)/shard_map/all_to_all | solution.py:362
  306.9 14.1 %shard_map.133 = (bf16[4096,512]{1,0:T(8,128)(2,1)}, bf16[512,512]{1,0:T(8,128)(2,1)}) custom-call(bf16[16,16,32,256]{3,2,1,0:T(8,128)(2,1)} %all-to-all-done.3.arrived, bf16[512,4096]{1,0:T(8,128)(2,1)} %get-tuple-element.25.tokens_t, bf16[4096,512]{1,0:T(8,128)(2,1)} %get-tuple-element.26.value, bf16[4096,512]{1,0:T(8,128)(2,1)} %cotangent.3, ...), custom_call_target="tpu_custom_call" | custom-call | flops 5400000000 | bytes 26214400 | tf_op jit(solution)/shard_map/pallas_call | solution.py:444
  324.2 1.9 collective-permute-start.1
  326.1 10.8 %collective-permute-done.1 = bf16[2,2,32,640]{3,2,0,1:T(8,128)(2,1)S(1)} collective-permute-done((bf16[2,2,32,640]{3,2,0,1:T(8,128)(2,1)S(1)}, bf16[2,2,32,640]{3,2,0,1:T(8,128)(2,1)S(1)}, u32[]{:S(2)}, u32[]{:S(2)}) %collective-permute-start.1) | collective-permute-done | bytes 163872 | tf_op jit(solution)/shard_map/ppermute | solution.py:298
  337.1 40.1 %collective-permute-done.2 = bf16[2,32,640]{2,1,0:T(8,128)(2,1)S(1)} collective-permute-done((bf16[2,32,640]{2,1,0:T(8,128)(2,1)S(1)}, bf16[2,32,640]{2,1,0:T(8,128)(2,1)S(1)}, u32[]{:S(2)}, u32[]{:S(2)}) %collective-permute-start.2) | collective-permute-done | bytes 81952 | tf_op jit(solution)/shard_map/ppermute | solution.py:298
  377.3 4.6 %collective-permute-start.3 = (bf16[32,640]{1,0:T(8,128)(2,1)S(1)}, bf16[32,640]{1,0:T(8,128)(2,1)S(1)}, u32[]{:S(2)}, u32[]{:S(2)}) collective-permute-start(bf16[32,640]{1,0:T(8,128)(2,1)S(1)} %dynamic-slice_bitcast_fusion.3), channel_id=1, source_target_pairs={{0,8},{1,9},{2,10},{3,11},{4,12},{5,13},{6,14},{7,15},{8,0},{9,1},... | collective-permute-start | bytes 122888 | tf_op jit(solution)/shard_map/ppermute | solution.py:298
  381.9 20.8 %collective-permute-done.3 = bf16[32,640]{1,0:T(8,128)(2,1)S(1)} collective-permute-done((bf16[32,640]{1,0:T(8,128)(2,1)S(1)}, bf16[32,640]{1,0:T(8,128)(2,1)S(1)}, u32[]{:S(2)}, u32[]{:S(2)}) %collective-permute-start.3) | collective-permute-done | bytes 40992 | tf_op jit(solution)/shard_map/ppermute | solution.py:298
  403.3 5.4 %shard_map.134 = (bf16[2,128,512]{2,1,0:T(8,128)(2,1)}, bf16[2,128,512]{2,1,0:T(8,128)(2,1)}) custom-call(bf16[16,16,32,256]{3,2,1,0:T(8,128)(2,1)} %all-to-all-done.2.arrived, bf16[4096,512]{1,0:T(8,128)(2,1)} %get-tuple-element.31.turned, f32[512,512]{1,0:T(8,128)} %get-tuple-element.32.direct, f32[1,1]{1,0:T(1,128)} %constant.77.clone.1.factor, ...), custom_call_target="tpu_custom_call" | custom-call | flops 2200000000 | bytes 9961472 | tf_op jit(solution)/shard_map/pallas_call | solution.py:477
  408.8 3.8 shard_map.135.rest_1_
  420.8 3.7 shard_map.136.rest_1_
  425.2 2.0 collective-permute-start.7
  427.5 3.8 shard_map.137.rest_1_
  431.3 1.9 collective-permute-done.7
  434.6 3.7 shard_map.138
  (79 shorter events, 21.5 us)
Async XLA Ops:
  6.9 85.1 %all-to-all-start.1 = ((bf16[16,16,32,256]{3,2,1,0:T(8,128)(2,1)}), bf16[16,16,32,256]{3,2,1,0:T(8,128)(2,1)}, u32[]{:S(2)}, u32[]{:S(2)}) async-start(bf16[16,16,32,256]{3,2,1,0:T(8,128)(2,1)} %shard_map.130), calls=%async_computation.1 | async-start | bytes 8388608 | tf_op jit(solution)/shard_map/all_to_all | solution.py:362
  92.0 19.8 %copy-start.6 = (bf16[256,256]{1,0:T(8,128)(2,1)S(1)}, bf16[256,256]{1,0:T(8,128)(2,1)}, u32[]{:S(2)}) copy-start(bf16[256,256]{1,0:T(8,128)(2,1)} %first.1) | copy-start | bytes 393220
  92.0 97.5 %all-to-all-start = ((bf16[16,16,32,256]{3,2,1,0:T(8,128)(2,1)}), bf16[16,16,32,256]{3,2,1,0:T(8,128)(2,1)}, u32[]{:S(2)}, u32[]{:S(2)}) async-start(bf16[16,16,32,256]{3,2,1,0:T(8,128)(2,1)} %get-tuple-element.21), calls=%async_computation | async-start | bytes 8388608 | tf_op jit(solution)/shard_map/all_to_all | solution.py:362
  189.5 19.8 %copy-start.7 = (bf16[256,256]{1,0:T(8,128)(2,1)S(1)}, bf16[256,256]{1,0:T(8,128)(2,1)}, u32[]{:S(2)}) copy-start(bf16[256,256]{1,0:T(8,128)(2,1)} %second.1) | copy-start | bytes 393220
  189.5 20.6 %copy-start.8 = (bf16[256,256]{1,0:T(8,128)(2,1)S(1)}, bf16[256,256]{1,0:T(8,128)(2,1)}, u32[]{:S(2)}) copy-start(bf16[256,256]{1,0:T(8,128)(2,1)} %third.1) | copy-start | bytes 393220
  189.6 97.5 %all-to-all-start.3 = ((bf16[16,16,32,256]{3,2,1,0:T(8,128)(2,1)}), bf16[16,16,32,256]{3,2,1,0:T(8,128)(2,1)}, u32[]{:S(2)}, u32[]{:S(2)}) async-start(bf16[16,16,32,256]{3,2,1,0:T(8,128)(2,1)} %bitcast.59), calls=%async_computation.3 | async-start | bytes 8388608 | tf_op jit(solution)/shard_map/all_to_all | solution.py:362
  287.1 19.9 %copy-start.9 = (f32[1,512]{1,0:T(1,128)S(1)}, f32[1,512]{1,0:T(1,128)}, u32[]{:S(2)}) copy-start(f32[1,512]{1,0:T(1,128)} %get-tuple-element.34) | copy-start | bytes 6148
  287.1 115.7 %all-to-all-start.2 = ((bf16[16,16,32,256]{3,2,1,0:T(8,128)(2,1)}), bf16[16,16,32,256]{3,2,1,0:T(8,128)(2,1)}, u32[]{:S(2)}, u32[]{:S(2)}) async-start(bf16[16,16,32,256]{3,2,1,0:T(8,128)(2,1)} %bitcast.58), calls=%async_computation.2 | async-start | bytes 8388608 | tf_op jit(solution)/shard_map/all_to_all | solution.py:362
  322.4 1.7 collective-permute-start
  324.2 12.8 %collective-permute-start.1 = (bf16[2,2,32,640]{3,2,0,1:T(8,128)(2,1)S(1)}, bf16[2,2,32,640]{3,2,0,1:T(8,128)(2,1)S(1)}, u32[]{:S(2)}, u32[]{:S(2)}) collective-permute-start(bf16[2,2,32,640]{3,2,0,1:T(8,128)(2,1)S(1)} %dynamic-slice_bitcast_fusion), channel_id=1, source_target_pairs={{0,2},{1,3},{2,0},{3,1},{4,6},{5,7},{6,4},{7,5},{8,10},{9,11},{10,... | collective-permute-start | bytes 491528 | tf_op jit(solution)/shard_map/ppermute | solution.py:298
  337.0 40.2 %collective-permute-start.2 = (bf16[2,32,640]{2,1,0:T(8,128)(2,1)S(1)}, bf16[2,32,640]{2,1,0:T(8,128)(2,1)S(1)}, u32[]{:S(2)}, u32[]{:S(2)}) collective-permute-start(bf16[2,32,640]{2,1,0:T(8,128)(2,1)S(1)} %dynamic-slice_bitcast_fusion.2), channel_id=1, source_target_pairs={{0,4},{1,5},{2,6},{3,7},{4,0},{5,1},{6,2},{7,3},{8,12},{9,13},{10,... | collective-permute-start | bytes 245768 | tf_op jit(solution)/shard_map/ppermute | solution.py:298
  377.3 25.4 %collective-permute-start.3 = (bf16[32,640]{1,0:T(8,128)(2,1)S(1)}, bf16[32,640]{1,0:T(8,128)(2,1)S(1)}, u32[]{:S(2)}, u32[]{:S(2)}) collective-permute-start(bf16[32,640]{1,0:T(8,128)(2,1)S(1)} %dynamic-slice_bitcast_fusion.3), channel_id=1, source_target_pairs={{0,8},{1,9},{2,10},{3,11},{4,12},{5,13},{6,14},{7,15},{8,0},{9,1},... | collective-permute-start | bytes 122888 | tf_op jit(solution)/shard_map/ppermute | solution.py:298
  402.7 9.9 %collective-permute-start.10 = (bf16[32,640]{1,0:T(8,128)(2,1)S(1)}, bf16[32,640]{1,0:T(8,128)(2,1)S(1)}, u32[]{:S(2)}, u32[]{:S(2)}) collective-permute-start(bf16[32,640]{1,0:T(8,128)(2,1)S(1)} %fusion.17._), channel_id=1, source_target_pairs={{0,8},{1,9},{2,10},{3,11},{4,12},{5,13},{6,14},{7,15},{8,0},{9,1},... | collective-permute-start | bytes 122888 | tf_op jit(solution)/shard_map/ppermute | solution.py:298
  408.7 5.6 %collective-permute-start.4 = (bf16[2,128,512]{2,1,0:T(8,128)(2,1)}, bf16[2,128,512]{2,1,0:T(8,128)(2,1)S(1)}, u32[]{:S(2)}, u32[]{:S(2)}) collective-permute-start(bf16[2,128,512]{2,1,0:T(8,128)(2,1)} %get-tuple-element.36.rest_0_), channel_id=1, source_target_pairs={{0,1},{1,0},{2,3},{3,2},{4,5},{5,4},{6,7},{7,6},{8,9},{9,8},{10,11... | collective-permute-start | bytes 786440 | tf_op jit(solution)/shard_map/ppermute | solution.py:298
  412.7 4.9 %collective-permute-start.11 = (bf16[2,32,640]{2,1,0:T(8,128)(2,1)S(1)}, bf16[2,32,640]{2,1,0:T(8,128)(2,1)S(1)}, u32[]{:S(2)}, u32[]{:S(2)}) collective-permute-start(bf16[2,32,640]{2,1,0:T(8,128)(2,1)S(1)} %fusion.16), channel_id=1, source_target_pairs={{0,4},{1,5},{2,6},{3,7},{4,0},{5,1},{6,2},{7,3},{8,12},{9,13},{10,... | collective-permute-start | bytes 245768 | tf_op jit(solution)/shard_map/ppermute | solution.py:298
  414.4 6.4 %copy-start.4 = (bf16[128,512]{1,0:T(8,128)(2,1)}, bf16[128,512]{1,0:T(8,128)(2,1)S(1)}, u32[]{:S(2)}) copy-start(bf16[128,512]{1,0:T(8,128)(2,1)S(1)} %dynamic-slice_bitcast_fusion.1.rest_0_) | copy-start | bytes 393220
  414.4 5.7 %collective-permute-start.5 = (bf16[128,512]{1,0:T(8,128)(2,1)S(1)}, bf16[128,512]{1,0:T(8,128)(2,1)S(1)}, u32[]{:S(2)}, u32[]{:S(2)}) collective-permute-start(bf16[128,512]{1,0:T(8,128)(2,1)S(1)} %dynamic-slice_bitcast_fusion.1.rest_0_), channel_id=1, source_target_pairs={{0,2},{1,3},{2,0},{3,1},{4,6},{5,7},{6,4},{7,5},{8,10},{9,11},{10,... | collective-permute-start | bytes 393224 | tf_op jit(solution)/shard_map/ppermute | solution.py:298
  417.7 6.9 %collective-permute-start.12 = (bf16[2,2,32,640]{3,2,0,1:T(8,128)(2,1)S(1)}, bf16[2,2,32,640]{3,2,0,1:T(8,128)(2,1)S(1)}, u32[]{:S(2)}, u32[]{:S(2)}) collective-permute-start(bf16[2,2,32,640]{3,2,0,1:T(8,128)(2,1)S(1)} %fusion.13), channel_id=1, source_target_pairs={{0,2},{1,3},{2,0},{3,1},{4,6},{5,7},{6,4},{7,5},{8,10},{9,11},{10,... | collective-permute-start | bytes 491528 | tf_op jit(solution)/shard_map/ppermute | solution.py:298
  420.1 5.0 %collective-permute-start.6 = (bf16[128,512]{1,0:T(8,128)(2,1)S(1)}, bf16[128,512]{1,0:T(8,128)(2,1)S(1)}, u32[]{:S(2)}, u32[]{:S(2)}) collective-permute-start(bf16[128,512]{1,0:T(8,128)(2,1)S(1)} %fusion.10.rest_0_), channel_id=1, source_target_pairs={{0,4},{1,5},{2,6},{3,7},{4,0},{5,1},{6,2},{7,3},{8,12},{9,13},{10,... | collective-permute-start | bytes 393224 | tf_op jit(solution)/shard_map/ppermute | solution.py:298
  425.2 7.9 %copy-start = (bf16[128,512]{1,0:T(8,128)(2,1)}, bf16[128,512]{1,0:T(8,128)(2,1)S(1)}, u32[]{:S(2)}) copy-start(bf16[128,512]{1,0:T(8,128)(2,1)S(1)} %add_convert_fusion.2.rest_0_) | copy-start | bytes 393220
  425.2 7.9 %collective-permute-start.7 = (bf16[128,512]{1,0:T(8,128)(2,1)S(1)}, bf16[128,512]{1,0:T(8,128)(2,1)S(1)}, u32[]{:S(2)}, u32[]{:S(2)}) collective-permute-start(bf16[128,512]{1,0:T(8,128)(2,1)S(1)} %add_convert_fusion.2.rest_0_), channel_id=1, source_target_pairs={{0,8},{1,9},{2,10},{3,11},{4,12},{5,13},{6,14},{7,15},{8,0},{9,1},... | collective-permute-start | bytes 393224 | tf_op jit(solution)/shard_map/ppermute | solution.py:298
  427.4 10.9 %collective-permute-start.13 = (bf16[2,2,2,32,640]{4,3,0,1,2:T(8,128)(2,1)S(1)}, bf16[2,2,2,32,640]{4,3,0,1,2:T(8,128)(2,1)S(1)}, u32[]{:S(2)}, u32[]{:S(2)}) collective-permute-start(bf16[2,2,2,32,640]{4,3,0,1,2:T(8,128)(2,1)S(1)} %fusion.6), channel_id=1, source_target_pairs={{0,1},{1,0},{2,3},{3,2},{4,5},{5,4},{6,7},{7,6},{8,9},{9,8},{10,11... | collective-permute-start | bytes 983048 | tf_op jit(solution)/shard_map/ppermute | solution.py:298
  433.2 5.6 %collective-permute-start.8 = (bf16[128,512]{1,0:T(8,128)(2,1)S(1)}, bf16[128,512]{1,0:T(8,128)(2,1)S(1)}, u32[]{:S(2)}, u32[]{:S(2)}) collective-permute-start(bf16[128,512]{1,0:T(8,128)(2,1)S(1)} %add_convert_fusion.1), channel_id=1, source_target_pairs={{0,2},{1,3},{2,0},{3,1},{4,6},{5,7},{6,4},{7,5},{8,10},{9,11},{10,... | collective-permute-start | bytes 393224 | tf_op jit(solution)/shard_map/ppermute | solution.py:298
  439.0 1.6 collective-permute-start.9
  (4 other events, 15.0 us)

commit v17 on v16

--- a/solution.py
+++ b/solution.py
@@ -363,7 +363,7 @@
 
     unread = pl.BlockSpec(memory_space=pl.ANY)
     one_sent = pl.pallas_call(
-        functools.partial(send_value_kernel, min(2, rows)),
+        functools.partial(send_value_kernel, per),
         in_specs=[unread] * 2,
         out_specs=unread,
         out_shape=shape(sections),
@@ -371,8 +371,8 @@
             pltpu.VMEM((local_rows, D), bf16),
             pltpu.VMEM((D, D), bf16),
             pltpu.VMEM(sections, bf16),
-            pltpu.SemaphoreType.DMA((rows // min(2, rows) + 1,)),
-            pltpu.SemaphoreType.DMA((rows // min(2, rows),)),
+            pltpu.SemaphoreType.DMA((rows // per + 1,)),
+            pltpu.SemaphoreType.DMA((rows // per,)),
         ],
         compiler_params=params(),
         cost_estimate=cost(2.1, 9),

time: 443 us -> 442 us (level)
  no operation moved by 1% of the time
where the time goes in v17:
time: 442 us
  waiting for transfers between devices  245 us (55%)
  Pallas kernels  104 us (24%)
  starting transfers between devices  83 us (19%)
  other arithmetic  5.98 us (1%)
    all_to_all x4, waiting for transfers between devices, transfer(): return lax.all_to_all(array, 'seq', split_axis=0, concat_axis=0, tiled=True)  166 us
    ppermute x14, waiting for transfers between devices, from_partner(): return lax.ppermute(array, 'seq', [(i, i ^ 1 << b) for i in range(n)])  78.4 us
    all_to_all x4, starting transfers between devices, transfer(): return lax.all_to_all(array, 'seq', split_axis=0, concat_axis=0, tiled=True)  66.9 us
    pallas_call x1, Pallas kernels, on_device(): pl.pallas_call(home_forward_kernel, grid=(chans // GROUP,), in_specs=[at_...  26 us
    pallas_call x1, Pallas kernels, on_device(): pl.pallas_call(home_backward_kernel, grid=(chans // GROUP,), in_specs=[at...  20.6 us
    pallas_call x1, Pallas kernels, on_device(): pl.pallas_call(d_three_kernel, grid=(rows // per,), in_specs=[row, row, s...  17.1 us
    ppermute x14, starting transfers between devices, from_partner(): return lax.ppermute(array, 'seq', [(i, i ^ 1 << b) for i in range(n)])  16 us
    pallas_call x4, Pallas kernels, piece(): pl.pallas_call(tokens_kernel, grid=(pieces[i],), in_specs=[pl.BlockSpec((...  15 us
  transfers between devices with their start and end apart: 18, of which 12 were waited for; matrix products, arithmetic and copies ran while one was open for 2% of the time, Pallas kernels for 22%

profile of v17, /device:TPU:0, one launch (start us, length us, event | category | flops | bytes accessed | tf_op | source)
XLA Modules:
  0.0 441.7 jit_solution(5258535799762421464)
XLA Ops:
  0.6 5.6 %shard_map.130 = bf16[16,16,32,256]{3,2,1,0:T(8,128)(2,1)} custom-call(bf16[4096,512]{1,0:T(8,128)(2,1)} %tokens.3, bf16[512,512]{1,0:T(8,128)(2,1)} %w_value.3), custom_call_target="tpu_custom_call" | custom-call | flops 2100000000 | bytes 9437184 | tf_op jit(solution)/shard_map/pallas_call | solution.py:365
  6.2 7.5 %all-to-all-start.1 = ((bf16[16,16,32,256]{3,2,1,0:T(8,128)(2,1)}), bf16[16,16,32,256]{3,2,1,0:T(8,128)(2,1)}, u32[]{:S(2)}, u32[]{:S(2)}) async-start(bf16[16,16,32,256]{3,2,1,0:T(8,128)(2,1)} %shard_map.130), calls=%async_computation.1 | async-start | bytes 8388608 | tf_op jit(solution)/shard_map/all_to_all | solution.py:362
  13.7 17.1 %shard_map.129 = (bf16[16,16,32,256]{3,2,1,0:T(8,128)(2,1)}, bf16[4096,512]{1,0:T(8,128)(2,1)}, bf16[4096,512]{1,0:T(8,128)(2,1)}, bf16[512,4096]{1,0:T(8,128)(2...) custom-call(bf16[4096,512]{1,0:T(8,128)(2,1)} %tokens.3, ...), custom_call_target="tpu_custom_call" | custom-call | flops 8600000512 | bytes 31457280 | tf_op jit(solution)/shard_map/pallas_call | solution.py:382
  30.7 60.6 %all-to-all-done.1 = bf16[16,16,32,256]{3,2,1,0:T(8,128)(2,1)} async-done(((bf16[16,16,32,256]{3,2,1,0:T(8,128)(2,1)}), bf16[16,16,32,256]{3,2,1,0:T(8,128)(2,1)}, u32[]{:S(2)}, u32[]{:S(2)}) %all-to-all-start.1) | async-done | bytes 4194336 | tf_op jit(solution)/shard_map/all_to_all | solution.py:362
  91.3 19.8 %all-to-all-start = ((bf16[16,16,32,256]{3,2,1,0:T(8,128)(2,1)}), bf16[16,16,32,256]{3,2,1,0:T(8,128)(2,1)}, u32[]{:S(2)}, u32[]{:S(2)}) async-start(bf16[16,16,32,256]{3,2,1,0:T(8,128)(2,1)} %get-tuple-element.21), calls=%async_computation | async-start | bytes 8388608 | tf_op jit(solution)/shard_map/all_to_all | solution.py:362
  112.7 26.0 %shard_map.131 = (bf16[256,32,256]{2,1,0:T(8,128)(2,1)}, f32[32,256,256]{2,1,0:T(8,128)}) custom-call(bf16[256,32,256]{2,1,0:T(8,128)(2,1)} %bitcast.2.arrived, bf16[32,256,256]{2,1,0:T(8,128)(2,1)} %kernel.3, bf16[256,256]{1,0:T(8,128)(2,1)} %bitcast.60, bf16[256,256]{1,0:T(8,128)(2,1)} %second.1, bf16[256,256]{1,0:T(8,128)(2,1)} %third.1, ...), custom_call_target="tpu_custom_call" | custom-call | flops 5400000000 | bytes 20971520 | tf_op jit(solution)/shard_map/pallas_call | solution.py:406
  138.6 50.2 %all-to-all-done = bf16[16,16,32,256]{3,2,1,0:T(8,128)(2,1)} async-done(((bf16[16,16,32,256]{3,2,1,0:T(8,128)(2,1)}), bf16[16,16,32,256]{3,2,1,0:T(8,128)(2,1)}, u32[]{:S(2)}, u32[]{:S(2)}) %all-to-all-start) | async-done | bytes 4194336 | tf_op jit(solution)/shard_map/all_to_all | solution.py:362
  188.9 19.8 %all-to-all-start.3 = ((bf16[16,16,32,256]{3,2,1,0:T(8,128)(2,1)}), bf16[16,16,32,256]{3,2,1,0:T(8,128)(2,1)}, u32[]{:S(2)}, u32[]{:S(2)}) async-start(bf16[16,16,32,256]{3,2,1,0:T(8,128)(2,1)} %bitcast.59), calls=%async_computation.3 | async-start | bytes 8388608 | tf_op jit(solution)/shard_map/all_to_all | solution.py:362
  210.2 20.6 %shard_map.132 = (bf16[256,32,256]{2,1,0:T(8,128)(2,1)}, bf16[32,256,256]{2,1,0:T(8,128)(2,1)}) custom-call(bf16[256,32,256]{2,1,0:T(8,128)(2,1)} %bitcast.1.arrived, bf16[32,256,256]{2,1,0:T(8,128)(2,1)} %kernel.3, f32[32,256,256]{2,1,0:T(8,128)} %get-tuple-element.22.spectrum, bf16[256,256]{1,0:T(8,128)(2,1)} %bitcast.75, bf16[256,256]{1,0:T(8,128)(2,1)} %bitcast.76, ...), custom_call_target="tpu_custom_call" | custom-call | flops 4300000256 | bytes 25165824 | tf_op jit(solution)/shard_map/pallas_call | solution.py:425
  230.8 55.5 %all-to-all-done.3.arrived = bf16[16,16,32,256]{3,2,1,0:T(8,128)(2,1)} async-done(((bf16[16,16,32,256]{3,2,1,0:T(8,128)(2,1)}), bf16[16,16,32,256]{3,2,1,0:T(8,128)(2,1)}, u32[]{:S(2)}, u32[]{:S(2)}) %all-to-all-start.3) | async-done | bytes 4194336 | tf_op jit(solution)/shard_map/all_to_all | solution.py:362
  286.4 19.8 %all-to-all-start.2 = ((bf16[16,16,32,256]{3,2,1,0:T(8,128)(2,1)}), bf16[16,16,32,256]{3,2,1,0:T(8,128)(2,1)}, u32[]{:S(2)}, u32[]{:S(2)}) async-start(bf16[16,16,32,256]{3,2,1,0:T(8,128)(2,1)} %bitcast.58), calls=%async_computation.2 | async-start | bytes 8388608 | tf_op jit(solution)/shard_map/all_to_all | solution.py:362
  306.2 14.1 %shard_map.133 = (bf16[4096,512]{1,0:T(8,128)(2,1)}, bf16[512,512]{1,0:T(8,128)(2,1)}) custom-call(bf16[16,16,32,256]{3,2,1,0:T(8,128)(2,1)} %all-to-all-done.3.arrived, bf16[512,4096]{1,0:T(8,128)(2,1)} %get-tuple-element.25.tokens_t, bf16[4096,512]{1,0:T(8,128)(2,1)} %get-tuple-element.26.value, bf16[4096,512]{1,0:T(8,128)(2,1)} %cotangent.3, ...), custom_call_target="tpu_custom_call" | custom-call | flops 5400000000 | bytes 26214400 | tf_op jit(solution)/shard_map/pallas_call | solution.py:444
  323.5 1.9 collective-permute-start.1
  325.4 10.8 %collective-permute-done.1 = bf16[2,2,32,640]{3,2,0,1:T(8,128)(2,1)S(1)} collective-permute-done((bf16[2,2,32,640]{3,2,0,1:T(8,128)(2,1)S(1)}, bf16[2,2,32,640]{3,2,0,1:T(8,128)(2,1)S(1)}, u32[]{:S(2)}, u32[]{:S(2)}) %collective-permute-start.1) | collective-permute-done | bytes 163872 | tf_op jit(solution)/shard_map/ppermute | solution.py:298
  336.4 40.1 %collective-permute-done.2 = bf16[2,32,640]{2,1,0:T(8,128)(2,1)S(1)} collective-permute-done((bf16[2,32,640]{2,1,0:T(8,128)(2,1)S(1)}, bf16[2,32,640]{2,1,0:T(8,128)(2,1)S(1)}, u32[]{:S(2)}, u32[]{:S(2)}) %collective-permute-start.2) | collective-permute-done | bytes 81952 | tf_op jit(solution)/shard_map/ppermute | solution.py:298
  376.6 4.6 %collective-permute-start.3 = (bf16[32,640]{1,0:T(8,128)(2,1)S(1)}, bf16[32,640]{1,0:T(8,128)(2,1)S(1)}, u32[]{:S(2)}, u32[]{:S(2)}) collective-permute-start(bf16[32,640]{1,0:T(8,128)(2,1)S(1)} %dynamic-slice_bitcast_fusion.3), channel_id=1, source_target_pairs={{0,8},{1,9},{2,10},{3,11},{4,12},{5,13},{6,14},{7,15},{8,0},{9,1},... | collective-permute-start | bytes 122888 | tf_op jit(solution)/shard_map/ppermute | solution.py:298
  381.2 20.8 %collective-permute-done.3 = bf16[32,640]{1,0:T(8,128)(2,1)S(1)} collective-permute-done((bf16[32,640]{1,0:T(8,128)(2,1)S(1)}, bf16[32,640]{1,0:T(8,128)(2,1)S(1)}, u32[]{:S(2)}, u32[]{:S(2)}) %collective-permute-start.3) | collective-permute-done | bytes 40992 | tf_op jit(solution)/shard_map/ppermute | solution.py:298
  402.6 5.4 %shard_map.134 = (bf16[2,128,512]{2,1,0:T(8,128)(2,1)}, bf16[2,128,512]{2,1,0:T(8,128)(2,1)}) custom-call(bf16[16,16,32,256]{3,2,1,0:T(8,128)(2,1)} %all-to-all-done.2.arrived, bf16[4096,512]{1,0:T(8,128)(2,1)} %get-tuple-element.31.turned, f32[512,512]{1,0:T(8,128)} %get-tuple-element.32.direct, f32[1,1]{1,0:T(1,128)} %constant.77.clone.1.factor, ...), custom_call_target="tpu_custom_call" | custom-call | flops 2200000000 | bytes 9961472 | tf_op jit(solution)/shard_map/pallas_call | solution.py:477
  408.1 3.8 shard_map.135.rest_1_
  420.2 3.7 shard_map.136.rest_1_
  424.5 2.0 collective-permute-start.7
  426.8 3.8 shard_map.137.rest_1_
  430.6 1.9 collective-permute-done.7
  433.9 3.7 shard_map.138
  (79 shorter events, 21.6 us)
Async XLA Ops:
  6.2 85.1 %all-to-all-start.1 = ((bf16[16,16,32,256]{3,2,1,0:T(8,128)(2,1)}), bf16[16,16,32,256]{3,2,1,0:T(8,128)(2,1)}, u32[]{:S(2)}, u32[]{:S(2)}) async-start(bf16[16,16,32,256]{3,2,1,0:T(8,128)(2,1)} %shard_map.130), calls=%async_computation.1 | async-start | bytes 8388608 | tf_op jit(solution)/shard_map/all_to_all | solution.py:362
  91.3 19.8 %copy-start.6 = (bf16[256,256]{1,0:T(8,128)(2,1)S(1)}, bf16[256,256]{1,0:T(8,128)(2,1)}, u32[]{:S(2)}) copy-start(bf16[256,256]{1,0:T(8,128)(2,1)} %first.1) | copy-start | bytes 393220
  91.3 97.5 %all-to-all-start = ((bf16[16,16,32,256]{3,2,1,0:T(8,128)(2,1)}), bf16[16,16,32,256]{3,2,1,0:T(8,128)(2,1)}, u32[]{:S(2)}, u32[]{:S(2)}) async-start(bf16[16,16,32,256]{3,2,1,0:T(8,128)(2,1)} %get-tuple-element.21), calls=%async_computation | async-start | bytes 8388608 | tf_op jit(solution)/shard_map/all_to_all | solution.py:362
  188.9 19.8 %copy-start.7 = (bf16[256,256]{1,0:T(8,128)(2,1)S(1)}, bf16[256,256]{1,0:T(8,128)(2,1)}, u32[]{:S(2)}) copy-start(bf16[256,256]{1,0:T(8,128)(2,1)} %second.1) | copy-start | bytes 393220
  188.9 20.6 %copy-start.8 = (bf16[256,256]{1,0:T(8,128)(2,1)S(1)}, bf16[256,256]{1,0:T(8,128)(2,1)}, u32[]{:S(2)}) copy-start(bf16[256,256]{1,0:T(8,128)(2,1)} %third.1) | copy-start | bytes 393220
  188.9 97.5 %all-to-all-start.3 = ((bf16[16,16,32,256]{3,2,1,0:T(8,128)(2,1)}), bf16[16,16,32,256]{3,2,1,0:T(8,128)(2,1)}, u32[]{:S(2)}, u32[]{:S(2)}) async-start(bf16[16,16,32,256]{3,2,1,0:T(8,128)(2,1)} %bitcast.59), calls=%async_computation.3 | async-start | bytes 8388608 | tf_op jit(solution)/shard_map/all_to_all | solution.py:362
  286.4 19.9 %copy-start.9 = (f32[1,512]{1,0:T(1,128)S(1)}, f32[1,512]{1,0:T(1,128)}, u32[]{:S(2)}) copy-start(f32[1,512]{1,0:T(1,128)} %get-tuple-element.34) | copy-start | bytes 6148
  286.4 115.7 %all-to-all-start.2 = ((bf16[16,16,32,256]{3,2,1,0:T(8,128)(2,1)}), bf16[16,16,32,256]{3,2,1,0:T(8,128)(2,1)}, u32[]{:S(2)}, u32[]{:S(2)}) async-start(bf16[16,16,32,256]{3,2,1,0:T(8,128)(2,1)} %bitcast.58), calls=%async_computation.2 | async-start | bytes 8388608 | tf_op jit(solution)/shard_map/all_to_all | solution.py:362
  321.7 1.7 collective-permute-start
  323.5 12.8 %collective-permute-start.1 = (bf16[2,2,32,640]{3,2,0,1:T(8,128)(2,1)S(1)}, bf16[2,2,32,640]{3,2,0,1:T(8,128)(2,1)S(1)}, u32[]{:S(2)}, u32[]{:S(2)}) collective-permute-start(bf16[2,2,32,640]{3,2,0,1:T(8,128)(2,1)S(1)} %dynamic-slice_bitcast_fusion), channel_id=1, source_target_pairs={{0,2},{1,3},{2,0},{3,1},{4,6},{5,7},{6,4},{7,5},{8,10},{9,11},{10,... | collective-permute-start | bytes 491528 | tf_op jit(solution)/shard_map/ppermute | solution.py:298
  336.3 40.2 %collective-permute-start.2 = (bf16[2,32,640]{2,1,0:T(8,128)(2,1)S(1)}, bf16[2,32,640]{2,1,0:T(8,128)(2,1)S(1)}, u32[]{:S(2)}, u32[]{:S(2)}) collective-permute-start(bf16[2,32,640]{2,1,0:T(8,128)(2,1)S(1)} %dynamic-slice_bitcast_fusion.2), channel_id=1, source_target_pairs={{0,4},{1,5},{2,6},{3,7},{4,0},{5,1},{6,2},{7,3},{8,12},{9,13},{10,... | collective-permute-start | bytes 245768 | tf_op jit(solution)/shard_map/ppermute | solution.py:298
  376.6 25.4 %collective-permute-start.3 = (bf16[32,640]{1,0:T(8,128)(2,1)S(1)}, bf16[32,640]{1,0:T(8,128)(2,1)S(1)}, u32[]{:S(2)}, u32[]{:S(2)}) collective-permute-start(bf16[32,640]{1,0:T(8,128)(2,1)S(1)} %dynamic-slice_bitcast_fusion.3), channel_id=1, source_target_pairs={{0,8},{1,9},{2,10},{3,11},{4,12},{5,13},{6,14},{7,15},{8,0},{9,1},... | collective-permute-start | bytes 122888 | tf_op jit(solution)/shard_map/ppermute | solution.py:298
  402.0 9.9 %collective-permute-start.10 = (bf16[32,640]{1,0:T(8,128)(2,1)S(1)}, bf16[32,640]{1,0:T(8,128)(2,1)S(1)}, u32[]{:S(2)}, u32[]{:S(2)}) collective-permute-start(bf16[32,640]{1,0:T(8,128)(2,1)S(1)} %fusion.17._), channel_id=1, source_target_pairs={{0,8},{1,9},{2,10},{3,11},{4,12},{5,13},{6,14},{7,15},{8,0},{9,1},... | collective-permute-start | bytes 122888 | tf_op jit(solution)/shard_map/ppermute | solution.py:298
  408.0 5.6 %collective-permute-start.4 = (bf16[2,128,512]{2,1,0:T(8,128)(2,1)}, bf16[2,128,512]{2,1,0:T(8,128)(2,1)S(1)}, u32[]{:S(2)}, u32[]{:S(2)}) collective-permute-start(bf16[2,128,512]{2,1,0:T(8,128)(2,1)} %get-tuple-element.36.rest_0_), channel_id=1, source_target_pairs={{0,1},{1,0},{2,3},{3,2},{4,5},{5,4},{6,7},{7,6},{8,9},{9,8},{10,11... | collective-permute-start | bytes 786440 | tf_op jit(solution)/shard_map/ppermute | solution.py:298
  412.0 4.9 %collective-permute-start.11 = (bf16[2,32,640]{2,1,0:T(8,128)(2,1)S(1)}, bf16[2,32,640]{2,1,0:T(8,128)(2,1)S(1)}, u32[]{:S(2)}, u32[]{:S(2)}) collective-permute-start(bf16[2,32,640]{2,1,0:T(8,128)(2,1)S(1)} %fusion.16), channel_id=1, source_target_pairs={{0,4},{1,5},{2,6},{3,7},{4,0},{5,1},{6,2},{7,3},{8,12},{9,13},{10,... | collective-permute-start | bytes 245768 | tf_op jit(solution)/shard_map/ppermute | solution.py:298
  413.7 6.4 %copy-start.4 = (bf16[128,512]{1,0:T(8,128)(2,1)}, bf16[128,512]{1,0:T(8,128)(2,1)S(1)}, u32[]{:S(2)}) copy-start(bf16[128,512]{1,0:T(8,128)(2,1)S(1)} %dynamic-slice_bitcast_fusion.1.rest_0_) | copy-start | bytes 393220
  413.7 5.7 %collective-permute-start.5 = (bf16[128,512]{1,0:T(8,128)(2,1)S(1)}, bf16[128,512]{1,0:T(8,128)(2,1)S(1)}, u32[]{:S(2)}, u32[]{:S(2)}) collective-permute-start(bf16[128,512]{1,0:T(8,128)(2,1)S(1)} %dynamic-slice_bitcast_fusion.1.rest_0_), channel_id=1, source_target_pairs={{0,2},{1,3},{2,0},{3,1},{4,6},{5,7},{6,4},{7,5},{8,10},{9,11},{10,... | collective-permute-start | bytes 393224 | tf_op jit(solution)/shard_map/ppermute | solution.py:298
  417.0 6.9 %collective-permute-start.12 = (bf16[2,2,32,640]{3,2,0,1:T(8,128)(2,1)S(1)}, bf16[2,2,32,640]{3,2,0,1:T(8,128)(2,1)S(1)}, u32[]{:S(2)}, u32[]{:S(2)}) collective-permute-start(bf16[2,2,32,640]{3,2,0,1:T(8,128)(2,1)S(1)} %fusion.13), channel_id=1, source_target_pairs={{0,2},{1,3},{2,0},{3,1},{4,6},{5,7},{6,4},{7,5},{8,10},{9,11},{10,... | collective-permute-start | bytes 491528 | tf_op jit(solution)/shard_map/ppermute | solution.py:298
  419.4 5.0 %collective-permute-start.6 = (bf16[128,512]{1,0:T(8,128)(2,1)S(1)}, bf16[128,512]{1,0:T(8,128)(2,1)S(1)}, u32[]{:S(2)}, u32[]{:S(2)}) collective-permute-start(bf16[128,512]{1,0:T(8,128)(2,1)S(1)} %fusion.10.rest_0_), channel_id=1, source_target_pairs={{0,4},{1,5},{2,6},{3,7},{4,0},{5,1},{6,2},{7,3},{8,12},{9,13},{10,... | collective-permute-start | bytes 393224 | tf_op jit(solution)/shard_map/ppermute | solution.py:298
  424.5 7.9 %copy-start = (bf16[128,512]{1,0:T(8,128)(2,1)}, bf16[128,512]{1,0:T(8,128)(2,1)S(1)}, u32[]{:S(2)}) copy-start(bf16[128,512]{1,0:T(8,128)(2,1)S(1)} %add_convert_fusion.2.rest_0_) | copy-start | bytes 393220
  424.5 7.9 %collective-permute-start.7 = (bf16[128,512]{1,0:T(8,128)(2,1)S(1)}, bf16[128,512]{1,0:T(8,128)(2,1)S(1)}, u32[]{:S(2)}, u32[]{:S(2)}) collective-permute-start(bf16[128,512]{1,0:T(8,128)(2,1)S(1)} %add_convert_fusion.2.rest_0_), channel_id=1, source_target_pairs={{0,8},{1,9},{2,10},{3,11},{4,12},{5,13},{6,14},{7,15},{8,0},{9,1},... | collective-permute-start | bytes 393224 | tf_op jit(solution)/shard_map/ppermute | solution.py:298
  426.7 11.0 %collective-permute-start.13 = (bf16[2,2,2,32,640]{4,3,0,1,2:T(8,128)(2,1)S(1)}, bf16[2,2,2,32,640]{4,3,0,1,2:T(8,128)(2,1)S(1)}, u32[]{:S(2)}, u32[]{:S(2)}) collective-permute-start(bf16[2,2,2,32,640]{4,3,0,1,2:T(8,128)(2,1)S(1)} %fusion.6), channel_id=1, source_target_pairs={{0,1},{1,0},{2,3},{3,2},{4,5},{5,4},{6,7},{7,6},{8,9},{9,8},{10,11... | collective-permute-start | bytes 983048 | tf_op jit(solution)/shard_map/ppermute | solution.py:298
  432.5 5.6 %collective-permute-start.8 = (bf16[128,512]{1,0:T(8,128)(2,1)S(1)}, bf16[128,512]{1,0:T(8,128)(2,1)S(1)}, u32[]{:S(2)}, u32[]{:S(2)}) collective-permute-start(bf16[128,512]{1,0:T(8,128)(2,1)S(1)} %add_convert_fusion.1), channel_id=1, source_target_pairs={{0,2},{1,3},{2,0},{3,1},{4,6},{5,7},{6,4},{7,5},{8,10},{9,11},{10,... | collective-permute-start | bytes 393224 | tf_op jit(solution)/shard_map/ppermute | solution.py:298
  438.3 1.6 collective-permute-start.9
  (4 other events, 15.0 us)
